TPU v7x, 32 devices: a whole 2x2x4 slice. The times are simulated.
32 devices in a mesh: dp: 8 (over z, y), tensor: 4 (over x, core).
Axes of the slice: x: 2, y: 2, z: 4, core: 2. Of those that a mesh axis runs over, the one named last changes fastest.
Arguments:
- block_in: bfloat16 [20480, 1024], P(('dp', 'tensor')), may hold values from -6 to 6
- encoder_out: bfloat16 [8192, 1024], P(('dp', 'tensor')), may hold values from -6 to 6
- out_grad: bfloat16 [20480, 1024], P(('dp', 'tensor')), may hold values from -6 to 6
- bounds: int32 [8, 2], P('dp'), may hold values from 1024 to 2304, as said below
- enc_lengths: int32 [8], P('dp'), may hold values from 512 to 1024, as said below
- norm_params: float32 [3, 2, 1024], replicated, may hold values from -0.3 to 1.4, as said below
- w_qkv: bfloat16 [1024, 3, 1024], P('dp', None, 'tensor'), may hold values from -0.1875 to 0.1875
- w_self_out: bfloat16 [1024, 1024], P('tensor', 'dp'), may hold values from -0.375 to 0.375
- w_cross_q: bfloat16 [1024, 1024], P('dp', 'tensor'), may hold values from -0.1875 to 0.1875
- w_cross_kv: bfloat16 [1024, 2, 1024], P('dp', None, 'tensor'), may hold values from -0.1875 to 0.1875
- w_cross_out: bfloat16 [1024, 1024], P('tensor', 'dp'), may hold values from -0.375 to 0.375
- w_up: bfloat16 [1024, 4096], P('dp', 'tensor'), may hold values from -0.1875 to 0.1875
- w_down: bfloat16 [4096, 1024], P('tensor', 'dp'), may hold values from -0.09375 to 0.09375
- biases: float32 [7, 1024], replicated, may hold values from -1 to 1
- up_bias: float32 [4096], replicated, may hold values from -1 to 1
Outputs:
- output: float32 [20480, 1024], P(('dp', 'tensor'))
- input_grad: float32 [20480, 1024], P(('dp', 'tensor'))
- encoder_grad: float32 [8192, 1024], P(('dp', 'tensor'))
- grad_norm_params: float32 [3, 2, 1024], replicated
- grad_qkv: float32 [1024, 3, 1024], P('dp', None, 'tensor')
- grad_self_out: float32 [1024, 1024], P('tensor', 'dp')
- grad_cross_q: float32 [1024, 1024], P('dp', 'tensor')
- grad_cross_kv: float32 [1024, 2, 1024], P('dp', None, 'tensor')
- grad_cross_out: float32 [1024, 1024], P('tensor', 'dp')
- grad_up: float32 [1024, 4096], P('dp', 'tensor')
- grad_down: float32 [4096, 1024], P('tensor', 'dp')
- grad_biases: float32 [7, 1024], replicated
- grad_up_bias: float32 [4096], replicated
Inputs may be any that keep to these rules, and one draw needn't show every extreme that they name: bounds[g, 0] is the length of group g's prompt, between 1024 and 2048, and equals 2048 in some group; the 2 continuations that follow are of equal length, rise in position and fill the group's 2560 tokens. Group g's valid encoder outputs are its first enc_lengths[g] rows; some group has all 1024. norm_params[i, 0] are gains, norm_params[i, 1] shifts.
All inputs are finite; a program needn't handle non-finite values.
Results may differ from a plain program's by a relative error of at most 0.02.
Values may be sent and summed in bfloat16 or wider, within the bound.
A program may use at most 256 MiB of HBM per device.

v0:
```python
import math

import jax
import jax.numpy as jnp
from jax import lax
from jax.sharding import PartitionSpec as P

H = 16


EPSILON = 1e-05
NEGATIVE = -1e30


def layer_norm(inputs, gain_row, shift_row):
    center = inputs - jnp.mean(inputs, axis=-1, keepdims=True)
    spread = jnp.mean(center * center, axis=-1, keepdims=True)
    return center * lax.rsqrt(spread + EPSILON) * gain_row + shift_row


def gelu_slope(values_in):
    normal_cdf = 0.5 * (1.0 + lax.erf(values_in * (1.0 / math.sqrt(2.0))))
    density = jnp.exp(-0.5 * values_in * values_in) * (1.0 / math.sqrt(2.0 * math.pi))
    return normal_cdf + values_in * density


def widen(row_block):
    return lax.all_gather(row_block, "tensor", axis=0, tiled=True)


def narrow(row_terms):
    return lax.psum_scatter(row_terms, "tensor", scatter_dimension=0, tiled=True)


def self_rule(bound_row, row_total):
    columns = jnp.arange(row_total, dtype=jnp.int32)
    prompt_len = bound_row[0]

    def segment(places):
        return jnp.sum((places[:, None] >= bound_row[None, :]).astype(jnp.int32), axis=-1)

    column_segment = segment(columns)

    def allowed(row_places):
        causal = columns[None, :] <= row_places[:, None]
        shared = (columns[None, :] < prompt_len) | (
            column_segment[None, :] == segment(row_places)[:, None]
        )
        return causal & shared

    return allowed


def cross_rule(enc_limit, row_total):
    columns = jnp.arange(row_total, dtype=jnp.int32)

    def allowed(row_places):
        return jnp.broadcast_to(columns[None, :] < enc_limit, (row_places.shape[0], row_total))

    return allowed


def attend_forward(queries, key_rows, value_rows, allowed_fn, heads):
    row_count, width = queries.shape
    head_size = width // heads
    block_rows = min(512, row_count)
    block_count = row_count // block_rows
    score_scale = 1.0 / math.sqrt(head_size)
    key_heads = key_rows.reshape(key_rows.shape[0], heads, head_size)
    value_heads = value_rows.reshape(value_rows.shape[0], heads, head_size)
    query_blocks = queries.reshape(block_count, block_rows, heads, head_size)
    block_starts = jnp.arange(block_count, dtype=jnp.int32) * block_rows

    def one_block(operands):
        query_block, block_start = operands
        scores = (
            jnp.einsum("qhd,khd->hqk", query_block, key_heads, preferred_element_type=jnp.float32)
            * score_scale
        )
        allowed = allowed_fn(block_start + jnp.arange(block_rows, dtype=jnp.int32))
        scores = jnp.where(allowed[None], scores, NEGATIVE)
        largest = jnp.max(scores, axis=-1, keepdims=True)
        expos = jnp.exp(scores - largest)
        row_sums = jnp.sum(expos, axis=-1, keepdims=True)
        weights = (expos / row_sums).astype(jnp.bfloat16)
        result = jnp.einsum(
            "hqk,khd->qhd", weights, value_heads, preferred_element_type=jnp.float32
        )
        return (result.astype(jnp.bfloat16), (largest + jnp.log(row_sums))[..., 0])

    results, log_sums = lax.map(one_block, (query_blocks, block_starts))
    return (results.reshape(row_count, width), log_sums)


def attend_backward(queries, key_rows, value_rows, mixed_grad, log_sums, allowed_fn, heads):
    row_count, width = queries.shape
    head_size = width // heads
    block_rows = min(512, row_count)
    block_count = row_count // block_rows
    score_scale = 1.0 / math.sqrt(head_size)
    key_heads = key_rows.reshape(key_rows.shape[0], heads, head_size)
    value_heads = value_rows.reshape(value_rows.shape[0], heads, head_size)
    query_blocks = queries.reshape(block_count, block_rows, heads, head_size)
    grad_blocks = mixed_grad.reshape(block_count, block_rows, heads, head_size)
    block_starts = jnp.arange(block_count, dtype=jnp.int32) * block_rows

    def one_block(carried, operands):
        key_grad, value_grad = carried
        query_block, grad_block, block_start, lse_block = operands
        scores = (
            jnp.einsum("qhd,khd->hqk", query_block, key_heads, preferred_element_type=jnp.float32)
            * score_scale
        )
        allowed = allowed_fn(block_start + jnp.arange(block_rows, dtype=jnp.int32))
        scores = jnp.where(allowed[None], scores, NEGATIVE)
        weights = jnp.exp(scores - lse_block[..., None])
        weights_low = weights.astype(jnp.bfloat16)
        weight_grad = jnp.einsum(
            "qhd,khd->hqk", grad_block, value_heads, preferred_element_type=jnp.float32
        )
        row_inner = jnp.sum(weights * weight_grad, axis=-1, keepdims=True)
        score_grad = (weights * (weight_grad - row_inner)).astype(jnp.bfloat16)
        query_grad = (
            jnp.einsum("hqk,khd->qhd", score_grad, key_heads, preferred_element_type=jnp.float32)
            * score_scale
        )
        key_grad = (
            key_grad
            + jnp.einsum(
                "hqk,qhd->khd", score_grad, query_block, preferred_element_type=jnp.float32
            )
            * score_scale
        )
        value_grad = value_grad + jnp.einsum(
            "hqk,qhd->khd", weights_low, grad_block, preferred_element_type=jnp.float32
        )
        return ((key_grad, value_grad), query_grad)

    zero_grad = jnp.zeros((key_rows.shape[0], heads, head_size), jnp.float32)
    (key_grad, value_grad), query_grad = lax.scan(
        one_block, (zero_grad, zero_grad), (query_blocks, grad_blocks, block_starts, log_sums)
    )
    return (
        query_grad.reshape(row_count, width).astype(jnp.bfloat16),
        key_grad.reshape(key_rows.shape[0], width).astype(jnp.bfloat16),
        value_grad.reshape(key_rows.shape[0], width).astype(jnp.bfloat16),
    )


def on_device(
    block_in,
    encoder_out,
    out_grad,
    bounds,
    enc_lengths,
    norm_params,
    w_qkv,
    w_self_out,
    w_cross_q,
    w_cross_kv,
    w_cross_out,
    w_up,
    w_down,
    biases,
    up_bias,
):
    members = lax.axis_size("tensor")
    member = lax.axis_index("tensor")
    group_count = float(lax.axis_size("dp"))
    full_qkv, full_self_out, full_cross_q, full_cross_kv, full_cross_out, full_up, full_down = (
        lax.all_gather(w_qkv, "dp", axis=0, tiled=True),
        lax.all_gather(w_self_out, "dp", axis=1, tiled=True),
        lax.all_gather(w_cross_q, "dp", axis=0, tiled=True),
        lax.all_gather(w_cross_kv, "dp", axis=0, tiled=True),
        lax.all_gather(w_cross_out, "dp", axis=1, tiled=True),
        lax.all_gather(w_up, "dp", axis=0, tiled=True),
        lax.all_gather(w_down, "dp", axis=1, tiled=True),
    )
    local_width = full_self_out.shape[0]
    local_hidden = full_up.shape[1]
    heads = H // members
    own_rows = block_in.shape[0]

    def local_slice(vector, width):
        return lax.dynamic_slice_in_dim(vector, member * width, width)

    def placed(local_sum, full_width, width):
        return lax.dynamic_update_slice_in_dim(
            jnp.zeros((full_width,), jnp.float32), local_sum, member * width, 0
        )

    def collect(row_terms):
        return narrow(row_terms)

    def spread(row_low):
        return widen(row_low)

    def norm_back(rows, incoming, which):
        _, pull_rows = jax.vjp(layer_norm, rows, norm_params[which, 0], norm_params[which, 1])
        rows_grad, gain_grad, shift_grad = pull_rows(incoming)
        return (rows_grad, gain_grad, shift_grad)

    model_width = block_in.shape[1]
    row_total = own_rows * members
    enc_total = encoder_out.shape[0] * members
    self_mask = self_rule(bounds[0], row_total)
    cross_mask = cross_rule(enc_lengths[0], enc_total)
    start_rows = block_in.astype(jnp.float32)
    first_in = spread(
        layer_norm(start_rows, norm_params[0, 0], norm_params[0, 1]).astype(jnp.bfloat16)
    )
    projected = jnp.einsum("nd,dke->nke", first_in, full_qkv, preferred_element_type=jnp.float32)
    queries = (projected[:, 0] + local_slice(biases[0], local_width)).astype(jnp.bfloat16)
    key_rows = projected[:, 1].astype(jnp.bfloat16)
    value_rows = (projected[:, 2] + local_slice(biases[1], local_width)).astype(jnp.bfloat16)
    self_mixed, self_lse = attend_forward(queries, key_rows, value_rows, self_mask, heads)
    after_self = (
        start_rows
        + collect(jnp.dot(self_mixed, full_self_out, preferred_element_type=jnp.float32))
        + biases[2]
    )
    second_in = spread(
        layer_norm(after_self, norm_params[1, 0], norm_params[1, 1]).astype(jnp.bfloat16)
    )
    cross_queries = (
        jnp.dot(second_in, full_cross_q, preferred_element_type=jnp.float32)
        + local_slice(biases[3], local_width)
    ).astype(jnp.bfloat16)
    enc_all = lax.all_gather(encoder_out, "tensor", axis=0, tiled=True)
    cross_proj = jnp.einsum(
        "nd,dke->nke", enc_all, full_cross_kv, preferred_element_type=jnp.float32
    )
    cross_keys = cross_proj[:, 0].astype(jnp.bfloat16)
    cross_values = (cross_proj[:, 1] + local_slice(biases[4], local_width)).astype(jnp.bfloat16)
    cross_mixed, cross_lse = attend_forward(
        cross_queries, cross_keys, cross_values, cross_mask, heads
    )
    after_cross = (
        after_self
        + collect(jnp.dot(cross_mixed, full_cross_out, preferred_element_type=jnp.float32))
        + biases[5]
    )
    third_in = spread(
        layer_norm(after_cross, norm_params[2, 0], norm_params[2, 1]).astype(jnp.bfloat16)
    )
    pre_act = jnp.dot(third_in, full_up, preferred_element_type=jnp.float32) + local_slice(
        up_bias, local_hidden
    )
    hidden = jax.nn.gelu(pre_act, approximate=False).astype(jnp.bfloat16)
    output = (
        after_cross
        + collect(jnp.dot(hidden, full_down, preferred_element_type=jnp.float32))
        + biases[6]
    )
    back_qkv, back_self_out, back_cross_q, back_cross_kv, back_cross_out, back_up, back_down = (
        full_qkv,
        full_self_out,
        full_cross_q,
        full_cross_kv,
        full_cross_out,
        full_up,
        full_down,
    )
    bias_down_grad = jnp.sum(out_grad.astype(jnp.float32), axis=0)
    ffn_wide = widen(out_grad)
    cot_rows = out_grad.astype(jnp.float32)
    grad_down = jnp.einsum("nf,nd->fd", hidden, ffn_wide, preferred_element_type=jnp.float32)
    hidden_grad = jnp.einsum("nd,fd->nf", ffn_wide, back_down, preferred_element_type=jnp.float32)
    pre_grad = (hidden_grad * gelu_slope(pre_act)).astype(jnp.bfloat16)
    bias_up_grad = jnp.sum(pre_grad.astype(jnp.float32), axis=0)
    grad_up = jnp.einsum("nd,nf->df", third_in, pre_grad, preferred_element_type=jnp.float32)
    third_grad = collect(
        jnp.einsum("nf,df->nd", pre_grad, back_up, preferred_element_type=jnp.float32)
    )
    rows_three, gain_three, shift_three = norm_back(after_cross, third_grad, 2)
    cross_rows_grad = cot_rows + rows_three
    cross_low = cross_rows_grad.astype(jnp.bfloat16)
    bias_co_grad = jnp.sum(cross_low.astype(jnp.float32), axis=0)
    cross_wide = spread(cross_low)
    grad_cross_out = jnp.einsum(
        "nc,nd->cd", cross_mixed, cross_wide, preferred_element_type=jnp.float32
    )
    cross_mixed_grad = jnp.einsum(
        "nd,cd->nc", cross_wide, back_cross_out, preferred_element_type=jnp.float32
    ).astype(jnp.bfloat16)
    cross_dq, cross_dk, cross_dv = attend_backward(
        cross_queries, cross_keys, cross_values, cross_mixed_grad, cross_lse, cross_mask, heads
    )
    bias_cq_grad = jnp.sum(cross_dq.astype(jnp.float32), axis=0)
    bias_cv_grad = jnp.sum(cross_dv.astype(jnp.float32), axis=0)
    grad_cross_q = jnp.einsum("nd,nc->dc", second_in, cross_dq, preferred_element_type=jnp.float32)
    cross_kv_grad = jnp.stack([cross_dk, cross_dv], axis=1)
    grad_cross_kv = jnp.einsum(
        "nd,nkc->dkc", enc_all, cross_kv_grad, preferred_element_type=jnp.float32
    )
    encoder_grad = lax.psum_scatter(
        jnp.einsum(
            "nkc,dkc->nd", cross_kv_grad, back_cross_kv, preferred_element_type=jnp.float32
        ).astype(jnp.bfloat16),
        "tensor",
        scatter_dimension=0,
        tiled=True,
    ).astype(jnp.float32)
    second_grad = collect(
        jnp.einsum("nc,dc->nd", cross_dq, back_cross_q, preferred_element_type=jnp.float32)
    )
    rows_two, gain_two, shift_two = norm_back(after_self, second_grad, 1)
    self_rows_grad = cross_rows_grad + rows_two
    self_low = self_rows_grad.astype(jnp.bfloat16)
    bias_so_grad = jnp.sum(self_low.astype(jnp.float32), axis=0)
    self_wide = spread(self_low)
    grad_self_out = jnp.einsum(
        "nc,nd->cd", self_mixed, self_wide, preferred_element_type=jnp.float32
    )
    self_mixed_grad = jnp.einsum(
        "nd,cd->nc", self_wide, back_self_out, preferred_element_type=jnp.float32
    ).astype(jnp.bfloat16)
    self_dq, self_dk, self_dv = attend_backward(
        queries, key_rows, value_rows, self_mixed_grad, self_lse, self_mask, heads
    )
    bias_q_grad = jnp.sum(self_dq.astype(jnp.float32), axis=0)
    bias_v_grad = jnp.sum(self_dv.astype(jnp.float32), axis=0)
    qkv_grad = jnp.stack([self_dq, self_dk, self_dv], axis=1)
    grad_qkv = jnp.einsum("nd,nkc->dkc", first_in, qkv_grad, preferred_element_type=jnp.float32)
    first_grad = collect(
        jnp.einsum("nkc,dkc->nd", qkv_grad, back_qkv, preferred_element_type=jnp.float32)
    )
    rows_one, gain_one, shift_one = norm_back(start_rows, first_grad, 0)
    input_grad = self_rows_grad + rows_one
    norm_terms = jnp.stack(
        [
            jnp.stack([gain_one, shift_one]),
            jnp.stack([gain_two, shift_two]),
            jnp.stack([gain_three, shift_three]),
        ]
    )
    bias_terms = jnp.stack(
        [
            placed(bias_q_grad, model_width, local_width),
            placed(bias_v_grad, model_width, local_width),
            bias_so_grad,
            placed(bias_cq_grad, model_width, local_width),
            placed(bias_cv_grad, model_width, local_width),
            bias_co_grad,
            bias_down_grad,
        ]
    )
    up_terms = placed(bias_up_grad, up_bias.shape[0], local_hidden)
    norm_total, bias_total, up_total = lax.psum(
        (norm_terms, bias_terms, up_terms), ("dp", "tensor")
    )
    (
        summed_qkv,
        summed_self_out,
        summed_cross_q,
        summed_cross_kv,
        summed_cross_out,
        summed_up,
        summed_down,
    ) = (
        lax.psum_scatter(grad_qkv, "dp", scatter_dimension=0, tiled=True),
        lax.psum_scatter(grad_self_out, "dp", scatter_dimension=1, tiled=True),
        lax.psum_scatter(grad_cross_q, "dp", scatter_dimension=0, tiled=True),
        lax.psum_scatter(grad_cross_kv, "dp", scatter_dimension=0, tiled=True),
        lax.psum_scatter(grad_cross_out, "dp", scatter_dimension=1, tiled=True),
        lax.psum_scatter(grad_up, "dp", scatter_dimension=0, tiled=True),
        lax.psum_scatter(grad_down, "dp", scatter_dimension=1, tiled=True),
    )
    return (
        output,
        input_grad,
        encoder_grad,
        norm_total / group_count,
        summed_qkv / group_count,
        summed_self_out / group_count,
        summed_cross_q / group_count,
        summed_cross_kv / group_count,
        summed_cross_out / group_count,
        summed_up / group_count,
        summed_down / group_count,
        bias_total / group_count,
        up_total / group_count,
    )


def solution(mesh):
    placed = (
        P(("dp", "tensor"), None),
        P(("dp", "tensor"), None),
        P(("dp", "tensor"), None),
        P("dp", None),
        P("dp"),
        P(),
        P("dp", None, "tensor"),
        P("tensor", "dp"),
        P("dp", "tensor"),
        P("dp", None, "tensor"),
        P("tensor", "dp"),
        P("dp", "tensor"),
        P("tensor", "dp"),
        P(),
        P(),
    )
    return jax.shard_map(
        on_device,
        mesh=mesh,
        in_specs=placed,
        out_specs=(
            P(("dp", "tensor"), None),
            P(("dp", "tensor"), None),
            P(("dp", "tensor"), None),
            P(),
            P("dp", None, "tensor"),
            P("tensor", "dp"),
            P("dp", "tensor"),
            P("dp", None, "tensor"),
            P("tensor", "dp"),
            P("dp", "tensor"),
            P("tensor", "dp"),
            P(),
            P(),
        ),
        check_vma=False,
    )
```

profile of v0, /device:TPU:0, one launch (start us, length us, event | category | flops | bytes accessed | tf_op | source)
XLA Modules:
  0.0 2095.6 jit_solution(2000178694717379922)
XLA Ops:
  15.1 32.3 %all_gather.44 = bf16[256,1024]{1,0:T(8,128)(2,1)} all-gather(bf16[256,128]{1,0:T(8,128)(2,1)S(1)} %copy-done.62), channel_id=1, replica_groups=mesh['dp'=8,'tensor'=4] {'dp'}, dimensions={1}, use_global_device_ids=true | all-gather | bytes 589824 | tf_op jit(solution)/shard_map/all_gather | solution.py:172
  47.5 14.3 all-gather.14.cloned.1.call-done
  61.7 41.4 %all-gather.12.cloned.1.call-done = bf16[2560,1024]{1,0:T(8,128)(2,1)} async-done(((bf16[640,1024]{1,0:T(8,128)(2,1)}), bf16[2560,1024]{1,0:T(8,128)(2,1)}) %all-gather.12.cloned.1.call-update) | async-done | bytes 5242896 | tf_op jit(solution)/shard_map/all_gather | solution.py:28
  103.1 6.7 fusion.114
  123.3 160.4 %while.59 = (s32[]{:T(128)}, bf16[5,512,4,64]{1,3,2,0:T(8,128)(2,1)S(1)}, f32[5,4,512]{2,1,0:T(4,128)S(1)}, s32[5]{0:T(128)S(1)}, s32[]{:T(128)S(1)}, /*index=5*...) while((s32[]{:T(128)}, ...), condition=%wide.region_7.8_spmd.clone.clone, body=%wide.region_3.7_spmd.clone.clone.sunk | while | flops 1410469376 | bytes 155280560 | solution.py:91
  132.3 7.0 copy-done
  145.0 10.3 fusion.269
  164.3 7.0 copy-done
  177.1 10.3 fusion.269
  196.4 7.0 copy-done
  209.1 10.3 fusion.269
  228.4 7.0 copy-done
  241.1 10.3 fusion.269
  260.4 7.0 copy-done
  273.2 10.3 fusion.269
  294.3 83.1 %reduce-scatter.15.cloned.1.call-done = f32[640,1024]{1,0:T(8,128)} async-done(((f32[2560,1024]{1,0:T(8,128)}), f32[640,1024]{1,0:T(8,128)}) %reduce-scatter.15.cloned.1.call-update) | async-done | bytes 2621456 | tf_op jit(solution)/shard_map/reduce_scatter | solution.py:32
  384.1 33.8 %all_gather.46 = bf16[1024,256]{1,0:T(8,128)(2,1)} all-gather(bf16[128,256]{1,0:T(8,128)(2,1)S(1)} %copy-done.63), channel_id=1, replica_groups=mesh['dp'=8,'tensor'=4] {'dp'}, dimensions={0}, use_global_device_ids=true | all-gather | bytes 589824 | tf_op jit(solution)/shard_map/all_gather | solution.py:173
  417.9 28.3 %all_gather.49 = bf16[256,1024]{1,0:T(8,128)(2,1)} all-gather(bf16[256,128]{1,0:T(8,128)(2,1)S(1)} %copy-done.64), channel_id=1, replica_groups=mesh['dp'=8,'tensor'=4] {'dp'}, dimensions={1}, use_global_device_ids=true | all-gather | bytes 589824 | tf_op jit(solution)/shard_map/all_gather | solution.py:175
  451.0 38.2 %all-gather.16.cloned.1.call-done = bf16[2560,1024]{1,0:T(8,128)(2,1)} async-done(((bf16[640,1024]{1,0:T(8,128)(2,1)}), bf16[2560,1024]{1,0:T(8,128)(2,1)}) %all-gather.16.cloned.1.call-update) | async-done | bytes 5242896 | tf_op jit(solution)/shard_map/all_gather | solution.py:28
  505.8 41.1 %while.58 = (s32[]{:T(128)}, bf16[5,512,4,64]{1,3,2,0:T(8,128)(2,1)}, f32[5,4,512]{2,1,0:T(4,128)S(1)}, s32[]{:T(128)}, bf16[5,512,4,64]{1,3,2,0:T(8,128)(2,1)},...) while((s32[]{:T(128)}, bf16[5,512,4,64]{1,3,2,0:T(8,128)(2,1)}, ...), condition=%wide.region_14.15_spmd.clone, body=%wide.region_11.14_spmd.clone.sunk | while | flops 562166784 | bytes 28905608 | solution.py:91
  557.2 84.7 %reduce-scatter.17.cloned.1.call-done = f32[640,1024]{1,0:T(8,128)} async-done(((f32[2560,1024]{1,0:T(8,128)}), f32[640,1024]{1,0:T(8,128)}) %reduce-scatter.17.cloned.1.call-update) | async-done | bytes 2621456 | tf_op jit(solution)/shard_map/reduce_scatter | solution.py:32
  649.1 44.2 %all-gather.24.cloned.1.call-done = bf16[1024,1024]{1,0:T(8,128)(2,1)} async-done(((bf16[128,1024]{1,0:T(8,128)(2,1)}), bf16[1024,1024]{1,0:T(8,128)(2,1)}) %all-gather.24.cloned.1.call-update) | async-done | bytes 2097168 | tf_op jit(solution)/shard_map/all_gather | solution.py:176
  693.3 41.1 %all-gather.22.cloned.1.call-done = bf16[2560,1024]{1,0:T(8,128)(2,1)} async-done(((bf16[640,1024]{1,0:T(8,128)(2,1)}), bf16[2560,1024]{1,0:T(8,128)(2,1)}) %all-gather.22.cloned.1.call-update) | async-done | bytes 5242896 | tf_op jit(solution)/shard_map/all_gather | solution.py:28
  734.4 31.4 %fusion.98 = (bf16[2560,1024]{1,0:T(8,128)(2,1)}, f32[2560,1024]{1,0:T(8,128)}) fusion(f32[1024]{0:T(1024)S(1)} %dynamic_slice.52, bf16[2560,1024]{1,0:T(8,128)(2,1)} %all-gather.22.cloned.1.call-done, bf16[1024,1024]{1,0:T(8,128)(2,1)} %all-gather.24.cloned.1.call-done), kind=kOutput, calls=%fused_computation.116 | convolution fusion | flops 5541724160 | bytes 23072768 | tf_op jit(solution)/shard_map/dot_general | solution.py:246
  765.8 21.6 %all-gather.26.cloned.1.call-done = bf16[1024,1024]{1,0:T(8,128)(2,1)} async-done(((bf16[1024,128]{1,0:T(8,128)(2,1)}), bf16[1024,1024]{1,0:T(8,128)(2,1)}) %all-gather.26.cloned.1.call-update) | async-done | bytes 2097168 | tf_op jit(solution)/shard_map/all_gather | solution.py:177
  787.4 40.2 %all-gather.28.cloned.1.call-done = bf16[2560,1024]{1,0:T(8,128)(2,1)} async-done(((bf16[640,1024]{1,0:T(8,128)(2,1)}), bf16[2560,1024]{1,0:T(8,128)(2,1)}) %all-gather.28.cloned.1.call-update) | async-done | bytes 5242896 | tf_op jit(solution)/shard_map/all_gather | solution.py:28
  827.6 13.1 convert_reduce_fusion
  843.0 8.4 fusion.163
  853.0 12.0 fusion.162
  865.1 71.8 %reduce-scatter.21.cloned.1.call-done = f32[640,1024]{1,0:T(8,128)} async-done(((f32[2560,1024]{1,0:T(8,128)}), f32[640,1024]{1,0:T(8,128)}) %reduce-scatter.21.cloned.1.call-update) | async-done | bytes 2621456 | tf_op jit(solution)/shard_map/reduce_scatter | solution.py:32
  940.2 84.7 %reduce-scatter.19.cloned.1.call-done = f32[640,1024]{1,0:T(8,128)} async-done(((f32[2560,1024]{1,0:T(8,128)}), f32[640,1024]{1,0:T(8,128)}) %reduce-scatter.19.cloned.1.call-update) | async-done | bytes 2621456 | tf_op jit(solution)/shard_map/reduce_scatter | solution.py:32
  1032.2 40.5 %all-gather.30.cloned.1.call-done = bf16[2560,1024]{1,0:T(8,128)(2,1)} async-done(((bf16[640,1024]{1,0:T(8,128)(2,1)}), bf16[2560,1024]{1,0:T(8,128)(2,1)}) %all-gather.30.cloned.1.call-update) | async-done | bytes 5242896 | tf_op jit(solution)/shard_map/all_gather | solution.py:28
  1084.3 78.0 %while.60 = (s32[]{:T(128)}, f32[1024,4,64]{0,2,1:T(8,128)S(1)}, f32[1024,4,64]{0,2,1:T(8,128)}, bf16[5,512,4,64]{1,3,2,0:T(8,128)(2,1)S(1)}, bf16[5,512,4,64]{1...) while((s32[]{:T(128)}, f32[1024,4,64]{0,2,1:T(8,128)S(1)}, ...), condition=%wide.region_24.25_spmd.clone, body=%wide.region_22.24_spmd.clone.sunk | while | flops 1375075328 | bytes 78704856 | solution.py:140
  1170.7 85.2 %reduce-scatter.23.cloned.1.call-done = f32[640,1024]{1,0:T(8,128)} async-done(((f32[2560,1024]{1,0:T(8,128)}), f32[640,1024]{1,0:T(8,128)}) %reduce-scatter.23.cloned.1.call-update) | async-done | bytes 2621456 | tf_op jit(solution)/shard_map/reduce_scatter | solution.py:32
  1264.7 10.6 fusion.168
  1275.3 10.5 fusion.169
  1325.5 347.3 %while.61 = (s32[]{:T(128)}, f32[2560,4,64]{0,2,1:T(8,128)}, f32[2560,4,64]{0,2,1:T(8,128)}, bf16[5,512,4,64]{1,3,2,0:T(8,128)(2,1)}, bf16[5,512,4,64]{1,3,2,0:T...) while((s32[]{:T(128)}, f32[2560,4,64]{0,2,1:T(8,128)}, ...), condition=%wide.region_31.32_spmd.clone.clone, body=%wide.region_28.31_spmd.clone.clone.sunk | while | flops 3442740736 | bytes 204817712 | solution.py:140
  1330.0 12.1 fusion.292
  1342.1 10.3 fusion.296
  1352.4 16.4 multiply_reduce_fusion.11
  1368.8 16.2 multiply_convert_fusion.5
  1398.9 12.1 fusion.292
  1411.0 10.1 fusion.296
  1421.2 16.7 multiply_reduce_fusion.11
  1437.8 16.1 multiply_convert_fusion.5
  1468.8 11.9 fusion.292
  1480.7 10.2 fusion.296
  1490.9 16.4 multiply_reduce_fusion.11
  1507.3 15.9 multiply_convert_fusion.5
  1538.1 11.8 fusion.292
  1549.9 10.1 fusion.296
  1560.0 16.4 multiply_reduce_fusion.11
  1576.4 16.0 multiply_convert_fusion.5
  1607.2 11.8 fusion.292
  1619.1 10.1 fusion.296
  1629.2 16.6 multiply_reduce_fusion.11
  1645.8 16.1 multiply_convert_fusion.5
  1687.8 10.5 convolution_bitcast_fusion
  1699.7 9.4 fusion.112
  1719.7 6.2 reduce-scatter.27.cloned.1.call-done
  1729.9 63.7 %reduce-scatter.31.cloned.1.call-done = f32[256,128]{1,0:T(8,128)} async-done(((f32[256,1024]{1,0:T(8,128)}), f32[256,128]{1,0:T(8,128)}) %reduce-scatter.31.cloned.1.call-update) | async-done | bytes 131088 | tf_op jit(solution)/shard_map/reduce_scatter | solution.py:362
  1795.2 85.2 %reduce-scatter.25.cloned.1.call-done = f32[640,1024]{1,0:T(8,128)} async-done(((f32[2560,1024]{1,0:T(8,128)}), f32[640,1024]{1,0:T(8,128)}) %reduce-scatter.25.cloned.1.call-update) | async-done | bytes 2621456 | tf_op jit(solution)/shard_map/reduce_scatter | solution.py:32
  1890.4 68.7 %reduce-scatter.29.cloned.1.call-done = f32[128,3,256]{2,0,1:T(8,128)} async-done(((f32[1024,3,256]{2,0,1:T(8,128)}), f32[128,3,256]{2,0,1:T(8,128)}) %reduce-scatter.29.cloned.1.call-update) | async-done | bytes 393232 | tf_op jit(solution)/shard_map/reduce_scatter | solution.py:361
  1960.8 123.9 %all-reduce.3.cloned.1.call-done = (f32[3,2,1024]{2,1,0:T(2,128)}, f32[7,1024]{1,0:T(8,128)}, f32[4096]{0:T(1024)}) async-done(((f32[3,2,1024]{2,1,0:T(2,128)}, f32[7,1024]{1,0:T(8,128)}, f32[4096]{0:T(1024)}), (f32[3,2,1024]{2,1,0:T(2,128)}, f32[7,1024]{1,0:T(8,128)}, f32[4096]{0:T(1024)})) %all-reduce.3.cloned.1.call-update) | async-done | bytes 69648 | tf_op jit(solution)/shard_map/psum | solution.py:349
  (573 shorter events, 472.3 us)
Async XLA Ops:
  7.2 54.5 %all-gather.14.cloned.1.call-start = ((), (), s32[]{:S(2)}) async-start(), calls=%async_computation.15 | async-start | bytes 1769472 | tf_op jit(solution)/shard_map/all_gather | solution.py:171
  9.1 94.0 %all-gather.12.cloned.1.call-start = ((), (), s32[]{:S(2)}) async-start(), calls=%async_computation.14 | async-start | bytes 6553600 | tf_op jit(solution)/shard_map/all_gather | solution.py:28
  11.9 98.0 %copy-start.54 = (f32[640]{0:T(1024)}, f32[640]{0:T(1024)S(1)}, u32[]{:S(2)}) copy-start(f32[640]{0:T(1024)S(1)} %fusion.138) | copy-start | bytes 7684
  12.5 97.3 %copy-start.50 = (f32[1,1,1024]{2,1,0:T(1,128)}, f32[1,1,1024]{2,1,0:T(1,128)S(1)}, u32[]{:S(2)}) copy-start(f32[1,1,1024]{2,1,0:T(1,128)S(1)} %get-tuple-element.719) | copy-start | bytes 12292
  14.1 363.3 %reduce-scatter.15.cloned.1.call-start = ((), (), s32[]{:S(2)}) async-start(), calls=%async_computation.16 | async-start | bytes 13107200 | tf_op jit(solution)/shard_map/reduce_scatter | solution.py:32
  291.9 85.5 %copy-start.77 = (f32[1,1024]{1,0:T(1,128)S(1)}, f32[1,1024]{1,0:T(1,128)}, u32[]{:S(2)}) copy-start(f32[1,1024]{1,0:T(1,128)} %get-tuple-element.711) | copy-start | bytes 12292
  292.0 154.3 %all-gather.20.cloned.1.call-start = ((), (), s32[]{:S(2)}) async-start(), calls=%async_computation.19 | async-start | bytes 1179648 | tf_op jit(solution)/shard_map/all_gather | solution.py:174
  293.6 153.1 %all-gather.18.cloned.1.call-start = ((), (), s32[]{:S(2)}) async-start(), calls=%async_computation.18 | async-start | bytes 2621440 | tf_op jit(solution)/shard_map/all_gather | solution.py:229
  294.2 195.0 %all-gather.16.cloned.1.call-start = ((), (), s32[]{:S(2)}) async-start(), calls=%async_computation.17 | async-start | bytes 6553600 | tf_op jit(solution)/shard_map/all_gather | solution.py:28
  379.9 261.9 %copy-start.2 = (f32[640,1024]{1,0:T(8,128)}, f32[640,1024]{1,0:T(8,128)S(1)}, u32[]{:S(2)}) copy-start(f32[640,1024]{1,0:T(8,128)S(1)} %get-tuple-element.694) | copy-start | bytes 7864324
  381.0 36.9 %copy-start.64 = (bf16[256,128]{1,0:T(8,128)(2,1)S(1)}, bf16[256,128]{1,0:T(8,128)(2,1)}, u32[]{:S(2)}) copy-start(bf16[256,128]{1,0:T(8,128)(2,1)} %param.33) | copy-start | bytes 196612
  382.6 259.3 %reduce-scatter.17.cloned.1.call-start = ((), (), s32[]{:S(2)}) async-start(), calls=%async_computation.20 | async-start | bytes 13107200 | tf_op jit(solution)/shard_map/reduce_scatter | solution.py:32
  556.3 85.5 %copy-start.76 = (f32[1,1024]{1,0:T(1,128)S(1)}, f32[1,1024]{1,0:T(1,128)}, u32[]{:S(2)}) copy-start(f32[1,1024]{1,0:T(1,128)} %get-tuple-element.714) | copy-start | bytes 12292
  556.4 136.9 %all-gather.24.cloned.1.call-start = ((), (), s32[]{:S(2)}) async-start(), calls=%async_computation.22 | async-start | bytes 2359296 | tf_op jit(solution)/shard_map/all_gather | solution.py:176
  557.1 177.3 %all-gather.22.cloned.1.call-start = ((), (), s32[]{:S(2)}) async-start(), calls=%async_computation.21 | async-start | bytes 6553600 | tf_op jit(solution)/shard_map/all_gather | solution.py:28
  647.0 140.4 %all-gather.26.cloned.1.call-start = ((), (), s32[]{:S(2)}) async-start(), calls=%async_computation.23 | async-start | bytes 2359296 | tf_op jit(solution)/shard_map/all_gather | solution.py:177
  647.6 180.0 %all-gather.28.cloned.1.call-start = ((), (), s32[]{:S(2)}) async-start(), calls=%async_computation.25 | async-start | bytes 6553600 | tf_op jit(solution)/shard_map/all_gather | solution.py:28
  648.3 288.6 %reduce-scatter.21.cloned.1.call-start = ((), (), s32[]{:S(2)}) async-start(), calls=%async_computation.26 | async-start | bytes 13107200 | tf_op jit(solution)/shard_map/reduce_scatter | solution.py:32
  827.6 15.4 copy-start.88
  851.5 173.4 %reduce-scatter.19.cloned.1.call-start = ((), (), s32[]{:S(2)}) async-start(), calls=%async_computation.24 | async-start | bytes 13107200 | tf_op jit(solution)/shard_map/reduce_scatter | solution.py:32
  865.1 71.9 %copy-start.7 = (f32[640,1024]{1,0:T(8,128)S(1)}, f32[640,1024]{1,0:T(8,128)}, u32[]{:S(2)}) copy-start(f32[640,1024]{1,0:T(8,128)} %copy-done.6) | copy-start | bytes 7864324
  865.1 159.8 %copy-start.75 = (f32[1,1024]{1,0:T(1,128)S(1)}, f32[1,1024]{1,0:T(1,128)}, u32[]{:S(2)}) copy-start(f32[1,1024]{1,0:T(1,128)} %get-tuple-element.708) | copy-start | bytes 12292
  865.1 207.6 %all-gather.30.cloned.1.call-start = ((), (), s32[]{:S(2)}) async-start(), calls=%async_computation.27 | async-start | bytes 6553600 | tf_op jit(solution)/shard_map/all_gather | solution.py:28
  1029.9 230.3 %copy-start.56 = (f32[640]{0:T(1024)}, f32[640]{0:T(1024)S(1)}, u32[]{:S(2)}) copy-start(f32[640]{0:T(1024)S(1)} %negate_multiply_fusion.3) | copy-start | bytes 7684
  1029.9 42.7 %copy-start.36 = (bf16[256,1024]{1,0:T(8,128)(2,1)S(1)}, bf16[256,1024]{1,0:T(8,128)(2,1)}, u32[]{:S(2)}) copy-start(bf16[256,1024]{1,0:T(8,128)(2,1)} %all_gather.49) | copy-start | bytes 1572868
  1032.1 223.9 %reduce-scatter.23.cloned.1.call-start = ((), (), s32[]{:S(2)}) async-start(), calls=%async_computation.28 | async-start | bytes 13107200 | tf_op jit(solution)/shard_map/reduce_scatter | solution.py:32
  1170.5 85.5 %copy-start.3 = (f32[640,1024]{1,0:T(8,128)S(1)}, f32[640,1024]{1,0:T(8,128)}, u32[]{:S(2)}) copy-start(f32[640,1024]{1,0:T(8,128)} %copy-done.2) | copy-start | bytes 7864324
  1170.5 85.5 %copy-start.53 = (f32[640]{0:T(1024)S(1)}, f32[640]{0:T(1024)}, u32[]{:S(2)}) copy-start(f32[640]{0:T(1024)} %copy-done.52) | copy-start | bytes 7684
  1170.5 85.5 %copy-start.59 = (f32[1,1,1024]{2,1,0:T(1,128)S(1)}, f32[1,1,1024]{2,1,0:T(1,128)}, u32[]{:S(2)}) copy-start(f32[1,1,1024]{2,1,0:T(1,128)} %get-tuple-element.717) | copy-start | bytes 12292
  1170.5 85.5 %copy-start.61 = (f32[640]{0:T(1024)S(1)}, f32[640]{0:T(1024)}, u32[]{:S(2)}) copy-start(f32[640]{0:T(1024)} %copy-done.60) | copy-start | bytes 7684
  1170.5 88.9 %copy-start.72 = (f32[640]{0:T(1024)S(1)}, f32[640]{0:T(1024)}, u32[]{:S(2)}) copy-start(f32[640]{0:T(1024)} %copy-done.71) | copy-start | bytes 7684
  1170.5 136.2 %all-gather.32.cloned.1.call-start = ((), (), s32[]{:S(2)}) async-start(), calls=%async_computation.29 | async-start | bytes 6553600 | tf_op jit(solution)/shard_map/all_gather | solution.py:28
  1264.6 445.7 %reduce-scatter.39.cloned.1.call-start = ((), (), s32[]{:S(2)}) async-start(), calls=%async_computation.37 | async-start | bytes 4718592 | tf_op jit(solution)/shard_map/reduce_scatter | solution.py:366
  1275.3 436.9 %reduce-scatter.41.cloned.1.call-start = ((), (), s32[]{:S(2)}) async-start(), calls=%async_computation.38 | async-start | bytes 4718592 | tf_op jit(solution)/shard_map/reduce_scatter | solution.py:367
  1285.8 428.8 %reduce-scatter.37.cloned.1.call-start = ((), (), s32[]{:S(2)}) async-start(), calls=%async_computation.36 | async-start | bytes 1179648 | tf_op jit(solution)/shard_map/reduce_scatter | solution.py:365
  1292.1 424.2 %reduce-scatter.33.cloned.1.call-start = ((), (), s32[]{:S(2)}) async-start(), calls=%async_computation.34 | async-start | bytes 1179648 | tf_op jit(solution)/shard_map/reduce_scatter | solution.py:363
  1297.5 420.4 %reduce-scatter.35.cloned.1.call-start = ((), (), s32[]{:S(2)}) async-start(), calls=%async_computation.35 | async-start | bytes 2359296 | tf_op jit(solution)/shard_map/reduce_scatter | solution.py:364
  1303.9 421.9 %reduce-scatter.27.cloned.1.call-start = ((), (), s32[]{:S(2)}) async-start(), calls=%async_computation.31 | async-start | bytes 2621440 | tf_op jit(solution)/shard_map/reduce_scatter | solution.py:296
  1306.6 487.0 %reduce-scatter.31.cloned.1.call-start = ((), (), s32[]{:S(2)}) async-start(), calls=%async_computation.33 | async-start | bytes 1179648 | tf_op jit(solution)/shard_map/reduce_scatter | solution.py:362
  1324.2 556.2 %reduce-scatter.25.cloned.1.call-start = ((), (), s32[]{:S(2)}) async-start(), calls=%async_computation.30 | async-start | bytes 13107200 | tf_op jit(solution)/shard_map/reduce_scatter | solution.py:32
  1330.0 22.4 %copy-start.1 = (pred[512,2560]{1,0:T(8,128)(4,1)}, pred[512,2560]{1,0:T(8,128)(4,1)S(1)}, u32[]{:S(2)}) copy-start(pred[512,2560]{1,0:T(8,128)(4,1)S(1)} %fusion.294) | copy-start | bytes 3932164 | tf_op jit(solution)/shard_map/while
  1330.0 12.1 copy-start.30
  1352.4 16.4 copy-start.31
  1398.9 22.3 %copy-start.1 = (pred[512,2560]{1,0:T(8,128)(4,1)}, pred[512,2560]{1,0:T(8,128)(4,1)S(1)}, u32[]{:S(2)}) copy-start(pred[512,2560]{1,0:T(8,128)(4,1)S(1)} %fusion.294) | copy-start | bytes 3932164 | tf_op jit(solution)/shard_map/while
  1398.9 12.1 copy-start.30
  1421.2 16.7 copy-start.31
  1468.8 22.2 %copy-start.1 = (pred[512,2560]{1,0:T(8,128)(4,1)}, pred[512,2560]{1,0:T(8,128)(4,1)S(1)}, u32[]{:S(2)}) copy-start(pred[512,2560]{1,0:T(8,128)(4,1)S(1)} %fusion.294) | copy-start | bytes 3932164 | tf_op jit(solution)/shard_map/while
  1468.8 11.9 copy-start.30
  1490.9 16.4 copy-start.31
  1538.0 22.0 %copy-start.1 = (pred[512,2560]{1,0:T(8,128)(4,1)}, pred[512,2560]{1,0:T(8,128)(4,1)S(1)}, u32[]{:S(2)}) copy-start(pred[512,2560]{1,0:T(8,128)(4,1)S(1)} %fusion.294) | copy-start | bytes 3932164 | tf_op jit(solution)/shard_map/while
  1560.0 16.4 copy-start.31
  1607.2 22.0 %copy-start.1 = (pred[512,2560]{1,0:T(8,128)(4,1)}, pred[512,2560]{1,0:T(8,128)(4,1)S(1)}, u32[]{:S(2)}) copy-start(pred[512,2560]{1,0:T(8,128)(4,1)S(1)} %fusion.294) | copy-start | bytes 3932164 | tf_op jit(solution)/shard_map/while
  1629.2 16.6 copy-start.31
  1698.4 260.7 %reduce-scatter.29.cloned.1.call-start = ((), (), s32[]{:S(2)}) async-start(), calls=%async_computation.32 | async-start | bytes 3538944 | tf_op jit(solution)/shard_map/reduce_scatter | solution.py:361
  1709.2 375.6 %all-reduce.3.cloned.1.call-start = ((), (), s32[]{:S(2)}) async-start(), calls=%async_computation.39 | async-start | bytes 147456 | tf_op jit(solution)/shard_map/psum | solution.py:349
  1710.3 17.7 copy-start.65
  1712.2 15.8 copy-start.80
  1712.2 15.8 copy-start.81
  1714.4 166.0 %copy-start.9 = (bf16[640,1024]{1,0:T(8,128)(2,1)S(1)}, bf16[640,1024]{1,0:T(8,128)(2,1)}, u32[]{:S(2)}) copy-start(bf16[640,1024]{1,0:T(8,128)(2,1)} %param.23) | copy-start | bytes 3932164
  1714.4 166.0 %copy-start.48 = (f32[640]{0:T(1024)S(1)}, f32[640]{0:T(1024)}, u32[]{:S(2)}) copy-start(f32[640]{0:T(1024)} %copy-done.47) | copy-start | bytes 7684
  1714.4 166.0 %copy-start.51 = (f32[1,1,1024]{2,1,0:T(1,128)S(1)}, f32[1,1,1024]{2,1,0:T(1,128)}, u32[]{:S(2)}) copy-start(f32[1,1,1024]{2,1,0:T(1,128)} %copy-done.50) | copy-start | bytes 12292
  1728.0 154.9 %copy-start.70 = (f32[640]{0:T(1024)S(1)}, f32[640]{0:T(1024)}, u32[]{:S(2)}) copy-start(f32[640]{0:T(1024)} %copy-done.69) | copy-start | bytes 7684
  1728.0 154.9 %copy-start.55 = (f32[640]{0:T(1024)S(1)}, f32[640]{0:T(1024)}, u32[]{:S(2)}) copy-start(f32[640]{0:T(1024)} %copy-done.54) | copy-start | bytes 7684
  1728.1 158.1 %copy-start.18 = (bf16[640,1024]{1,0:T(8,128)(2,1)S(1)}, bf16[640,1024]{1,0:T(8,128)(2,1)}, u32[]{:S(2)}) copy-start(bf16[640,1024]{1,0:T(8,128)(2,1)} %param.25) | copy-start | bytes 3932164
  (84 other events, 287.4 us)
Sparse Core Ops, SparseCore 0:
  10.7 51.0 all-gather.13
  63.9 39.2 all-gather.11
  292.1 85.2 reduce-scatter.14
  379.9 43.4 all-gather.19
  424.8 21.9 all-gather.17
  448.8 40.4 all-gather.15
  556.5 85.2 reduce-scatter.16
  644.0 49.2 all-gather.23
  695.4 38.9 all-gather.21
  736.3 51.0 all-gather.25
  789.0 38.6 all-gather.27
  851.6 85.2 reduce-scatter.20
  939.5 85.2 reduce-scatter.18
  1032.2 40.4 all-gather.29
  1170.6 85.2 reduce-scatter.22
  1264.8 40.4 all-gather.31
  1308.7 87.8 reduce-scatter.38
  1400.6 88.0 reduce-scatter.40
  1492.1 63.5 reduce-scatter.36
  1559.3 62.4 reduce-scatter.32
  1625.4 67.3 reduce-scatter.34
  1695.4 30.4 reduce-scatter.26
  1729.7 63.8 reduce-scatter.30
  1796.0 84.3 reduce-scatter.24
  1884.0 75.0 reduce-scatter.28
  1966.1 118.5 all-reduce.2
where the time goes:
time: 2110 us; the launch traced here: 2100 us
  waiting for transfers between devices  1040 us (49%)
  matrix products  585 us (28%)
  other arithmetic  232 us (11%)
  local copies, waits for them, and re-layouts  123 us (6%)
  blocking collectives  94.5 us (4%)
    reduce_scatter x6, waiting for transfers between devices, narrow(): lax.psum_scatter(row_terms, 'tensor', scatter_dimension=0, tiled=True)  495 us
    all_gather x6, waiting for transfers between devices, widen(): return lax.all_gather(row_block, 'tensor', axis=0, tiled=True)  201 us
    psum x1, waiting for transfers between devices, on_device(): lax.psum((norm_terms, bias_terms, up_terms), ('dp', 'tensor'))  124 us
    dot_general x20, matrix products, one_block(): jnp.einsum('qhd,khd->hqk', query_block, key_heads, preferred_element_type...  111 us
    dot_general x10, matrix products, one_block(): jnp.einsum('qhd,khd->hqk', grad_block, value_heads, preferred_element_typ...  102 us
    convert_element_type x10, other arithmetic, one_block(): score_grad = (weights * (weight_grad - row_inner)).astype(jnp.bfloat16)  91.5 us
    reduce_scatter x1, waiting for transfers between devices, on_device(): lax.psum_scatter(grad_qkv, 'dp', scatter_dimension=0, tiled=True)  68.7 us
    dot_general x10, matrix products, one_block(): jnp.einsum('hqk,khd->qhd', weights, value_heads, preferred_element_type=j...  67.1 us
  transfers between devices with their start and end apart: 26, of which 19 were waited for; matrix products, arithmetic and copies ran while one was open for 25% of the time, Pallas kernels for 0%

commit v1 on v0

v1 whole, which is shorter than its diff:
```python
import functools
import math

import jax
import jax.numpy as jnp
from jax import lax
from jax.experimental import pallas as pl
from jax.experimental.pallas import tpu as pltpu
from jax.sharding import PartitionSpec as P

H = 16
EPSILON = 1e-05
NEGATIVE = -1e30
F32 = jnp.float32
BF16 = jnp.bfloat16
VMEM_LIMIT = 56 * 2**20


def dot_nt(a, b):
    return lax.dot_general(a, b, (((1,), (1,)), ((), ())), preferred_element_type=F32)


def dot_nn(a, b):
    return lax.dot_general(a, b, (((1,), (0,)), ((), ())), preferred_element_type=F32)


def dot_tn(a, b):
    return lax.dot_general(a, b, (((0,), (0,)), ((), ())), preferred_element_type=F32)


def layer_norm(inputs, gain_row, shift_row):
    center = inputs - jnp.mean(inputs, axis=-1, keepdims=True)
    spread = jnp.mean(center * center, axis=-1, keepdims=True)
    return center * lax.rsqrt(spread + EPSILON) * gain_row + shift_row


def gelu_slope(values_in):
    normal_cdf = 0.5 * (1.0 + lax.erf(values_in * (1.0 / math.sqrt(2.0))))
    density = jnp.exp(-0.5 * values_in * values_in) * (1.0 / math.sqrt(2.0 * math.pi))
    return normal_cdf + values_in * density


def head_only(x, h, size):
    lane = lax.broadcasted_iota(jnp.int32, x.shape, 1)
    return jnp.where((lane >= h * size) & (lane < (h + 1) * size), x, jnp.zeros_like(x))


def self_bad(b_ref, q_start, k_start, bq, bk, causal):
    qi = q_start + lax.broadcasted_iota(jnp.int32, (1, bq), 1)
    kj = k_start + lax.broadcasted_iota(jnp.int32, (bk, 1), 0)
    bad = (qi >= b_ref[0, 1]) & ((kj >= b_ref[0, 0]) & (kj < b_ref[0, 1]))
    if causal:
        bad = bad | (kj > qi)
    return bad


def over_keys(i, bq, bk, safe, block):
    first_mixed = jnp.minimum(i * bq // bk, safe // bk)
    diagonal = i * bq // bk

    def plain(j, c):
        block(j, "none")
        return c

    def split(j, c):
        block(j, "segment")
        return c

    lax.fori_loop(0, first_mixed, plain, 0)
    lax.fori_loop(first_mixed, diagonal, split, 0)
    for step in range(bq // bk):
        block(diagonal + step, "causal")


def self_forward_kernel(b_ref, q_ref, k_ref, vt_ref, ot_ref, lse_ref, m_s, l_s, acc, *, bk, heads, safe):
    i = pl.program_id(0)
    bq, width = q_ref.shape
    hd = width // heads
    m_s[...] = jnp.full_like(m_s, NEGATIVE)
    l_s[...] = jnp.zeros_like(l_s)
    acc[...] = jnp.zeros_like(acc)
    scaled = q_ref[...] * jnp.asarray(1.0 / math.sqrt(hd), BF16)
    q_heads = [head_only(scaled, h, hd) for h in range(heads)]

    def block(j, mode):
        rows = pl.ds(pl.multiple_of(j * bk, bk), bk)
        keys = k_ref[rows, :]
        m_old = m_s[...]
        l_old = l_s[...]
        scores = [dot_nt(keys, q_heads[h]) for h in range(heads)]
        if mode != "none":
            bad = self_bad(b_ref, i * bq, j * bk, bq, bk, mode == "causal")
            scores = [jnp.where(bad, NEGATIVE, s) for s in scores]
        m_out, l_out, a_out = [], [], []
        for h in range(heads):
            part = slice(h * hd, (h + 1) * hd)
            m_new = jnp.maximum(m_old[h : h + 1, :], jnp.max(scores[h], axis=0, keepdims=True))
            shrink = jnp.exp(m_old[h : h + 1, :] - m_new)
            expos = jnp.exp(scores[h] - m_new)
            l_out.append(l_old[h : h + 1, :] * shrink + jnp.sum(expos, axis=0, keepdims=True))
            m_out.append(m_new)
            a_out.append(acc[part, :] * shrink + dot_nn(vt_ref[part, rows], expos.astype(BF16)))
        m_s[...] = jnp.concatenate(m_out, 0)
        l_s[...] = jnp.concatenate(l_out, 0)
        for h in range(heads):
            acc[h * hd : (h + 1) * hd, :] = a_out[h]

    over_keys(i, bq, bk, safe, block)
    inverse = 1.0 / l_s[...]
    for h in range(heads):
        part = slice(h * hd, (h + 1) * hd)
        ot_ref[part, :] = (acc[part, :] * inverse[h : h + 1, :]).astype(BF16)
    lse_ref[...] = m_s[...] + jnp.log(l_s[...])


def self_forward(bounds, queries, keys, values_t, heads, safe):
    n, width = queries.shape
    bq = bk = 512
    return pl.pallas_call(
        functools.partial(self_forward_kernel, bk=bk, heads=heads, safe=safe),
        grid=(n // bq,),
        in_specs=[
            pl.BlockSpec(memory_space=pltpu.SMEM),
            pl.BlockSpec((bq, width), lambda i: (i, 0)),
            pl.BlockSpec((n, width), lambda i: (0, 0)),
            pl.BlockSpec((width, n), lambda i: (0, 0)),
        ],
        out_specs=[
            pl.BlockSpec((width, bq), lambda i: (0, i)),
            pl.BlockSpec((heads, bq), lambda i: (0, i)),
        ],
        out_shape=[
            jax.ShapeDtypeStruct((width, n), BF16),
            jax.ShapeDtypeStruct((heads, n), F32),
        ],
        scratch_shapes=[
            pltpu.VMEM((heads, bq), F32),
            pltpu.VMEM((heads, bq), F32),
            pltpu.VMEM((width, bq), F32),
        ],
        compiler_params=pltpu.CompilerParams(vmem_limit_bytes=VMEM_LIMIT),
        cost_estimate=pl.CostEstimate(
            flops=12 * n * n * width, bytes_accessed=8 * n * width, transcendentals=n * n * heads // 2
        ),
        name="self_forward",
    )(bounds, queries, keys, values_t)


def self_backward_kernel(
    b_ref, q_ref, k_ref, v_ref, kt_ref, do_ref, lse_ref, dl_ref, dqt_ref, dk_ref, dv_ref, dka, dva, dqa, *, bk, heads, safe
):
    i = pl.program_id(0)
    bq, width = q_ref.shape
    hd = width // heads
    scale = 1.0 / math.sqrt(hd)

    @pl.when(i == 0)
    def _():
        dka[...] = jnp.zeros_like(dka)
        dva[...] = jnp.zeros_like(dva)

    scaled = q_ref[...] * jnp.asarray(scale, BF16)
    grads = do_ref[...]
    q_heads = [head_only(scaled, h, hd) for h in range(heads)]
    d_heads = [head_only(grads, h, hd) for h in range(heads)]
    lse = lse_ref[...]
    inner = dl_ref[...]
    dqa[...] = jnp.zeros_like(dqa)

    def block(j, mode):
        rows = pl.ds(pl.multiple_of(j * bk, bk), bk)
        keys = k_ref[rows, :]
        values = v_ref[rows, :]
        scores = [dot_nt(keys, q_heads[h]) for h in range(heads)]
        dprobs = [dot_nt(values, d_heads[h]) for h in range(heads)]
        if mode != "none":
            bad = self_bad(b_ref, i * bq, j * bk, bq, bk, mode == "causal")
            scores = [jnp.where(bad, NEGATIVE, s) for s in scores]
        dv_sum, dk_sum = None, None
        for h in range(heads):
            part = slice(h * hd, (h + 1) * hd)
            probs = jnp.exp(scores[h] - lse[h : h + 1, :])
            ds = (probs * (dprobs[h] - inner[h : h + 1, :])).astype(BF16)
            dv_h = dot_nn(probs.astype(BF16), d_heads[h])
            dk_h = dot_nn(ds, q_heads[h])
            dv_sum = dv_h if dv_sum is None else dv_sum + dv_h
            dk_sum = dk_h if dk_sum is None else dk_sum + dk_h
            dqa[part, :] += dot_nn(kt_ref[part, rows], ds)
        dva[rows, :] += dv_sum
        dka[rows, :] += dk_sum

    over_keys(i, bq, bk, safe, block)
    dqt_ref[...] = (dqa[...] * scale).astype(BF16)

    @pl.when(i == pl.num_programs(0) - 1)
    def _():
        dk_ref[...] = dka[...].astype(BF16)
        dv_ref[...] = dva[...].astype(BF16)


def self_backward(bounds, queries, keys, values, keys_t, grads, lse, inner, heads, safe):
    n, width = queries.shape
    bq = bk = 512
    whole = pl.BlockSpec((n, width), lambda i: (0, 0))
    some = pl.BlockSpec((bq, width), lambda i: (i, 0))
    per_row = pl.BlockSpec((heads, bq), lambda i: (0, i))
    return pl.pallas_call(
        functools.partial(self_backward_kernel, bk=bk, heads=heads, safe=safe),
        grid=(n // bq,),
        in_specs=[
            pl.BlockSpec(memory_space=pltpu.SMEM),
            some,
            whole,
            whole,
            pl.BlockSpec((width, n), lambda i: (0, 0)),
            some,
            per_row,
            per_row,
        ],
        out_specs=[pl.BlockSpec((width, bq), lambda i: (0, i)), whole, whole],
        out_shape=[
            jax.ShapeDtypeStruct((width, n), BF16),
            jax.ShapeDtypeStruct((n, width), BF16),
            jax.ShapeDtypeStruct((n, width), BF16),
        ],
        scratch_shapes=[
            pltpu.VMEM((n, width), F32),
            pltpu.VMEM((n, width), F32),
            pltpu.VMEM((width, bq), F32),
        ],
        compiler_params=pltpu.CompilerParams(vmem_limit_bytes=VMEM_LIMIT),
        cost_estimate=pl.CostEstimate(
            flops=24 * n * n * width, bytes_accessed=16 * n * width, transcendentals=n * n * heads // 2
        ),
        name="self_backward",
    )(bounds, queries, keys, values, keys_t, grads, lse, inner)


def cross_forward_kernel(ok_ref, q_ref, k_ref, vt_ref, ot_ref, lse_ref, *, heads):
    rows, width = q_ref.shape[1:]
    hd = width // heads
    scaled = q_ref[0] * jnp.asarray(1.0 / math.sqrt(hd), BF16)
    keys = k_ref[0]
    ok = ok_ref[...] > 0.0
    scores = [dot_nt(keys, head_only(scaled, h, hd)) for h in range(heads)]
    for h in range(heads):
        part = slice(h * hd, (h + 1) * hd)
        s = jnp.where(ok, scores[h], NEGATIVE)
        largest = jnp.max(s, axis=0, keepdims=True)
        expos = jnp.exp(s - largest)
        total = jnp.sum(expos, axis=0, keepdims=True)
        mixed = dot_nn(vt_ref[0, part, :], expos.astype(BF16))
        ot_ref[0, part, :] = (mixed * (1.0 / total)).astype(BF16)
        lse_ref[0, h : h + 1, :] = largest + jnp.log(total)


def cross_forward(ok, queries, keys, values_t, heads):
    parts, rows, width = queries.shape
    n = keys.shape[1]
    return pl.pallas_call(
        functools.partial(cross_forward_kernel, heads=heads),
        grid=(parts,),
        in_specs=[
            pl.BlockSpec((n, 1), lambda i: (0, 0)),
            pl.BlockSpec((1, rows, width), lambda i: (i, 0, 0)),
            pl.BlockSpec((1, n, width), lambda i: (i, 0, 0)),
            pl.BlockSpec((1, width, n), lambda i: (i, 0, 0)),
        ],
        out_specs=[
            pl.BlockSpec((1, width, rows), lambda i: (i, 0, 0)),
            pl.BlockSpec((1, heads, rows), lambda i: (i, 0, 0)),
        ],
        out_shape=[
            jax.ShapeDtypeStruct((parts, width, rows), BF16),
            jax.ShapeDtypeStruct((parts, heads, rows), F32),
        ],
        compiler_params=pltpu.CompilerParams(vmem_limit_bytes=VMEM_LIMIT),
        cost_estimate=pl.CostEstimate(
            flops=24 * parts * rows * n * width,
            bytes_accessed=8 * parts * n * width,
            transcendentals=parts * rows * n * heads,
        ),
        name="cross_forward",
    )(ok, queries, keys, values_t)


def cross_backward_kernel(
    ok_ref, q_ref, k_ref, v_ref, kt_ref, do_ref, lse_ref, dl_ref, dqt_ref, dk_ref, dv_ref, *, heads, bk
):
    rows, width = q_ref.shape[1:]
    n = k_ref.shape[1]
    hd = width // heads
    scale = 1.0 / math.sqrt(hd)
    scaled = q_ref[0] * jnp.asarray(scale, BF16)
    grads = do_ref[0]
    q_heads = [head_only(scaled, h, hd) for h in range(heads)]
    d_heads = [head_only(grads, h, hd) for h in range(heads)]
    lse = lse_ref[0]
    inner = dl_ref[0]
    dq = [None] * heads
    for j in range(n // bk):
        span = slice(j * bk, (j + 1) * bk)
        keys = k_ref[0, span, :]
        values = v_ref[0, span, :]
        ok = ok_ref[span, :] > 0.0
        scores = [dot_nt(keys, q_heads[h]) for h in range(heads)]
        dprobs = [dot_nt(values, d_heads[h]) for h in range(heads)]
        dv_sum, dk_sum = None, None
        for h in range(heads):
            part = slice(h * hd, (h + 1) * hd)
            probs = jnp.exp(jnp.where(ok, scores[h], NEGATIVE) - lse[h : h + 1, :])
            ds = (probs * (dprobs[h] - inner[h : h + 1, :])).astype(BF16)
            dv_h = dot_nn(probs.astype(BF16), d_heads[h])
            dk_h = dot_nn(ds, q_heads[h])
            dv_sum = dv_h if dv_sum is None else dv_sum + dv_h
            dk_sum = dk_h if dk_sum is None else dk_sum + dk_h
            dq_h = dot_nn(kt_ref[0, part, span], ds)
            dq[h] = dq_h if dq[h] is None else dq[h] + dq_h
        dv_ref[0, span, :] = dv_sum.astype(BF16)
        dk_ref[0, span, :] = dk_sum.astype(BF16)
    for h in range(heads):
        dqt_ref[0, h * hd : (h + 1) * hd, :] = (dq[h] * scale).astype(BF16)


def cross_backward(ok, queries, keys, values, keys_t, grads, lse, inner, heads):
    parts, rows, width = queries.shape
    n = keys.shape[1]
    by_row = pl.BlockSpec((1, rows, width), lambda i: (i, 0, 0))
    by_key = pl.BlockSpec((1, n, width), lambda i: (i, 0, 0))
    stat = pl.BlockSpec((1, heads, rows), lambda i: (i, 0, 0))
    return pl.pallas_call(
        functools.partial(cross_backward_kernel, heads=heads, bk=512),
        grid=(parts,),
        in_specs=[
            pl.BlockSpec((n, 1), lambda i: (0, 0)),
            by_row,
            by_key,
            by_key,
            pl.BlockSpec((1, width, n), lambda i: (i, 0, 0)),
            by_row,
            stat,
            stat,
        ],
        out_specs=[pl.BlockSpec((1, width, rows), lambda i: (i, 0, 0)), by_key, by_key],
        out_shape=[
            jax.ShapeDtypeStruct((parts, width, rows), BF16),
            jax.ShapeDtypeStruct((parts, n, width), BF16),
            jax.ShapeDtypeStruct((parts, n, width), BF16),
        ],
        compiler_params=pltpu.CompilerParams(vmem_limit_bytes=VMEM_LIMIT),
        cost_estimate=pl.CostEstimate(
            flops=48 * parts * rows * n * width,
            bytes_accessed=16 * parts * n * width,
            transcendentals=parts * rows * n * heads,
        ),
        name="cross_backward",
    )(ok, queries, keys, values, keys_t, grads, lse, inner)


def swap(value, axis, distance):
    size = lax.axis_size(axis)
    return lax.ppermute(value, axis, [(i, i ^ distance) for i in range(size)])


def dp_distances():
    n = lax.axis_size("dp")
    found = []
    while n > 1:
        n //= 2
        found.append(n)
    return found


def reorder_kernel(order_ref, in_ref, out_ref):
    out_ref[...] = in_ref[0]


def in_order(stack):
    n, rows, columns = stack.shape
    place = jnp.arange(n, dtype=jnp.int32) ^ lax.axis_index("dp")
    order = jnp.zeros_like(place)
    for bit, distance in enumerate(dp_distances()):
        order = order + (place // distance % 2) * 2**bit
    return pl.pallas_call(
        reorder_kernel,
        grid_spec=pltpu.PrefetchScalarGridSpec(
            num_scalar_prefetch=1,
            grid=(n,),
            in_specs=[pl.BlockSpec((1, rows, columns), lambda i, order_ref: (order_ref[i], 0, 0))],
            out_specs=pl.BlockSpec((rows, columns), lambda i, order_ref: (i, 0)),
        ),
        out_shape=jax.ShapeDtypeStruct((n * rows, columns), stack.dtype),
        cost_estimate=pl.CostEstimate(flops=0, bytes_accessed=4 * n * rows * columns, transcendentals=0),
        name="in_order",
    )(order, stack)


def gather_dp(shard):
    stack = shard[None]
    for distance in dp_distances():
        stack = jnp.concatenate([stack, swap(stack, "dp", distance)], 0)
    return in_order(stack)


def gather_all(shard, x_last):
    distances = dp_distances()
    stack = shard[None]
    for distance in distances[:-1]:
        stack = jnp.concatenate([stack, swap(stack, "dp", distance)], 0)
    last = distances[-1]
    if x_last:
        near = in_order(jnp.concatenate([stack, swap(stack, "dp", last)], 0))
        far = swap(near, "tensor", 2)
    else:
        there = swap(stack, "tensor", 2)
        near = in_order(jnp.concatenate([stack, swap(stack, "dp", last)], 0))
        far = in_order(jnp.concatenate([there, swap(there, "dp", last)], 0))
    return [near, swap(near, "tensor", 1), far, swap(far, "tensor", 1)]


def add_low(a, b):
    return (a.astype(F32) + b.astype(F32)).astype(BF16)


def reduce_dp(total, distances):
    n = lax.axis_size("dp")
    me = lax.axis_index("dp")
    rows, columns = total.shape[0] // n, total.shape[1]
    shape = [2] * len(dp_distances()) + [rows, columns]
    axes = list(dp_distances())
    total = total.reshape(shape)
    for step, distance in enumerate(distances):
        axis = axes.index(distance)
        axes.pop(axis)
        mine = me // distance % 2
        keep = lax.dynamic_index_in_dim(total, mine, axis, keepdims=False)
        give = lax.dynamic_index_in_dim(total, 1 - mine, axis, keepdims=False)
        got = swap(give, "dp", distance)
        total = keep.astype(F32) + got.astype(F32)
        if step < len(distances) - 1:
            total = total.astype(BF16)
    return total


def reduce_all(pieces, x_first):
    near = add_low(pieces[0], swap(pieces[1], "tensor", 1))
    far = add_low(pieces[2], swap(pieces[3], "tensor", 1))
    order = dp_distances()[::-1]
    if x_first:
        return reduce_dp(add_low(near, swap(far, "tensor", 2)), order)
    n = lax.axis_size("dp")
    me = lax.axis_index("dp")
    rows, columns = near.shape[0] // n, near.shape[1]
    mine = me % 2

    def halve(total):
        total = total.reshape(n // 2, 2, rows, columns)
        keep = lax.dynamic_index_in_dim(total, mine, 1, keepdims=False)
        give = lax.dynamic_index_in_dim(total, 1 - mine, 1, keepdims=False)
        return add_low(keep, swap(give, "dp", 1))

    near, far = halve(near), halve(far)
    total = add_low(near, swap(far, "tensor", 2))
    axes = dp_distances()[:-1]
    total = total.reshape([2] * len(axes) + [rows, columns])
    for step, distance in enumerate(order[1:]):
        axis = axes.index(distance)
        axes.pop(axis)
        own = me // distance % 2
        keep = lax.dynamic_index_in_dim(total, own, axis, keepdims=False)
        give = lax.dynamic_index_in_dim(total, 1 - own, axis, keepdims=False)
        total = keep.astype(F32) + swap(give, "dp", distance).astype(F32)
        if step < len(order) - 2:
            total = total.astype(BF16)
    return total


def sum_everywhere(value):
    for distance in (1, 2):
        value = value + swap(value, "tensor", distance)
    for distance in dp_distances():
        value = value + swap(value, "dp", distance)
    return value


def widen(rows_low):
    member = lax.axis_index("tensor")
    count, width = rows_low.shape
    other = swap(rows_low, "tensor", 2)
    parts = [rows_low, swap(rows_low, "tensor", 1), other, swap(other, "tensor", 1)]
    out = jnp.zeros((4 * count, width), rows_low.dtype)
    for distance, part in enumerate(parts):
        out = lax.dynamic_update_slice(out, part, ((member ^ distance) * count, 0))
    return out


def narrow(rows_low):
    member = lax.axis_index("tensor")
    count = rows_low.shape[0] // 4
    parts = [
        lax.dynamic_slice_in_dim(rows_low, (member ^ distance) * count, count, 0)
        for distance in range(4)
    ]
    far = add_low(parts[2], swap(parts[3], "tensor", 1))
    got = swap(far, "tensor", 2)
    near = parts[0].astype(F32) + swap(parts[1], "tensor", 1).astype(F32)
    return near + got.astype(F32)


def on_device(
    block_in,
    encoder_out,
    out_grad,
    bounds,
    enc_lengths,
    norm_params,
    w_qkv,
    w_self_out,
    w_cross_q,
    w_cross_kv,
    w_cross_out,
    w_up,
    w_down,
    biases,
    up_bias,
):
    member = lax.axis_index("tensor")
    groups = float(lax.axis_size("dp"))
    width = w_cross_q.shape[1]
    hidden_width = w_up.shape[1]
    heads = H // 4
    own_rows, model_width = block_in.shape
    enc_rows = encoder_out.shape[0]
    w_rows = w_cross_q.shape[0]

    def block_of(vector, size, distance):
        return lax.dynamic_slice_in_dim(vector, (member ^ distance) * size, size)

    def blocks_placed(parts):
        size = parts[0].shape[0]
        out = jnp.zeros((4 * size,), F32)
        for distance, part in enumerate(parts):
            out = lax.dynamic_update_slice_in_dim(out, part, (member ^ distance) * size, 0)
        return out

    def norm_back(rows, incoming, which):
        _, pull_rows = jax.vjp(layer_norm, rows, norm_params[which, 0], norm_params[which, 1])
        return pull_rows(incoming)

    start_rows = block_in.astype(F32)
    first_in = widen(layer_norm(start_rows, norm_params[0, 0], norm_params[0, 1]).astype(BF16))
    self_w = gather_dp(jnp.concatenate([w_qkv.reshape(w_rows, 3 * width), w_self_out.T], axis=1))
    cross_w = gather_all(
        jnp.concatenate([w_cross_q, w_cross_kv.reshape(w_rows, 2 * width), w_cross_out.T], axis=1), False
    )
    up_w = gather_all(w_up, False)
    down_w = gather_all(w_down.T, True)
    w_query = [w[:, :width] for w in cross_w]
    w_keyval = [w[:, width : 3 * width] for w in cross_w]
    w_out = [w[:, 3 * width :] for w in cross_w]

    projected = dot_nn(first_in, self_w[:, : 3 * width])
    queries = (projected[:, :width] + block_of(biases[0], width, 0)).astype(BF16)
    key_rows = projected[:, width : 2 * width].astype(BF16)
    value_rows = (projected[:, 2 * width :] + block_of(biases[1], width, 0)).astype(BF16)
    self_safe = 1024
    self_mixed_t, self_lse = self_forward(bounds, queries, key_rows, value_rows.T, heads, self_safe)
    self_out_w = self_w[:, 3 * width :]
    after_self = (
        start_rows
        + narrow(lax.dot_general(self_mixed_t, self_out_w, (((0,), (1,)), ((), ())), preferred_element_type=F32).astype(BF16))
        + biases[2]
    )

    own_kv = []
    for distance in range(4):
        shift = jnp.concatenate([jnp.zeros((width,), F32), block_of(biases[4], width, distance)])
        own_kv.append((dot_nn(encoder_out, w_keyval[distance]) + shift).astype(BF16))
    own_kv = jnp.stack(own_kv)
    far_kv = swap(own_kv, "tensor", 2)
    kv_from = [own_kv, swap(own_kv, "tensor", 1), far_kv, swap(far_kv, "tensor", 1)]
    cross_kv = jnp.stack(
        [jnp.concatenate([kv_from[d][j ^ d] for d in range(4)], 0) for j in range(4)]
    )
    cross_keys = cross_kv[:, :, :width]
    cross_values = cross_kv[:, :, width:]
    places = jnp.concatenate(
        [(member ^ d) * enc_rows + jnp.arange(enc_rows, dtype=jnp.int32) for d in range(4)]
    )
    ok = (places < enc_lengths[0]).astype(F32)[:, None]

    second_in = layer_norm(after_self, norm_params[1, 0], norm_params[1, 1]).astype(BF16)
    cross_queries = jnp.stack(
        [
            (dot_nn(second_in, w_query[d]) + block_of(biases[3], width, d)).astype(BF16)
            for d in range(4)
        ]
    )
    cross_mixed_t, cross_lse = cross_forward(
        ok, cross_queries, cross_keys, jnp.swapaxes(cross_values, 1, 2), heads
    )
    after_cross = after_self + biases[5]
    for d in range(4):
        after_cross = after_cross + lax.dot_general(
            cross_mixed_t[d], w_out[d], (((0,), (1,)), ((), ())), preferred_element_type=F32
        )

    third_in = layer_norm(after_cross, norm_params[2, 0], norm_params[2, 1]).astype(BF16)
    cot_rows = out_grad.astype(F32)
    bias_down_grad = jnp.sum(cot_rows, axis=0)
    output = after_cross + biases[6]
    third_grad = 0.0
    down_pieces, up_pieces, bias_up_parts = [], [], []
    for d in range(4):
        pre_act = dot_nn(third_in, up_w[d]) + block_of(up_bias, hidden_width, d)
        hidden = jax.nn.gelu(pre_act, approximate=False).astype(BF16)
        output = output + dot_nt(hidden, down_w[d])
        hidden_grad = dot_nn(out_grad, down_w[d])
        pre_grad = (hidden_grad * gelu_slope(pre_act)).astype(BF16)
        down_pieces.append(dot_tn(out_grad, hidden).astype(BF16))
        up_pieces.append(dot_tn(third_in, pre_grad).astype(BF16))
        bias_up_parts.append(jnp.sum(pre_grad.astype(F32), axis=0))
        third_grad = third_grad + dot_nt(pre_grad, up_w[d])
    summed_up = reduce_all(up_pieces, False)
    summed_down = reduce_all(down_pieces, True).T
    rows_three, gain_three, shift_three = norm_back(after_cross, third_grad, 2)
    cross_rows_grad = cot_rows + rows_three

    cross_low = cross_rows_grad.astype(BF16)
    bias_co_grad = jnp.sum(cross_low.astype(F32), axis=0)
    cross_mixed_grad = jnp.stack([dot_nn(cross_low, w_out[d]).astype(BF16) for d in range(4)])
    cross_inner = jnp.sum(
        cross_mixed_t.reshape(4, heads, width // heads, own_rows).astype(F32)
        * jnp.swapaxes(cross_mixed_grad, 1, 2).reshape(4, heads, width // heads, own_rows).astype(F32),
        axis=2,
    )
    cross_dq_t, part_dk, part_dv = cross_backward(
        ok,
        cross_queries,
        cross_keys,
        cross_values,
        jnp.swapaxes(cross_keys, 1, 2),
        cross_mixed_grad,
        cross_lse,
        cross_inner,
        heads,
    )
    second_grad = 0.0
    for d in range(4):
        second_grad = second_grad + lax.dot_general(
            cross_dq_t[d], w_query[d], (((0,), (1,)), ((), ())), preferred_element_type=F32
        )
    rows_two, gain_two, shift_two = norm_back(after_self, second_grad, 1)
    self_rows_grad = cross_rows_grad + rows_two
    self_low = self_rows_grad.astype(BF16)
    bias_so_grad = jnp.sum(self_low.astype(F32), axis=0)
    self_wide = widen(self_low)

    part_kv = jnp.concatenate([part_dk, part_dv], axis=2).reshape(4, 4, enc_rows, 2 * width)

    def for_member(d):
        return jnp.stack([part_kv[j ^ d, d] for j in range(4)])

    far_dkv = add_low(for_member(2), swap(for_member(3), "tensor", 1))
    near_dkv = for_member(0).astype(F32) + swap(for_member(1), "tensor", 1).astype(F32)
    dkv = (near_dkv + swap(far_dkv, "tensor", 2).astype(F32)).astype(BF16)
    encoder_grad = 0.0
    for d in range(4):
        encoder_grad = encoder_grad + dot_nt(dkv[d], w_keyval[d])
    cross_pieces = []
    for d in range(4):
        cross_pieces.append(
            jnp.concatenate(
                [
                    lax.dot_general(
                        second_in, cross_dq_t[d], (((0,), (1,)), ((), ())), preferred_element_type=F32
                    ).astype(BF16),
                    dot_tn(encoder_out, dkv[d]).astype(BF16),
                    lax.dot_general(
                        cross_low, cross_mixed_t[d], (((0,), (1,)), ((), ())), preferred_element_type=F32
                    ).astype(BF16),
                ],
                axis=1,
            )
        )
    summed_cross = reduce_all(cross_pieces, False)
    bias_cq_grad = blocks_placed([jnp.sum(cross_dq_t[d].astype(F32), axis=1) for d in range(4)])
    bias_cv_grad = blocks_placed([jnp.sum(dkv[d, :, width:].astype(F32), axis=0) for d in range(4)])
    bias_up_grad = blocks_placed(bias_up_parts)

    self_mixed_grad = dot_nn(self_wide, self_out_w).astype(BF16)
    self_inner = jnp.sum(
        self_mixed_t.reshape(heads, width // heads, 4 * own_rows).astype(F32)
        * self_mixed_grad.T.reshape(heads, width // heads, 4 * own_rows).astype(F32),
        axis=1,
    )
    self_dq_t, self_dk, self_dv = self_backward(
        bounds, queries, key_rows, value_rows, key_rows.T, self_mixed_grad, self_lse, self_inner, heads, self_safe
    )
    grad_so_t = lax.dot_general(
        self_wide, self_mixed_t, (((0,), (1,)), ((), ())), preferred_element_type=F32
    ).astype(BF16)
    qkv_grad = jnp.concatenate([self_dq_t.T, self_dk, self_dv], axis=1)
    first_terms = dot_nt(qkv_grad, self_w[:, : 3 * width]).astype(BF16)
    first_grad = narrow(first_terms)
    summed_self = reduce_dp(
        jnp.concatenate([dot_tn(first_in, qkv_grad).astype(BF16), grad_so_t], axis=1), dp_distances()[::-1]
    )
    column_sums = jnp.sum(qkv_grad.astype(F32), axis=0)
    rows_one, gain_one, shift_one = norm_back(start_rows, first_grad, 0)
    input_grad = self_rows_grad + rows_one

    def only_own(part):
        out = jnp.zeros((model_width,), F32)
        return lax.dynamic_update_slice_in_dim(out, part, member * width, 0)

    early = sum_everywhere(
        jnp.concatenate(
            [
                gain_two,
                shift_two,
                gain_three,
                shift_three,
                bias_so_grad,
                bias_cq_grad,
                bias_cv_grad,
                bias_co_grad,
                bias_down_grad,
                bias_up_grad,
            ]
        ).reshape(-1, 128)
    ).reshape(-1, model_width)
    late = sum_everywhere(
        jnp.concatenate(
            [gain_one, shift_one, only_own(column_sums[:width]), only_own(column_sums[2 * width :])]
        ).reshape(-1, 128)
    ).reshape(-1, model_width)
    norm_total = jnp.stack([late[0], late[1], early[0], early[1], early[2], early[3]]).reshape(
        norm_params.shape
    )
    bias_total = jnp.stack([late[2], late[3], early[4], early[5], early[6], early[7], early[8]])
    up_total = early[9:].reshape(-1)
    scale = 1.0 / groups
    return (
        output,
        input_grad,
        encoder_grad,
        norm_total * scale,
        summed_self[:, : 3 * width].reshape(w_qkv.shape) * scale,
        summed_self[:, 3 * width :].T * scale,
        summed_cross[:, :width] * scale,
        summed_cross[:, width : 3 * width].reshape(w_cross_kv.shape) * scale,
        summed_cross[:, 3 * width :].T * scale,
        summed_up * scale,
        summed_down * scale,
        bias_total * scale,
        up_total * scale,
    )


def solution(mesh):
    rows = P(("dp", "tensor"), None)
    placed = (
        rows,
        rows,
        rows,
        P("dp", None),
        P("dp"),
        P(),
        P("dp", None, "tensor"),
        P("tensor", "dp"),
        P("dp", "tensor"),
        P("dp", None, "tensor"),
        P("tensor", "dp"),
        P("dp", "tensor"),
        P("tensor", "dp"),
        P(),
        P(),
    )
    return jax.shard_map(
        on_device,
        mesh=mesh,
        in_specs=placed,
        out_specs=(
            rows,
            rows,
            rows,
            P(),
            P("dp", None, "tensor"),
            P("tensor", "dp"),
            P("dp", "tensor"),
            P("dp", None, "tensor"),
            P("tensor", "dp"),
            P("dp", "tensor"),
            P("tensor", "dp"),
            P(),
            P(),
        ),
        check_vma=False,
    )
```

time: 2110 us -> 925 us (0.44)
  waiting for transfers between devices: 1040 us -> 215 us
  matrix products: 585 us -> 196 us
  Pallas kernels: 0 us -> 176 us
  other arithmetic: 232 us -> 106 us
  blocking collectives: 94.5 us -> 0 us
  starting transfers between devices: 1.24 us -> 67.1 us
  local copies, waits for them, and re-layouts: 123 us -> 149 us
    reduce_scatter x14 -> x0, waiting for transfers between devices: 633 us -> none  [the longest x6 495 us: narrow(): lax.psum_scatter(row_terms, 'tensor', scatter_dimension=0, tiled=True)]
    dot_general x91 -> x66, matrix products: 585 us -> 196 us  [the longest x22 82.6 us: dot_nn(): lax.dot_general(a, b, (((1,), (0,)), ((), ())), preferred_element_type=F32)]
    all_gather x11 -> x0, waiting for transfers between devices: 282 us -> none  [the longest x6 201 us: widen(): return lax.all_gather(row_block, 'tensor', axis=0, tiled=True)]
    ppermute x0 -> x74, waiting for transfers between devices: none -> 215 us  [swap(): return lax.ppermute(value, axis, [(i, i ^ distance) for i in range(size)])]
    pallas_call x0 -> x10, Pallas kernels: none -> 176 us  [the longest x1 50.7 us: self_backward(): pl.pallas_call(functools.partial(self_backward_kernel, bk=bk, heads=heads...]
    psum x1 -> x0, waiting for transfers between devices: 124 us -> none  [on_device(): lax.psum((norm_terms, bias_terms, up_terms), ('dp', 'tensor'))]
    all_gather x3 -> x0, blocking collectives: 94.5 us -> none  [the longest x1 33.8 us: on_device(): lax.all_gather(w_cross_q, 'dp', axis=0, tiled=True)]
    convert_element_type x19 -> x21, other arithmetic: 105 us -> 37.5 us  [the longest x10 27.7 us: add_low(): return (a.astype(F32) + b.astype(F32)).astype(BF16)]
  transfers between devices with their start and end apart: 26 -> 74, of which waited for: 19 -> 20; matrix products, arithmetic and copies ran while one was open for 25% -> 41% of each run, Pallas kernels for 0% -> 15%
where the time goes in v1:
time: 925 us; the launch traced here: 914 us
  waiting for transfers between devices  215 us (23%)
  matrix products  196 us (21%)
  Pallas kernels  176 us (19%)
  local copies, waits for them, and re-layouts  149 us (16%)
  other arithmetic  106 us (11%)
  starting transfers between devices  67.1 us (7%)
    ppermute x74, waiting for transfers between devices, swap(): return lax.ppermute(value, axis, [(i, i ^ distance) for i in range(size)])  215 us
    dot_general x22, matrix products, dot_nn(): lax.dot_general(a, b, (((1,), (0,)), ((), ())), preferred_element_type=F32)  82.6 us
    ppermute x74, starting transfers between devices, swap(): return lax.ppermute(value, axis, [(i, i ^ distance) for i in range(size)])  67.1 us
    unnamed x318, local copies, waits for them, and re-layouts  54.4 us
    pallas_call x1, Pallas kernels, self_backward(): pl.pallas_call(functools.partial(self_backward_kernel, bk=bk, heads=heads...  50.7 us
    dot_general x13, matrix products, dot_nt(): lax.dot_general(a, b, (((1,), (1,)), ((), ())), preferred_element_type=F32)  44.5 us
    dot_general x13, matrix products, dot_tn(): lax.dot_general(a, b, (((0,), (0,)), ((), ())), preferred_element_type=F32)  39 us
    pallas_call x6, Pallas kernels, in_order(): pl.pallas_call(reorder_kernel, grid_spec=pltpu.PrefetchScalarGridSpec(num...  38.3 us
  transfers between devices with their start and end apart: 74, of which 20 were waited for; matrix products, arithmetic and copies ran while one was open for 41% of the time, Pallas kernels for 15%

profile of v1, /device:TPU:0, one launch (start us, length us, event | category | flops | bytes accessed | tf_op | source)
XLA Modules:
  0.0 913.7 jit_solution(6990084883128198189)
XLA Ops:
  15.7 17.9 %collective-permute-done.3 = bf16[1,128,1024]{2,1,0:T(8,128)(2,1)S(1)} collective-permute-done((bf16[1,128,1024]{2,1,0:T(8,128)(2,1)S(1)}, bf16[1,128,1024]{2,1,0:T(8,128)(2,1)S(1)}, u32[]{:S(2)}, u32[]{:S(2)}) %collective-permute-start.3) | collective-permute-done | bytes 262176 | tf_op jit(solution)/shard_map/ppermute | solution.py:362
  41.5 13.7 %collective-permute-done.4 = bf16[2,128,1024]{2,1,0:T(8,128)(2,1)} collective-permute-done((bf16[2,128,1024]{2,1,0:T(8,128)(2,1)}, bf16[2,128,1024]{2,1,0:T(8,128)(2,1)}, u32[]{:S(2)}, u32[]{:S(2)}) %collective-permute-start.4) | collective-permute-done | bytes 524320 | tf_op jit(solution)/shard_map/ppermute | solution.py:362
  59.6 12.3 %collective-permute-done.10 = bf16[2,128,1024]{2,1,0:T(8,128)(2,1)} collective-permute-done((bf16[2,128,1024]{2,1,0:T(8,128)(2,1)}, bf16[2,128,1024]{2,1,0:T(8,128)(2,1)}, u32[]{:S(2)}, u32[]{:S(2)}) %collective-permute-start.10) | collective-permute-done | bytes 524320 | tf_op jit(solution)/shard_map/ppermute | solution.py:362
  76.0 9.6 %collective-permute-done.20 = bf16[2,128,1024]{2,1,0:T(8,128)(2,1)S(1)} collective-permute-done((bf16[2,128,1024]{2,1,0:T(8,128)(2,1)S(1)}, bf16[2,128,1024]{2,1,0:T(8,128)(2,1)S(1)}, u32[]{:S(2)}, u32[]{:S(2)}) %collective-permute-start.20) | collective-permute-done | bytes 524320 | tf_op jit(solution)/shard_map/ppermute | solution.py:362
  96.8 6.3 in_order.6
  107.8 6.3 fusion.88
  122.6 32.2 %self_forward.1 = (bf16[256,2560]{1,0:T(8,128)(2,1)}, f32[4,2560]{1,0:T(4,128)}) custom-call(s32[1,2]{1,0:T(1,128)} %b_ref.3, bf16[2560,256]{1,0:T(8,128)(2,1)} %get-tuple-element.117.q_ref, bf16[2560,256]{1,0:T(8,128)(2,1)} %copy.226.k_ref, bf16[256,2560]{1,0:T(8,128)(2,1)} %copy.227.vt_ref), custom_call_target="tpu_custom_call" | custom-call | flops 20132659200 | bytes 5242880 | tf_op jit(solution)/shard_map/self_forward/pallas_call | solution.py:119
  166.4 6.3 in_order.7
  176.0 6.3 in_order.8
  192.8 6.3 in_order.9
  202.0 6.3 in_order.10
  208.3 3.3 add_convert_fusion.8
  218.4 6.7 in_order.11
  232.7 10.8 %collective-permute-done.8 = bf16[640,1024]{0,1:T(8,128)(2,1)} collective-permute-done((bf16[640,1024]{0,1:T(8,128)(2,1)}, bf16[640,1024]{0,1:T(8,128)(2,1)}, u32[]{:S(2)}, u32[]{:S(2)}) %collective-permute-start.8) | collective-permute-done | bytes 1310752 | tf_op jit(solution)/shard_map/ppermute | solution.py:362
  251.2 59.2 %collective-permute-done.17 = bf16[4,256,512]{1,2,0:T(8,128)(2,1)S(1)} collective-permute-done((bf16[4,256,512]{1,2,0:T(8,128)(2,1)S(1)}, bf16[4,256,512]{1,2,0:T(8,128)(2,1)S(1)}, u32[]{:S(2)}, u32[]{:S(2)}) %collective-permute-start.17) | collective-permute-done | bytes 1048608 | tf_op jit(solution)/shard_map/ppermute | solution.py:362
  317.0 3.9 slice_bitcast_fusion.41
  320.9 3.9 copy.234.k_ref
  324.8 19.7 %cross_forward.1 = (bf16[4,256,640]{2,1,0:T(8,128)(2,1)}, f32[4,4,640]{2,1,0:T(4,128)}) custom-call(f32[1024,1]{1,0:T(8,128)} %convert_element_type.587.ok_ref, bf16[4,640,256]{2,1,0:T(8,128)(2,1)} %pad_maximum_fusion.12.q_ref, bf16[4,1024,256]{2,1,0:T(8,128)(2,1)} %copy.234.k_ref, bf16[4,256,1024]{2,1,0:T(8,128)(2,1)} %get-tuple-element.139.vt_ref), custom_call_target="tpu_custom_call" | custom-call | flops 16106127360 | bytes 8388608 | tf_op jit(solution)/shard_map/cross_forward/pallas_call | solution.py:260
  351.7 9.7 %fusion.16 = (bf16[640,1024]{1,0:T(8,128)(2,1)}, f32[640,1024]{1,0:T(8,128)S(1)}) fusion(f32[1024]{0:T(1024)S(1)} %get-tuple-element.196, bf16[640,1024]{0,1:T(8,128)(2,1)S(1)} %add_convert_fusion.6, bf16[1024,1024]{1,0:T(8,128)(2,1)} %in_order.9), kind=kOutput, calls=%fused_computation.46 | convolution fusion | flops 1385431040 | bytes 7344128 | tf_op jit(solution)/shard_map/dot_general | solution.py:24
  361.4 9.2 %fusion.22 = (bf16[640,1024]{1,0:T(8,128)(2,1)}, f32[640,1024]{1,0:T(8,128)S(1)}) fusion(f32[1024]{0:T(1024)S(1)} %get-tuple-element.197, bf16[640,1024]{0,1:T(8,128)(2,1)S(1)} %add_convert_fusion.6, bf16[1024,1024]{1,0:T(8,128)(2,1)} %in_order.11), kind=kOutput, calls=%fused_computation.52 | convolution fusion | flops 1385431040 | bytes 7344128 | tf_op jit(solution)/shard_map/dot_general | solution.py:24
  370.6 9.6 %fusion.25 = (bf16[640,1024]{1,0:T(8,128)(2,1)}, f32[640,1024]{1,0:T(8,128)S(1)}) fusion(f32[1024]{0:T(1024)S(1)} %get-tuple-element.194, bf16[640,1024]{0,1:T(8,128)(2,1)S(1)} %add_convert_fusion.6, bf16[1024,1024]{1,0:T(8,128)(2,1)} %collective-permute-done.30), kind=kOutput, calls=%fused_computation.55 | convolution fusion | flops 1385431040 | bytes 7344128 | tf_op jit(solution)/shard_map/dot_general | solution.py:24
  382.8 3.9 fusion.215
  386.7 4.1 convert_reduce_fusion.4
  390.8 4.5 convert_reduce_fusion.3
  395.3 3.9 fusion.217
  399.2 9.6 %fusion.19 = (bf16[640,1024]{1,0:T(8,128)(2,1)}, f32[640,1024]{1,0:T(8,128)S(1)}) fusion(f32[1024]{0:T(1024)S(1)} %get-tuple-element.195, bf16[640,1024]{0,1:T(8,128)(2,1)S(1)} %add_convert_fusion.6, bf16[1024,1024]{1,0:T(8,128)(2,1)} %collective-permute-done.25), kind=kOutput, calls=%fused_computation.49 | convolution fusion | flops 1385431040 | bytes 7344128 | tf_op jit(solution)/shard_map/dot_general | solution.py:24
  408.8 4.0 convert_reduce_fusion.5
  412.9 3.9 fusion.216
  416.8 4.4 multiply_reduce_fusion
  442.0 3.9 copy.256.v_ref
  446.0 35.4 %cross_backward.1 = (bf16[4,256,640]{2,1,0:T(8,128)(2,1)}, bf16[4,1024,256]{2,1,0:T(8,128)(2,1)}, bf16[4,1024,256]{2,1,0:T(8,128)(2,1)}) custom-call(f32[1024,1]{1,0:T(8,128)} %convert_element_type.587.ok_ref, bf16[4,640,256]{2,1,0:T(8,128)(2,1)} %pad_maximum_fusion.12.q_ref, bf16[4,1024,256]{2,1,0:T(8,128)(2,1)} %copy.234.k_ref, ...), custom_call_target="tpu_custom_call" | custom-call | flops 32212254720 | bytes 16777216 | tf_op jit(solution)/shard_map/cross_backward/pallas_call | solution.py:331
  527.3 3.5 fusion.213
  530.8 3.4 fusion.214
  534.3 5.1 add_add_fusion.7
  539.4 3.3 copy.282
  559.3 12.8 %collective-permute-done.40 = bf16[4,256,512]{2,1,0:T(8,128)(2,1)S(1)} collective-permute-done((bf16[4,256,512]{2,1,0:T(8,128)(2,1)S(1)}, bf16[4,256,512]{2,1,0:T(8,128)(2,1)S(1)}, u32[]{:S(2)}, u32[]{:S(2)}) %collective-permute-start.40) | collective-permute-done | bytes 1048608 | tf_op jit(solution)/shard_map/ppermute | solution.py:362
  589.4 3.4 add_convert_fusion.1
  594.5 3.7 add_convert_fusion.2
  600.6 5.4 fusion
  607.3 5.0 bitcast_multiply_fusion
  615.3 50.7 %self_backward.1 = (bf16[256,2560]{1,0:T(8,128)(2,1)}, bf16[2560,256]{1,0:T(8,128)(2,1)}, bf16[2560,256]{1,0:T(8,128)(2,1)}) custom-call(s32[1,2]{1,0:T(1,128)} %b_ref.3, bf16[2560,256]{1,0:T(8,128)(2,1)} %get-tuple-element.117.q_ref, bf16[2560,256]{1,0:T(8,128)(2,1)} %copy.226.k_ref, bf16[2560,256]{1,0:T(8,128)(2,1)} %copy-done.30, ...), custom_call_target="tpu_custom_call" | custom-call | flops 40265318400 | bytes 10485760 | tf_op jit(solution)/shard_map/self_backward/pallas_call | solution.py:207
  668.2 9.2 %convolution_convert_fusion.1 = bf16[2560,1024]{0,1:T(8,128)(2,1)} fusion(bf16[1024,1024]{1,0:T(8,128)(2,1)} %in_order.6, bf16[2560,256]{1,0:T(8,128)(2,1)} %get-tuple-element.30, bf16[2560,256]{1,0:T(8,128)(2,1)} %get-tuple-element.29, bf16[2560,256]{1,0:T(8,128)(2,1)S(1)} %bitcast.444), kind=kOutput, calls=%fused_computation.2 | convolution fusion | flops 4040949760 | bytes 10747904 | tf_op jit(solution)/shard_map/dot_general | solution.py:20
  677.5 6.9 convolution_convert_fusion.5
  687.5 3.4 reshape.314
  690.9 4.3 constant_dynamic-slice_fusion.9
  704.0 16.7 %collective-permute-done.51 = bf16[2,2,128,1024]{2,3,0,1:T(8,128)(2,1)S(1)} collective-permute-done((bf16[2,2,128,1024]{2,3,0,1:T(8,128)(2,1)S(1)}, bf16[2,2,128,1024]{2,3,0,1:T(8,128)(2,1)S(1)}, u32[]{:S(2)}, u32[]{:S(2)}) %collective-permute-start.51) | collective-permute-done | bytes 1048608 | tf_op jit(solution)/shard_map/ppermute | solution.py:362
  732.5 3.9 add_convert_fusion.3
  742.5 8.5 constant_dynamic-slice_fusion.7
  751.0 6.3 constant_dynamic-slice_fusion.5
  757.3 5.8 copy.319
  763.1 6.0 copy.318
  769.1 5.8 copy.321
  775.0 4.5 copy.320
  779.6 10.7 %collective-permute-done.65 = bf16[4,128,1024]{2,1,0:T(8,128)(2,1)} collective-permute-done((bf16[4,128,1024]{2,1,0:T(8,128)(2,1)}, bf16[4,128,1024]{2,1,0:T(8,128)(2,1)}, u32[]{:S(2)}, u32[]{:S(2)}) %collective-permute-start.65) | collective-permute-done | bytes 1048608 | tf_op jit(solution)/shard_map/ppermute | solution.py:362
  800.1 3.7 add_convert_fusion
  806.2 5.0 collective-permute-done.53
  818.0 3.4 collective-permute-start.67
  837.6 7.5 collective-permute-done.57
  851.9 3.9 collective-permute-start.48
  855.9 8.4 collective-permute-done.71
  873.3 3.7 collective-permute-done.50
  881.4 4.3 collective-permute-done.72
  889.8 8.0 collective-permute-done.59
  902.2 8.7 collective-permute-done.60
  (672 shorter events, 327.0 us)
Async XLA Ops:
  9.1 50.5 %collective-permute-start.1 = (bf16[640,1024]{0,1:T(8,128)(2,1)}, bf16[640,1024]{0,1:T(8,128)(2,1)}, u32[]{:S(2)}, u32[]{:S(2)}) collective-permute-start(bf16[640,1024]{0,1:T(8,128)(2,1)} %get-tuple-element.115), channel_id=1, source_target_pairs={{0,2},{1,3},{2,0},{3,1},{4,6},{5,7},{6,4},{7,5},{8,10},{9,11},{10,... | collective-permute-start | bytes 3932168 | tf_op jit(solution)/shard_map/ppermute | solution.py:362
  12.5 21.2 %collective-permute-start.3 = (bf16[1,128,1024]{2,1,0:T(8,128)(2,1)S(1)}, bf16[1,128,1024]{2,1,0:T(8,128)(2,1)S(1)}, u32[]{:S(2)}, u32[]{:S(2)}) collective-permute-start(bf16[1,128,1024]{2,1,0:T(8,128)(2,1)S(1)} %maximum_bitcast_fusion.4), channel_id=1, source_target_pairs={{0,16},{4,20},{8,24},{12,28},{16,0},{20,4},{24,8},{28,12},{1,17},{... | collective-permute-start | bytes 786440 | tf_op jit(solution)/shard_map/ppermute | solution.py:362
  15.3 22.9 %collective-permute-start.9 = (bf16[1,128,1024]{2,1,0:T(8,128)(2,1)S(1)}, bf16[1,128,1024]{2,1,0:T(8,128)(2,1)S(1)}, u32[]{:S(2)}, u32[]{:S(2)}) collective-permute-start(bf16[1,128,1024]{2,1,0:T(8,128)(2,1)S(1)} %maximum_bitcast_fusion.5), channel_id=1, source_target_pairs={{0,16},{4,20},{8,24},{12,28},{16,0},{20,4},{24,8},{28,12},{1,17},{... | collective-permute-start | bytes 786440 | tf_op jit(solution)/shard_map/ppermute | solution.py:362
  34.5 20.7 %collective-permute-start.4 = (bf16[2,128,1024]{2,1,0:T(8,128)(2,1)}, bf16[2,128,1024]{2,1,0:T(8,128)(2,1)}, u32[]{:S(2)}, u32[]{:S(2)}) collective-permute-start(bf16[2,128,1024]{2,1,0:T(8,128)(2,1)} %pad_maximum_fusion.21), channel_id=1, source_target_pairs={{0,8},{4,12},{8,0},{12,4},{16,24},{20,28},{24,16},{28,20},{1,9},{5... | collective-permute-start | bytes 1572872 | tf_op jit(solution)/shard_map/ppermute | solution.py:362
  34.5 52.6 %collective-permute-start = (bf16[640,1024]{0,1:T(8,128)(2,1)}, bf16[640,1024]{0,1:T(8,128)(2,1)}, u32[]{:S(2)}, u32[]{:S(2)}) collective-permute-start(bf16[640,1024]{0,1:T(8,128)(2,1)} %get-tuple-element.115), channel_id=1, source_target_pairs={{0,1},{1,0},{2,3},{3,2},{4,5},{5,4},{6,7},{7,6},{8,9},{9,8},{10,11... | collective-permute-start | bytes 3932168 | tf_op jit(solution)/shard_map/ppermute | solution.py:362
  34.6 23.4 %collective-permute-start.19 = (bf16[1,128,1024]{2,1,0:T(8,128)(2,1)S(1)}, bf16[1,128,1024]{2,1,0:T(8,128)(2,1)S(1)}, u32[]{:S(2)}, u32[]{:S(2)}) collective-permute-start(bf16[1,128,1024]{2,1,0:T(8,128)(2,1)S(1)} %bitcast.455), channel_id=1, source_target_pairs={{0,16},{4,20},{8,24},{12,28},{16,0},{20,4},{24,8},{28,12},{1,17},{... | collective-permute-start | bytes 786440 | tf_op jit(solution)/shard_map/ppermute | solution.py:362
  39.1 32.8 %collective-permute-start.10 = (bf16[2,128,1024]{2,1,0:T(8,128)(2,1)}, bf16[2,128,1024]{2,1,0:T(8,128)(2,1)}, u32[]{:S(2)}, u32[]{:S(2)}) collective-permute-start(bf16[2,128,1024]{2,1,0:T(8,128)(2,1)} %pad_maximum_fusion.22), channel_id=1, source_target_pairs={{0,8},{4,12},{8,0},{12,4},{16,24},{20,28},{24,16},{28,20},{1,9},{5... | collective-permute-start | bytes 1572872 | tf_op jit(solution)/shard_map/ppermute | solution.py:362
  55.3 18.8 %collective-permute-start.22 = (bf16[1,128,1024]{2,1,0:T(8,128)(2,1)S(1)}, bf16[1,128,1024]{2,1,0:T(8,128)(2,1)S(1)}, u32[]{:S(2)}, u32[]{:S(2)}) collective-permute-start(bf16[1,128,1024]{2,1,0:T(8,128)(2,1)S(1)} %bitcast.451), channel_id=1, source_target_pairs={{0,16},{4,20},{8,24},{12,28},{16,0},{20,4},{24,8},{28,12},{1,17},{... | collective-permute-start | bytes 786440 | tf_op jit(solution)/shard_map/ppermute | solution.py:362
  58.0 35.8 %collective-permute-start.5 = (bf16[4,128,1024]{2,1,0:T(8,128)(2,1)S(1)}, bf16[4,128,1024]{2,1,0:T(8,128)(2,1)S(1)}, u32[]{:S(2)}, u32[]{:S(2)}) collective-permute-start(bf16[4,128,1024]{2,1,0:T(8,128)(2,1)S(1)} %pad_maximum_fusion.14), channel_id=1, source_target_pairs={{0,4},{4,0},{8,12},{12,8},{16,20},{20,16},{24,28},{28,24},{1,5},{5... | collective-permute-start | bytes 3145736 | tf_op jit(solution)/shard_map/ppermute | solution.py:362
  59.6 44.1 %collective-permute-start.2 = (bf16[640,1024]{0,1:T(8,128)(2,1)}, bf16[640,1024]{0,1:T(8,128)(2,1)}, u32[]{:S(2)}, u32[]{:S(2)}) collective-permute-start(bf16[640,1024]{0,1:T(8,128)(2,1)} %collective-permute-done.1), channel_id=1, source_target_pairs={{0,1},{1,0},{2,3},{3,2},{4,5},{5,4},{6,7},{7,6},{8,9},{9,8},{10,11... | collective-permute-start | bytes 3932168 | tf_op jit(solution)/shard_map/ppermute | solution.py:362
  71.9 13.7 %collective-permute-start.20 = (bf16[2,128,1024]{2,1,0:T(8,128)(2,1)S(1)}, bf16[2,128,1024]{2,1,0:T(8,128)(2,1)S(1)}, u32[]{:S(2)}, u32[]{:S(2)}) collective-permute-start(bf16[2,128,1024]{2,1,0:T(8,128)(2,1)S(1)} %pad_maximum_fusion.23), channel_id=1, source_target_pairs={{0,8},{4,12},{8,0},{12,4},{16,24},{20,28},{24,16},{28,20},{1,9},{5... | collective-permute-start | bytes 1572872 | tf_op jit(solution)/shard_map/ppermute | solution.py:362
  74.1 29.1 %collective-permute-start.13 = (bf16[4,128,1024]{2,1,0:T(8,128)(2,1)}, bf16[4,128,1024]{2,1,0:T(8,128)(2,1)}, u32[]{:S(2)}, u32[]{:S(2)}) collective-permute-start(bf16[4,128,1024]{2,1,0:T(8,128)(2,1)} %pad_maximum_fusion.15), channel_id=1, source_target_pairs={{0,2},{1,3},{2,0},{3,1},{4,6},{5,7},{6,4},{7,5},{8,10},{9,11},{10,... | collective-permute-start | bytes 3145736 | tf_op jit(solution)/shard_map/ppermute | solution.py:362
  85.7 75.2 %collective-permute-start.23 = (bf16[2,128,1024]{2,1,0:T(8,128)(2,1)}, bf16[2,128,1024]{2,1,0:T(8,128)(2,1)}, u32[]{:S(2)}, u32[]{:S(2)}) collective-permute-start(bf16[2,128,1024]{2,1,0:T(8,128)(2,1)} %pad_maximum_fusion.24), channel_id=1, source_target_pairs={{0,8},{4,12},{8,0},{12,4},{16,24},{20,28},{24,16},{28,20},{1,9},{5... | collective-permute-start | bytes 1572872 | tf_op jit(solution)/shard_map/ppermute | solution.py:362
  87.1 75.9 %collective-permute-start.11 = (bf16[4,128,1024]{2,1,0:T(8,128)(2,1)}, bf16[4,128,1024]{2,1,0:T(8,128)(2,1)}, u32[]{:S(2)}, u32[]{:S(2)}) collective-permute-start(bf16[4,128,1024]{2,1,0:T(8,128)(2,1)} %pad_maximum_fusion.15), channel_id=1, source_target_pairs={{0,4},{4,0},{8,12},{12,8},{16,20},{20,16},{24,28},{28,24},{1,5},{5... | collective-permute-start | bytes 3145736 | tf_op jit(solution)/shard_map/ppermute | solution.py:362
  93.8 88.6 %collective-permute-start.21 = (bf16[4,128,1024]{2,1,0:T(8,128)(2,1)}, bf16[4,128,1024]{2,1,0:T(8,128)(2,1)}, u32[]{:S(2)}, u32[]{:S(2)}) collective-permute-start(bf16[4,128,1024]{2,1,0:T(8,128)(2,1)} %pad_maximum_fusion.17), channel_id=1, source_target_pairs={{0,4},{4,0},{8,12},{12,8},{16,20},{20,16},{24,28},{28,24},{1,5},{5... | collective-permute-start | bytes 3145736 | tf_op jit(solution)/shard_map/ppermute | solution.py:362
  103.2 85.2 %collective-permute-start.27 = (bf16[4,128,1024]{2,1,0:T(8,128)(2,1)}, bf16[4,128,1024]{2,1,0:T(8,128)(2,1)}, u32[]{:S(2)}, u32[]{:S(2)}) collective-permute-start(bf16[4,128,1024]{2,1,0:T(8,128)(2,1)} %pad_maximum_fusion.17), channel_id=1, source_target_pairs={{0,2},{1,3},{2,0},{3,1},{4,6},{5,7},{6,4},{7,5},{8,10},{9,11},{10,... | collective-permute-start | bytes 3145736 | tf_op jit(solution)/shard_map/ppermute | solution.py:362
  103.7 69.1 %collective-permute-start.14 = (bf16[4,128,1024]{2,1,0:T(8,128)(2,1)}, bf16[4,128,1024]{2,1,0:T(8,128)(2,1)}, u32[]{:S(2)}, u32[]{:S(2)}) collective-permute-start(bf16[4,128,1024]{2,1,0:T(8,128)(2,1)} %collective-permute-done.13), channel_id=1, source_target_pairs={{0,4},{4,0},{8,12},{12,8},{16,20},{20,16},{24,28},{28,24},{1,5},{5... | collective-permute-start | bytes 3145736 | tf_op jit(solution)/shard_map/ppermute | solution.py:362
  160.9 47.4 %collective-permute-start.7 = (bf16[640,1024]{0,1:T(8,128)(2,1)}, bf16[640,1024]{0,1:T(8,128)(2,1)}, u32[]{:S(2)}, u32[]{:S(2)}) collective-permute-start(bf16[640,1024]{0,1:T(8,128)(2,1)} %get-tuple-element.121), channel_id=1, source_target_pairs={{0,1},{1,0},{2,3},{3,2},{4,5},{5,4},{6,7},{7,6},{8,9},{9,8},{10,11... | collective-permute-start | bytes 3932168 | tf_op jit(solution)/shard_map/ppermute | solution.py:362
  163.0 36.0 %collective-permute-start.24 = (bf16[4,128,1024]{2,1,0:T(8,128)(2,1)}, bf16[4,128,1024]{2,1,0:T(8,128)(2,1)}, u32[]{:S(2)}, u32[]{:S(2)}) collective-permute-start(bf16[4,128,1024]{2,1,0:T(8,128)(2,1)} %pad_maximum_fusion.18), channel_id=1, source_target_pairs={{0,4},{4,0},{8,12},{12,8},{16,20},{20,16},{24,28},{28,24},{1,5},{5... | collective-permute-start | bytes 3145736 | tf_op jit(solution)/shard_map/ppermute | solution.py:362
  172.7 54.1 %collective-permute-start.12 = (bf16[1024,1024]{1,0:T(8,128)(2,1)}, bf16[1024,1024]{1,0:T(8,128)(2,1)}, u32[]{:S(2)}, u32[]{:S(2)}) collective-permute-start(bf16[1024,1024]{1,0:T(8,128)(2,1)} %in_order.7), channel_id=1, source_target_pairs={{0,1},{1,0},{2,3},{3,2},{4,5},{5,4},{6,7},{7,6},{8,9},{9,8},{10,11... | collective-permute-start | bytes 6291464 | tf_op jit(solution)/shard_map/ppermute | solution.py:362
  182.3 46.8 %collective-permute-start.15 = (bf16[1024,1024]{1,0:T(8,128)(2,1)}, bf16[1024,1024]{1,0:T(8,128)(2,1)}, u32[]{:S(2)}, u32[]{:S(2)}) collective-permute-start(bf16[1024,1024]{1,0:T(8,128)(2,1)} %in_order.8), channel_id=1, source_target_pairs={{0,1},{1,0},{2,3},{3,2},{4,5},{5,4},{6,7},{7,6},{8,9},{9,8},{10,11... | collective-permute-start | bytes 6291464 | tf_op jit(solution)/shard_map/ppermute | solution.py:362
  188.4 26.6 %collective-permute-start.28 = (bf16[4,128,1024]{2,1,0:T(8,128)(2,1)}, bf16[4,128,1024]{2,1,0:T(8,128)(2,1)}, u32[]{:S(2)}, u32[]{:S(2)}) collective-permute-start(bf16[4,128,1024]{2,1,0:T(8,128)(2,1)} %collective-permute-done.27), channel_id=1, source_target_pairs={{0,4},{4,0},{8,12},{12,8},{16,20},{20,16},{24,28},{28,24},{1,5},{5... | collective-permute-start | bytes 3145736 | tf_op jit(solution)/shard_map/ppermute | solution.py:362
  208.3 22.8 %collective-permute-start.6 = (bf16[640,1024]{0,1:T(8,128)(2,1)}, bf16[640,1024]{0,1:T(8,128)(2,1)}, u32[]{:S(2)}, u32[]{:S(2)}) collective-permute-start(bf16[640,1024]{0,1:T(8,128)(2,1)} %get-tuple-element.120), channel_id=1, source_target_pairs={{0,1},{1,0},{2,3},{3,2},{4,5},{5,4},{6,7},{7,6},{8,9},{9,8},{10,11... | collective-permute-start | bytes 3932168 | tf_op jit(solution)/shard_map/ppermute | solution.py:362
  211.6 31.9 %collective-permute-start.8 = (bf16[640,1024]{0,1:T(8,128)(2,1)}, bf16[640,1024]{0,1:T(8,128)(2,1)}, u32[]{:S(2)}, u32[]{:S(2)}) collective-permute-start(bf16[640,1024]{0,1:T(8,128)(2,1)} %add_convert_fusion.8), channel_id=1, source_target_pairs={{0,2},{1,3},{2,0},{3,1},{4,6},{5,7},{6,4},{7,5},{8,10},{9,11},{10,... | collective-permute-start | bytes 3932168 | tf_op jit(solution)/shard_map/ppermute | solution.py:362
  215.0 193.8 %collective-permute-start.26 = (bf16[1024,1024]{1,0:T(8,128)(2,1)}, bf16[1024,1024]{1,0:T(8,128)(2,1)}, u32[]{:S(2)}, u32[]{:S(2)}) collective-permute-start(bf16[1024,1024]{1,0:T(8,128)(2,1)} %in_order.10), channel_id=1, source_target_pairs={{0,1},{1,0},{2,3},{3,2},{4,5},{5,4},{6,7},{7,6},{8,9},{9,8},{10,11... | collective-permute-start | bytes 6291464 | tf_op jit(solution)/shard_map/ppermute | solution.py:362
  226.8 88.2 %collective-permute-start.29 = (bf16[1024,1024]{1,0:T(8,128)(2,1)}, bf16[1024,1024]{1,0:T(8,128)(2,1)}, u32[]{:S(2)}, u32[]{:S(2)}) collective-permute-start(bf16[1024,1024]{1,0:T(8,128)(2,1)} %in_order.10), channel_id=1, source_target_pairs={{0,2},{1,3},{2,0},{3,1},{4,6},{5,7},{6,4},{7,5},{8,10},{9,11},{10,... | collective-permute-start | bytes 6291464 | tf_op jit(solution)/shard_map/ppermute | solution.py:362
  229.2 170.0 %collective-permute-start.25 = (bf16[1024,1024]{1,0:T(8,128)(2,1)}, bf16[1024,1024]{1,0:T(8,128)(2,1)}, u32[]{:S(2)}, u32[]{:S(2)}) collective-permute-start(bf16[1024,1024]{1,0:T(8,128)(2,1)} %in_order.9), channel_id=1, source_target_pairs={{0,1},{1,0},{2,3},{3,2},{4,5},{5,4},{6,7},{7,6},{8,9},{9,8},{10,11... | collective-permute-start | bytes 6291464 | tf_op jit(solution)/shard_map/ppermute | solution.py:362
  231.1 79.3 %collective-permute-start.17 = (bf16[4,256,512]{1,2,0:T(8,128)(2,1)S(1)}, bf16[4,256,512]{1,2,0:T(8,128)(2,1)S(1)}, u32[]{:S(2)}, u32[]{:S(2)}) collective-permute-start(bf16[4,256,512]{1,2,0:T(8,128)(2,1)S(1)} %pad_maximum_fusion.16), channel_id=1, source_target_pairs={{0,2},{1,3},{2,0},{3,1},{4,6},{5,7},{6,4},{7,5},{8,10},{9,11},{10,... | collective-permute-start | bytes 3145736 | tf_op jit(solution)/shard_map/ppermute | solution.py:362
  243.4 72.2 %collective-permute-start.16 = (bf16[4,256,512]{1,2,0:T(8,128)(2,1)S(1)}, bf16[4,256,512]{1,2,0:T(8,128)(2,1)S(1)}, u32[]{:S(2)}, u32[]{:S(2)}) collective-permute-start(bf16[4,256,512]{1,2,0:T(8,128)(2,1)S(1)} %pad_maximum_fusion.16), channel_id=1, source_target_pairs={{0,1},{1,0},{2,3},{3,2},{4,5},{5,4},{6,7},{7,6},{8,9},{9,8},{10,11... | collective-permute-start | bytes 3145736 | tf_op jit(solution)/shard_map/ppermute | solution.py:362
  315.0 55.6 %collective-permute-start.30 = (bf16[1024,1024]{1,0:T(8,128)(2,1)}, bf16[1024,1024]{1,0:T(8,128)(2,1)}, u32[]{:S(2)}, u32[]{:S(2)}) collective-permute-start(bf16[1024,1024]{1,0:T(8,128)(2,1)} %in_order.11), channel_id=1, source_target_pairs={{0,1},{1,0},{2,3},{3,2},{4,5},{5,4},{6,7},{7,6},{8,9},{9,8},{10,11... | collective-permute-start | bytes 6291464 | tf_op jit(solution)/shard_map/ppermute | solution.py:362
  315.6 75.1 %collective-permute-start.31 = (bf16[1024,1024]{1,0:T(8,128)(2,1)}, bf16[1024,1024]{1,0:T(8,128)(2,1)}, u32[]{:S(2)}, u32[]{:S(2)}) collective-permute-start(bf16[1024,1024]{1,0:T(8,128)(2,1)} %collective-permute-done.29), channel_id=1, source_target_pairs={{0,1},{1,0},{2,3},{3,2},{4,5},{5,4},{6,7},{7,6},{8,9},{9,8},{10,11... | collective-permute-start | bytes 6291464 | tf_op jit(solution)/shard_map/ppermute | solution.py:362
  495.4 57.9 %collective-permute-start.32 = (bf16[640,1024]{0,1:T(8,128)(2,1)}, bf16[640,1024]{0,1:T(8,128)(2,1)}, u32[]{:S(2)}, u32[]{:S(2)}) collective-permute-start(bf16[640,1024]{0,1:T(8,128)(2,1)} %get-tuple-element.105), channel_id=1, source_target_pairs={{0,1},{1,0},{2,3},{3,2},{4,5},{5,4},{6,7},{7,6},{8,9},{9,8},{10,11... | collective-permute-start | bytes 3932168 | tf_op jit(solution)/shard_map/ppermute | solution.py:362
  495.8 60.4 %collective-permute-start.33 = (bf16[640,1024]{0,1:T(8,128)(2,1)}, bf16[640,1024]{0,1:T(8,128)(2,1)}, u32[]{:S(2)}, u32[]{:S(2)}) collective-permute-start(bf16[640,1024]{0,1:T(8,128)(2,1)} %get-tuple-element.105), channel_id=1, source_target_pairs={{0,2},{1,3},{2,0},{3,1},{4,6},{5,7},{6,4},{7,5},{8,10},{9,11},{10,... | collective-permute-start | bytes 3932168 | tf_op jit(solution)/shard_map/ppermute | solution.py:362
  516.7 42.2 %collective-permute-start.38 = (bf16[4,256,512]{2,1,0:T(8,128)(2,1)}, bf16[4,256,512]{2,1,0:T(8,128)(2,1)}, u32[]{:S(2)}, u32[]{:S(2)}) collective-permute-start(bf16[4,256,512]{2,1,0:T(8,128)(2,1)} %pad_maximum_fusion.19), channel_id=1, source_target_pairs={{0,1},{1,0},{2,3},{3,2},{4,5},{5,4},{6,7},{7,6},{8,9},{9,8},{10,11... | collective-permute-start | bytes 3145736 | tf_op jit(solution)/shard_map/ppermute | solution.py:362
  517.8 26.9 %collective-permute-start.39 = (bf16[4,256,512]{2,1,0:T(8,128)(2,1)}, bf16[4,256,512]{2,1,0:T(8,128)(2,1)}, u32[]{:S(2)}, u32[]{:S(2)}) collective-permute-start(bf16[4,256,512]{2,1,0:T(8,128)(2,1)} %pad_maximum_fusion.20), channel_id=1, source_target_pairs={{0,1},{1,0},{2,3},{3,2},{4,5},{5,4},{6,7},{7,6},{8,9},{9,8},{10,11... | collective-permute-start | bytes 3145736 | tf_op jit(solution)/shard_map/ppermute | solution.py:362
  524.1 76.5 %collective-permute-start.69 = (bf16[1024,1024]{1,0:T(8,128)(2,1)}, bf16[1024,1024]{1,0:T(8,128)(2,1)}, u32[]{:S(2)}, u32[]{:S(2)}) collective-permute-start(bf16[1024,1024]{1,0:T(8,128)(2,1)} %convert_bitcast_fusion), channel_id=1, source_target_pairs={{0,1},{1,0},{2,3},{3,2},{4,5},{5,4},{6,7},{7,6},{8,9},{9,8},{10,11... | collective-permute-start | bytes 6291464 | tf_op jit(solution)/shard_map/ppermute | solution.py:362
  546.4 25.6 %collective-permute-start.40 = (bf16[4,256,512]{2,1,0:T(8,128)(2,1)S(1)}, bf16[4,256,512]{2,1,0:T(8,128)(2,1)S(1)}, u32[]{:S(2)}, u32[]{:S(2)}) collective-permute-start(bf16[4,256,512]{2,1,0:T(8,128)(2,1)S(1)} %add_convert_fusion.12), channel_id=1, source_target_pairs={{0,2},{1,3},{2,0},{3,1},{4,6},{5,7},{6,4},{7,5},{8,10},{9,11},{10,... | collective-permute-start | bytes 3145736 | tf_op jit(solution)/shard_map/ppermute | solution.py:362
  553.3 40.7 %collective-permute-start.61 = (bf16[1024,1024]{1,0:T(8,128)(2,1)}, bf16[1024,1024]{1,0:T(8,128)(2,1)}, u32[]{:S(2)}, u32[]{:S(2)}) collective-permute-start(bf16[1024,1024]{1,0:T(8,128)(2,1)} %convolution_convert_fusion.4), channel_id=1, source_target_pairs={{0,1},{1,0},{2,3},{3,2},{4,5},{5,4},{6,7},{7,6},{8,9},{9,8},{10,11... | collective-permute-start | bytes 6291464 | tf_op jit(solution)/shard_map/ppermute | solution.py:362
  556.2 32.7 %collective-permute-start.63 = (bf16[1024,1024]{1,0:T(8,128)(2,1)}, bf16[1024,1024]{1,0:T(8,128)(2,1)}, u32[]{:S(2)}, u32[]{:S(2)}) collective-permute-start(bf16[1024,1024]{1,0:T(8,128)(2,1)} %convolution_convert_fusion.3), channel_id=1, source_target_pairs={{0,1},{1,0},{2,3},{3,2},{4,5},{5,4},{6,7},{7,6},{8,9},{9,8},{10,11... | collective-permute-start | bytes 6291464 | tf_op jit(solution)/shard_map/ppermute | solution.py:362
  559.0 47.0 %collective-permute-start.34 = (bf16[640,1024]{0,1:T(8,128)(2,1)}, bf16[640,1024]{0,1:T(8,128)(2,1)S(1)}, u32[]{:S(2)}, u32[]{:S(2)}) collective-permute-start(bf16[640,1024]{0,1:T(8,128)(2,1)} %collective-permute-done.33), channel_id=1, source_target_pairs={{0,1},{1,0},{2,3},{3,2},{4,5},{5,4},{6,7},{7,6},{8,9},{9,8},{10,11... | collective-permute-start | bytes 3932168 | tf_op jit(solution)/shard_map/ppermute | solution.py:362
  577.3 149.2 %collective-permute-start.54 = (bf16[1024,1024]{0,1:T(8,128)(2,1)}, bf16[1024,1024]{0,1:T(8,128)(2,1)}, u32[]{:S(2)}, u32[]{:S(2)}) collective-permute-start(bf16[1024,1024]{0,1:T(8,128)(2,1)} %pad_maximum_fusion.10), channel_id=1, source_target_pairs={{0,1},{1,0},{2,3},{3,2},{4,5},{5,4},{6,7},{7,6},{8,9},{9,8},{10,11... | collective-permute-start | bytes 6291464 | tf_op jit(solution)/shard_map/ppermute | solution.py:362
  588.8 141.8 %collective-permute-start.56 = (bf16[1024,1024]{0,1:T(8,128)(2,1)}, bf16[1024,1024]{0,1:T(8,128)(2,1)}, u32[]{:S(2)}, u32[]{:S(2)}) collective-permute-start(bf16[1024,1024]{0,1:T(8,128)(2,1)} %pad_maximum_fusion.11), channel_id=1, source_target_pairs={{0,1},{1,0},{2,3},{3,2},{4,5},{5,4},{6,7},{7,6},{8,9},{9,8},{10,11... | collective-permute-start | bytes 6291464 | tf_op jit(solution)/shard_map/ppermute | solution.py:362
  594.0 106.7 %collective-permute-start.64 = (bf16[4,128,1024]{2,1,0:T(8,128)(2,1)}, bf16[4,128,1024]{2,1,0:T(8,128)(2,1)}, u32[]{:S(2)}, u32[]{:S(2)}) collective-permute-start(bf16[4,128,1024]{2,1,0:T(8,128)(2,1)} %dynamic-slice_bitcast_fusion), channel_id=1, source_target_pairs={{0,4},{4,0},{8,12},{12,8},{16,20},{20,16},{24,28},{28,24},{1,5},{5... | collective-permute-start | bytes 3145736 | tf_op jit(solution)/shard_map/ppermute | solution.py:362
  695.5 25.2 %collective-permute-start.51 = (bf16[2,2,128,1024]{2,3,0,1:T(8,128)(2,1)S(1)}, bf16[2,2,128,1024]{2,3,0,1:T(8,128)(2,1)S(1)}, u32[]{:S(2)}, u32[]{:S(2)}) collective-permute-start(bf16[2,2,128,1024]{2,3,0,1:T(8,128)(2,1)S(1)} %bitcast.464), channel_id=1, source_target_pairs={{0,4},{4,0},{8,12},{12,8},{16,20},{20,16},{24,28},{28,24},{1,5},{5... | collective-permute-start | bytes 3145736 | tf_op jit(solution)/shard_map/ppermute | solution.py:362
  699.8 22.5 %collective-permute-start.36 = (bf16[640,1024]{0,1:T(8,128)(2,1)S(1)}, bf16[640,1024]{0,1:T(8,128)(2,1)S(1)}, u32[]{:S(2)}, u32[]{:S(2)}) collective-permute-start(bf16[640,1024]{0,1:T(8,128)(2,1)S(1)} %get-tuple-element.119), channel_id=1, source_target_pairs={{0,1},{1,0},{2,3},{3,2},{4,5},{5,4},{6,7},{7,6},{8,9},{9,8},{10,11... | collective-permute-start | bytes 3932168 | tf_op jit(solution)/shard_map/ppermute | solution.py:362
  700.7 95.4 %collective-permute-start.68 = (bf16[1024,1024]{1,0:T(8,128)(2,1)}, bf16[1024,1024]{1,0:T(8,128)(2,1)}, u32[]{:S(2)}, u32[]{:S(2)}) collective-permute-start(bf16[1024,1024]{1,0:T(8,128)(2,1)} %convert_bitcast_fusion.1), channel_id=1, source_target_pairs={{0,1},{1,0},{2,3},{3,2},{4,5},{5,4},{6,7},{7,6},{8,9},{9,8},{10,11... | collective-permute-start | bytes 6291464 | tf_op jit(solution)/shard_map/ppermute | solution.py:362
  720.7 77.0 %collective-permute-start.70 = (bf16[1024,1024]{1,0:T(8,128)(2,1)}, bf16[1024,1024]{1,0:T(8,128)(2,1)}, u32[]{:S(2)}, u32[]{:S(2)}) collective-permute-start(bf16[1024,1024]{1,0:T(8,128)(2,1)} %fusion), channel_id=1, source_target_pairs={{0,2},{1,3},{2,0},{3,1},{4,6},{5,7},{6,4},{7,5},{8,10},{9,11},{10,... | collective-permute-start | bytes 6291464 | tf_op jit(solution)/shard_map/ppermute | solution.py:362
  722.3 57.1 %collective-permute-start.62 = (bf16[4,128,1024]{2,1,0:T(8,128)(2,1)}, bf16[4,128,1024]{2,1,0:T(8,128)(2,1)}, u32[]{:S(2)}, u32[]{:S(2)}) collective-permute-start(bf16[4,128,1024]{2,1,0:T(8,128)(2,1)} %dynamic-slice_bitcast_fusion.1), channel_id=1, source_target_pairs={{0,4},{4,0},{8,12},{12,8},{16,20},{20,16},{24,28},{28,24},{1,5},{5... | collective-permute-start | bytes 3145736 | tf_op jit(solution)/shard_map/ppermute | solution.py:362
  726.5 63.8 %collective-permute-start.65 = (bf16[4,128,1024]{2,1,0:T(8,128)(2,1)}, bf16[4,128,1024]{2,1,0:T(8,128)(2,1)}, u32[]{:S(2)}, u32[]{:S(2)}) collective-permute-start(bf16[4,128,1024]{2,1,0:T(8,128)(2,1)} %fusion.81), channel_id=1, source_target_pairs={{0,2},{1,3},{2,0},{3,1},{4,6},{5,7},{6,4},{7,5},{8,10},{9,11},{10,... | collective-permute-start | bytes 3145736 | tf_op jit(solution)/shard_map/ppermute | solution.py:362
  730.6 63.6 %collective-permute-start.52 = (bf16[2,128,1024]{1,2,0:T(8,128)(2,1)}, bf16[2,128,1024]{1,2,0:T(8,128)(2,1)S(1)}, u32[]{:S(2)}, u32[]{:S(2)}) collective-permute-start(bf16[2,128,1024]{1,2,0:T(8,128)(2,1)} %dynamic-slice_bitcast_fusion.4), channel_id=1, source_target_pairs={{0,8},{4,12},{8,0},{12,4},{16,24},{20,28},{24,16},{28,20},{1,9},{5... | collective-permute-start | bytes 1572872 | tf_op jit(solution)/shard_map/ppermute | solution.py:362
  779.5 38.5 %collective-permute-start.35 = (bf16[640,1024]{0,1:T(8,128)(2,1)}, bf16[640,1024]{0,1:T(8,128)(2,1)}, u32[]{:S(2)}, u32[]{:S(2)}) collective-permute-start(bf16[640,1024]{0,1:T(8,128)(2,1)} %get-tuple-element.118), channel_id=1, source_target_pairs={{0,1},{1,0},{2,3},{3,2},{4,5},{5,4},{6,7},{7,6},{8,9},{9,8},{10,11... | collective-permute-start | bytes 3932168 | tf_op jit(solution)/shard_map/ppermute | solution.py:362
  790.3 31.1 %collective-permute-start.37 = (bf16[640,1024]{0,1:T(8,128)(2,1)}, bf16[640,1024]{0,1:T(8,128)(2,1)}, u32[]{:S(2)}, u32[]{:S(2)}) collective-permute-start(bf16[640,1024]{0,1:T(8,128)(2,1)} %add_convert_fusion.5), channel_id=1, source_target_pairs={{0,2},{1,3},{2,0},{3,1},{4,6},{5,7},{6,4},{7,5},{8,10},{9,11},{10,... | collective-permute-start | bytes 3932168 | tf_op jit(solution)/shard_map/ppermute | solution.py:362
  794.2 22.0 %collective-permute-start.66 = (bf16[2,128,1024]{2,1,0:T(8,128)(2,1)}, bf16[2,128,1024]{2,1,0:T(8,128)(2,1)}, u32[]{:S(2)}, u32[]{:S(2)}) collective-permute-start(bf16[2,128,1024]{2,1,0:T(8,128)(2,1)} %dynamic-slice_bitcast_fusion.3), channel_id=1, source_target_pairs={{0,8},{4,12},{8,0},{12,4},{16,24},{20,28},{24,16},{28,20},{1,9},{5... | collective-permute-start | bytes 1572872 | tf_op jit(solution)/shard_map/ppermute | solution.py:362
  796.1 81.7 %collective-permute-start.55 = (bf16[4,128,1024]{2,1,0:T(8,128)(2,1)}, bf16[4,128,1024]{2,1,0:T(8,128)(2,1)}, u32[]{:S(2)}, u32[]{:S(2)}) collective-permute-start(bf16[4,128,1024]{2,1,0:T(8,128)(2,1)} %bitcast.129), channel_id=1, source_target_pairs={{0,4},{4,0},{8,12},{12,8},{16,20},{20,16},{24,28},{28,24},{1,5},{5... | collective-permute-start | bytes 3145736 | tf_op jit(solution)/shard_map/ppermute | solution.py:362
  797.7 13.5 %collective-permute-start.53 = (bf16[128,1024]{0,1:T(8,128)(2,1)S(1)}, bf16[128,1024]{0,1:T(8,128)(2,1)S(1)}, u32[]{:S(2)}, u32[]{:S(2)}) collective-permute-start(bf16[128,1024]{0,1:T(8,128)(2,1)S(1)} %dynamic-slice_bitcast_fusion.8), channel_id=1, source_target_pairs={{0,16},{4,20},{8,24},{12,28},{16,0},{20,4},{24,8},{28,12},{1,17},{... | collective-permute-start | bytes 786440 | tf_op jit(solution)/shard_map/ppermute | solution.py:362
  811.2 33.9 %collective-permute-start.57 = (bf16[4,128,1024]{2,1,0:T(8,128)(2,1)}, bf16[4,128,1024]{2,1,0:T(8,128)(2,1)}, u32[]{:S(2)}, u32[]{:S(2)}) collective-permute-start(bf16[4,128,1024]{2,1,0:T(8,128)(2,1)} %bitcast.133), channel_id=1, source_target_pairs={{0,4},{4,0},{8,12},{12,8},{16,20},{20,16},{24,28},{28,24},{1,5},{5... | collective-permute-start | bytes 3145736 | tf_op jit(solution)/shard_map/ppermute | solution.py:362
  816.2 48.1 %collective-permute-start.71 = (bf16[2,2,128,1024]{3,2,0,1:T(8,128)(2,1)}, bf16[2,2,128,1024]{3,2,0,1:T(8,128)(2,1)}, u32[]{:S(2)}, u32[]{:S(2)}) collective-permute-start(bf16[2,2,128,1024]{3,2,0,1:T(8,128)(2,1)} %bitcast.465), channel_id=1, source_target_pairs={{0,4},{4,0},{8,12},{12,8},{16,20},{20,16},{24,28},{28,24},{1,5},{5... | collective-permute-start | bytes 3145736 | tf_op jit(solution)/shard_map/ppermute | solution.py:362
  834.8 16.7 %collective-permute-start.43 = (f32[32,128]{1,0:T(8,128)S(1)}, f32[32,128]{1,0:T(8,128)S(1)}, u32[]{:S(2)}, u32[]{:S(2)}) collective-permute-start(f32[32,128]{1,0:T(8,128)S(1)} %add.810), channel_id=1, source_target_pairs={{0,16},{4,20},{8,24},{12,28},{16,0},{20,4},{24,8},{28,12},{1,17},{... | collective-permute-start | bytes 49160 | tf_op jit(solution)/shard_map/ppermute | solution.py:362
  836.9 15.0 %collective-permute-start.47 = (f32[104,128]{1,0:T(8,128)S(1)}, f32[104,128]{1,0:T(8,128)S(1)}, u32[]{:S(2)}, u32[]{:S(2)}) collective-permute-start(f32[104,128]{1,0:T(8,128)S(1)} %bitcast_add_fusion.2), channel_id=1, source_target_pairs={{0,2},{1,3},{2,0},{3,1},{4,6},{5,7},{6,4},{7,5},{8,10},{9,11},{10,... | collective-permute-start | bytes 159752 | tf_op jit(solution)/shard_map/ppermute | solution.py:362
  847.7 30.1 %collective-permute-start.58 = (bf16[4,128,1024]{2,1,0:T(8,128)(2,1)}, bf16[4,128,1024]{2,1,0:T(8,128)(2,1)}, u32[]{:S(2)}, u32[]{:S(2)}) collective-permute-start(bf16[4,128,1024]{2,1,0:T(8,128)(2,1)} %fusion.83), channel_id=1, source_target_pairs={{0,2},{1,3},{2,0},{3,1},{4,6},{5,7},{6,4},{7,5},{8,10},{9,11},{10,... | collective-permute-start | bytes 3145736 | tf_op jit(solution)/shard_map/ppermute | solution.py:362
  851.6 14.7 %collective-permute-start.44 = (f32[32,128]{1,0:T(8,128)S(1)}, f32[32,128]{1,0:T(8,128)S(1)}, u32[]{:S(2)}, u32[]{:S(2)}) collective-permute-start(f32[32,128]{1,0:T(8,128)S(1)} %add.811), channel_id=1, source_target_pairs={{0,8},{4,12},{8,0},{12,4},{16,24},{20,28},{24,16},{28,20},{1,9},{5... | collective-permute-start | bytes 49160 | tf_op jit(solution)/shard_map/ppermute | solution.py:362
  851.9 16.1 %collective-permute-start.48 = (f32[104,128]{1,0:T(8,128)S(1)}, f32[104,128]{1,0:T(8,128)S(1)}, u32[]{:S(2)}, u32[]{:S(2)}) collective-permute-start(f32[104,128]{1,0:T(8,128)S(1)} %fusion.297), channel_id=1, source_target_pairs={{0,16},{4,20},{8,24},{12,28},{16,0},{20,4},{24,8},{28,12},{1,17},{... | collective-permute-start | bytes 159752 | tf_op jit(solution)/shard_map/ppermute | solution.py:362
  869.2 16.5 %collective-permute-start.72 = (bf16[2,128,1024]{2,1,0:T(8,128)(2,1)}, bf16[2,128,1024]{2,1,0:T(8,128)(2,1)}, u32[]{:S(2)}, u32[]{:S(2)}) collective-permute-start(bf16[2,128,1024]{2,1,0:T(8,128)(2,1)} %dynamic-slice_bitcast_fusion.2), channel_id=1, source_target_pairs={{0,8},{4,12},{8,0},{12,4},{16,24},{20,28},{24,16},{28,20},{1,9},{5... | collective-permute-start | bytes 1572872 | tf_op jit(solution)/shard_map/ppermute | solution.py:362
  881.1 16.6 %collective-permute-start.59 = (bf16[2,128,1024]{1,2,0:T(8,128)(2,1)}, bf16[2,128,1024]{1,2,0:T(8,128)(2,1)S(1)}, u32[]{:S(2)}, u32[]{:S(2)}) collective-permute-start(bf16[2,128,1024]{1,2,0:T(8,128)(2,1)} %bitcast.476), channel_id=1, source_target_pairs={{0,8},{4,12},{8,0},{12,4},{16,24},{20,28},{24,16},{28,20},{1,9},{5... | collective-permute-start | bytes 1572872 | tf_op jit(solution)/shard_map/ppermute | solution.py:362
  (155 other events, 1904.9 us)

commit v2 on v1

--- a/solution.py
+++ b/solution.py
@@ -55,26 +55,261 @@
 
 
 def over_keys(i, bq, bk, safe, block):
-    first_mixed = jnp.minimum(i * bq // bk, safe // bk)
-    diagonal = i * bq // bk
-
-    def plain(j, c):
-        block(j, "none")
+    diagonal = i * (bq // bk)
+
+    def visit(j, c):
+        @pl.when(j < safe // bk)
+        def _():
+            block(j, "none")
+
+        @pl.when(j >= safe // bk)
+        def _():
+            block(j, "segment")
+
         return c
 
-    def split(j, c):
-        block(j, "segment")
-        return c
-
-    lax.fori_loop(0, first_mixed, plain, 0)
-    lax.fori_loop(first_mixed, diagonal, split, 0)
+    lax.fori_loop(0, diagonal, visit, 0)
     for step in range(bq // bk):
         block(diagonal + step, "causal")
 
 
-def self_forward_kernel(b_ref, q_ref, k_ref, vt_ref, ot_ref, lse_ref, m_s, l_s, acc, *, bk, heads, safe):
+CORE = ("tensor", 1)
+X = ("tensor", 2)
+Y = ("dp", 1)
+ANY = pl.BlockSpec(memory_space=pl.ANY)
+
+
+class Links:
+    def __init__(self, send_sems, recv_sems, local_sems):
+        self.dp = lax.axis_index("dp")
+        self.tensor = lax.axis_index("tensor")
+        self.send_sems, self.recv_sems, self.local_sems = send_sems, recv_sems, local_sems
+        self.used = 0
+        self.used_local = 0
+
+    def partner(self, way):
+        axis, distance = way
+        if axis == "tensor":
+            return (self.dp, self.tensor ^ distance)
+        return (self.dp ^ distance, self.tensor)
+
+    def greet(self, ways):
+        barrier = pltpu.get_barrier_semaphore()
+        for way in ways:
+            pl.semaphore_signal(
+                barrier, inc=1, device_id=self.partner(way), device_id_type=pl.DeviceIdType.MESH
+            )
+        pl.semaphore_wait(barrier, len(ways))
+
+    def copy(self, source, target, way):
+        k = self.used
+        self.used += 1
+        return pltpu.make_async_remote_copy(
+            src_ref=source,
+            dst_ref=target,
+            send_sem=self.send_sems.at[k],
+            recv_sem=self.recv_sems.at[k],
+            device_id=self.partner(way),
+            device_id_type=pl.DeviceIdType.MESH,
+        )
+
+    def local(self, source, target):
+        k = self.used_local
+        self.used_local += 1
+        return pltpu.make_async_copy(source, target, self.local_sems.at[k])
+
+
+def link_scratch(copies, local):
+    return [
+        pltpu.SemaphoreType.DMA((copies,)),
+        pltpu.SemaphoreType.DMA((copies,)),
+        pltpu.SemaphoreType.DMA((local,)),
+    ]
+
+
+def z_distances(n):
+    found = []
+    m = n // 2
+    while m > 1:
+        m //= 2
+        found.append(m)
+    return found
+
+
+def z_ways(n):
+    return [("dp", 2 * distance) for distance in z_distances(n)]
+
+
+def column_stages(links, shard, column, n):
+    z = links.dp // 2
+    held = [z]
+    stages = []
+    for distance in z_distances(n):
+        stages.append(
+            [
+                (
+                    links.copy(shard if k == 0 else column.at[index], column.at[index], ("dp", 2 * distance)),
+                    index ^ distance,
+                )
+                for k, index in enumerate(held)
+            ]
+        )
+        held = held + [index ^ distance for index in held]
+    return stages
+
+
+class Spread:
+    def __init__(self, links, column, whole):
+        y = links.dp % 2
+        half = column.shape[0] // 2
+        low, high = pl.ds(0, half), pl.ds(half, half)
+        near, near_core, far, far_core = whole
+        self.own = links.local(column, near.at[:, y])
+        self.first = [
+            links.copy(column, near.at[:, y], Y),
+            links.copy(column, far.at[:, y], X),
+        ]
+        self.core = [links.copy(column, near_core.at[:, y], CORE)]
+        self.second = [
+            links.copy(near.at[low, 1 - y], far.at[low, 1 - y], X),
+            links.copy(far.at[high, y], far.at[high, y], Y),
+        ]
+        self.core_second = [
+            links.copy(near.at[:, 1 - y], near_core.at[:, 1 - y], CORE),
+            links.copy(far.at[:, y], far_core.at[:, y], CORE),
+        ]
+        self.core_third = [links.copy(far.at[:, 1 - y], far_core.at[:, 1 - y], CORE)]
+
+    def start(self):
+        self.own.start()
+        for copy in self.first + self.core:
+            copy.start()
+
+    def middle(self):
+        for copy in self.first:
+            copy.wait_recv()
+        for copy in self.second + self.core_second:
+            copy.start()
+
+    def end(self):
+        for copy in self.second:
+            copy.wait_recv()
+        for copy in self.core_third:
+            copy.start()
+        self.own.wait()
+        for copy in self.first + self.second:
+            copy.wait_send()
+        for copy in self.core + self.core_second + self.core_third:
+            copy.wait()
+
+
+def start_kernel(
+    rows_ref, enc_ref, self_ref, cross_ref, rows_out, enc_out, self_out, cross_out, send_sems, recv_sems, local_sems, *, n
+):
+    links = Links(send_sems, recv_sems, local_sems)
+    member, z, y = links.tensor, links.dp // 2, links.dp % 2
+    links.greet([CORE, X, Y] + z_ways(n))
+
+    def place(ref, index, size):
+        return ref.at[pl.ds(pl.multiple_of(index * size, size), size)]
+
+    groups = [(rows_ref, rows_out, rows_ref.shape[0]), (enc_ref, enc_out, enc_ref.shape[0])]
+    local, started, arrived = [], [], []
+    for source, target, size in groups:
+        local.append(links.local(source, place(target, member, size)))
+    local.append(links.local(self_ref, self_out.at[z, y]))
+    local.append(links.local(cross_ref, cross_out.at[z]))
+    for copy in local:
+        copy.start()
+
+    def go(copy):
+        copy.start()
+        started.append(copy)
+        return copy
+
+    def got(copy):
+        copy.wait_recv()
+        arrived.append(copy)
+
+    along_x = [go(links.copy(source, place(target, member, size), X)) for source, target, size in groups]
+    go(links.copy(self_ref, self_out.at[z, y], Y))
+    for source, target, size in groups:
+        go(links.copy(source, place(target, member, size), CORE))
+    self_stages = column_stages(links, self_ref, self_out.at[:, y], n)
+    cross_stages = column_stages(links, cross_ref, cross_out, n)
+    for self_stage, cross_stage in zip(self_stages, cross_stages):
+        for copy, _ in self_stage:
+            go(copy)
+        for copy, _ in cross_stage:
+            go(copy)
+        for copy, index in self_stage:
+            got(copy)
+            go(links.copy(self_out.at[index, y], self_out.at[index, y], Y))
+        for copy, _ in cross_stage:
+            got(copy)
+    for copy, (_, target, size) in zip(along_x, groups):
+        got(copy)
+        there = place(target, member ^ 2, size)
+        go(links.copy(there, there, CORE))
+    for copy in local:
+        copy.wait()
+    for copy in started:
+        copy.wait_send()
+        if not any(copy is other for other in arrived):
+            copy.wait_recv()
+
+
+def start_gather(rows_low, enc_low, self_shard, cross_shard):
+    n = lax.axis_size("dp")
+    r, c = self_shard.shape
+    copies = 3 * n + 8
+    return pl.pallas_call(
+        functools.partial(start_kernel, n=n),
+        in_specs=[ANY] * 4,
+        out_specs=[ANY] * 4,
+        out_shape=[
+            jax.ShapeDtypeStruct((4 * rows_low.shape[0], rows_low.shape[1]), BF16),
+            jax.ShapeDtypeStruct((4 * enc_low.shape[0], enc_low.shape[1]), BF16),
+            jax.ShapeDtypeStruct((n // 2, 2, r, c), BF16),
+            jax.ShapeDtypeStruct((n // 2,) + cross_shard.shape, BF16),
+        ],
+        scratch_shapes=link_scratch(copies, 4),
+        compiler_params=pltpu.CompilerParams(collective_id=0, has_side_effects=True),
+        cost_estimate=pl.CostEstimate(flops=0, bytes_accessed=100 * 2**20, transcendentals=0),
+        name="start_gather",
+    )(rows_low, enc_low, self_shard, cross_shard)
+
+
+def self_forward_kernel(
+    b_ref, q_ref, k_ref, vt_ref, column_ref, shard_ref,
+    ot_ref, lse_ref, w0, w1, w2, w3, next_column,
+    m_s, l_s, acc, send_sems, recv_sems, local_sems, *, bk, heads, safe, n
+):
     i = pl.program_id(0)
+    last = pl.num_programs(0) - 1
     bq, width = q_ref.shape
+    links = Links(send_sems, recv_sems, local_sems)
+    spread = Spread(links, column_ref, (w0, w1, w2, w3))
+    keep = links.local(shard_ref, next_column.at[links.dp // 2])
+    stages = column_stages(links, shard_ref, next_column, n)
+
+    @pl.when(i == 0)
+    def _():
+        links.greet([CORE, X, Y] + z_ways(n))
+        spread.start()
+        keep.start()
+        for copy, _ in stages[0]:
+            copy.start()
+
+    @pl.when(i == last)
+    def _():
+        spread.middle()
+        for k in range(1, len(stages)):
+            for copy, _ in stages[k - 1]:
+                copy.wait_recv()
+            for copy, _ in stages[k]:
+                copy.start()
+
     hd = width // heads
     m_s[...] = jnp.full_like(m_s, NEGATIVE)
     l_s[...] = jnp.zeros_like(l_s)
@@ -112,38 +347,58 @@
         ot_ref[part, :] = (acc[part, :] * inverse[h : h + 1, :]).astype(BF16)
     lse_ref[...] = m_s[...] + jnp.log(l_s[...])
 
-
-def self_forward(bounds, queries, keys, values_t, heads, safe):
+    @pl.when(i == last)
+    def _():
+        spread.end()
+        keep.wait()
+        for k, stage in enumerate(stages):
+            for copy, _ in stage:
+                copy.wait_send()
+                if k == len(stages) - 1:
+                    copy.wait_recv()
+
+
+def self_forward(bounds, queries, keys, values_t, column, shard, heads, safe):
     n, width = queries.shape
     bq = bk = 512
+    dp = lax.axis_size("dp")
+    m, r, c = column.shape
     return pl.pallas_call(
-        functools.partial(self_forward_kernel, bk=bk, heads=heads, safe=safe),
+        functools.partial(self_forward_kernel, bk=bk, heads=heads, safe=safe, n=dp),
         grid=(n // bq,),
         in_specs=[
             pl.BlockSpec(memory_space=pltpu.SMEM),
             pl.BlockSpec((bq, width), lambda i: (i, 0)),
             pl.BlockSpec((n, width), lambda i: (0, 0)),
             pl.BlockSpec((width, n), lambda i: (0, 0)),
+            ANY,
+            ANY,
         ],
         out_specs=[
             pl.BlockSpec((width, bq), lambda i: (0, i)),
             pl.BlockSpec((heads, bq), lambda i: (0, i)),
-        ],
+        ]
+        + [ANY] * 5,
         out_shape=[
             jax.ShapeDtypeStruct((width, n), BF16),
             jax.ShapeDtypeStruct((heads, n), F32),
-        ],
+        ]
+        + [jax.ShapeDtypeStruct((m, 2, r, c), BF16)] * 4
+        + [jax.ShapeDtypeStruct((m,) + shard.shape, BF16)],
         scratch_shapes=[
             pltpu.VMEM((heads, bq), F32),
             pltpu.VMEM((heads, bq), F32),
             pltpu.VMEM((width, bq), F32),
-        ],
-        compiler_params=pltpu.CompilerParams(vmem_limit_bytes=VMEM_LIMIT),
+        ]
+        + link_scratch(8 + m, 2),
+        compiler_params=pltpu.CompilerParams(
+            vmem_limit_bytes=VMEM_LIMIT, collective_id=1, has_side_effects=True
+        ),
         cost_estimate=pl.CostEstimate(
             flops=12 * n * n * width, bytes_accessed=8 * n * width, transcendentals=n * n * heads // 2
         ),
         name="self_forward",
-    )(bounds, queries, keys, values_t)
+    )(bounds, queries, keys, values_t, column, shard)
 
 
 def self_backward_kernel(
@@ -236,7 +491,18 @@
     )(bounds, queries, keys, values, keys_t, grads, lse, inner)
 
 
-def cross_forward_kernel(ok_ref, q_ref, k_ref, vt_ref, ot_ref, lse_ref, *, heads):
+def cross_forward_kernel(
+    ok_ref, q_ref, k_ref, vt_ref, column_ref, ot_ref, lse_ref, w0, w1, w2, w3, send_sems, recv_sems, local_sems, *, heads
+):
+    i = pl.program_id(0)
+    last = pl.num_programs(0) - 1
+    spread = Spread(links := Links(send_sems, recv_sems, local_sems), column_ref, (w0, w1, w2, w3))
+
+    @pl.when(i == 0)
+    def _():
+        links.greet([CORE, X, Y])
+        spread.start()
+
     rows, width = q_ref.shape[1:]
     hd = width // heads
     scaled = q_ref[0] * jnp.asarray(1.0 / math.sqrt(hd), BF16)
@@ -253,9 +519,15 @@
         ot_ref[0, part, :] = (mixed * (1.0 / total)).astype(BF16)
         lse_ref[0, h : h + 1, :] = largest + jnp.log(total)
 
-
-def cross_forward(ok, queries, keys, values_t, heads):
+    @pl.when(i == last)
+    def _():
+        spread.middle()
+        spread.end()
+
+
+def cross_forward(ok, queries, keys, values_t, column, heads):
     parts, rows, width = queries.shape
+    m, r, c = column.shape
     n = keys.shape[1]
     return pl.pallas_call(
         functools.partial(cross_forward_kernel, heads=heads),
@@ -265,23 +537,29 @@
             pl.BlockSpec((1, rows, width), lambda i: (i, 0, 0)),
             pl.BlockSpec((1, n, width), lambda i: (i, 0, 0)),
             pl.BlockSpec((1, width, n), lambda i: (i, 0, 0)),
+            ANY,
         ],
         out_specs=[
             pl.BlockSpec((1, width, rows), lambda i: (i, 0, 0)),
             pl.BlockSpec((1, heads, rows), lambda i: (i, 0, 0)),
-        ],
+        ]
+        + [ANY] * 4,
         out_shape=[
             jax.ShapeDtypeStruct((parts, width, rows), BF16),
             jax.ShapeDtypeStruct((parts, heads, rows), F32),
-        ],
-        compiler_params=pltpu.CompilerParams(vmem_limit_bytes=VMEM_LIMIT),
+        ]
+        + [jax.ShapeDtypeStruct((m, 2, r, c), BF16)] * 4,
+        scratch_shapes=link_scratch(8, 1),
+        compiler_params=pltpu.CompilerParams(
+            vmem_limit_bytes=VMEM_LIMIT, collective_id=2, has_side_effects=True
+        ),
         cost_estimate=pl.CostEstimate(
             flops=24 * parts * rows * n * width,
             bytes_accessed=8 * parts * n * width,
             transcendentals=parts * rows * n * heads,
         ),
         name="cross_forward",
-    )(ok, queries, keys, values_t)
+    )(ok, queries, keys, values_t, column)
 
 
 def cross_backward_kernel(
@@ -371,53 +649,6 @@
     return found
 
 
-def reorder_kernel(order_ref, in_ref, out_ref):
-    out_ref[...] = in_ref[0]
-
-
-def in_order(stack):
-    n, rows, columns = stack.shape
-    place = jnp.arange(n, dtype=jnp.int32) ^ lax.axis_index("dp")
-    order = jnp.zeros_like(place)
-    for bit, distance in enumerate(dp_distances()):
-        order = order + (place // distance % 2) * 2**bit
-    return pl.pallas_call(
-        reorder_kernel,
-        grid_spec=pltpu.PrefetchScalarGridSpec(
-            num_scalar_prefetch=1,
-            grid=(n,),
-            in_specs=[pl.BlockSpec((1, rows, columns), lambda i, order_ref: (order_ref[i], 0, 0))],
-            out_specs=pl.BlockSpec((rows, columns), lambda i, order_ref: (i, 0)),
-        ),
-        out_shape=jax.ShapeDtypeStruct((n * rows, columns), stack.dtype),
-        cost_estimate=pl.CostEstimate(flops=0, bytes_accessed=4 * n * rows * columns, transcendentals=0),
-        name="in_order",
-    )(order, stack)
-
-
-def gather_dp(shard):
-    stack = shard[None]
-    for distance in dp_distances():
-        stack = jnp.concatenate([stack, swap(stack, "dp", distance)], 0)
-    return in_order(stack)
-
-
-def gather_all(shard, x_last):
-    distances = dp_distances()
-    stack = shard[None]
-    for distance in distances[:-1]:
-        stack = jnp.concatenate([stack, swap(stack, "dp", distance)], 0)
-    last = distances[-1]
-    if x_last:
-        near = in_order(jnp.concatenate([stack, swap(stack, "dp", last)], 0))
-        far = swap(near, "tensor", 2)
-    else:
-        there = swap(stack, "tensor", 2)
-        near = in_order(jnp.concatenate([stack, swap(stack, "dp", last)], 0))
-        far = in_order(jnp.concatenate([there, swap(there, "dp", last)], 0))
-    return [near, swap(near, "tensor", 1), far, swap(far, "tensor", 1)]
-
-
 def add_low(a, b):
     return (a.astype(F32) + b.astype(F32)).astype(BF16)
 
@@ -548,23 +779,33 @@
         return pull_rows(incoming)
 
     start_rows = block_in.astype(F32)
-    first_in = widen(layer_norm(start_rows, norm_params[0, 0], norm_params[0, 1]).astype(BF16))
-    self_w = gather_dp(jnp.concatenate([w_qkv.reshape(w_rows, 3 * width), w_self_out.T], axis=1))
-    cross_w = gather_all(
-        jnp.concatenate([w_cross_q, w_cross_kv.reshape(w_rows, 2 * width), w_cross_out.T], axis=1), False
-    )
-    up_w = gather_all(w_up, False)
-    down_w = gather_all(w_down.T, True)
-    w_query = [w[:, :width] for w in cross_w]
-    w_keyval = [w[:, width : 3 * width] for w in cross_w]
-    w_out = [w[:, 3 * width :] for w in cross_w]
+    first_in, enc_all, self_w, cross_column = start_gather(
+        layer_norm(start_rows, norm_params[0, 0], norm_params[0, 1]).astype(BF16),
+        encoder_out,
+        jnp.concatenate([w_qkv.reshape(w_rows, 3 * width), w_self_out.T], axis=1),
+        jnp.concatenate([w_cross_q, w_cross_kv.reshape(w_rows, 2 * width), w_cross_out.T], axis=1),
+    )
+    self_w = self_w.reshape(model_width, 4 * width)
 
     projected = dot_nn(first_in, self_w[:, : 3 * width])
     queries = (projected[:, :width] + block_of(biases[0], width, 0)).astype(BF16)
     key_rows = projected[:, width : 2 * width].astype(BF16)
     value_rows = (projected[:, 2 * width :] + block_of(biases[1], width, 0)).astype(BF16)
     self_safe = 1024
-    self_mixed_t, self_lse = self_forward(bounds, queries, key_rows, value_rows.T, heads, self_safe)
+    self_mixed_t, self_lse, *cross_w, ffn_column = self_forward(
+        bounds,
+        queries,
+        key_rows,
+        value_rows.T,
+        cross_column,
+        jnp.concatenate([w_up, w_down.T], axis=1),
+        heads,
+        self_safe,
+    )
+    cross_w = [w.reshape(model_width, 4 * width) for w in cross_w]
+    w_query = [w[:, :width] for w in cross_w]
+    w_keyval = [w[:, width : 3 * width] for w in cross_w]
+    w_out = [w[:, 3 * width :] for w in cross_w]
     self_out_w = self_w[:, 3 * width :]
     after_self = (
         start_rows
@@ -572,22 +813,14 @@
         + biases[2]
     )
 
-    own_kv = []
-    for distance in range(4):
-        shift = jnp.concatenate([jnp.zeros((width,), F32), block_of(biases[4], width, distance)])
-        own_kv.append((dot_nn(encoder_out, w_keyval[distance]) + shift).astype(BF16))
-    own_kv = jnp.stack(own_kv)
-    far_kv = swap(own_kv, "tensor", 2)
-    kv_from = [own_kv, swap(own_kv, "tensor", 1), far_kv, swap(far_kv, "tensor", 1)]
-    cross_kv = jnp.stack(
-        [jnp.concatenate([kv_from[d][j ^ d] for d in range(4)], 0) for j in range(4)]
-    )
-    cross_keys = cross_kv[:, :, :width]
-    cross_values = cross_kv[:, :, width:]
-    places = jnp.concatenate(
-        [(member ^ d) * enc_rows + jnp.arange(enc_rows, dtype=jnp.int32) for d in range(4)]
-    )
-    ok = (places < enc_lengths[0]).astype(F32)[:, None]
+    cross_keys, cross_values = [], []
+    for d in range(4):
+        projected = dot_nn(enc_all, w_keyval[d])
+        cross_keys.append(projected[:, :width].astype(BF16))
+        cross_values.append((projected[:, width:] + block_of(biases[4], width, d)).astype(BF16))
+    cross_keys = jnp.stack(cross_keys)
+    cross_values = jnp.stack(cross_values)
+    ok = (jnp.arange(4 * enc_rows, dtype=jnp.int32) < enc_lengths[0]).astype(F32)[:, None]
 
     second_in = layer_norm(after_self, norm_params[1, 0], norm_params[1, 1]).astype(BF16)
     cross_queries = jnp.stack(
@@ -596,9 +829,12 @@
             for d in range(4)
         ]
     )
-    cross_mixed_t, cross_lse = cross_forward(
-        ok, cross_queries, cross_keys, jnp.swapaxes(cross_values, 1, 2), heads
-    )
+    cross_mixed_t, cross_lse, *ffn_w = cross_forward(
+        ok, cross_queries, cross_keys, jnp.swapaxes(cross_values, 1, 2), ffn_column, heads
+    )
+    ffn_w = [w.reshape(model_width, 2 * hidden_width) for w in ffn_w]
+    up_w = [w[:, :hidden_width] for w in ffn_w]
+    down_w = [w[:, hidden_width:] for w in ffn_w]
     after_cross = after_self + biases[5]
     for d in range(4):
         after_cross = after_cross + lax.dot_general(
@@ -659,7 +895,8 @@
     part_kv = jnp.concatenate([part_dk, part_dv], axis=2).reshape(4, 4, enc_rows, 2 * width)
 
     def for_member(d):
-        return jnp.stack([part_kv[j ^ d, d] for j in range(4)])
+        rows = lax.dynamic_index_in_dim(part_kv, member ^ d, 1, keepdims=False)
+        return jnp.stack([rows[j ^ d] for j in range(4)])
 
     far_dkv = add_low(for_member(2), swap(for_member(3), "tensor", 1))
     near_dkv = for_member(0).astype(F32) + swap(for_member(1), "tensor", 1).astype(F32)

time: 925 us -> 849 us (0.918)
  Pallas kernels: 176 us -> 296 us
  waiting for transfers between devices: 215 us -> 98.7 us
  starting transfers between devices: 67.1 us -> 35.8 us
  matrix products: 196 us -> 174 us
  other arithmetic: 106 us -> 93.9 us
  local copies, waits for them, and re-layouts: 149 us -> 137 us
    ppermute x74 -> x45, waiting for transfers between devices: 215 us -> 98.7 us  [swap(): return lax.ppermute(value, axis, [(i, i ^ distance) for i in range(size)])]
    pallas_call x1, Pallas kernels: 19.7 us -> 78.8 us  [cross_forward(): pl.pallas_call(functools.partial(cross_forward_kernel, heads=heads), grid...]
    pallas_call x6 -> x1, Pallas kernels: 38.3 us -> 77.3 us  [start_gather(): pl.pallas_call(functools.partial(start_kernel, n=n), in_specs=[ANY] * 4,...]
    ppermute x74 -> x45, starting transfers between devices: 67.1 us -> 35.8 us  [swap(): return lax.ppermute(value, axis, [(i, i ^ distance) for i in range(size)])]
    concatenate x14 -> x2, other arithmetic: 26.4 us -> 1.68 us  [the longest x1 0.85 us: on_device(): jnp.concatenate([w_qkv.reshape(w_rows, 3 * width), w_self_out.T], axis=1)]
    pallas_call x1, Pallas kernels: 32.2 us -> 53.6 us  [self_forward(): pl.pallas_call(functools.partial(self_forward_kernel, bk=bk, heads=heads,...]
    dot_general x13, matrix products: 44.5 us -> 25 us  [dot_nt(): lax.dot_general(a, b, (((1,), (1,)), ((), ())), preferred_element_type=F32)]
    unnamed x318 -> x320, local copies, waits for them, and re-layouts: 54.4 us -> 50.3 us
  transfers between devices with their start and end apart: 74 -> 45, of which waited for: 20 -> 13; matrix products, arithmetic and copies ran while one was open for 41% -> 30% of each run, Pallas kernels for 15% -> 6%
where the time goes in v2:
time: 849 us; the launch traced here: 839 us
  Pallas kernels  296 us (35%)
  matrix products  174 us (20%)
  local copies, waits for them, and re-layouts  137 us (16%)
  waiting for transfers between devices  98.7 us (12%)
  other arithmetic  93.9 us (11%)
  starting transfers between devices  35.8 us (4%)
    ppermute x45, waiting for transfers between devices, swap(): return lax.ppermute(value, axis, [(i, i ^ distance) for i in range(size)])  98.7 us
    dot_general x22, matrix products, dot_nn(): lax.dot_general(a, b, (((1,), (0,)), ((), ())), preferred_element_type=F32)  79.9 us
    pallas_call x1, Pallas kernels, cross_forward(): pl.pallas_call(functools.partial(cross_forward_kernel, heads=heads), grid...  78.8 us
    pallas_call x1, Pallas kernels, start_gather(): pl.pallas_call(functools.partial(start_kernel, n=n), in_specs=[ANY] * 4,...  77.3 us
    pallas_call x1, Pallas kernels, self_forward(): pl.pallas_call(functools.partial(self_forward_kernel, bk=bk, heads=heads,...  53.6 us
    pallas_call x1, Pallas kernels, self_backward(): pl.pallas_call(functools.partial(self_backward_kernel, bk=bk, heads=heads...  50.6 us
    unnamed x320, local copies, waits for them, and re-layouts  50.3 us
    dot_general x13, matrix products, dot_tn(): lax.dot_general(a, b, (((0,), (0,)), ((), ())), preferred_element_type=F32)  38.9 us
  transfers between devices with their start and end apart: 45, of which 13 were waited for; matrix products, arithmetic and copies ran while one was open for 30% of the time, Pallas kernels for 6%

profile of v2, /device:TPU:0, one launch (start us, length us, event | category | flops | bytes accessed | tf_op | source)
XLA Modules:
  0.0 838.6 jit_solution(6802798703233483975)
XLA Ops:
  9.4 77.3 %start_gather.1 = (bf16[2560,1024]{1,0:T(8,128)(2,1)}, bf16[1024,1024]{1,0:T(8,128)(2,1)}, bf16[4,2,128,1024]{3,2,1,0:T(8,128)(2,1)}, bf16[4,128,1024]{2,1,0:T(8,128)(2,1)}) custom-call(bf16[640,1024]{1,0:T(8,128)(2,1)} %fusion.9.rows_ref, bf16[256,1024]{1,0:T(8,128)(2,1)} %enc_ref.1, bf16[128,1024]{1,0:T(8,128)(2,1)} %get-tuple-element.214.self_ref, ...), custom_call_target="tpu_custom_call" | custom-call | bytes 104857600 | tf_op jit(solution)/shard_map/start_gather/pallas_call | solution.py:266
  86.6 6.6 fusion.128
  93.3 3.2 copy-done.29
  97.6 4.0 fusion.50
  108.5 53.6 %self_forward.1 = (bf16[256,2560]{1,0:T(8,128)(2,1)}, f32[4,2560]{1,0:T(4,128)}, bf16[4,2,128,1024]{3,2,1,0:T(8,128)(2,1)}, bf16[4,2,128,1024]{3,2,1,0:T(8,128)(...) custom-call(s32[1,2]{1,0:T(1,128)} %b_ref.3, ...), custom_call_target="tpu_custom_call" | custom-call | flops 20132659200 | bytes 5242880 | tf_op jit(solution)/shard_map/self_forward/pallas_call | solution.py:366
  162.1 5.4 convolution_convert_fusion
  167.5 3.4 constant_dynamic-slice_fusion.21
  171.4 4.6 fusion.173
  178.1 3.0 fusion.170
  181.2 2.6 fusion.166
  183.8 2.6 fusion.162
  186.4 3.3 add_convert_fusion.8
  213.5 3.2 fusion.249
  216.7 2.7 copy.76.k_ref
  221.1 3.0 fusion.255
  231.6 78.8 %cross_forward.1 = (bf16[4,256,640]{2,1,0:T(8,128)(2,1)}, f32[4,4,640]{2,1,0:T(4,128)}, bf16[4,2,128,2048]{3,2,1,0:T(8,128)(2,1)}, bf16[4,2,128,2048]{3,2,1,0:T(...) custom-call(f32[1024,1]{1,0:T(8,128)} %fusion.182.ok_ref, ...), custom_call_target="tpu_custom_call" | custom-call | flops 16106127360 | bytes 8388608 | tf_op jit(solution)/shard_map/cross_forward/pallas_call | solution.py:532
  317.6 8.5 %fusion.16 = (bf16[640,1024]{1,0:T(8,128)(2,1)}, f32[640,1024]{1,0:T(8,128)S(1)}) fusion(f32[1024]{0:T(1024)S(1)} %get-tuple-element.180, bf16[640,1024]{1,0:T(8,128)(2,1)S(1)} %add_convert_fusion.6, bf16[1024,2048]{1,0:T(8,128)(2,1)S(1)} %bitcast.406), kind=kOutput, calls=%fused_computation.45 | convolution fusion | flops 1385431040 | bytes 7344128 | tf_op jit(solution)/shard_map/dot_general | solution.py:24
  326.1 3.1 convert_reduce_fusion.6
  329.2 8.1 fusion.19
  337.4 3.1 convert_reduce_fusion.5
  340.5 8.1 fusion.22
  348.6 2.5 convert_reduce_fusion.4
  351.2 8.2 fusion.25
  359.3 2.7 convert_reduce_fusion.3
  385.5 3.3 copy.83
  388.8 2.6 bitcast_reduce_fusion.1.dl_ref
  391.4 35.6 %cross_backward.1 = (bf16[4,256,640]{2,1,0:T(8,128)(2,1)}, bf16[4,1024,256]{2,1,0:T(8,128)(2,1)}, bf16[4,1024,256]{2,1,0:T(8,128)(2,1)}) custom-call(f32[1024,1]{1,0:T(8,128)} %fusion.182.ok_ref, bf16[4,640,256]{2,1,0:T(8,128)(2,1)} %pad_maximum_fusion.7.q_ref, bf16[4,1024,256]{2,1,0:T(8,128)(2,1)} %copy.76.k_ref, ...), custom_call_target="tpu_custom_call" | custom-call | flops 32212254720 | bytes 16777216 | tf_op jit(solution)/shard_map/cross_backward/pallas_call | solution.py:609
  433.8 2.7 multiply_reduce_fusion.1
  442.3 3.2 convolution_convert_fusion.4
  456.5 3.2 convert_bitcast_fusion
  475.0 3.5 add_add_fusion.7
  478.4 3.2 fusion.263
  482.5 3.3 convolution_convert_fusion.3
  487.7 3.3 convert_bitcast_fusion.1
  492.8 2.5 constant_dynamic-update-slice_fusion.2
  499.4 3.4 add_convert_fusion.2
  504.2 4.9 fusion
  514.2 10.0 %collective-permute-done.11 = bf16[4,256,512]{2,1,0:T(8,128)(2,1)S(1)} collective-permute-done((bf16[4,256,512]{2,1,0:T(8,128)(2,1)S(1)}, bf16[4,256,512]{2,1,0:T(8,128)(2,1)S(1)}, u32[]{:S(2)}, u32[]{:S(2)}) %collective-permute-start.11) | collective-permute-done | bytes 1048608 | tf_op jit(solution)/shard_map/ppermute | solution.py:640
  529.8 2.8 pad_maximum_fusion.5
  540.2 4.1 bitcast_multiply_fusion
  546.3 2.6 bitcast_reduce_fusion.dl_ref
  548.9 50.6 %self_backward.1 = (bf16[256,2560]{1,0:T(8,128)(2,1)}, bf16[2560,256]{1,0:T(8,128)(2,1)}, bf16[2560,256]{1,0:T(8,128)(2,1)}) custom-call(s32[1,2]{1,0:T(1,128)} %b_ref.3, bf16[2560,256]{1,0:T(8,128)(2,1)} %get-tuple-element.115.q_ref, bf16[2560,256]{1,0:T(8,128)(2,1)} %copy.69.k_ref, bf16[2560,256]{1,0:T(8,128)(2,1)} %copy-done.32, ...), custom_call_target="tpu_custom_call" | custom-call | flops 40265318400 | bytes 10485760 | tf_op jit(solution)/shard_map/self_backward/pallas_call | solution.py:462
  601.4 6.6 convolution_convert_fusion.1
  608.1 8.7 %convolution_convert_fusion.5 = bf16[1024,768]{0,1:T(8,128)(2,1)S(1)} fusion(bf16[2560,1024]{1,0:T(8,128)(2,1)} %get-tuple-element.36, bf16[2560,256]{1,0:T(8,128)(2,1)S(1)} %copy-done.79, bf16[2560,256]{1,0:T(8,128)(2,1)S(1)} %copy-done.77, bf16[2560,256]{1,0:T(8,128)(2,1)S(1)} %bitcast.403), kind=kOutput, calls=%fused_computation.227 | convolution fusion | flops 4039114752 | bytes 10747904 | tf_op jit(solution)/shard_map/dot_general | solution.py:28
  621.7 3.4 reshape.330
  625.2 4.3 constant_dynamic-slice_fusion.9
  635.7 20.1 %collective-permute-done.22 = bf16[2,2,128,1024]{2,3,0,1:T(8,128)(2,1)S(1)} collective-permute-done((bf16[2,2,128,1024]{2,3,0,1:T(8,128)(2,1)S(1)}, bf16[2,2,128,1024]{2,3,0,1:T(8,128)(2,1)S(1)}, u32[]{:S(2)}, u32[]{:S(2)}) %collective-permute-start.22) | collective-permute-done | bytes 1048608 | tf_op jit(solution)/shard_map/ppermute | solution.py:640
  658.2 3.7 add_convert_fusion.5
  662.1 3.7 add_convert_fusion
  668.0 9.9 %collective-permute-done.33 = bf16[4,128,1024]{2,1,0:T(8,128)(2,1)S(1)} collective-permute-done((bf16[4,128,1024]{2,1,0:T(8,128)(2,1)S(1)}, bf16[4,128,1024]{2,1,0:T(8,128)(2,1)S(1)}, u32[]{:S(2)}, u32[]{:S(2)}) %collective-permute-start.33) | collective-permute-done | bytes 1048608 | tf_op jit(solution)/shard_map/ppermute | solution.py:640
  689.9 3.1 reshape.331
  693.0 3.2 reshape.332
  696.3 8.7 %constant_dynamic-slice_fusion.7 = (bf16[4,1,128,1024]{2,1,0,3:T(2,128)(2,1)}, bf16[4,1,128,1024]{2,1,0,3:T(2,128)(2,1)}) fusion(bf16[4,2,128,1024]{2,1,0,3:T(2,128)(2,1)} %reshape.331, s32[]{:T(128)S(6)} %select_n.186, s32[]{:T(128)S(6)} %select_n.187), kind=kLoop, calls=%fused_computation.438 | loop fusion | bytes 4194312 | tf_op jit(solution)/shard_map/jit(dynamic_index_in_dim)/dynamic_slice | solution.py:689
  708.7 6.3 constant_dynamic-slice_fusion.5
  715.0 6.0 copy.120
  721.0 4.3 copy.119
  725.3 6.0 copy.122
  731.3 4.4 copy.121
  745.1 3.1 fusion.10
  748.3 3.1 fusion.252
  761.6 20.5 %collective-permute-done.28 = bf16[4,128,1024]{2,1,0:T(8,128)(2,1)S(1)} collective-permute-done((bf16[4,128,1024]{2,1,0:T(8,128)(2,1)}, bf16[4,128,1024]{2,1,0:T(8,128)(2,1)S(1)}, u32[]{:S(2)}, u32[]{:S(2)}) %collective-permute-start.28) | collective-permute-done | bytes 1048608 | tf_op jit(solution)/shard_map/ppermute | solution.py:640
  799.6 5.8 collective-permute-done.29
  811.6 12.5 %collective-permute-done.30 = bf16[2,128,1024]{1,2,0:T(8,128)(2,1)S(1)} collective-permute-done((bf16[2,128,1024]{1,2,0:T(8,128)(2,1)S(1)}, bf16[2,128,1024]{1,2,0:T(8,128)(2,1)S(1)}, u32[]{:S(2)}, u32[]{:S(2)}) %collective-permute-start.30) | collective-permute-done | bytes 524320 | tf_op jit(solution)/shard_map/ppermute | solution.py:640
  827.6 8.4 %collective-permute-done.31 = bf16[128,1024]{0,1:T(8,128)(2,1)S(1)} collective-permute-done((bf16[128,1024]{0,1:T(8,128)(2,1)S(1)}, bf16[128,1024]{0,1:T(8,128)(2,1)S(1)}, u32[]{:S(2)}, u32[]{:S(2)}) %collective-permute-start.31) | collective-permute-done | bytes 262176 | tf_op jit(solution)/shard_map/ppermute | solution.py:640
  (582 shorter events, 232.7 us)
Async XLA Ops:
  1.6 222.9 %copy-start.102 = (f32[1,1,1024]{2,1,0:T(1,128)}, f32[1,1,1024]{2,1,0:T(1,128)S(1)}, u32[]{:S(2)}) copy-start(f32[1,1,1024]{2,1,0:T(1,128)S(1)} %get-tuple-element.172) | copy-start | bytes 12292
  5.6 81.0 %copy-start.104 = (f32[640]{0:T(1024)}, f32[640]{0:T(1024)S(1)}, u32[]{:S(2)}) copy-start(f32[640]{0:T(1024)S(1)} %fusion.242) | copy-start | bytes 7684
  106.0 56.1 %copy-start.31 = (bf16[2560,256]{0,1:T(8,128)(2,1)}, bf16[2560,256]{0,1:T(8,128)(2,1)S(1)}, u32[]{:S(2)}) copy-start(bf16[2560,256]{0,1:T(8,128)(2,1)S(1)} %copy.127) | copy-start | bytes 3932164
  170.9 15.5 %collective-permute-start.1 = (bf16[640,1024]{1,0:T(8,128)(2,1)}, bf16[640,1024]{1,0:T(8,128)(2,1)}, u32[]{:S(2)}, u32[]{:S(2)}) collective-permute-start(bf16[640,1024]{1,0:T(8,128)(2,1)} %get-tuple-element.119), channel_id=1, source_target_pairs={{0,1},{1,0},{2,3},{3,2},{4,5},{5,4},{6,7},{7,6},{8,9},{9,8},{10,11... | collective-permute-start | bytes 3932168 | tf_op jit(solution)/shard_map/ppermute | solution.py:640
  170.9 50.2 %collective-permute-start = (bf16[640,1024]{1,0:T(8,128)(2,1)}, bf16[640,1024]{1,0:T(8,128)(2,1)}, u32[]{:S(2)}, u32[]{:S(2)}) collective-permute-start(bf16[640,1024]{1,0:T(8,128)(2,1)} %get-tuple-element.118), channel_id=1, source_target_pairs={{0,1},{1,0},{2,3},{3,2},{4,5},{5,4},{6,7},{7,6},{8,9},{9,8},{10,11... | collective-permute-start | bytes 3932168 | tf_op jit(solution)/shard_map/ppermute | solution.py:640
  189.7 31.4 %collective-permute-start.2 = (bf16[640,1024]{1,0:T(8,128)(2,1)}, bf16[640,1024]{1,0:T(8,128)(2,1)}, u32[]{:S(2)}, u32[]{:S(2)}) collective-permute-start(bf16[640,1024]{1,0:T(8,128)(2,1)} %add_convert_fusion.8), channel_id=1, source_target_pairs={{0,2},{1,3},{2,0},{3,1},{4,6},{5,7},{6,4},{7,5},{8,10},{9,11},{10,... | collective-permute-start | bytes 3932168 | tf_op jit(solution)/shard_map/ppermute | solution.py:640
  224.0 89.2 %copy-start = (f32[640,1024]{1,0:T(8,128)}, f32[640,1024]{1,0:T(8,128)S(1)}, u32[]{:S(2)}) copy-start(f32[640,1024]{1,0:T(8,128)S(1)} %get-tuple-element.113) | copy-start | bytes 7864324
  315.8 35.4 %copy-start.81 = (bf16[640,1024]{1,0:T(8,128)(2,1)}, bf16[640,1024]{1,0:T(8,128)(2,1)S(1)}, u32[]{:S(2)}) copy-start(bf16[640,1024]{1,0:T(8,128)(2,1)S(1)} %add_convert_fusion.6) | copy-start | bytes 3932164
  329.2 37.7 %copy-start.72 = (bf16[640,1024]{1,0:T(8,128)(2,1)}, bf16[640,1024]{1,0:T(8,128)(2,1)S(1)}, u32[]{:S(2)}) copy-start(bf16[640,1024]{1,0:T(8,128)(2,1)S(1)} %get-tuple-element.207) | copy-start | bytes 3932164
  340.5 21.6 %copy-start.140 = (bf16[640,1024]{1,0:T(8,128)(2,1)}, bf16[640,1024]{1,0:T(8,128)(2,1)S(1)}, u32[]{:S(2)}) copy-start(bf16[640,1024]{1,0:T(8,128)(2,1)S(1)} %get-tuple-element.209) | copy-start | bytes 3932164
  370.2 67.2 %copy-start.108 = (f32[640]{0:T(1024)}, f32[640]{0:T(1024)S(1)}, u32[]{:S(2)}) copy-start(f32[640]{0:T(1024)S(1)} %negate_multiply_fusion.6) | copy-start | bytes 7684
  441.0 51.6 %collective-permute-start.3 = (bf16[640,1024]{1,0:T(8,128)(2,1)}, bf16[640,1024]{1,0:T(8,128)(2,1)}, u32[]{:S(2)}, u32[]{:S(2)}) collective-permute-start(bf16[640,1024]{1,0:T(8,128)(2,1)} %get-tuple-element.105), channel_id=1, source_target_pairs={{0,1},{1,0},{2,3},{3,2},{4,5},{5,4},{6,7},{7,6},{8,9},{9,8},{10,11... | collective-permute-start | bytes 3932168 | tf_op jit(solution)/shard_map/ppermute | solution.py:640
  441.5 53.8 %collective-permute-start.4 = (bf16[640,1024]{1,0:T(8,128)(2,1)}, bf16[640,1024]{1,0:T(8,128)(2,1)}, u32[]{:S(2)}, u32[]{:S(2)}) collective-permute-start(bf16[640,1024]{1,0:T(8,128)(2,1)} %get-tuple-element.105), channel_id=1, source_target_pairs={{0,2},{1,3},{2,0},{3,1},{4,6},{5,7},{6,4},{7,5},{8,10},{9,11},{10,... | collective-permute-start | bytes 3932168 | tf_op jit(solution)/shard_map/ppermute | solution.py:640
  464.6 21.1 %collective-permute-start.10 = (bf16[4,256,512]{2,1,0:T(8,128)(2,1)}, bf16[4,256,512]{2,1,0:T(8,128)(2,1)}, u32[]{:S(2)}, u32[]{:S(2)}) collective-permute-start(bf16[4,256,512]{2,1,0:T(8,128)(2,1)} %pad_maximum_fusion.10), channel_id=1, source_target_pairs={{0,1},{1,0},{2,3},{3,2},{4,5},{5,4},{6,7},{7,6},{8,9},{9,8},{10,11... | collective-permute-start | bytes 3145736 | tf_op jit(solution)/shard_map/ppermute | solution.py:640
  467.1 37.0 %collective-permute-start.40 = (bf16[1024,1024]{1,0:T(8,128)(2,1)}, bf16[1024,1024]{1,0:T(8,128)(2,1)}, u32[]{:S(2)}, u32[]{:S(2)}) collective-permute-start(bf16[1024,1024]{1,0:T(8,128)(2,1)} %convert_bitcast_fusion), channel_id=1, source_target_pairs={{0,1},{1,0},{2,3},{3,2},{4,5},{5,4},{6,7},{7,6},{8,9},{9,8},{10,11... | collective-permute-start | bytes 6291464 | tf_op jit(solution)/shard_map/ppermute | solution.py:640
  467.7 30.5 %collective-permute-start.32 = (bf16[1024,1024]{1,0:T(8,128)(2,1)}, bf16[1024,1024]{1,0:T(8,128)(2,1)}, u32[]{:S(2)}, u32[]{:S(2)}) collective-permute-start(bf16[1024,1024]{1,0:T(8,128)(2,1)} %convolution_convert_fusion.4), channel_id=1, source_target_pairs={{0,1},{1,0},{2,3},{3,2},{4,5},{5,4},{6,7},{7,6},{8,9},{9,8},{10,11... | collective-permute-start | bytes 6291464 | tf_op jit(solution)/shard_map/ppermute | solution.py:640
  485.8 23.3 %collective-permute-start.34 = (bf16[1024,1024]{1,0:T(8,128)(2,1)S(1)}, bf16[1024,1024]{1,0:T(8,128)(2,1)S(1)}, u32[]{:S(2)}, u32[]{:S(2)}) collective-permute-start(bf16[1024,1024]{1,0:T(8,128)(2,1)S(1)} %convolution_convert_fusion.3), channel_id=1, source_target_pairs={{0,1},{1,0},{2,3},{3,2},{4,5},{5,4},{6,7},{7,6},{8,9},{9,8},{10,11... | collective-permute-start | bytes 6291464 | tf_op jit(solution)/shard_map/ppermute | solution.py:640
  492.6 20.4 %collective-permute-start.9 = (bf16[4,256,512]{2,1,0:T(8,128)(2,1)S(1)}, bf16[4,256,512]{2,1,0:T(8,128)(2,1)S(1)}, u32[]{:S(2)}, u32[]{:S(2)}) collective-permute-start(bf16[4,256,512]{2,1,0:T(8,128)(2,1)S(1)} %copy-done.91), channel_id=1, source_target_pairs={{0,1},{1,0},{2,3},{3,2},{4,5},{5,4},{6,7},{7,6},{8,9},{9,8},{10,11... | collective-permute-start | bytes 3145736 | tf_op jit(solution)/shard_map/ppermute | solution.py:640
  495.3 139.0 %collective-permute-start.39 = (bf16[1024,1024]{1,0:T(8,128)(2,1)}, bf16[1024,1024]{1,0:T(8,128)(2,1)}, u32[]{:S(2)}, u32[]{:S(2)}) collective-permute-start(bf16[1024,1024]{1,0:T(8,128)(2,1)} %convert_bitcast_fusion.1), channel_id=1, source_target_pairs={{0,1},{1,0},{2,3},{3,2},{4,5},{5,4},{6,7},{7,6},{8,9},{9,8},{10,11... | collective-permute-start | bytes 6291464 | tf_op jit(solution)/shard_map/ppermute | solution.py:640
  498.2 26.0 %collective-permute-start.11 = (bf16[4,256,512]{2,1,0:T(8,128)(2,1)S(1)}, bf16[4,256,512]{2,1,0:T(8,128)(2,1)S(1)}, u32[]{:S(2)}, u32[]{:S(2)}) collective-permute-start(bf16[4,256,512]{2,1,0:T(8,128)(2,1)S(1)} %add_convert_fusion.12), channel_id=1, source_target_pairs={{0,2},{1,3},{2,0},{3,1},{4,6},{5,7},{6,4},{7,5},{8,10},{9,11},{10,... | collective-permute-start | bytes 3145736 | tf_op jit(solution)/shard_map/ppermute | solution.py:640
  504.2 34.3 %collective-permute-start.5 = (bf16[640,1024]{1,0:T(8,128)(2,1)}, bf16[640,1024]{1,0:T(8,128)(2,1)}, u32[]{:S(2)}, u32[]{:S(2)}) collective-permute-start(bf16[640,1024]{1,0:T(8,128)(2,1)} %collective-permute-done.4), channel_id=1, source_target_pairs={{0,1},{1,0},{2,3},{3,2},{4,5},{5,4},{6,7},{7,6},{8,9},{9,8},{10,11... | collective-permute-start | bytes 3932168 | tf_op jit(solution)/shard_map/ppermute | solution.py:640
  509.1 15.2 %copy-start.85 = (bf16[1,256,512]{2,1,0:T(8,128)(2,1)S(1)}, bf16[1,256,512]{2,1,0:T(8,128)(2,1)}, u32[]{:S(2)}) copy-start(bf16[1,256,512]{2,1,0:T(8,128)(2,1)} %get-tuple-element.135) | copy-start | bytes 786436
  509.1 152.8 %collective-permute-start.41 = (bf16[1024,1024]{1,0:T(8,128)(2,1)}, bf16[1024,1024]{1,0:T(8,128)(2,1)}, u32[]{:S(2)}, u32[]{:S(2)}) collective-permute-start(bf16[1024,1024]{1,0:T(8,128)(2,1)} %fusion), channel_id=1, source_target_pairs={{0,2},{1,3},{2,0},{3,1},{4,6},{5,7},{6,4},{7,5},{8,10},{9,11},{10,... | collective-permute-start | bytes 6291464 | tf_op jit(solution)/shard_map/ppermute | solution.py:640
  513.0 119.1 %collective-permute-start.35 = (bf16[4,128,1024]{2,1,0:T(8,128)(2,1)}, bf16[4,128,1024]{2,1,0:T(8,128)(2,1)}, u32[]{:S(2)}, u32[]{:S(2)}) collective-permute-start(bf16[4,128,1024]{2,1,0:T(8,128)(2,1)} %dynamic-slice_bitcast_fusion), channel_id=1, source_target_pairs={{0,4},{4,0},{8,12},{12,8},{16,20},{20,16},{24,28},{28,24},{1,5},{5... | collective-permute-start | bytes 3145736 | tf_op jit(solution)/shard_map/ppermute | solution.py:640
  599.5 19.1 %slice-start.2 = ((s8[5242880]{0:T(1024)(128)(4,1)}), s8[1048576]{0:T(1024)(128)(4,1)S(1)}, s32[]{:S(2)}) async-start(s8[5242880]{0:T(1024)(128)(4,1)} %bitcast.397), calls=%async_computation.2 | async-start | bytes 2097152
  601.4 17.2 %slice-start.3 = ((s8[5242880]{0:T(1024)(128)(4,1)}), s8[4194304]{0:T(1024)(128)(4,1)S(1)}, s32[]{:S(2)}) async-start(s8[5242880]{0:T(1024)(128)(4,1)} %bitcast.397), calls=%async_computation.3 | async-start | bytes 8388608
  618.6 37.2 %collective-permute-start.7 = (bf16[640,1024]{1,0:T(8,128)(2,1)}, bf16[640,1024]{1,0:T(8,128)(2,1)}, u32[]{:S(2)}, u32[]{:S(2)}) collective-permute-start(bf16[640,1024]{1,0:T(8,128)(2,1)} %get-tuple-element.117), channel_id=1, source_target_pairs={{0,1},{1,0},{2,3},{3,2},{4,5},{5,4},{6,7},{7,6},{8,9},{9,8},{10,11... | collective-permute-start | bytes 3932168 | tf_op jit(solution)/shard_map/ppermute | solution.py:640
  629.8 26.0 %collective-permute-start.22 = (bf16[2,2,128,1024]{2,3,0,1:T(8,128)(2,1)S(1)}, bf16[2,2,128,1024]{2,3,0,1:T(8,128)(2,1)S(1)}, u32[]{:S(2)}, u32[]{:S(2)}) collective-permute-start(bf16[2,2,128,1024]{2,3,0,1:T(8,128)(2,1)S(1)} %bitcast.448), channel_id=1, source_target_pairs={{0,4},{4,0},{8,12},{12,8},{16,20},{20,16},{24,28},{28,24},{1,5},{5... | collective-permute-start | bytes 3145736 | tf_op jit(solution)/shard_map/ppermute | solution.py:640
  631.2 24.5 %copy-start.50 = (bf16[1024,1024]{0,1:T(8,128)(2,1)S(1)}, bf16[1024,1024]{0,1:T(8,128)(2,1)}, u32[]{:S(2)}) copy-start(bf16[1024,1024]{0,1:T(8,128)(2,1)} %pad_maximum_fusion.6) | copy-start | bytes 6291460
  632.1 52.1 %collective-permute-start.25 = (bf16[1024,1024]{0,1:T(8,128)(2,1)S(1)}, bf16[1024,1024]{0,1:T(8,128)(2,1)S(1)}, u32[]{:S(2)}, u32[]{:S(2)}) collective-permute-start(bf16[1024,1024]{0,1:T(8,128)(2,1)S(1)} %copy-done.51), channel_id=1, source_target_pairs={{0,1},{1,0},{2,3},{3,2},{4,5},{5,4},{6,7},{7,6},{8,9},{9,8},{10,11... | collective-permute-start | bytes 6291464 | tf_op jit(solution)/shard_map/ppermute | solution.py:640
  634.4 43.5 %collective-permute-start.33 = (bf16[4,128,1024]{2,1,0:T(8,128)(2,1)S(1)}, bf16[4,128,1024]{2,1,0:T(8,128)(2,1)S(1)}, u32[]{:S(2)}, u32[]{:S(2)}) collective-permute-start(bf16[4,128,1024]{2,1,0:T(8,128)(2,1)S(1)} %copy-done.90), channel_id=1, source_target_pairs={{0,4},{4,0},{8,12},{12,8},{16,20},{20,16},{24,28},{28,24},{1,5},{5... | collective-permute-start | bytes 3145736 | tf_op jit(solution)/shard_map/ppermute | solution.py:640
  655.8 30.5 %collective-permute-start.27 = (bf16[1024,1024]{0,1:T(8,128)(2,1)S(1)}, bf16[1024,1024]{0,1:T(8,128)(2,1)S(1)}, u32[]{:S(2)}, u32[]{:S(2)}) collective-permute-start(bf16[1024,1024]{0,1:T(8,128)(2,1)S(1)} %copy-done.50), channel_id=1, source_target_pairs={{0,1},{1,0},{2,3},{3,2},{4,5},{5,4},{6,7},{7,6},{8,9},{9,8},{10,11... | collective-permute-start | bytes 6291464 | tf_op jit(solution)/shard_map/ppermute | solution.py:640
  655.8 25.6 %collective-permute-start.36 = (bf16[4,128,1024]{2,1,0:T(8,128)(2,1)S(1)}, bf16[4,128,1024]{2,1,0:T(8,128)(2,1)S(1)}, u32[]{:S(2)}, u32[]{:S(2)}) collective-permute-start(bf16[4,128,1024]{2,1,0:T(8,128)(2,1)S(1)} %fusion.81), channel_id=1, source_target_pairs={{0,2},{1,3},{2,0},{3,1},{4,6},{5,7},{6,4},{7,5},{8,10},{9,11},{10,... | collective-permute-start | bytes 3145736 | tf_op jit(solution)/shard_map/ppermute | solution.py:640
  661.9 81.8 %collective-permute-start.6 = (bf16[640,1024]{1,0:T(8,128)(2,1)}, bf16[640,1024]{1,0:T(8,128)(2,1)S(1)}, u32[]{:S(2)}, u32[]{:S(2)}) collective-permute-start(bf16[640,1024]{1,0:T(8,128)(2,1)} %get-tuple-element.116), channel_id=1, source_target_pairs={{0,1},{1,0},{2,3},{3,2},{4,5},{5,4},{6,7},{7,6},{8,9},{9,8},{10,11... | collective-permute-start | bytes 3932168 | tf_op jit(solution)/shard_map/ppermute | solution.py:640
  665.8 16.8 %copy-start.44 = (bf16[1024,1024]{1,0:T(8,128)(2,1)S(1)}, bf16[1024,1024]{1,0:T(8,128)(2,1)}, u32[]{:S(2)}) copy-start(bf16[1024,1024]{1,0:T(8,128)(2,1)} %copy-done.43) | copy-start | bytes 6291460
  668.0 17.2 %copy-start.40 = (bf16[1024,512]{0,1:T(8,128)(2,1)S(1)}, bf16[1024,512]{0,1:T(8,128)(2,1)}, u32[]{:S(2)}) copy-start(bf16[1024,512]{0,1:T(8,128)(2,1)} %fusion.130) | copy-start | bytes 3145732
  668.0 17.2 %copy-start.54 = (bf16[1024,256]{0,1:T(8,128)(2,1)S(1)}, bf16[1024,256]{0,1:T(8,128)(2,1)}, u32[]{:S(2)}) copy-start(bf16[1024,256]{0,1:T(8,128)(2,1)} %convolution_convert_fusion.17) | copy-start | bytes 1572868
  668.0 17.2 %copy-start.55 = (bf16[1024,256]{0,1:T(8,128)(2,1)S(1)}, bf16[1024,256]{0,1:T(8,128)(2,1)}, u32[]{:S(2)}) copy-start(bf16[1024,256]{0,1:T(8,128)(2,1)} %convolution_convert_fusion.18) | copy-start | bytes 1572868
  677.9 27.2 %collective-permute-start.23 = (bf16[2,128,1024]{1,2,0:T(8,128)(2,1)}, bf16[2,128,1024]{1,2,0:T(8,128)(2,1)}, u32[]{:S(2)}, u32[]{:S(2)}) collective-permute-start(bf16[2,128,1024]{1,2,0:T(8,128)(2,1)} %dynamic-slice_bitcast_fusion.4), channel_id=1, source_target_pairs={{0,8},{4,12},{8,0},{12,4},{16,24},{20,28},{24,16},{28,20},{1,9},{5... | collective-permute-start | bytes 1572872 | tf_op jit(solution)/shard_map/ppermute | solution.py:640
  681.4 63.7 %collective-permute-start.8 = (bf16[640,1024]{1,0:T(8,128)(2,1)}, bf16[640,1024]{1,0:T(8,128)(2,1)}, u32[]{:S(2)}, u32[]{:S(2)}) collective-permute-start(bf16[640,1024]{1,0:T(8,128)(2,1)} %add_convert_fusion.5), channel_id=1, source_target_pairs={{0,2},{1,3},{2,0},{3,1},{4,6},{5,7},{6,4},{7,5},{8,10},{9,11},{10,... | collective-permute-start | bytes 3932168 | tf_op jit(solution)/shard_map/ppermute | solution.py:640
  684.4 101.6 %collective-permute-start.42 = (bf16[2,2,128,1024]{3,2,0,1:T(8,128)(2,1)}, bf16[2,2,128,1024]{3,2,0,1:T(8,128)(2,1)}, u32[]{:S(2)}, u32[]{:S(2)}) collective-permute-start(bf16[2,2,128,1024]{3,2,0,1:T(8,128)(2,1)} %bitcast.392), channel_id=1, source_target_pairs={{0,4},{4,0},{8,12},{12,8},{16,20},{20,16},{24,28},{28,24},{1,5},{5... | collective-permute-start | bytes 3145736 | tf_op jit(solution)/shard_map/ppermute | solution.py:640
  686.3 55.3 %collective-permute-start.37 = (bf16[2,128,1024]{2,1,0:T(8,128)(2,1)}, bf16[2,128,1024]{2,1,0:T(8,128)(2,1)}, u32[]{:S(2)}, u32[]{:S(2)}) collective-permute-start(bf16[2,128,1024]{2,1,0:T(8,128)(2,1)} %dynamic-slice_bitcast_fusion.3), channel_id=1, source_target_pairs={{0,8},{4,12},{8,0},{12,4},{16,24},{20,28},{24,16},{28,20},{1,9},{5... | collective-permute-start | bytes 1572872 | tf_op jit(solution)/shard_map/ppermute | solution.py:640
  707.0 28.7 %collective-permute-start.24 = (bf16[128,1024]{0,1:T(8,128)(2,1)}, bf16[128,1024]{0,1:T(8,128)(2,1)}, u32[]{:S(2)}, u32[]{:S(2)}) collective-permute-start(bf16[128,1024]{0,1:T(8,128)(2,1)} %dynamic-slice_bitcast_fusion.24), channel_id=1, source_target_pairs={{0,16},{4,20},{8,24},{12,28},{16,0},{20,4},{24,8},{28,12},{1,17},{... | collective-permute-start | bytes 786440 | tf_op jit(solution)/shard_map/ppermute | solution.py:640
  735.8 63.8 %collective-permute-start.26 = (bf16[4,128,1024]{2,1,0:T(8,128)(2,1)}, bf16[4,128,1024]{2,1,0:T(8,128)(2,1)}, u32[]{:S(2)}, u32[]{:S(2)}) collective-permute-start(bf16[4,128,1024]{2,1,0:T(8,128)(2,1)} %bitcast.446), channel_id=1, source_target_pairs={{0,4},{4,0},{8,12},{12,8},{16,20},{20,16},{24,28},{28,24},{1,5},{5... | collective-permute-start | bytes 3145736 | tf_op jit(solution)/shard_map/ppermute | solution.py:640
  741.5 40.6 %collective-permute-start.28 = (bf16[4,128,1024]{2,1,0:T(8,128)(2,1)}, bf16[4,128,1024]{2,1,0:T(8,128)(2,1)S(1)}, u32[]{:S(2)}, u32[]{:S(2)}) collective-permute-start(bf16[4,128,1024]{2,1,0:T(8,128)(2,1)} %bitcast.447), channel_id=1, source_target_pairs={{0,4},{4,0},{8,12},{12,8},{16,20},{20,16},{24,28},{28,24},{1,5},{5... | collective-permute-start | bytes 3145736 | tf_op jit(solution)/shard_map/ppermute | solution.py:640
  743.7 12.8 %collective-permute-start.38 = (bf16[128,1024]{1,0:T(8,128)(2,1)S(1)}, bf16[128,1024]{1,0:T(8,128)(2,1)S(1)}, u32[]{:S(2)}, u32[]{:S(2)}) collective-permute-start(bf16[128,1024]{1,0:T(8,128)(2,1)S(1)} %dynamic-slice_bitcast_fusion.22), channel_id=1, source_target_pairs={{0,16},{4,20},{8,24},{12,28},{16,0},{20,4},{24,8},{28,12},{1,17},{... | collective-permute-start | bytes 786440 | tf_op jit(solution)/shard_map/ppermute | solution.py:640
  751.4 2.8 collective-permute-start.12
  751.9 30.2 %copy-start.36 = (bf16[4,1,128,1024]{3,2,0,1:T(8,128)(2,1)S(1)}, bf16[4,1,128,1024]{3,2,0,1:T(8,128)(2,1)}, u32[]{:S(2)}) copy-start(bf16[4,1,128,1024]{3,2,0,1:T(8,128)(2,1)} %copy.121) | copy-start | bytes 3145732
  754.2 31.8 %copy-start.35 = (bf16[2,2,1,128,1024]{4,3,2,1,0:T(8,128)(2,1)S(1)}, bf16[2,2,1,128,1024]{4,3,2,1,0:T(8,128)(2,1)}, u32[]{:S(2)}) copy-start(bf16[2,2,1,128,1024]{4,3,2,1,0:T(8,128)(2,1)} %get-tuple-element.136) | copy-start | bytes 3145732
  754.2 6.0 collective-permute-start.17
  756.5 3.7 collective-permute-start.13
  760.2 23.6 %collective-permute-start.14 = (f32[32,128]{1,0:T(8,128)S(1)}, f32[32,128]{1,0:T(8,128)S(1)}, u32[]{:S(2)}, u32[]{:S(2)}) collective-permute-start(f32[32,128]{1,0:T(8,128)S(1)} %add.699), channel_id=1, source_target_pairs={{0,16},{4,20},{8,24},{12,28},{16,0},{20,4},{24,8},{28,12},{1,17},{... | collective-permute-start | bytes 49160 | tf_op jit(solution)/shard_map/ppermute | solution.py:640
  760.3 24.4 %collective-permute-start.18 = (f32[104,128]{1,0:T(8,128)S(1)}, f32[104,128]{1,0:T(8,128)S(1)}, u32[]{:S(2)}, u32[]{:S(2)}) collective-permute-start(f32[104,128]{1,0:T(8,128)S(1)} %bitcast_add_fusion.2), channel_id=1, source_target_pairs={{0,2},{1,3},{2,0},{3,1},{4,6},{5,7},{6,4},{7,5},{8,10},{9,11},{10,... | collective-permute-start | bytes 159752 | tf_op jit(solution)/shard_map/ppermute | solution.py:640
  782.5 22.8 %collective-permute-start.29 = (bf16[4,128,1024]{2,1,0:T(8,128)(2,1)S(1)}, bf16[4,128,1024]{2,1,0:T(8,128)(2,1)}, u32[]{:S(2)}, u32[]{:S(2)}) collective-permute-start(bf16[4,128,1024]{2,1,0:T(8,128)(2,1)S(1)} %fusion.83), channel_id=1, source_target_pairs={{0,2},{1,3},{2,0},{3,1},{4,6},{5,7},{6,4},{7,5},{8,10},{9,11},{10,... | collective-permute-start | bytes 3145736 | tf_op jit(solution)/shard_map/ppermute | solution.py:640
  783.9 21.5 %copy-start.38 = (bf16[4,1,128,1024]{3,2,0,1:T(8,128)(2,1)S(1)}, bf16[4,1,128,1024]{3,2,0,1:T(8,128)(2,1)}, u32[]{:S(2)}) copy-start(bf16[4,1,128,1024]{3,2,0,1:T(8,128)(2,1)} %copy.119) | copy-start | bytes 3145732
  783.9 3.8 collective-permute-start.15
  784.7 5.1 collective-permute-start.19
  787.7 5.0 collective-permute-start.16
  789.8 4.8 collective-permute-start.20
  792.0 17.0 %collective-permute-start.43 = (bf16[2,128,1024]{2,1,0:T(8,128)(2,1)}, bf16[2,128,1024]{2,1,0:T(8,128)(2,1)}, u32[]{:S(2)}, u32[]{:S(2)}) collective-permute-start(bf16[2,128,1024]{2,1,0:T(8,128)(2,1)} %dynamic-slice_bitcast_fusion.2), channel_id=1, source_target_pairs={{0,8},{4,12},{8,0},{12,4},{16,24},{20,28},{24,16},{28,20},{1,9},{5... | collective-permute-start | bytes 1572872 | tf_op jit(solution)/shard_map/ppermute | solution.py:640
  794.6 4.2 collective-permute-start.21
  807.9 16.2 %collective-permute-start.30 = (bf16[2,128,1024]{1,2,0:T(8,128)(2,1)S(1)}, bf16[2,128,1024]{1,2,0:T(8,128)(2,1)S(1)}, u32[]{:S(2)}, u32[]{:S(2)}) collective-permute-start(bf16[2,128,1024]{1,2,0:T(8,128)(2,1)S(1)} %bitcast.456), channel_id=1, source_target_pairs={{0,8},{4,12},{8,0},{12,4},{16,24},{20,28},{24,16},{28,20},{1,9},{5... | collective-permute-start | bytes 1572872 | tf_op jit(solution)/shard_map/ppermute | solution.py:640
  810.2 15.4 %collective-permute-start.44 = (bf16[128,1024]{1,0:T(8,128)(2,1)S(1)}, bf16[128,1024]{1,0:T(8,128)(2,1)}, u32[]{:S(2)}, u32[]{:S(2)}) collective-permute-start(bf16[128,1024]{1,0:T(8,128)(2,1)S(1)} %dynamic-slice_bitcast_fusion.21), channel_id=1, source_target_pairs={{0,16},{4,20},{8,24},{12,28},{16,0},{20,4},{24,8},{28,12},{1,17},{... | collective-permute-start | bytes 786440 | tf_op jit(solution)/shard_map/ppermute | solution.py:640
  824.3 11.7 %collective-permute-start.31 = (bf16[128,1024]{0,1:T(8,128)(2,1)S(1)}, bf16[128,1024]{0,1:T(8,128)(2,1)S(1)}, u32[]{:S(2)}, u32[]{:S(2)}) collective-permute-start(bf16[128,1024]{0,1:T(8,128)(2,1)S(1)} %dynamic-slice_bitcast_fusion.23), channel_id=1, source_target_pairs={{0,16},{4,20},{8,24},{12,28},{16,0},{20,4},{24,8},{28,12},{1,17},{... | collective-permute-start | bytes 786440 | tf_op jit(solution)/shard_map/ppermute | solution.py:640
  (127 other events, 526.3 us)

commit v3 on v2

--- a/solution.py
+++ b/solution.py
@@ -163,7 +163,7 @@
         y = links.dp % 2
         half = column.shape[0] // 2
         low, high = pl.ds(0, half), pl.ds(half, half)
-        near, near_core, far, far_core = whole
+        near, near_core, far, far_core = (whole.at[k] for k in range(4))
         self.own = links.local(column, near.at[:, y])
         self.first = [
             links.copy(column, near.at[:, y], Y),
@@ -201,6 +201,128 @@
             copy.wait_send()
         for copy in self.core + self.core_second + self.core_third:
             copy.wait()
+
+
+def add_to(total_ref, other_ref):
+    def one(k, c):
+        total_ref[k] = (total_ref[k].astype(F32) + other_ref[k].astype(F32)).astype(BF16)
+        return c
+
+    lax.fori_loop(0, total_ref.shape[0], one, 0)
+
+
+class Gather:
+    def __init__(self, links, near, far, buffers, core=None):
+        y = links.dp % 2
+        self.column, self.over_y, self.over_x, self.got_y, self.got_x, self.sum_y, self.sum_x = buffers[:7]
+        m = self.column.shape[0]
+        low, high = pl.ds(0, m // 2), pl.ds(m // 2, m // 2)
+        self.low, self.high = low, high
+        self.loads = [
+            links.local(near.at[:, y], self.column),
+            links.local(near.at[:, 1 - y], self.over_y),
+            links.local(far.at[:, y], self.over_x),
+        ]
+        self.core = []
+        diagonal = far.at[:, 1 - y]
+        if core is not None:
+            diagonal, near_core, far_core = buffers[7:]
+            self.loads.append(links.local(far.at[:, 1 - y], diagonal))
+            self.core = [links.copy(core[0], near_core, CORE), links.copy(core[1], far_core, CORE)]
+            self.core_sums = [
+                (self.column, near_core.at[:, y]),
+                (self.over_y, near_core.at[:, 1 - y]),
+                (self.over_x, far_core.at[:, y]),
+                (diagonal, far_core.at[:, 1 - y]),
+            ]
+        self.first = [
+            links.copy(diagonal.at[low], self.got_y, X),
+            links.copy(diagonal.at[high], self.got_x, Y),
+        ]
+        self.second = [
+            links.copy(self.over_x, self.sum_x, X),
+            links.copy(self.over_y, self.sum_y, Y),
+        ]
+
+    def start(self):
+        for copy in self.loads + self.core:
+            copy.start()
+        if not self.core:
+            for copy in self.first:
+                copy.start()
+
+    def after_core(self):
+        for copy in self.loads:
+            copy.wait()
+        for copy in self.core:
+            copy.wait_recv()
+        for total, other in self.core_sums:
+            add_to(total, other)
+        for copy in self.first:
+            copy.start()
+
+    def middle(self):
+        if not self.core:
+            for copy in self.loads:
+                copy.wait()
+        for copy in self.first:
+            copy.wait_recv()
+        add_to(self.over_y.at[self.low], self.got_y)
+        add_to(self.over_x.at[self.high], self.got_x)
+        for copy in self.second:
+            copy.start()
+
+    def end(self):
+        for copy in self.second:
+            copy.wait_recv()
+        add_to(self.column, self.sum_y)
+        add_to(self.column, self.sum_x)
+        for copy in self.first + self.second + self.core:
+            copy.wait_send()
+
+
+def gather_scratch(m, r, c, core):
+    whole = pltpu.VMEM((m, r, c), BF16)
+    half = pltpu.VMEM((m // 2, r, c), BF16)
+    kept = [whole] * 3 + [half] * 2 + [whole] * 2
+    if core:
+        kept += [whole] + [pltpu.VMEM((m, 2, r, c), BF16)] * 2
+    return kept
+
+
+class Collect:
+    def __init__(self, links, column, slots):
+        z = links.dp // 2
+        self.column, self.slots, self.z = column, slots, z
+        m = column.shape[0]
+        distances = z_distances(2 * m)[::-1]
+        self.stages = []
+        first = 0
+        for step, distance in enumerate(distances):
+            kept = [0]
+            for other in distances[step + 1 :]:
+                kept = kept + [k ^ other for k in kept]
+            self.stages.append(
+                [
+                    (links.copy(column.at[z ^ distance ^ k], slots.at[first + i], ("dp", 2 * distance)), first + i, z ^ k)
+                    for i, k in enumerate(kept)
+                ]
+            )
+            first += len(kept)
+
+    def start(self, step):
+        for copy, _, _ in self.stages[step]:
+            copy.start()
+
+    def finish(self, step):
+        for copy, slot, index in self.stages[step]:
+            copy.wait_recv()
+            self.column[index] = (self.column[index].astype(F32) + self.slots[slot].astype(F32)).astype(BF16)
+
+    def drain(self):
+        for stage in self.stages:
+            for copy, _, _ in stage:
+                copy.wait_send()
 
 
 def start_kernel(
@@ -282,14 +404,14 @@
 
 def self_forward_kernel(
     b_ref, q_ref, k_ref, vt_ref, column_ref, shard_ref,
-    ot_ref, lse_ref, w0, w1, w2, w3, next_column,
+    ot_ref, lse_ref, whole, next_column,
     m_s, l_s, acc, send_sems, recv_sems, local_sems, *, bk, heads, safe, n
 ):
     i = pl.program_id(0)
     last = pl.num_programs(0) - 1
     bq, width = q_ref.shape
     links = Links(send_sems, recv_sems, local_sems)
-    spread = Spread(links, column_ref, (w0, w1, w2, w3))
+    spread = Spread(links, column_ref, whole)
     keep = links.local(shard_ref, next_column.at[links.dp // 2])
     stages = column_stages(links, shard_ref, next_column, n)
 
@@ -378,12 +500,12 @@
             pl.BlockSpec((width, bq), lambda i: (0, i)),
             pl.BlockSpec((heads, bq), lambda i: (0, i)),
         ]
-        + [ANY] * 5,
+        + [ANY] * 2,
         out_shape=[
             jax.ShapeDtypeStruct((width, n), BF16),
             jax.ShapeDtypeStruct((heads, n), F32),
         ]
-        + [jax.ShapeDtypeStruct((m, 2, r, c), BF16)] * 4
+        + [jax.ShapeDtypeStruct((4, m, 2, r, c), BF16)]
         + [jax.ShapeDtypeStruct((m,) + shard.shape, BF16)],
         scratch_shapes=[
             pltpu.VMEM((heads, bq), F32),
@@ -402,9 +524,42 @@
 
 
 def self_backward_kernel(
-    b_ref, q_ref, k_ref, v_ref, kt_ref, do_ref, lse_ref, dl_ref, dqt_ref, dk_ref, dv_ref, dka, dva, dqa, *, bk, heads, safe
+    b_ref, q_ref, k_ref, v_ref, kt_ref, do_ref, lse_ref, dl_ref, up_ref, down_ref, g0, g1, g2, g3,
+    dqt_ref, dk_ref, dv_ref, up_out, down_out, cross_out, dka, dva, dqa, *scratch, bk, heads, safe
 ):
     i = pl.program_id(0)
+    links = Links(*scratch[14:])
+    columns = scratch[10:12]
+    collects = [Collect(links, column, slots) for column, slots in zip(columns, scratch[12:14])]
+    loads = [links.local(ref, column) for ref, column in zip((up_ref, down_ref), columns)]
+    cross = Gather(links, g0, g2, scratch[:10], (g1, g3))
+    leave = links.local(cross.column, cross_out)
+    stages = len(collects[0].stages)
+
+    @pl.when(i == 0)
+    def _():
+        links.greet([CORE, X, Y] + [("dp", 2 * d) for d in z_distances(2 * columns[0].shape[0])])
+        cross.start()
+        for copy in loads:
+            copy.start()
+        for copy in loads:
+            copy.wait()
+        for c in collects:
+            c.start(0)
+
+    @pl.when(i == 2)
+    def _():
+        cross.after_core()
+
+    @pl.when(i == 3)
+    def _():
+        cross.middle()
+        for step in range(stages - 1):
+            for c in collects:
+                c.finish(step)
+            for c in collects:
+                c.start(step + 1)
+
     bq, width = q_ref.shape
     hd = width // heads
     scale = 1.0 / math.sqrt(hd)
@@ -451,10 +606,23 @@
     def _():
         dk_ref[...] = dka[...].astype(BF16)
         dv_ref[...] = dva[...].astype(BF16)
-
-
-def self_backward(bounds, queries, keys, values, keys_t, grads, lse, inner, heads, safe):
+        cross.end()
+        leave.start()
+        for c, out in zip(collects, (up_out, down_out)):
+            c.finish(stages - 1)
+            out[...] = c.column[c.z].astype(F32)
+        for c in collects:
+            c.drain()
+        leave.wait()
+
+
+def self_backward(
+    bounds, queries, keys, values, keys_t, grads, lse, inner, up_column, down_column, cross_pieces, heads, safe
+):
     n, width = queries.shape
+    m, r, c = up_column.shape
+    cross_c = cross_pieces[0].shape[3]
+    done = pl.BlockSpec((r, c), lambda i: (0, 0))
     bq = bk = 512
     whole = pl.BlockSpec((n, width), lambda i: (0, 0))
     some = pl.BlockSpec((bq, width), lambda i: (i, 0))
@@ -471,32 +639,43 @@
             some,
             per_row,
             per_row,
-        ],
-        out_specs=[pl.BlockSpec((width, bq), lambda i: (0, i)), whole, whole],
+        ]
+        + [ANY] * 6,
+        out_specs=[pl.BlockSpec((width, bq), lambda i: (0, i)), whole, whole, done, done, ANY],
         out_shape=[
             jax.ShapeDtypeStruct((width, n), BF16),
             jax.ShapeDtypeStruct((n, width), BF16),
             jax.ShapeDtypeStruct((n, width), BF16),
+            jax.ShapeDtypeStruct((r, c), F32),
+            jax.ShapeDtypeStruct((r, c), F32),
+            jax.ShapeDtypeStruct((m, r, cross_c), BF16),
         ],
         scratch_shapes=[
             pltpu.VMEM((n, width), F32),
             pltpu.VMEM((n, width), F32),
             pltpu.VMEM((width, bq), F32),
-        ],
-        compiler_params=pltpu.CompilerParams(vmem_limit_bytes=VMEM_LIMIT),
+        ]
+        + gather_scratch(m, r, cross_c, True)
+        + [pltpu.VMEM((m, r, c), BF16)] * 2
+        + [pltpu.VMEM((m, r, c), BF16)] * 2
+        + link_scratch(6 + 2 * m, 7),
+        compiler_params=pltpu.CompilerParams(
+            vmem_limit_bytes=VMEM_LIMIT, collective_id=5, has_side_effects=True
+        ),
         cost_estimate=pl.CostEstimate(
             flops=24 * n * n * width, bytes_accessed=16 * n * width, transcendentals=n * n * heads // 2
         ),
         name="self_backward",
-    )(bounds, queries, keys, values, keys_t, grads, lse, inner)
+    )(bounds, queries, keys, values, keys_t, grads, lse, inner, up_column, down_column, *cross_pieces)
 
 
 def cross_forward_kernel(
-    ok_ref, q_ref, k_ref, vt_ref, column_ref, ot_ref, lse_ref, w0, w1, w2, w3, send_sems, recv_sems, local_sems, *, heads
+    ok_ref, q_ref, k_ref, vt_ref, column_ref, ot_ref, lse_ref, whole, send_sems, recv_sems, local_sems, *, heads
 ):
     i = pl.program_id(0)
     last = pl.num_programs(0) - 1
-    spread = Spread(links := Links(send_sems, recv_sems, local_sems), column_ref, (w0, w1, w2, w3))
+    links = Links(send_sems, recv_sems, local_sems)
+    spread = Spread(links, column_ref, whole)
 
     @pl.when(i == 0)
     def _():
@@ -543,12 +722,12 @@
             pl.BlockSpec((1, width, rows), lambda i: (i, 0, 0)),
             pl.BlockSpec((1, heads, rows), lambda i: (i, 0, 0)),
         ]
-        + [ANY] * 4,
+        + [ANY],
         out_shape=[
             jax.ShapeDtypeStruct((parts, width, rows), BF16),
             jax.ShapeDtypeStruct((parts, heads, rows), F32),
         ]
-        + [jax.ShapeDtypeStruct((m, 2, r, c), BF16)] * 4,
+        + [jax.ShapeDtypeStruct((4, m, 2, r, c), BF16)],
         scratch_shapes=link_scratch(8, 1),
         compiler_params=pltpu.CompilerParams(
             vmem_limit_bytes=VMEM_LIMIT, collective_id=2, has_side_effects=True
@@ -562,9 +741,135 @@
     )(ok, queries, keys, values_t, column)
 
 
+def feed_forward_kernel(
+    x_ref, xt_ref, dy_ref, dyt_ref, up_ref, down_ref, b_ref,
+    out_ref, back_ref, gup_ref, gdown_ref, bias_ref,
+    give, got, send_sems, recv_sems, local_sems, *, chunks
+):
+    s = pl.program_id(0)
+    links = Links(send_sems, recv_sems, local_sems)
+    turn = s // chunks
+    chunk = s % chunks
+    pair = turn // 2
+    slot = pair * chunks + chunk
+    theirs = turn % 2 == 0
+    to_core = pltpu.make_async_remote_copy(
+        src_ref=give.at[chunk],
+        dst_ref=got.at[slot],
+        send_sem=send_sems.at[slot],
+        recv_sem=recv_sems.at[slot],
+        device_id=links.partner(CORE),
+        device_id_type=pl.DeviceIdType.MESH,
+    )
+
+    @pl.when(s == 0)
+    def _():
+        links.greet([CORE])
+        out_ref[...] = jnp.zeros_like(out_ref)
+        back_ref[...] = jnp.zeros_like(back_ref)
+
+    pre_act = dot_nn(x_ref[...], up_ref[0]) + b_ref[0]
+    hidden_grad = dot_nn(dy_ref[...], down_ref[0])
+    normal_cdf = 0.5 * (1.0 + lax.erf(pre_act * (1.0 / math.sqrt(2.0))))
+    density = jnp.exp(-0.5 * pre_act * pre_act) * (1.0 / math.sqrt(2.0 * math.pi))
+    hidden = (pre_act * normal_cdf).astype(BF16)
+    pre_grad = (hidden_grad * (normal_cdf + pre_act * density)).astype(BF16)
+    bias_ref[0] = jnp.sum(pre_grad.astype(F32), axis=0, keepdims=True)
+
+    @pl.when(turn % 2 == 1)
+    def _():
+        to_core.wait_send()
+
+    give[chunk, 0] = dot_nn(xt_ref[...], pre_grad).astype(BF16)
+    give[chunk, 1] = dot_nn(dyt_ref[...], hidden).astype(BF16)
+    out_ref[...] += dot_nt(hidden, down_ref[0])
+    back_ref[...] += dot_nt(pre_grad, up_ref[0])
+
+    @pl.when(theirs)
+    def _():
+        to_core.start()
+
+    @pl.when(jnp.logical_not(theirs))
+    def _():
+        to_core.wait_recv()
+        gup_ref[0] = (give[chunk, 0].astype(F32) + got[slot, 0].astype(F32)).astype(BF16)
+        gdown_ref[0] = (give[chunk, 1].astype(F32) + got[slot, 1].astype(F32)).astype(BF16)
+
+
+def feed_forward(x, dy, weights, bias):
+    rows, width = x.shape
+    hidden = weights.shape[2] // 2
+    size = min(512, hidden)
+    chunks = hidden // size
+
+    def block(s):
+        return (s // chunks) ^ 1
+
+    def placed(s):
+        turn = s // chunks
+        return (turn // 2, 0, (s % chunks) * (turn % 2))
+
+    rows_spec = pl.BlockSpec((rows, width), lambda s: (0, 0))
+    columns_spec = pl.BlockSpec((width, rows), lambda s: (0, 0))
+    grad_spec = pl.BlockSpec((1, width, size), placed)
+    bias_spec = pl.BlockSpec((1, 1, size), lambda s: (block(s), 0, s % chunks))
+    return pl.pallas_call(
+        functools.partial(feed_forward_kernel, chunks=chunks),
+        grid=(4 * chunks,),
+        in_specs=[
+            rows_spec,
+            columns_spec,
+            rows_spec,
+            columns_spec,
+            pl.BlockSpec((1, width, size), lambda s: (block(s), 0, s % chunks)),
+            pl.BlockSpec((1, width, size), lambda s: (block(s), 0, chunks + s % chunks)),
+            bias_spec,
+        ],
+        out_specs=[rows_spec, rows_spec, grad_spec, grad_spec, bias_spec],
+        out_shape=[
+            jax.ShapeDtypeStruct((rows, width), F32),
+            jax.ShapeDtypeStruct((rows, width), F32),
+            jax.ShapeDtypeStruct((2, width, hidden), BF16),
+            jax.ShapeDtypeStruct((2, width, hidden), BF16),
+            jax.ShapeDtypeStruct((4, 1, hidden), F32),
+        ],
+        scratch_shapes=[
+            pltpu.VMEM((chunks, 2, width, size), BF16),
+            pltpu.VMEM((2 * chunks, 2, width, size), BF16),
+        ]
+        + link_scratch(2 * chunks, 1),
+        compiler_params=pltpu.CompilerParams(
+            vmem_limit_bytes=VMEM_LIMIT, collective_id=3, has_side_effects=True
+        ),
+        cost_estimate=pl.CostEstimate(
+            flops=48 * rows * width * hidden, bytes_accessed=40 * 2**20, transcendentals=8 * rows * hidden
+        ),
+        name="feed_forward",
+    )(x, x.T, dy, dy.T, weights, weights, bias)
+
+
 def cross_backward_kernel(
-    ok_ref, q_ref, k_ref, v_ref, kt_ref, do_ref, lse_ref, dl_ref, dqt_ref, dk_ref, dv_ref, *, heads, bk
+    ok_ref, q_ref, k_ref, v_ref, kt_ref, do_ref, lse_ref, dl_ref, up_ref, down_ref,
+    dqt_ref, dk_ref, dv_ref, up_out, down_out, *scratch, heads, bk
 ):
+    i = pl.program_id(0)
+    links = Links(*scratch[14:])
+    sums = [
+        Gather(links, ref.at[0], ref.at[1], scratch[7 * k : 7 * k + 7]) for k, ref in enumerate((up_ref, down_ref))
+    ]
+    leave = [links.local(g.column, out) for g, out in zip(sums, (up_out, down_out))]
+
+    @pl.when(i == 0)
+    def _():
+        links.greet([X, Y])
+        for g in sums:
+            g.start()
+
+    @pl.when(i == 2)
+    def _():
+        for g in sums:
+            g.middle()
+
     rows, width = q_ref.shape[1:]
     n = k_ref.shape[1]
     hd = width // heads
@@ -599,9 +904,18 @@
     for h in range(heads):
         dqt_ref[0, h * hd : (h + 1) * hd, :] = (dq[h] * scale).astype(BF16)
 
-
-def cross_backward(ok, queries, keys, values, keys_t, grads, lse, inner, heads):
+    @pl.when(i == pl.num_programs(0) - 1)
+    def _():
+        for g, copy in zip(sums, leave):
+            g.end()
+            copy.start()
+        for copy in leave:
+            copy.wait()
+
+
+def cross_backward(ok, queries, keys, values, keys_t, grads, lse, inner, up_sum, down_sum, heads):
     parts, rows, width = queries.shape
+    _, m, _, r, c = up_sum.shape
     n = keys.shape[1]
     by_row = pl.BlockSpec((1, rows, width), lambda i: (i, 0, 0))
     by_key = pl.BlockSpec((1, n, width), lambda i: (i, 0, 0))
@@ -618,21 +932,28 @@
             by_row,
             stat,
             stat,
+            ANY,
+            ANY,
         ],
-        out_specs=[pl.BlockSpec((1, width, rows), lambda i: (i, 0, 0)), by_key, by_key],
+        out_specs=[pl.BlockSpec((1, width, rows), lambda i: (i, 0, 0)), by_key, by_key, ANY, ANY],
         out_shape=[
             jax.ShapeDtypeStruct((parts, width, rows), BF16),
             jax.ShapeDtypeStruct((parts, n, width), BF16),
             jax.ShapeDtypeStruct((parts, n, width), BF16),
+            jax.ShapeDtypeStruct((m, r, c), BF16),
+            jax.ShapeDtypeStruct((m, r, c), BF16),
         ],
-        compiler_params=pltpu.CompilerParams(vmem_limit_bytes=VMEM_LIMIT),
+        scratch_shapes=gather_scratch(m, r, c, False) * 2 + link_scratch(8, 8),
+        compiler_params=pltpu.CompilerParams(
+            vmem_limit_bytes=VMEM_LIMIT, collective_id=4, has_side_effects=True
+        ),
         cost_estimate=pl.CostEstimate(
             flops=48 * parts * rows * n * width,
             bytes_accessed=16 * parts * n * width,
             transcendentals=parts * rows * n * heads,
         ),
         name="cross_backward",
-    )(ok, queries, keys, values, keys_t, grads, lse, inner)
+    )(ok, queries, keys, values, keys_t, grads, lse, inner, up_sum, down_sum)
 
 
 def swap(value, axis, distance):
@@ -653,12 +974,11 @@
     return (a.astype(F32) + b.astype(F32)).astype(BF16)
 
 
-def reduce_dp(total, distances):
-    n = lax.axis_size("dp")
+def reduce_dp(total, distances, axes):
     me = lax.axis_index("dp")
-    rows, columns = total.shape[0] // n, total.shape[1]
-    shape = [2] * len(dp_distances()) + [rows, columns]
-    axes = list(dp_distances())
+    rows, columns = total.shape[0] // 2 ** len(axes), total.shape[1]
+    shape = [2] * len(axes) + [rows, columns]
+    axes = list(axes)
     total = total.reshape(shape)
     for step, distance in enumerate(distances):
         axis = axes.index(distance)
@@ -669,39 +989,6 @@
         got = swap(give, "dp", distance)
         total = keep.astype(F32) + got.astype(F32)
         if step < len(distances) - 1:
-            total = total.astype(BF16)
-    return total
-
-
-def reduce_all(pieces, x_first):
-    near = add_low(pieces[0], swap(pieces[1], "tensor", 1))
-    far = add_low(pieces[2], swap(pieces[3], "tensor", 1))
-    order = dp_distances()[::-1]
-    if x_first:
-        return reduce_dp(add_low(near, swap(far, "tensor", 2)), order)
-    n = lax.axis_size("dp")
-    me = lax.axis_index("dp")
-    rows, columns = near.shape[0] // n, near.shape[1]
-    mine = me % 2
-
-    def halve(total):
-        total = total.reshape(n // 2, 2, rows, columns)
-        keep = lax.dynamic_index_in_dim(total, mine, 1, keepdims=False)
-        give = lax.dynamic_index_in_dim(total, 1 - mine, 1, keepdims=False)
-        return add_low(keep, swap(give, "dp", 1))
-
-    near, far = halve(near), halve(far)
-    total = add_low(near, swap(far, "tensor", 2))
-    axes = dp_distances()[:-1]
-    total = total.reshape([2] * len(axes) + [rows, columns])
-    for step, distance in enumerate(order[1:]):
-        axis = axes.index(distance)
-        axes.pop(axis)
-        own = me // distance % 2
-        keep = lax.dynamic_index_in_dim(total, own, axis, keepdims=False)
-        give = lax.dynamic_index_in_dim(total, 1 - own, axis, keepdims=False)
-        total = keep.astype(F32) + swap(give, "dp", distance).astype(F32)
-        if step < len(order) - 2:
             total = total.astype(BF16)
     return total
 
@@ -756,7 +1043,8 @@
     up_bias,
 ):
     member = lax.axis_index("tensor")
-    groups = float(lax.axis_size("dp"))
+    groups_count = lax.axis_size("dp")
+    groups = float(groups_count)
     width = w_cross_q.shape[1]
     hidden_width = w_up.shape[1]
     heads = H // 4
@@ -792,7 +1080,7 @@
     key_rows = projected[:, width : 2 * width].astype(BF16)
     value_rows = (projected[:, 2 * width :] + block_of(biases[1], width, 0)).astype(BF16)
     self_safe = 1024
-    self_mixed_t, self_lse, *cross_w, ffn_column = self_forward(
+    self_mixed_t, self_lse, cross_w, ffn_column = self_forward(
         bounds,
         queries,
         key_rows,
@@ -802,10 +1090,10 @@
         heads,
         self_safe,
     )
-    cross_w = [w.reshape(model_width, 4 * width) for w in cross_w]
-    w_query = [w[:, :width] for w in cross_w]
-    w_keyval = [w[:, width : 3 * width] for w in cross_w]
-    w_out = [w[:, 3 * width :] for w in cross_w]
+    cross_w = cross_w.reshape(4, model_width, 4 * width)
+    w_query = [cross_w[d, :, :width] for d in range(4)]
+    w_keyval = [cross_w[d, :, width : 3 * width] for d in range(4)]
+    w_out = [cross_w[d, :, 3 * width :] for d in range(4)]
     self_out_w = self_w[:, 3 * width :]
     after_self = (
         start_rows
@@ -829,12 +1117,9 @@
             for d in range(4)
         ]
     )
-    cross_mixed_t, cross_lse, *ffn_w = cross_forward(
+    cross_mixed_t, cross_lse, ffn_w = cross_forward(
         ok, cross_queries, cross_keys, jnp.swapaxes(cross_values, 1, 2), ffn_column, heads
     )
-    ffn_w = [w.reshape(model_width, 2 * hidden_width) for w in ffn_w]
-    up_w = [w[:, :hidden_width] for w in ffn_w]
-    down_w = [w[:, hidden_width:] for w in ffn_w]
     after_cross = after_self + biases[5]
     for d in range(4):
         after_cross = after_cross + lax.dot_general(
@@ -844,21 +1129,13 @@
     third_in = layer_norm(after_cross, norm_params[2, 0], norm_params[2, 1]).astype(BF16)
     cot_rows = out_grad.astype(F32)
     bias_down_grad = jnp.sum(cot_rows, axis=0)
-    output = after_cross + biases[6]
-    third_grad = 0.0
-    down_pieces, up_pieces, bias_up_parts = [], [], []
-    for d in range(4):
-        pre_act = dot_nn(third_in, up_w[d]) + block_of(up_bias, hidden_width, d)
-        hidden = jax.nn.gelu(pre_act, approximate=False).astype(BF16)
-        output = output + dot_nt(hidden, down_w[d])
-        hidden_grad = dot_nn(out_grad, down_w[d])
-        pre_grad = (hidden_grad * gelu_slope(pre_act)).astype(BF16)
-        down_pieces.append(dot_tn(out_grad, hidden).astype(BF16))
-        up_pieces.append(dot_tn(third_in, pre_grad).astype(BF16))
-        bias_up_parts.append(jnp.sum(pre_grad.astype(F32), axis=0))
-        third_grad = third_grad + dot_nt(pre_grad, up_w[d])
-    summed_up = reduce_all(up_pieces, False)
-    summed_down = reduce_all(down_pieces, True).T
+    ffn_out, third_grad, up_sum, down_sum, bias_up_parts = feed_forward(
+        third_in,
+        out_grad,
+        ffn_w.reshape(4, model_width, 2 * hidden_width),
+        jnp.stack([block_of(up_bias, hidden_width, d) for d in range(4)])[:, None],
+    )
+    output = after_cross + biases[6] + ffn_out
     rows_three, gain_three, shift_three = norm_back(after_cross, third_grad, 2)
     cross_rows_grad = cot_rows + rows_three
 
@@ -870,7 +1147,8 @@
         * jnp.swapaxes(cross_mixed_grad, 1, 2).reshape(4, heads, width // heads, own_rows).astype(F32),
         axis=2,
     )
-    cross_dq_t, part_dk, part_dv = cross_backward(
+    by_shard = (2, groups_count // 2, 2, w_rows, hidden_width)
+    cross_dq_t, part_dk, part_dv, up_column, down_column = cross_backward(
         ok,
         cross_queries,
         cross_keys,
@@ -879,6 +1157,8 @@
         cross_mixed_grad,
         cross_lse,
         cross_inner,
+        up_sum.reshape(by_shard),
+        down_sum.reshape(by_shard),
         heads,
     )
     second_grad = 0.0
@@ -920,10 +1200,9 @@
                 axis=1,
             )
         )
-    summed_cross = reduce_all(cross_pieces, False)
     bias_cq_grad = blocks_placed([jnp.sum(cross_dq_t[d].astype(F32), axis=1) for d in range(4)])
     bias_cv_grad = blocks_placed([jnp.sum(dkv[d, :, width:].astype(F32), axis=0) for d in range(4)])
-    bias_up_grad = blocks_placed(bias_up_parts)
+    bias_up_grad = blocks_placed([bias_up_parts[d, 0] for d in range(4)])
 
     self_mixed_grad = dot_nn(self_wide, self_out_w).astype(BF16)
     self_inner = jnp.sum(
@@ -931,9 +1210,22 @@
         * self_mixed_grad.T.reshape(heads, width // heads, 4 * own_rows).astype(F32),
         axis=1,
     )
-    self_dq_t, self_dk, self_dv = self_backward(
-        bounds, queries, key_rows, value_rows, key_rows.T, self_mixed_grad, self_lse, self_inner, heads, self_safe
-    )
+    self_dq_t, self_dk, self_dv, summed_up, summed_down, cross_column = self_backward(
+        bounds,
+        queries,
+        key_rows,
+        value_rows,
+        key_rows.T,
+        self_mixed_grad,
+        self_lse,
+        self_inner,
+        up_column,
+        down_column,
+        [piece.reshape(groups_count // 2, 2, w_rows, 4 * width) for piece in cross_pieces],
+        heads,
+        self_safe,
+    )
+    summed_cross = reduce_dp(cross_column.reshape(-1, 4 * width), dp_distances()[-2::-1], dp_distances()[:-1])
     grad_so_t = lax.dot_general(
         self_wide, self_mixed_t, (((0,), (1,)), ((), ())), preferred_element_type=F32
     ).astype(BF16)
@@ -941,7 +1233,9 @@
     first_terms = dot_nt(qkv_grad, self_w[:, : 3 * width]).astype(BF16)
     first_grad = narrow(first_terms)
     summed_self = reduce_dp(
-        jnp.concatenate([dot_tn(first_in, qkv_grad).astype(BF16), grad_so_t], axis=1), dp_distances()[::-1]
+        jnp.concatenate([dot_tn(first_in, qkv_grad).astype(BF16), grad_so_t], axis=1),
+        dp_distances()[::-1],
+        dp_distances(),
     )
     column_sums = jnp.sum(qkv_grad.astype(F32), axis=0)
     rows_one, gain_one, shift_one = norm_back(start_rows, first_grad, 0)
@@ -989,7 +1283,7 @@
         summed_cross[:, width : 3 * width].reshape(w_cross_kv.shape) * scale,
         summed_cross[:, 3 * width :].T * scale,
         summed_up * scale,
-        summed_down * scale,
+        summed_down.T * scale,
         bias_total * scale,
         up_total * scale,
     )

time: 849 us -> 802 us (0.945)
  Pallas kernels: 296 us -> 397 us
  matrix products: 174 us -> 110 us
  waiting for transfers between devices: 98.7 us -> 61.1 us
  local copies, waits for them, and re-layouts: 137 us -> 114 us
  starting transfers between devices: 35.8 us -> 22.4 us
  other arithmetic: 93.9 us -> 84.2 us
    pallas_call x0 -> x1, Pallas kernels: none -> 48.2 us  [feed_forward(): pl.pallas_call(functools.partial(feed_forward_kernel, chunks=chunks), gri...]
    pallas_call x1, Pallas kernels: 35.6 us -> 75.7 us  [cross_backward(): pl.pallas_call(functools.partial(cross_backward_kernel, heads=heads, bk=5...]
    dot_general x22 -> x14, matrix products: 79.9 us -> 40.3 us  [dot_nn(): lax.dot_general(a, b, (((1,), (0,)), ((), ())), preferred_element_type=F32)]
    ppermute x45 -> x27, waiting for transfers between devices: 98.7 us -> 61.1 us  [swap(): return lax.ppermute(value, axis, [(i, i ^ distance) for i in range(size)])]
    dot_general x13 -> x5, matrix products: 38.9 us -> 15 us  [dot_tn(): lax.dot_general(a, b, (((0,), (0,)), ((), ())), preferred_element_type=F32)]
    dynamic_slice x4 -> x0, local copies, waits for them, and re-layouts: 15.4 us -> none  [the longest x2 15 us: halve(): keep = lax.dynamic_index_in_dim(total, mine, 1, keepdims=False)]
    unnamed x320 -> x204, local copies, waits for them, and re-layouts: 50.3 us -> 35.1 us
    ppermute x45 -> x27, starting transfers between devices: 35.8 us -> 22.4 us  [swap(): return lax.ppermute(value, axis, [(i, i ^ distance) for i in range(size)])]
  transfers between devices with their start and end apart: 45 -> 27, of which waited for: 13 -> 8; matrix products, arithmetic and copies ran while one was open for 30% -> 19% of each run, Pallas kernels for 6% -> 0%
where the time goes in v3:
time: 802 us; the launch traced here: 791 us
  Pallas kernels  397 us (50%)
  local copies, waits for them, and re-layouts  114 us (14%)
  matrix products  110 us (14%)
  other arithmetic  84.2 us (10%)
  waiting for transfers between devices  61.1 us (8%)
  starting transfers between devices  22.4 us (3%)
    pallas_call x1, Pallas kernels, cross_forward(): pl.pallas_call(functools.partial(cross_forward_kernel, heads=heads), grid...  79.6 us
    pallas_call x1, Pallas kernels, start_gather(): pl.pallas_call(functools.partial(start_kernel, n=n), in_specs=[ANY] * 4,...  77.3 us
    pallas_call x1, Pallas kernels, cross_backward(): pl.pallas_call(functools.partial(cross_backward_kernel, heads=heads, bk=5...  75.7 us
    pallas_call x1, Pallas kernels, self_backward(): pl.pallas_call(functools.partial(self_backward_kernel, bk=bk, heads=heads...  62.6 us
    ppermute x27, waiting for transfers between devices, swap(): return lax.ppermute(value, axis, [(i, i ^ distance) for i in range(size)])  61.1 us
    pallas_call x1, Pallas kernels, self_forward(): pl.pallas_call(functools.partial(self_forward_kernel, bk=bk, heads=heads,...  53.3 us
    pallas_call x1, Pallas kernels, feed_forward(): pl.pallas_call(functools.partial(feed_forward_kernel, chunks=chunks), gri...  48.2 us
    dot_general x14, matrix products, dot_nn(): lax.dot_general(a, b, (((1,), (0,)), ((), ())), preferred_element_type=F32)  40.3 us
  transfers between devices with their start and end apart: 27, of which 8 were waited for; matrix products, arithmetic and copies ran while one was open for 19% of the time, Pallas kernels for 0%

profile of v3, /device:TPU:0, one launch (start us, length us, event | category | flops | bytes accessed | tf_op | source)
XLA Modules:
  0.0 790.8 jit_solution(4635381732904597562)
XLA Ops:
  7.3 77.3 %start_gather.1 = (bf16[2560,1024]{1,0:T(8,128)(2,1)}, bf16[1024,1024]{1,0:T(8,128)(2,1)}, bf16[4,2,128,1024]{3,2,1,0:T(8,128)(2,1)}, bf16[4,128,1024]{2,1,0:T(8,128)(2,1)}) custom-call(bf16[640,1024]{1,0:T(8,128)(2,1)} %copy.85.rows_ref, bf16[256,1024]{1,0:T(8,128)(2,1)} %enc_ref.1, bf16[128,1024]{1,0:T(8,128)(2,1)} %get-tuple-element.209.self_ref, ...), custom_call_target="tpu_custom_call" | custom-call | bytes 104857600 | tf_op jit(solution)/shard_map/start_gather/pallas_call | solution.py:388
  84.5 6.6 fusion.17
  91.2 3.1 copy-done.17
  94.4 4.0 fusion.12
  104.4 53.3 %self_forward.1 = (bf16[256,2560]{1,0:T(8,128)(2,1)}, f32[4,2560]{1,0:T(4,128)}, bf16[4,4,2,128,1024]{4,3,2,1,0:T(8,128)(2,1)}, bf16[4,128,2048]{2,1,0:T(8,128)(2,1)}) custom-call(s32[1,2]{1,0:T(1,128)} %b_ref.3, bf16[2560,256]{1,0:T(8,128)(2,1)} %get-tuple-element.122.q_ref, bf16[2560,256]{1,0:T(8,128)(2,1)} %copy.88.k_ref, bf16[256,2560]{1,0:T(8,128)(2,1)} %copy.89.vt_ref, ...), custom_call_target="tpu_custom_call" | custom-call | flops 20132659200 | bytes 5242880 | tf_op jit(solution)/shard_map/self_forward/pallas_call | solution.py:488
  157.7 5.4 convolution_convert_fusion
  163.1 3.6 constant_dynamic-slice_fusion.15
  167.2 3.9 fusion.47
  171.1 3.9 fusion.49
  177.7 2.1 slice.543
  179.8 3.2 fusion.45
  183.9 2.5 fusion.43
  190.1 3.3 add_convert_fusion.3
  196.9 2.4 copy.95.vt_ref
  203.7 2.9 fusion.105
  206.6 2.6 copy.94.k_ref
  213.1 11.3 %collective-permute-done.2 = bf16[640,1024]{0,1:T(8,128)(2,1)} collective-permute-done((bf16[640,1024]{0,1:T(8,128)(2,1)}, bf16[640,1024]{0,1:T(8,128)(2,1)}, u32[]{:S(2)}, u32[]{:S(2)}) %collective-permute-start.2) | collective-permute-done | bytes 1310752 | tf_op jit(solution)/shard_map/ppermute | solution.py:961
  224.4 3.3 fusion.110
  236.6 79.6 %cross_forward.1 = (bf16[4,256,640]{2,1,0:T(8,128)(2,1)}, f32[4,4,640]{2,1,0:T(4,128)}, bf16[4,4,2,128,2048]{4,3,2,1,0:T(8,128)(2,1)}) custom-call(f32[1024,1]{1,0:T(8,128)} %fusion.54.ok_ref, bf16[4,640,256]{2,1,0:T(8,128)(2,1)} %pad_maximum_fusion.9.q_ref, bf16[4,1024,256]{2,1,0:T(8,128)(2,1)} %copy.94.k_ref, bf16[4,256,1024]{2,1,0:T(8,128)(2,1)} %copy.95.vt_ref, ...), custom_call_target="tpu_custom_call" | custom-call | flops 16106127360 | bytes 8388608 | tf_op jit(solution)/shard_map/cross_forward/pallas_call | solution.py:711
  321.3 2.1 fusion.118
  326.9 2.5 copy.101.x_ref
  329.4 48.2 %feed_forward.1 = (f32[640,1024]{1,0:T(8,128)}, f32[640,1024]{1,0:T(8,128)}, bf16[2,1024,1024]{2,1,0:T(8,128)(2,1)}, bf16[2,1024,1024]{2,1,0:T(8,128)(2,1)}, f32[4,1,1024]{2,1,0:T(1,128)}) custom-call(bf16[640,1024]{1,0:T(8,128)(2,1)} %copy.101.x_ref, bf16[1024,640]{1,0:T(8,128)(2,1)} %fusion.150.xt_ref, bf16[640,1024]{1,0:T(8,128)(2,1)} %dy_ref.1, ...), custom_call_target="tpu_custom_call" | custom-call | flops 32212254720 | bytes 41943040 | tf_op jit(solution)/shard_map/feed_forward/pallas_call | solution.py:816
  377.6 3.2 copy.104
  380.8 3.3 multiply_reduce_fusion
  384.1 3.2 copy.102
  387.4 5.1 fusion.109
  397.6 2.3 fusion.35
  400.0 2.3 fusion.36
  402.3 2.4 copy.109
  404.7 2.4 pad_maximum_fusion.10.do_ref
  409.1 3.2 copy.110
  412.3 2.6 bitcast_reduce_fusion.1.dl_ref
  414.9 75.7 %cross_backward.1 = (bf16[4,256,640]{2,1,0:T(8,128)(2,1)}, bf16[4,1024,256]{2,1,0:T(8,128)(2,1)}, bf16[4,1024,256]{2,1,0:T(8,128)(2,1)}, bf16[4,128,1024]{2,1,0:T(8,128)(2,1)}, bf16[4,128,1024]{2,1,0:T(8,128)(2,1)}) custom-call(f32[1024,1]{1,0:T(8,128)} %fusion.54.ok_ref, bf16[4,640,256]{2,1,0:T(8,128)(2,1)} %pad_maximum_fusion.9.q_ref, ...), custom_call_target="tpu_custom_call" | custom-call | flops 32212254720 | bytes 16777216 | tf_op jit(solution)/shard_map/cross_backward/pallas_call | solution.py:923
  501.7 2.4 multiply_reduce_fusion.1
  518.3 2.8 convolution_convert_fusion.12
  521.1 2.9 convolution_convert_fusion.13
  524.0 2.5 convolution_convert_fusion.14
  526.6 2.5 add_convert_fusion.5
  530.7 2.1 copy.131
  536.2 2.4 convolution_convert_fusion.16
  538.6 2.4 convolution_convert_fusion.15
  544.2 18.7 %collective-permute-done.8 = bf16[4,256,512]{2,1,0:T(8,128)(2,1)} collective-permute-done((bf16[4,256,512]{2,1,0:T(8,128)(2,1)}, bf16[4,256,512]{2,1,0:T(8,128)(2,1)}, u32[]{:S(2)}, u32[]{:S(2)}) %collective-permute-start.8) | collective-permute-done | bytes 1048608 | tf_op jit(solution)/shard_map/ppermute | solution.py:961
  570.0 2.6 copy.122
  574.3 2.6 copy.121
  578.6 2.6 copy.120
  582.8 2.6 copy.119
  592.7 2.7 fusion.24
  597.1 5.0 bitcast_multiply_fusion
  602.2 2.1 copy.118
  605.2 62.6 %self_backward.1 = (bf16[256,2560]{1,0:T(8,128)(2,1)}, bf16[2560,256]{1,0:T(8,128)(2,1)}, bf16[2560,256]{1,0:T(8,128)(2,1)}, f32[128,1024]{1,0:T(8,128)}, f32[12...) custom-call(s32[1,2]{1,0:T(1,128)} %b_ref.3, bf16[2560,256]{1,0:T(8,128)(2,1)} %get-tuple-element.122.q_ref, ...), custom_call_target="tpu_custom_call" | custom-call | flops 40265318400 | bytes 10485760 | tf_op jit(solution)/shard_map/self_backward/pallas_call | solution.py:630
  669.7 6.6 convolution_convert_fusion.1
  676.4 10.2 %convolution_convert_fusion.3 = bf16[1024,768]{0,1:T(8,128)(2,1)} fusion(bf16[2560,1024]{1,0:T(8,128)(2,1)} %get-tuple-element.40, bf16[2560,256]{1,0:T(8,128)(2,1)S(1)} %copy-done.43, bf16[2560,256]{1,0:T(8,128)(2,1)S(1)} %copy-done.41, bf16[2560,256]{1,0:T(8,128)(2,1)S(1)} %bitcast.378), kind=kOutput, calls=%fused_computation.63 | convolution fusion | flops 4039114752 | bytes 10747904 | tf_op jit(solution)/shard_map/dot_general | solution.py:28
  686.6 2.4 convolution_convert_fusion.8
  693.7 2.5 pad_maximum_fusion.8
  696.2 3.5 reshape.287
  699.8 6.3 constant_dynamic-slice_fusion.3
  715.2 3.1 add_convert_fusion
  719.3 15.1 %collective-permute-done.22 = bf16[2,2,128,1024]{2,3,0,1:T(8,128)(2,1)S(1)} collective-permute-done((bf16[2,2,128,1024]{2,3,0,1:T(8,128)(2,1)S(1)}, bf16[2,2,128,1024]{2,3,0,1:T(8,128)(2,1)S(1)}, u32[]{:S(2)}, u32[]{:S(2)}) %collective-permute-start.22) | collective-permute-done | bytes 1048608 | tf_op jit(solution)/shard_map/ppermute | solution.py:961
  739.2 9.3 %collective-permute-done.23 = bf16[2,128,1024]{1,2,0:T(8,128)(2,1)} collective-permute-done((bf16[2,128,1024]{1,2,0:T(8,128)(2,1)}, bf16[2,128,1024]{1,2,0:T(8,128)(2,1)}, u32[]{:S(2)}, u32[]{:S(2)}) %collective-permute-start.23) | collective-permute-done | bytes 524320 | tf_op jit(solution)/shard_map/ppermute | solution.py:961
  752.2 3.1 fusion.10
  757.4 3.0 convert_reduce_fusion.2
  776.8 2.3 collective-permute-done.19
  782.0 2.1 copy.132
  785.4 2.9 collective-permute-done.21
  (401 shorter events, 160.9 us)
Async XLA Ops:
  101.9 55.8 %copy-start.23 = (bf16[2560,256]{0,1:T(8,128)(2,1)}, bf16[2560,256]{0,1:T(8,128)(2,1)S(1)}, u32[]{:S(2)}) copy-start(bf16[2560,256]{0,1:T(8,128)(2,1)S(1)} %copy.153) | copy-start | bytes 3932164
  166.7 23.4 %collective-permute-start.1 = (bf16[640,1024]{0,1:T(8,128)(2,1)}, bf16[640,1024]{0,1:T(8,128)(2,1)}, u32[]{:S(2)}, u32[]{:S(2)}) collective-permute-start(bf16[640,1024]{0,1:T(8,128)(2,1)} %get-tuple-element.126), channel_id=1, source_target_pairs={{0,1},{1,0},{2,3},{3,2},{4,5},{5,4},{6,7},{7,6},{8,9},{9,8},{10,11... | collective-permute-start | bytes 3932168 | tf_op jit(solution)/shard_map/ppermute | solution.py:961
  166.7 46.4 %collective-permute-start = (bf16[640,1024]{0,1:T(8,128)(2,1)}, bf16[640,1024]{0,1:T(8,128)(2,1)}, u32[]{:S(2)}, u32[]{:S(2)}) collective-permute-start(bf16[640,1024]{0,1:T(8,128)(2,1)} %get-tuple-element.125), channel_id=1, source_target_pairs={{0,1},{1,0},{2,3},{3,2},{4,5},{5,4},{6,7},{7,6},{8,9},{9,8},{10,11... | collective-permute-start | bytes 3932168 | tf_op jit(solution)/shard_map/ppermute | solution.py:961
  189.9 5.0 copy-start.50
  190.1 5.0 copy-start.49
  193.4 31.0 %collective-permute-start.2 = (bf16[640,1024]{0,1:T(8,128)(2,1)}, bf16[640,1024]{0,1:T(8,128)(2,1)}, u32[]{:S(2)}, u32[]{:S(2)}) collective-permute-start(bf16[640,1024]{0,1:T(8,128)(2,1)} %add_convert_fusion.3), channel_id=1, source_target_pairs={{0,2},{1,3},{2,0},{3,1},{4,6},{5,7},{6,4},{7,5},{8,10},{9,11},{10,... | collective-permute-start | bytes 3932168 | tf_op jit(solution)/shard_map/ppermute | solution.py:961
  228.5 5.3 copy-start.45
  387.4 5.1 copy-start.8
  394.0 5.9 copy-start.36
  508.9 32.1 %collective-permute-start.3 = (bf16[640,1024]{0,1:T(8,128)(2,1)}, bf16[640,1024]{0,1:T(8,128)(2,1)}, u32[]{:S(2)}, u32[]{:S(2)}) collective-permute-start(bf16[640,1024]{0,1:T(8,128)(2,1)} %get-tuple-element.112), channel_id=1, source_target_pairs={{0,1},{1,0},{2,3},{3,2},{4,5},{5,4},{6,7},{7,6},{8,9},{9,8},{10,11... | collective-permute-start | bytes 3932168 | tf_op jit(solution)/shard_map/ppermute | solution.py:961
  508.9 32.1 %collective-permute-start.4 = (bf16[640,1024]{0,1:T(8,128)(2,1)}, bf16[640,1024]{0,1:T(8,128)(2,1)}, u32[]{:S(2)}, u32[]{:S(2)}) collective-permute-start(bf16[640,1024]{0,1:T(8,128)(2,1)} %get-tuple-element.112), channel_id=1, source_target_pairs={{0,2},{1,3},{2,0},{3,1},{4,6},{5,7},{6,4},{7,5},{8,10},{9,11},{10,... | collective-permute-start | bytes 3932168 | tf_op jit(solution)/shard_map/ppermute | solution.py:961
  512.7 31.5 %collective-permute-start.6 = (bf16[4,256,512]{2,1,0:T(8,128)(2,1)}, bf16[4,256,512]{2,1,0:T(8,128)(2,1)}, u32[]{:S(2)}, u32[]{:S(2)}) collective-permute-start(bf16[4,256,512]{2,1,0:T(8,128)(2,1)} %pad_maximum_fusion.11), channel_id=1, source_target_pairs={{0,1},{1,0},{2,3},{3,2},{4,5},{5,4},{6,7},{7,6},{8,9},{9,8},{10,11... | collective-permute-start | bytes 3145736 | tf_op jit(solution)/shard_map/ppermute | solution.py:961
  513.8 12.7 %collective-permute-start.7 = (bf16[4,256,512]{2,1,0:T(8,128)(2,1)}, bf16[4,256,512]{2,1,0:T(8,128)(2,1)}, u32[]{:S(2)}, u32[]{:S(2)}) collective-permute-start(bf16[4,256,512]{2,1,0:T(8,128)(2,1)} %pad_maximum_fusion.12), channel_id=1, source_target_pairs={{0,1},{1,0},{2,3},{3,2},{4,5},{5,4},{6,7},{7,6},{8,9},{9,8},{10,11... | collective-permute-start | bytes 3145736 | tf_op jit(solution)/shard_map/ppermute | solution.py:961
  516.0 8.1 %copy-start.47 = (bf16[640,1024]{0,1:T(8,128)(2,1)S(1)}, bf16[640,1024]{0,1:T(8,128)(2,1)}, u32[]{:S(2)}) copy-start(bf16[640,1024]{0,1:T(8,128)(2,1)} %copy-done.45) | copy-start | bytes 3932164
  521.1 5.4 copy-start.80
  521.1 5.4 copy-start.53
  521.1 5.4 copy-start.54
  521.1 5.5 copy-start.55
  521.1 5.5 copy-start.56
  524.0 6.7 copy-start.13
  529.1 33.8 %collective-permute-start.8 = (bf16[4,256,512]{2,1,0:T(8,128)(2,1)}, bf16[4,256,512]{2,1,0:T(8,128)(2,1)}, u32[]{:S(2)}, u32[]{:S(2)}) collective-permute-start(bf16[4,256,512]{2,1,0:T(8,128)(2,1)} %add_convert_fusion.5), channel_id=1, source_target_pairs={{0,2},{1,3},{2,0},{3,1},{4,6},{5,7},{6,4},{7,5},{8,10},{9,11},{10,... | collective-permute-start | bytes 3145736 | tf_op jit(solution)/shard_map/ppermute | solution.py:961
  541.0 21.9 %copy-start.52 = (bf16[1,256,512]{2,1,0:T(8,128)(2,1)S(1)}, bf16[1,256,512]{2,1,0:T(8,128)(2,1)}, u32[]{:S(2)}) copy-start(bf16[1,256,512]{2,1,0:T(8,128)(2,1)} %get-tuple-element.142) | copy-start | bytes 786436
  541.0 54.4 %collective-permute-start.5 = (bf16[640,1024]{0,1:T(8,128)(2,1)}, bf16[640,1024]{0,1:T(8,128)(2,1)}, u32[]{:S(2)}, u32[]{:S(2)}) collective-permute-start(bf16[640,1024]{0,1:T(8,128)(2,1)} %collective-permute-done.4), channel_id=1, source_target_pairs={{0,1},{1,0},{2,3},{3,2},{4,5},{5,4},{6,7},{7,6},{8,9},{9,8},{10,11... | collective-permute-start | bytes 3932168 | tf_op jit(solution)/shard_map/ppermute | solution.py:961
  544.2 21.3 %copy-start.21 = (bf16[2560,1024]{0,1:T(8,128)(2,1)}, bf16[2560,1024]{0,1:T(8,128)(2,1)S(1)}, u32[]{:S(2)}) copy-start(bf16[2560,1024]{0,1:T(8,128)(2,1)S(1)} %constant_dynamic-update-slice_fusion.1) | copy-start | bytes 15728644
  544.2 20.8 %copy-start.11 = (bf16[256,1024]{1,0:T(8,128)(2,1)S(1)}, bf16[256,1024]{1,0:T(8,128)(2,1)}, u32[]{:S(2)}) copy-start(bf16[256,1024]{1,0:T(8,128)(2,1)} %enc_ref.1) | copy-start | bytes 1572868
  565.4 4.4 copy-start.60
  565.4 4.4 copy-start.61
  587.4 8.0 %slice-start = ((s8[5242880]{0:T(1024)(128)(4,1)}), s8[4194304]{0:T(1024)(128)(4,1)S(1)}, s32[]{:S(2)}) async-start(s8[5242880]{0:T(1024)(128)(4,1)} %bitcast.372), calls=%async_computation | async-start | bytes 8388608
  590.9 4.5 slice-start.1
  597.1 5.0 copy-start.22
  667.8 18.8 %slice-start.2 = ((s8[5242880]{0:T(1024)(128)(4,1)}), s8[1048576]{0:T(1024)(128)(4,1)S(1)}, s32[]{:S(2)}) async-start(s8[5242880]{0:T(1024)(128)(4,1)} %bitcast.374), calls=%async_computation.2 | async-start | bytes 2097152
  669.7 6.6 copy-start.41
  669.7 6.6 copy-start.43
  669.7 16.8 %slice-start.3 = ((s8[5242880]{0:T(1024)(128)(4,1)}), s8[4194304]{0:T(1024)(128)(4,1)S(1)}, s32[]{:S(2)}) async-start(s8[5242880]{0:T(1024)(128)(4,1)} %bitcast.374), calls=%async_computation.3 | async-start | bytes 8388608
  676.4 12.6 %copy-start.24 = (bf16[2560,1024]{0,1:T(8,128)(2,1)}, bf16[2560,1024]{0,1:T(8,128)(2,1)S(1)}, u32[]{:S(2)}) copy-start(bf16[2560,1024]{0,1:T(8,128)(2,1)S(1)} %convolution_convert_fusion.1) | copy-start | bytes 15728644
  676.4 10.2 %copy-start.19 = (bf16[256,2560]{1,0:T(8,128)(2,1)S(1)}, bf16[256,2560]{1,0:T(8,128)(2,1)}, u32[]{:S(2)}) copy-start(bf16[256,2560]{1,0:T(8,128)(2,1)} %get-tuple-element.43) | copy-start | bytes 3932164
  690.7 24.6 %collective-permute-start.10 = (bf16[640,1024]{0,1:T(8,128)(2,1)}, bf16[640,1024]{0,1:T(8,128)(2,1)}, u32[]{:S(2)}, u32[]{:S(2)}) collective-permute-start(bf16[640,1024]{0,1:T(8,128)(2,1)} %get-tuple-element.124), channel_id=1, source_target_pairs={{0,1},{1,0},{2,3},{3,2},{4,5},{5,4},{6,7},{7,6},{8,9},{9,8},{10,11... | collective-permute-start | bytes 3932168 | tf_op jit(solution)/shard_map/ppermute | solution.py:961
  690.7 61.5 %collective-permute-start.9 = (bf16[640,1024]{0,1:T(8,128)(2,1)}, bf16[640,1024]{0,1:T(8,128)(2,1)}, u32[]{:S(2)}, u32[]{:S(2)}) collective-permute-start(bf16[640,1024]{0,1:T(8,128)(2,1)} %get-tuple-element.123), channel_id=1, source_target_pairs={{0,1},{1,0},{2,3},{3,2},{4,5},{5,4},{6,7},{7,6},{8,9},{9,8},{10,11... | collective-permute-start | bytes 3932168 | tf_op jit(solution)/shard_map/ppermute | solution.py:961
  693.1 19.2 %collective-permute-start.25 = (bf16[2,128,1024]{1,2,0:T(8,128)(2,1)}, bf16[2,128,1024]{1,2,0:T(8,128)(2,1)}, u32[]{:S(2)}, u32[]{:S(2)}) collective-permute-start(bf16[2,128,1024]{1,2,0:T(8,128)(2,1)} %bitcast.395), channel_id=1, source_target_pairs={{0,8},{4,12},{8,0},{12,4},{16,24},{20,28},{24,16},{28,20},{1,9},{5... | collective-permute-start | bytes 1572872 | tf_op jit(solution)/shard_map/ppermute | solution.py:961
  699.7 6.4 copy-start.42
  699.7 6.4 copy-start.44
  709.5 24.9 %collective-permute-start.22 = (bf16[2,2,128,1024]{2,3,0,1:T(8,128)(2,1)S(1)}, bf16[2,2,128,1024]{2,3,0,1:T(8,128)(2,1)S(1)}, u32[]{:S(2)}, u32[]{:S(2)}) collective-permute-start(bf16[2,2,128,1024]{2,3,0,1:T(8,128)(2,1)S(1)} %bitcast.390), channel_id=1, source_target_pairs={{0,4},{4,0},{8,12},{12,8},{16,20},{20,16},{24,28},{28,24},{1,5},{5... | collective-permute-start | bytes 3145736 | tf_op jit(solution)/shard_map/ppermute | solution.py:961
  713.4 20.9 %copy-start.15 = (bf16[2,2,1,128,1024]{3,2,1,0,4:T(2,128)(2,1)S(1)}, bf16[2,2,1,128,1024]{3,2,1,0,4:T(2,128)(2,1)}, u32[]{:S(2)}) copy-start(bf16[2,2,1,128,1024]{3,2,1,0,4:T(2,128)(2,1)} %get-tuple-element.144) | copy-start | bytes 3145732
  714.2 24.0 %collective-permute-start.26 = (bf16[128,1024]{0,1:T(8,128)(2,1)}, bf16[128,1024]{0,1:T(8,128)(2,1)}, u32[]{:S(2)}, u32[]{:S(2)}) collective-permute-start(bf16[128,1024]{0,1:T(8,128)(2,1)} %dynamic-slice_bitcast_fusion.17), channel_id=1, source_target_pairs={{0,16},{4,20},{8,24},{12,28},{16,0},{20,4},{24,8},{28,12},{1,17},{... | collective-permute-start | bytes 786440 | tf_op jit(solution)/shard_map/ppermute | solution.py:961
  718.3 33.9 %collective-permute-start.11 = (bf16[640,1024]{0,1:T(8,128)(2,1)}, bf16[640,1024]{0,1:T(8,128)(2,1)}, u32[]{:S(2)}, u32[]{:S(2)}) collective-permute-start(bf16[640,1024]{0,1:T(8,128)(2,1)} %add_convert_fusion), channel_id=1, source_target_pairs={{0,2},{1,3},{2,0},{3,1},{4,6},{5,7},{6,4},{7,5},{8,10},{9,11},{10,... | collective-permute-start | bytes 3932168 | tf_op jit(solution)/shard_map/ppermute | solution.py:961
  735.4 16.7 %copy-start.2 = (bf16[640,1024]{0,1:T(8,128)(2,1)S(1)}, bf16[640,1024]{0,1:T(8,128)(2,1)}, u32[]{:S(2)}) copy-start(bf16[640,1024]{0,1:T(8,128)(2,1)} %copy-done.1) | copy-start | bytes 3932164
  735.4 16.8 %copy-start.66 = (f32[640]{0:T(1024)S(1)}, f32[640]{0:T(1024)}, u32[]{:S(2)}) copy-start(f32[640]{0:T(1024)} %copy-done.65) | copy-start | bytes 7684
  735.4 16.8 %copy-start.69 = (f32[1,1,1024]{2,1,0:T(1,128)S(1)}, f32[1,1,1024]{2,1,0:T(1,128)}, u32[]{:S(2)}) copy-start(f32[1,1,1024]{2,1,0:T(1,128)} %copy-done.68) | copy-start | bytes 12292
  735.4 13.1 %collective-permute-start.23 = (bf16[2,128,1024]{1,2,0:T(8,128)(2,1)}, bf16[2,128,1024]{1,2,0:T(8,128)(2,1)}, u32[]{:S(2)}, u32[]{:S(2)}) collective-permute-start(bf16[2,128,1024]{1,2,0:T(8,128)(2,1)} %dynamic-slice_bitcast_fusion), channel_id=1, source_target_pairs={{0,8},{4,12},{8,0},{12,4},{16,24},{20,28},{24,16},{28,20},{1,9},{5... | collective-permute-start | bytes 1572872 | tf_op jit(solution)/shard_map/ppermute | solution.py:961
  750.4 4.9 copy-start.76
  750.4 4.9 copy-start.71
  750.4 20.2 %collective-permute-start.24 = (bf16[128,1024]{0,1:T(8,128)(2,1)}, bf16[128,1024]{0,1:T(8,128)(2,1)}, u32[]{:S(2)}, u32[]{:S(2)}) collective-permute-start(bf16[128,1024]{0,1:T(8,128)(2,1)} %dynamic-slice_bitcast_fusion.18), channel_id=1, source_target_pairs={{0,16},{4,20},{8,24},{12,28},{16,0},{20,4},{24,8},{28,12},{1,17},{... | collective-permute-start | bytes 786440 | tf_op jit(solution)/shard_map/ppermute | solution.py:961
  752.2 4.6 copy-start.7
  760.4 21.6 %copy-start.14 = (f32[640,1024]{0,1:T(8,128)S(1)}, f32[640,1024]{0,1:T(8,128)}, u32[]{:S(2)}) copy-start(f32[640,1024]{0,1:T(8,128)} %get-tuple-element.151) | copy-start | bytes 7864324
  760.4 1.7 collective-permute-start.12
  761.6 6.5 collective-permute-start.17
  762.1 3.9 collective-permute-start.13
  766.8 4.8 collective-permute-start.14
  769.0 4.2 collective-permute-start.18
  771.6 4.0 collective-permute-start.15
  774.0 5.1 collective-permute-start.19
  775.7 8.4 %collective-permute-start.16 = (f32[32,128]{1,0:T(8,128)S(1)}, f32[32,128]{1,0:T(8,128)S(1)}, u32[]{:S(2)}, u32[]{:S(2)}) collective-permute-start(f32[32,128]{1,0:T(8,128)S(1)} %add.524), channel_id=1, source_target_pairs={{0,4},{4,0},{8,12},{12,8},{16,20},{20,16},{24,28},{28,24},{1,5},{5... | collective-permute-start | bytes 49160 | tf_op jit(solution)/shard_map/ppermute | solution.py:961
  779.1 5.0 collective-permute-start.20
  784.1 4.2 collective-permute-start.21
  (51 other events, 130.9 us)

commit v4 on v3

--- a/solution.py
+++ b/solution.py
@@ -212,9 +212,9 @@
 
 
 class Gather:
-    def __init__(self, links, near, far, buffers, core=None):
+    def __init__(self, links, near, far, buffers):
         y = links.dp % 2
-        self.column, self.over_y, self.over_x, self.got_y, self.got_x, self.sum_y, self.sum_x = buffers[:7]
+        self.column, self.over_y, self.over_x, self.got_y, self.got_x, self.sum_y, self.sum_x = buffers
         m = self.column.shape[0]
         low, high = pl.ds(0, m // 2), pl.ds(m // 2, m // 2)
         self.low, self.high = low, high
@@ -223,18 +223,7 @@
             links.local(near.at[:, 1 - y], self.over_y),
             links.local(far.at[:, y], self.over_x),
         ]
-        self.core = []
         diagonal = far.at[:, 1 - y]
-        if core is not None:
-            diagonal, near_core, far_core = buffers[7:]
-            self.loads.append(links.local(far.at[:, 1 - y], diagonal))
-            self.core = [links.copy(core[0], near_core, CORE), links.copy(core[1], far_core, CORE)]
-            self.core_sums = [
-                (self.column, near_core.at[:, y]),
-                (self.over_y, near_core.at[:, 1 - y]),
-                (self.over_x, far_core.at[:, y]),
-                (diagonal, far_core.at[:, 1 - y]),
-            ]
         self.first = [
             links.copy(diagonal.at[low], self.got_y, X),
             links.copy(diagonal.at[high], self.got_x, Y),
@@ -245,26 +234,12 @@
         ]
 
     def start(self):
-        for copy in self.loads + self.core:
+        for copy in self.loads + self.first:
             copy.start()
-        if not self.core:
-            for copy in self.first:
-                copy.start()
-
-    def after_core(self):
+
+    def middle(self):
         for copy in self.loads:
             copy.wait()
-        for copy in self.core:
-            copy.wait_recv()
-        for total, other in self.core_sums:
-            add_to(total, other)
-        for copy in self.first:
-            copy.start()
-
-    def middle(self):
-        if not self.core:
-            for copy in self.loads:
-                copy.wait()
         for copy in self.first:
             copy.wait_recv()
         add_to(self.over_y.at[self.low], self.got_y)
@@ -277,17 +252,14 @@
             copy.wait_recv()
         add_to(self.column, self.sum_y)
         add_to(self.column, self.sum_x)
-        for copy in self.first + self.second + self.core:
+        for copy in self.first + self.second:
             copy.wait_send()
 
 
-def gather_scratch(m, r, c, core):
+def gather_scratch(m, r, c):
     whole = pltpu.VMEM((m, r, c), BF16)
     half = pltpu.VMEM((m // 2, r, c), BF16)
-    kept = [whole] * 3 + [half] * 2 + [whole] * 2
-    if core:
-        kept += [whole] + [pltpu.VMEM((m, 2, r, c), BF16)] * 2
-    return kept
+    return [whole] * 3 + [half] * 2 + [whole] * 2
 
 
 class Collect:
@@ -524,21 +496,21 @@
 
 
 def self_backward_kernel(
-    b_ref, q_ref, k_ref, v_ref, kt_ref, do_ref, lse_ref, dl_ref, up_ref, down_ref, g0, g1, g2, g3,
+    b_ref, q_ref, k_ref, v_ref, kt_ref, do_ref, lse_ref, dl_ref, up_ref, down_ref, cross_ref,
     dqt_ref, dk_ref, dv_ref, up_out, down_out, cross_out, dka, dva, dqa, *scratch, bk, heads, safe
 ):
     i = pl.program_id(0)
-    links = Links(*scratch[14:])
-    columns = scratch[10:12]
-    collects = [Collect(links, column, slots) for column, slots in zip(columns, scratch[12:14])]
+    links = Links(*scratch[11:])
+    columns = scratch[7:9]
+    collects = [Collect(links, column, slots) for column, slots in zip(columns, scratch[9:11])]
     loads = [links.local(ref, column) for ref, column in zip((up_ref, down_ref), columns)]
-    cross = Gather(links, g0, g2, scratch[:10], (g1, g3))
+    cross = Gather(links, cross_ref.at[0], cross_ref.at[1], scratch[:7])
     leave = links.local(cross.column, cross_out)
     stages = len(collects[0].stages)
 
     @pl.when(i == 0)
     def _():
-        links.greet([CORE, X, Y] + [("dp", 2 * d) for d in z_distances(2 * columns[0].shape[0])])
+        links.greet([X, Y] + z_ways(2 * columns[0].shape[0]))
         cross.start()
         for copy in loads:
             copy.start()
@@ -546,10 +518,6 @@
             copy.wait()
         for c in collects:
             c.start(0)
-
-    @pl.when(i == 2)
-    def _():
-        cross.after_core()
 
     @pl.when(i == 3)
     def _():
@@ -617,11 +585,11 @@
 
 
 def self_backward(
-    bounds, queries, keys, values, keys_t, grads, lse, inner, up_column, down_column, cross_pieces, heads, safe
+    bounds, queries, keys, values, keys_t, grads, lse, inner, up_column, down_column, cross_sum, heads, safe
 ):
     n, width = queries.shape
     m, r, c = up_column.shape
-    cross_c = cross_pieces[0].shape[3]
+    cross_c = cross_sum.shape[4]
     done = pl.BlockSpec((r, c), lambda i: (0, 0))
     bq = bk = 512
     whole = pl.BlockSpec((n, width), lambda i: (0, 0))
@@ -640,7 +608,7 @@
             per_row,
             per_row,
         ]
-        + [ANY] * 6,
+        + [ANY] * 3,
         out_specs=[pl.BlockSpec((width, bq), lambda i: (0, i)), whole, whole, done, done, ANY],
         out_shape=[
             jax.ShapeDtypeStruct((width, n), BF16),
@@ -655,10 +623,10 @@
             pltpu.VMEM((n, width), F32),
             pltpu.VMEM((width, bq), F32),
         ]
-        + gather_scratch(m, r, cross_c, True)
+        + gather_scratch(m, r, cross_c)
         + [pltpu.VMEM((m, r, c), BF16)] * 2
         + [pltpu.VMEM((m, r, c), BF16)] * 2
-        + link_scratch(6 + 2 * m, 7),
+        + link_scratch(4 + 2 * m, 6),
         compiler_params=pltpu.CompilerParams(
             vmem_limit_bytes=VMEM_LIMIT, collective_id=5, has_side_effects=True
         ),
@@ -666,11 +634,37 @@
             flops=24 * n * n * width, bytes_accessed=16 * n * width, transcendentals=n * n * heads // 2
         ),
         name="self_backward",
-    )(bounds, queries, keys, values, keys_t, grads, lse, inner, up_column, down_column, *cross_pieces)
+    )(bounds, queries, keys, values, keys_t, grads, lse, inner, up_column, down_column, cross_sum)
+
+
+def const(shape):
+    return pl.BlockSpec(shape, lambda *_: (0,) * len(shape), pipeline_mode=pl.Buffered(1))
+
+
+def normalized(rows):
+    center = rows - jnp.mean(rows, axis=-1, keepdims=True)
+    scale = lax.rsqrt(jnp.mean(center * center, axis=-1, keepdims=True) + EPSILON)
+    return center * scale, scale
+
+
+def norm_rows_back(rows, incoming, gain):
+    xhat, scale = normalized(rows)
+    e = incoming * gain
+    inner = jnp.mean(e * xhat, axis=-1, keepdims=True)
+    return scale * (e - jnp.mean(e, axis=-1, keepdims=True) - xhat * inner), incoming * xhat
+
+
+def by_rows(count, step, body):
+    def one(k, c):
+        body(pl.ds(pl.multiple_of(k * step, step), step))
+        return c
+
+    lax.fori_loop(0, count // step, one, 0)
 
 
 def cross_forward_kernel(
-    ok_ref, q_ref, k_ref, vt_ref, column_ref, ot_ref, lse_ref, whole, send_sems, recv_sems, local_sems, *, heads
+    ok_ref, x_ref, enc_ref, w_ref, bq_ref, bv_ref, rows_ref, shift_ref, norm_ref, column_ref,
+    q_out, k_out, v_out, ot_ref, lse_ref, after_ref, third_ref, whole, send_sems, recv_sems, local_sems, *, heads
 ):
     i = pl.program_id(0)
     last = pl.num_programs(0) - 1
@@ -681,70 +675,107 @@
     def _():
         links.greet([CORE, X, Y])
         spread.start()
-
-    rows, width = q_ref.shape[1:]
+        after_ref[...] = rows_ref[...] + shift_ref[...]
+
+    width = q_out.shape[2]
     hd = width // heads
-    scaled = q_ref[0] * jnp.asarray(1.0 / math.sqrt(hd), BF16)
-    keys = k_ref[0]
+    query = (dot_nn(x_ref[...], w_ref[0, :, :width]) + bq_ref[0]).astype(BF16)
+    key_value = dot_nn(enc_ref[...], w_ref[0, :, width : 3 * width])
+    keys = key_value[:, :width].astype(BF16)
+    values = (key_value[:, width:] + bv_ref[0]).astype(BF16)
+    q_out[0] = query
+    k_out[0] = keys
+    v_out[0] = values
+    values_t = values.T
+    scaled = query * jnp.asarray(1.0 / math.sqrt(hd), BF16)
     ok = ok_ref[...] > 0.0
     scores = [dot_nt(keys, head_only(scaled, h, hd)) for h in range(heads)]
+    mixed = []
     for h in range(heads):
         part = slice(h * hd, (h + 1) * hd)
         s = jnp.where(ok, scores[h], NEGATIVE)
         largest = jnp.max(s, axis=0, keepdims=True)
         expos = jnp.exp(s - largest)
         total = jnp.sum(expos, axis=0, keepdims=True)
-        mixed = dot_nn(vt_ref[0, part, :], expos.astype(BF16))
-        ot_ref[0, part, :] = (mixed * (1.0 / total)).astype(BF16)
+        mixed.append((dot_nn(values_t[part, :], expos.astype(BF16)) * (1.0 / total)).astype(BF16))
+        ot_ref[0, part, :] = mixed[h]
         lse_ref[0, h : h + 1, :] = largest + jnp.log(total)
+    after_ref[...] += dot_nt(jnp.concatenate(mixed, 0).T, w_ref[0, :, 3 * width :])
 
     @pl.when(i == last)
     def _():
         spread.middle()
+
+        def norm(rows):
+            xhat, _ = normalized(after_ref[rows, :])
+            third_ref[rows, :] = (xhat * norm_ref[0:1, :] + norm_ref[1:2, :]).astype(BF16)
+
+        by_rows(after_ref.shape[0], 128, norm)
         spread.end()
 
 
-def cross_forward(ok, queries, keys, values_t, column, heads):
-    parts, rows, width = queries.shape
+def cross_forward(ok, x, encoder, weights, q_shift, v_shift, rows, shift, norm, column, heads):
+    count, model = x.shape
+    n = encoder.shape[0]
+    parts, _, columns = weights.shape
+    width = columns // 4
     m, r, c = column.shape
-    n = keys.shape[1]
+
+    def by_part(*shape):
+        return pl.BlockSpec((1,) + shape, lambda i: (i,) + (0,) * len(shape))
+
     return pl.pallas_call(
         functools.partial(cross_forward_kernel, heads=heads),
         grid=(parts,),
         in_specs=[
-            pl.BlockSpec((n, 1), lambda i: (0, 0)),
-            pl.BlockSpec((1, rows, width), lambda i: (i, 0, 0)),
-            pl.BlockSpec((1, n, width), lambda i: (i, 0, 0)),
-            pl.BlockSpec((1, width, n), lambda i: (i, 0, 0)),
+            const((n, 1)),
+            const((count, model)),
+            const((n, model)),
+            by_part(model, columns),
+            by_part(1, width),
+            by_part(1, width),
+            const((count, model)),
+            const((1, model)),
+            const((2, model)),
             ANY,
         ],
         out_specs=[
-            pl.BlockSpec((1, width, rows), lambda i: (i, 0, 0)),
-            pl.BlockSpec((1, heads, rows), lambda i: (i, 0, 0)),
-        ]
-        + [ANY],
+            by_part(count, width),
+            by_part(n, width),
+            by_part(n, width),
+            by_part(width, count),
+            by_part(heads, count),
+            const((count, model)),
+            const((count, model)),
+            ANY,
+        ],
         out_shape=[
-            jax.ShapeDtypeStruct((parts, width, rows), BF16),
-            jax.ShapeDtypeStruct((parts, heads, rows), F32),
-        ]
-        + [jax.ShapeDtypeStruct((4, m, 2, r, c), BF16)],
+            jax.ShapeDtypeStruct((parts, count, width), BF16),
+            jax.ShapeDtypeStruct((parts, n, width), BF16),
+            jax.ShapeDtypeStruct((parts, n, width), BF16),
+            jax.ShapeDtypeStruct((parts, width, count), BF16),
+            jax.ShapeDtypeStruct((parts, heads, count), F32),
+            jax.ShapeDtypeStruct((count, model), F32),
+            jax.ShapeDtypeStruct((count, model), BF16),
+            jax.ShapeDtypeStruct((4, m, 2, r, c), BF16),
+        ],
         scratch_shapes=link_scratch(8, 1),
         compiler_params=pltpu.CompilerParams(
             vmem_limit_bytes=VMEM_LIMIT, collective_id=2, has_side_effects=True
         ),
         cost_estimate=pl.CostEstimate(
-            flops=24 * parts * rows * n * width,
+            flops=24 * parts * count * n * width,
             bytes_accessed=8 * parts * n * width,
-            transcendentals=parts * rows * n * heads,
+            transcendentals=parts * count * n * heads,
         ),
         name="cross_forward",
-    )(ok, queries, keys, values_t, column)
+    )(ok, x, encoder, weights, q_shift, v_shift, rows, shift, norm, column)
 
 
 def feed_forward_kernel(
-    x_ref, xt_ref, dy_ref, dyt_ref, up_ref, down_ref, b_ref,
-    out_ref, back_ref, gup_ref, gdown_ref, bias_ref,
-    give, got, send_sems, recv_sems, local_sems, *, chunks
+    x_ref, dy_ref, up_ref, down_ref, b_ref, after_ref, shift_ref, norm_ref,
+    out_ref, rows_out, low_out, sums_ref, gup_ref, gdown_ref, bias_ref,
+    xt_ref, dyt_ref, back_ref, give, got, send_sems, recv_sems, local_sems, *, chunks
 ):
     s = pl.program_id(0)
     links = Links(send_sems, recv_sems, local_sems)
@@ -765,8 +796,11 @@
     @pl.when(s == 0)
     def _():
         links.greet([CORE])
-        out_ref[...] = jnp.zeros_like(out_ref)
+        out_ref[...] = after_ref[...] + shift_ref[...]
         back_ref[...] = jnp.zeros_like(back_ref)
+        xt_ref[...] = x_ref[...].T
+        dyt_ref[...] = dy_ref[...].T
+        sums_ref[...] = jnp.zeros_like(sums_ref)
 
     pre_act = dot_nn(x_ref[...], up_ref[0]) + b_ref[0]
     hidden_grad = dot_nn(dy_ref[...], down_ref[0])
@@ -795,8 +829,23 @@
         gup_ref[0] = (give[chunk, 0].astype(F32) + got[slot, 0].astype(F32)).astype(BF16)
         gdown_ref[0] = (give[chunk, 1].astype(F32) + got[slot, 1].astype(F32)).astype(BF16)
 
-
-def feed_forward(x, dy, weights, bias):
+    @pl.when(s == pl.num_programs(0) - 1)
+    def _():
+        def norm_back(rows):
+            third = back_ref[rows, :]
+            upstream = dy_ref[rows, :].astype(F32)
+            rows_grad, gain_terms = norm_rows_back(after_ref[rows, :], third, norm_ref[0:1, :])
+            rows_grad = rows_grad + upstream
+            low = rows_grad.astype(BF16)
+            rows_out[rows, :] = rows_grad
+            low_out[rows, :] = low
+            for k, terms in enumerate((gain_terms, third, low.astype(F32), upstream)):
+                sums_ref[k : k + 1, :] += jnp.sum(terms, axis=0, keepdims=True)
+
+        by_rows(x_ref.shape[0], 128, norm_back)
+
+
+def feed_forward(x, dy, weights, bias, after, shift, norm):
     rows, width = x.shape
     hidden = weights.shape[2] // 2
     size = min(512, hidden)
@@ -809,8 +858,7 @@
         turn = s // chunks
         return (turn // 2, 0, (s % chunks) * (turn % 2))
 
-    rows_spec = pl.BlockSpec((rows, width), lambda s: (0, 0))
-    columns_spec = pl.BlockSpec((width, rows), lambda s: (0, 0))
+    rows_spec = const((rows, width))
     grad_spec = pl.BlockSpec((1, width, size), placed)
     bias_spec = pl.BlockSpec((1, 1, size), lambda s: (block(s), 0, s % chunks))
     return pl.pallas_call(
@@ -818,22 +866,28 @@
         grid=(4 * chunks,),
         in_specs=[
             rows_spec,
-            columns_spec,
             rows_spec,
-            columns_spec,
             pl.BlockSpec((1, width, size), lambda s: (block(s), 0, s % chunks)),
             pl.BlockSpec((1, width, size), lambda s: (block(s), 0, chunks + s % chunks)),
             bias_spec,
+            rows_spec,
+            const((1, width)),
+            const((2, width)),
         ],
-        out_specs=[rows_spec, rows_spec, grad_spec, grad_spec, bias_spec],
+        out_specs=[rows_spec, rows_spec, rows_spec, const((8, width)), grad_spec, grad_spec, bias_spec],
         out_shape=[
             jax.ShapeDtypeStruct((rows, width), F32),
             jax.ShapeDtypeStruct((rows, width), F32),
+            jax.ShapeDtypeStruct((rows, width), BF16),
+            jax.ShapeDtypeStruct((8, width), F32),
             jax.ShapeDtypeStruct((2, width, hidden), BF16),
             jax.ShapeDtypeStruct((2, width, hidden), BF16),
             jax.ShapeDtypeStruct((4, 1, hidden), F32),
         ],
         scratch_shapes=[
+            pltpu.VMEM((width, rows), BF16),
+            pltpu.VMEM((width, rows), BF16),
+            pltpu.VMEM((rows, width), F32),
             pltpu.VMEM((chunks, 2, width, size), BF16),
             pltpu.VMEM((2 * chunks, 2, width, size), BF16),
         ]
@@ -845,25 +899,41 @@
             flops=48 * rows * width * hidden, bytes_accessed=40 * 2**20, transcendentals=8 * rows * hidden
         ),
         name="feed_forward",
-    )(x, x.T, dy, dy.T, weights, weights, bias)
+    )(x, dy, weights, weights, bias, after, shift, norm)
 
 
 def cross_backward_kernel(
-    ok_ref, q_ref, k_ref, v_ref, kt_ref, do_ref, lse_ref, dl_ref, up_ref, down_ref,
-    dqt_ref, dk_ref, dv_ref, up_out, down_out, *scratch, heads, bk
+    ok_ref, low_ref, x_ref, enc_ref, w_ref, q_ref, k_ref, v_ref, mt_ref, lse_ref, up_ref, down_ref,
+    back_ref, enc_out, grad_ref, bq_ref, bv_ref, up_out, down_out,
+    low_t, x_t, enc_t, enc_acc, give, got, *scratch, heads, bk
 ):
     i = pl.program_id(0)
+    last = pl.num_programs(0) - 1
     links = Links(*scratch[14:])
     sums = [
         Gather(links, ref.at[0], ref.at[1], scratch[7 * k : 7 * k + 7]) for k, ref in enumerate((up_ref, down_ref))
     ]
     leave = [links.local(g.column, out) for g, out in zip(sums, (up_out, down_out))]
+    pair = i // 2
+    to_core = pltpu.make_async_remote_copy(
+        src_ref=give,
+        dst_ref=got.at[pair],
+        send_sem=links.send_sems.at[links.used + pair],
+        recv_sem=links.recv_sems.at[links.used + pair],
+        device_id=links.partner(CORE),
+        device_id_type=pl.DeviceIdType.MESH,
+    )
 
     @pl.when(i == 0)
     def _():
-        links.greet([X, Y])
+        links.greet([CORE, X, Y])
         for g in sums:
             g.start()
+        low_t[...] = low_ref[...].T
+        x_t[...] = x_ref[...].T
+        enc_t[...] = enc_ref[...].T
+        back_ref[...] = jnp.zeros_like(back_ref)
+        enc_acc[...] = jnp.zeros_like(enc_acc)
 
     @pl.when(i == 2)
     def _():
@@ -874,13 +944,18 @@
     n = k_ref.shape[1]
     hd = width // heads
     scale = 1.0 / math.sqrt(hd)
+    w_query, w_keyval, w_out = w_ref.at[0, :, :width], w_ref.at[0, :, width : 3 * width], w_ref.at[0, :, 3 * width :]
+    grads = dot_nn(low_ref[...], w_out[...]).astype(BF16)
+    mixed_t = mt_ref[0]
+    products = grads.T.astype(F32) * mixed_t.astype(F32)
+    inner = [jnp.sum(products[h * hd : (h + 1) * hd, :], axis=0, keepdims=True) for h in range(heads)]
     scaled = q_ref[0] * jnp.asarray(scale, BF16)
-    grads = do_ref[0]
     q_heads = [head_only(scaled, h, hd) for h in range(heads)]
     d_heads = [head_only(grads, h, hd) for h in range(heads)]
     lse = lse_ref[0]
-    inner = dl_ref[0]
+    keys_t = k_ref[0].T
     dq = [None] * heads
+    dkv = []
     for j in range(n // bk):
         span = slice(j * bk, (j + 1) * bk)
         keys = k_ref[0, span, :]
@@ -892,20 +967,42 @@
         for h in range(heads):
             part = slice(h * hd, (h + 1) * hd)
             probs = jnp.exp(jnp.where(ok, scores[h], NEGATIVE) - lse[h : h + 1, :])
-            ds = (probs * (dprobs[h] - inner[h : h + 1, :])).astype(BF16)
+            ds = (probs * (dprobs[h] - inner[h])).astype(BF16)
             dv_h = dot_nn(probs.astype(BF16), d_heads[h])
             dk_h = dot_nn(ds, q_heads[h])
             dv_sum = dv_h if dv_sum is None else dv_sum + dv_h
             dk_sum = dk_h if dk_sum is None else dk_sum + dk_h
-            dq_h = dot_nn(kt_ref[0, part, span], ds)
+            dq_h = dot_nn(keys_t[part, span], ds)
             dq[h] = dq_h if dq[h] is None else dq[h] + dq_h
-        dv_ref[0, span, :] = dv_sum.astype(BF16)
-        dk_ref[0, span, :] = dk_sum.astype(BF16)
-    for h in range(heads):
-        dqt_ref[0, h * hd : (h + 1) * hd, :] = (dq[h] * scale).astype(BF16)
-
-    @pl.when(i == pl.num_programs(0) - 1)
-    def _():
+        block = jnp.concatenate([dk_sum.astype(BF16), dv_sum.astype(BF16)], 1)
+        enc_acc[span, :] += dot_nt(block, w_keyval[...])
+        dkv.append(block)
+    dq = (jnp.concatenate(dq, 0) * scale).astype(BF16).T
+    dkv = jnp.concatenate(dkv, 0)
+    bq_ref[0] = jnp.sum(dq.astype(F32), axis=0, keepdims=True)
+    bv_ref[0] = jnp.sum(dkv[:, width:].astype(F32), axis=0, keepdims=True)
+    back_ref[...] += dot_nt(dq, w_query[...])
+
+    @pl.when(i % 2 == 1)
+    def _():
+        to_core.wait_send()
+
+    give[:, :width] = dot_nn(x_t[...], dq).astype(BF16)
+    give[:, width : 3 * width] = dot_nn(enc_t[...], dkv).astype(BF16)
+    give[:, 3 * width :] = dot_nn(low_t[...], mixed_t.T).astype(BF16)
+
+    @pl.when(i % 2 == 0)
+    def _():
+        to_core.start()
+
+    @pl.when(i % 2 == 1)
+    def _():
+        to_core.wait_recv()
+        grad_ref[0] = (give[...].astype(F32) + got[pair].astype(F32)).astype(BF16)
+
+    @pl.when(i == last)
+    def _():
+        enc_out[...] = enc_acc[...].astype(BF16)
         for g, copy in zip(sums, leave):
             g.end()
             copy.start()
@@ -913,47 +1010,71 @@
             copy.wait()
 
 
-def cross_backward(ok, queries, keys, values, keys_t, grads, lse, inner, up_sum, down_sum, heads):
-    parts, rows, width = queries.shape
+def cross_backward(ok, low, x, encoder, weights, queries, keys, values, mixed_t, lse, up_sum, down_sum, heads):
+    count, model = x.shape
+    n = encoder.shape[0]
+    parts, _, columns = weights.shape
+    width = columns // 4
     _, m, _, r, c = up_sum.shape
-    n = keys.shape[1]
-    by_row = pl.BlockSpec((1, rows, width), lambda i: (i, 0, 0))
-    by_key = pl.BlockSpec((1, n, width), lambda i: (i, 0, 0))
-    stat = pl.BlockSpec((1, heads, rows), lambda i: (i, 0, 0))
+
+    def by_part(*shape):
+        return pl.BlockSpec((1,) + shape, lambda i: (i ^ 1,) + (0,) * len(shape))
+
     return pl.pallas_call(
-        functools.partial(cross_backward_kernel, heads=heads, bk=512),
+        functools.partial(cross_backward_kernel, heads=heads, bk=256),
         grid=(parts,),
         in_specs=[
-            pl.BlockSpec((n, 1), lambda i: (0, 0)),
-            by_row,
-            by_key,
-            by_key,
-            pl.BlockSpec((1, width, n), lambda i: (i, 0, 0)),
-            by_row,
-            stat,
-            stat,
+            const((n, 1)),
+            const((count, model)),
+            const((count, model)),
+            const((n, model)),
+            by_part(model, columns),
+            by_part(count, width),
+            by_part(n, width),
+            by_part(n, width),
+            by_part(width, count),
+            by_part(heads, count),
             ANY,
             ANY,
         ],
-        out_specs=[pl.BlockSpec((1, width, rows), lambda i: (i, 0, 0)), by_key, by_key, ANY, ANY],
+        out_specs=[
+            const((count, model)),
+            const((n, model)),
+            pl.BlockSpec((1, model, columns), lambda i: (i // 2, 0, 0), pipeline_mode=pl.Buffered(1)),
+            by_part(1, width),
+            by_part(1, width),
+            ANY,
+            ANY,
+        ],
         out_shape=[
-            jax.ShapeDtypeStruct((parts, width, rows), BF16),
-            jax.ShapeDtypeStruct((parts, n, width), BF16),
-            jax.ShapeDtypeStruct((parts, n, width), BF16),
+            jax.ShapeDtypeStruct((count, model), F32),
+            jax.ShapeDtypeStruct((n, model), BF16),
+            jax.ShapeDtypeStruct((2, model, columns), BF16),
+            jax.ShapeDtypeStruct((parts, 1, width), F32),
+            jax.ShapeDtypeStruct((parts, 1, width), F32),
             jax.ShapeDtypeStruct((m, r, c), BF16),
             jax.ShapeDtypeStruct((m, r, c), BF16),
         ],
-        scratch_shapes=gather_scratch(m, r, c, False) * 2 + link_scratch(8, 8),
+        scratch_shapes=[
+            pltpu.VMEM((model, count), BF16),
+            pltpu.VMEM((model, count), BF16),
+            pltpu.VMEM((model, n), BF16),
+            pltpu.VMEM((n, model), F32),
+            pltpu.VMEM((model, columns), BF16),
+            pltpu.VMEM((2, model, columns), BF16),
+        ]
+        + gather_scratch(m, r, c) * 2
+        + link_scratch(10, 8),
         compiler_params=pltpu.CompilerParams(
-            vmem_limit_bytes=VMEM_LIMIT, collective_id=4, has_side_effects=True
+            vmem_limit_bytes=60 * 2**20, collective_id=4, has_side_effects=True
         ),
         cost_estimate=pl.CostEstimate(
-            flops=48 * parts * rows * n * width,
+            flops=48 * parts * count * n * width,
             bytes_accessed=16 * parts * n * width,
-            transcendentals=parts * rows * n * heads,
+            transcendentals=parts * count * n * heads,
         ),
         name="cross_backward",
-    )(ok, queries, keys, values, keys_t, grads, lse, inner, up_sum, down_sum)
+    )(ok, low, x, encoder, weights, queries, keys, values, mixed_t, lse, up_sum, down_sum)
 
 
 def swap(value, axis, distance):
@@ -1091,9 +1212,6 @@
         self_safe,
     )
     cross_w = cross_w.reshape(4, model_width, 4 * width)
-    w_query = [cross_w[d, :, :width] for d in range(4)]
-    w_keyval = [cross_w[d, :, width : 3 * width] for d in range(4)]
-    w_out = [cross_w[d, :, 3 * width :] for d in range(4)]
     self_out_w = self_w[:, 3 * width :]
     after_self = (
         start_rows
@@ -1101,107 +1219,61 @@
         + biases[2]
     )
 
-    cross_keys, cross_values = [], []
-    for d in range(4):
-        projected = dot_nn(enc_all, w_keyval[d])
-        cross_keys.append(projected[:, :width].astype(BF16))
-        cross_values.append((projected[:, width:] + block_of(biases[4], width, d)).astype(BF16))
-    cross_keys = jnp.stack(cross_keys)
-    cross_values = jnp.stack(cross_values)
     ok = (jnp.arange(4 * enc_rows, dtype=jnp.int32) < enc_lengths[0]).astype(F32)[:, None]
-
     second_in = layer_norm(after_self, norm_params[1, 0], norm_params[1, 1]).astype(BF16)
-    cross_queries = jnp.stack(
-        [
-            (dot_nn(second_in, w_query[d]) + block_of(biases[3], width, d)).astype(BF16)
-            for d in range(4)
-        ]
+
+    def all_blocks(vector, size):
+        return jnp.stack([block_of(vector, size, d) for d in range(4)])[:, None]
+
+    cross_q, cross_k, cross_v, cross_mixed_t, cross_lse, after_cross, third_in, ffn_w = cross_forward(
+        ok,
+        second_in,
+        enc_all,
+        cross_w,
+        all_blocks(biases[3], width),
+        all_blocks(biases[4], width),
+        after_self,
+        biases[5:6],
+        norm_params[2],
+        ffn_column,
+        heads,
     )
-    cross_mixed_t, cross_lse, ffn_w = cross_forward(
-        ok, cross_queries, cross_keys, jnp.swapaxes(cross_values, 1, 2), ffn_column, heads
-    )
-    after_cross = after_self + biases[5]
-    for d in range(4):
-        after_cross = after_cross + lax.dot_general(
-            cross_mixed_t[d], w_out[d], (((0,), (1,)), ((), ())), preferred_element_type=F32
-        )
-
-    third_in = layer_norm(after_cross, norm_params[2, 0], norm_params[2, 1]).astype(BF16)
-    cot_rows = out_grad.astype(F32)
-    bias_down_grad = jnp.sum(cot_rows, axis=0)
-    ffn_out, third_grad, up_sum, down_sum, bias_up_parts = feed_forward(
+
+    output, cross_rows_grad, cross_low, ffn_sums, up_sum, down_sum, bias_up_parts = feed_forward(
         third_in,
         out_grad,
         ffn_w.reshape(4, model_width, 2 * hidden_width),
-        jnp.stack([block_of(up_bias, hidden_width, d) for d in range(4)])[:, None],
+        all_blocks(up_bias, hidden_width),
+        after_cross,
+        biases[6:7],
+        norm_params[2],
     )
-    output = after_cross + biases[6] + ffn_out
-    rows_three, gain_three, shift_three = norm_back(after_cross, third_grad, 2)
-    cross_rows_grad = cot_rows + rows_three
-
-    cross_low = cross_rows_grad.astype(BF16)
-    bias_co_grad = jnp.sum(cross_low.astype(F32), axis=0)
-    cross_mixed_grad = jnp.stack([dot_nn(cross_low, w_out[d]).astype(BF16) for d in range(4)])
-    cross_inner = jnp.sum(
-        cross_mixed_t.reshape(4, heads, width // heads, own_rows).astype(F32)
-        * jnp.swapaxes(cross_mixed_grad, 1, 2).reshape(4, heads, width // heads, own_rows).astype(F32),
-        axis=2,
-    )
+    gain_three, shift_three, bias_co_grad, bias_down_grad = (ffn_sums[k] for k in range(4))
+
     by_shard = (2, groups_count // 2, 2, w_rows, hidden_width)
-    cross_dq_t, part_dk, part_dv, up_column, down_column = cross_backward(
+    second_grad, enc_terms, cross_sum, bias_cq_parts, bias_cv_parts, up_column, down_column = cross_backward(
         ok,
-        cross_queries,
-        cross_keys,
-        cross_values,
-        jnp.swapaxes(cross_keys, 1, 2),
-        cross_mixed_grad,
+        cross_low,
+        second_in,
+        enc_all,
+        cross_w,
+        cross_q,
+        cross_k,
+        cross_v,
+        cross_mixed_t,
         cross_lse,
-        cross_inner,
         up_sum.reshape(by_shard),
         down_sum.reshape(by_shard),
         heads,
     )
-    second_grad = 0.0
-    for d in range(4):
-        second_grad = second_grad + lax.dot_general(
-            cross_dq_t[d], w_query[d], (((0,), (1,)), ((), ())), preferred_element_type=F32
-        )
     rows_two, gain_two, shift_two = norm_back(after_self, second_grad, 1)
     self_rows_grad = cross_rows_grad + rows_two
     self_low = self_rows_grad.astype(BF16)
     bias_so_grad = jnp.sum(self_low.astype(F32), axis=0)
     self_wide = widen(self_low)
-
-    part_kv = jnp.concatenate([part_dk, part_dv], axis=2).reshape(4, 4, enc_rows, 2 * width)
-
-    def for_member(d):
-        rows = lax.dynamic_index_in_dim(part_kv, member ^ d, 1, keepdims=False)
-        return jnp.stack([rows[j ^ d] for j in range(4)])
-
-    far_dkv = add_low(for_member(2), swap(for_member(3), "tensor", 1))
-    near_dkv = for_member(0).astype(F32) + swap(for_member(1), "tensor", 1).astype(F32)
-    dkv = (near_dkv + swap(far_dkv, "tensor", 2).astype(F32)).astype(BF16)
-    encoder_grad = 0.0
-    for d in range(4):
-        encoder_grad = encoder_grad + dot_nt(dkv[d], w_keyval[d])
-    cross_pieces = []
-    for d in range(4):
-        cross_pieces.append(
-            jnp.concatenate(
-                [
-                    lax.dot_general(
-                        second_in, cross_dq_t[d], (((0,), (1,)), ((), ())), preferred_element_type=F32
-                    ).astype(BF16),
-                    dot_tn(encoder_out, dkv[d]).astype(BF16),
-                    lax.dot_general(
-                        cross_low, cross_mixed_t[d], (((0,), (1,)), ((), ())), preferred_element_type=F32
-                    ).astype(BF16),
-                ],
-                axis=1,
-            )
-        )
-    bias_cq_grad = blocks_placed([jnp.sum(cross_dq_t[d].astype(F32), axis=1) for d in range(4)])
-    bias_cv_grad = blocks_placed([jnp.sum(dkv[d, :, width:].astype(F32), axis=0) for d in range(4)])
+    encoder_grad = narrow(enc_terms)
+    bias_cq_grad = blocks_placed([bias_cq_parts[d, 0] for d in range(4)])
+    bias_cv_grad = blocks_placed([bias_cv_parts[d, 0] for d in range(4)])
     bias_up_grad = blocks_placed([bias_up_parts[d, 0] for d in range(4)])
 
     self_mixed_grad = dot_nn(self_wide, self_out_w).astype(BF16)
@@ -1221,7 +1293,7 @@
         self_inner,
         up_column,
         down_column,
-        [piece.reshape(groups_count // 2, 2, w_rows, 4 * width) for piece in cross_pieces],
+        cross_sum.reshape(2, groups_count // 2, 2, w_rows, 4 * width),
         heads,
         self_safe,
     )

time: 802 us -> 710 us (0.89)
  matrix products: 110 us -> 33.3 us
  local copies, waits for them, and re-layouts: 114 us -> 61.3 us
  waiting for transfers between devices: 61.1 us -> 113 us
  other arithmetic: 84.2 us -> 56.2 us
  Pallas kernels: 397 us -> 413 us
    ppermute x27, waiting for transfers between devices: 61.1 us -> 113 us  [swap(): return lax.ppermute(value, axis, [(i, i ^ distance) for i in range(size)])]
    dot_general x16 -> x0, matrix products: 31.9 us -> none  [the longest x4 9.1 us: on_device(): lax.dot_general(second_in, cross_dq_t[d], (((0,), (1,)), ((), ())), prefe...]
    dot_general x14 -> x2, matrix products: 40.3 us -> 10.8 us  [dot_nn(): lax.dot_general(a, b, (((1,), (0,)), ((), ())), preferred_element_type=F32)]
    unnamed x204 -> x115, local copies, waits for them, and re-layouts: 35.1 us -> 18.7 us
    concatenate x4 -> x0, local copies, waits for them, and re-layouts: 10.4 us -> none  [on_device(): jnp.concatenate([lax.dot_general(second_in, cross_dq_t[d], (((0,), (1,)),...]
    dot_general x5 -> x1, matrix products: 14.6 us -> 4.69 us  [dot_nt(): lax.dot_general(a, b, (((1,), (1,)), ((), ())), preferred_element_type=F32)]
    pallas_call x1, Pallas kernels: 75.7 us -> 85.2 us  [cross_backward(): pl.pallas_call(functools.partial(cross_backward_kernel, heads=heads, bk=2...]
    another operation x10 -> x3, other arithmetic: 9.31 us -> 0.05 us  [all_blocks(): return jnp.stack([block_of(vector, size, d) for d in range(4)])[:, None]]
  transfers between devices with their start and end apart: 27 -> 27, of which waited for: 8 -> 14; matrix products, arithmetic and copies ran while one was open for 19% -> 9% of each run, Pallas kernels for 0% -> 0%
where the time goes in v4:
time: 710 us; the launch traced here: 701 us
  Pallas kernels  413 us (58%)
  waiting for transfers between devices  113 us (16%)
  local copies, waits for them, and re-layouts  61.3 us (9%)
  other arithmetic  56.2 us (8%)
  matrix products  33.3 us (5%)
  starting transfers between devices  21.3 us (3%)
    ppermute x27, waiting for transfers between devices, swap(): return lax.ppermute(value, axis, [(i, i ^ distance) for i in range(size)])  113 us
    pallas_call x1, Pallas kernels, cross_backward(): pl.pallas_call(functools.partial(cross_backward_kernel, heads=heads, bk=2...  85.2 us
    pallas_call x1, Pallas kernels, cross_forward(): pl.pallas_call(functools.partial(cross_forward_kernel, heads=heads), grid...  83.2 us
    pallas_call x1, Pallas kernels, start_gather(): pl.pallas_call(functools.partial(start_kernel, n=n), in_specs=[ANY] * 4,...  77.3 us
    pallas_call x1, Pallas kernels, self_backward(): pl.pallas_call(functools.partial(self_backward_kernel, bk=bk, heads=heads...  62 us
    pallas_call x1, Pallas kernels, self_forward(): pl.pallas_call(functools.partial(self_forward_kernel, bk=bk, heads=heads,...  53.6 us
    pallas_call x1, Pallas kernels, feed_forward(): pl.pallas_call(functools.partial(feed_forward_kernel, chunks=chunks), gri...  51.7 us
    ppermute x27, starting transfers between devices, swap(): return lax.ppermute(value, axis, [(i, i ^ distance) for i in range(size)])  21.3 us
  transfers between devices with their start and end apart: 27, of which 14 were waited for; matrix products, arithmetic and copies ran while one was open for 9% of the time, Pallas kernels for 0%

profile of v4, /device:TPU:0, one launch (start us, length us, event | category | flops | bytes accessed | tf_op | source)
XLA Modules:
  0.0 700.8 jit_solution(4257011884248218834)
XLA Ops:
  0.7 1.7 convert_reduce_fusion.1
  2.4 1.8 fusion.9
  6.1 1.6 fusion.7.rows_ref
  8.6 77.3 %start_gather.1 = (bf16[2560,1024]{1,0:T(8,128)(2,1)}, bf16[1024,1024]{1,0:T(8,128)(2,1)}, bf16[4,2,128,1024]{3,2,1,0:T(8,128)(2,1)}, bf16[4,128,1024]{2,1,0:T(8,128)(2,1)}) custom-call(bf16[640,1024]{1,0:T(8,128)(2,1)} %fusion.7.rows_ref, bf16[256,1024]{1,0:T(8,128)(2,1)} %enc_ref.1, bf16[128,1024]{1,0:T(8,128)(2,1)} %get-tuple-element.199.self_ref, ...), custom_call_target="tpu_custom_call" | custom-call | bytes 104857600 | tf_op jit(solution)/shard_map/start_gather/pallas_call | solution.py:360
  85.9 6.6 fusion.16
  92.5 3.1 copy-done.15
  96.8 4.0 fusion.12
  102.0 1.6 copy.53.vt_ref
  103.5 1.7 copy.72
  105.2 1.5 copy.52.k_ref
  107.7 53.6 %self_forward.1 = (bf16[256,2560]{1,0:T(8,128)(2,1)}, f32[4,2560]{1,0:T(4,128)}, bf16[4,4,2,128,1024]{4,3,2,1,0:T(8,128)(2,1)}, bf16[4,128,2048]{2,1,0:T(8,128)(2,1)}) custom-call(s32[1,2]{1,0:T(1,128)} %b_ref.3, bf16[2560,256]{1,0:T(8,128)(2,1)} %get-tuple-element.126.q_ref, bf16[2560,256]{1,0:T(8,128)(2,1)} %copy.52.k_ref, bf16[256,2560]{1,0:T(8,128)(2,1)} %copy.53.vt_ref, ...), custom_call_target="tpu_custom_call" | custom-call | flops 20132659200 | bytes 5242880 | tf_op jit(solution)/shard_map/self_forward/pallas_call | solution.py:460
  161.3 5.4 convolution_convert_fusion
  166.7 3.4 constant_dynamic-slice_fusion.17
  170.6 4.7 collective-permute-done.1
  175.3 3.3 add_convert_fusion.2
  178.6 1.5 collective-permute-start.2
  184.2 25.6 %collective-permute-done.2 = bf16[640,1024]{1,0:T(8,128)(2,1)} collective-permute-done((bf16[640,1024]{1,0:T(8,128)(2,1)}, bf16[640,1024]{1,0:T(8,128)(2,1)}, u32[]{:S(2)}, u32[]{:S(2)}) %collective-permute-start.2) | collective-permute-done | bytes 1310752 | tf_op jit(solution)/shard_map/ppermute | solution.py:1082
  209.8 2.6 fusion.34
  212.7 1.5 add_convert_fusion.1.x_ref
  214.3 83.2 %cross_forward.1 = (bf16[4,640,256]{2,1,0:T(8,128)(2,1)}, bf16[4,1024,256]{2,1,0:T(8,128)(2,1)}, bf16[4,1024,256]{2,1,0:T(8,128)(2,1)}, bf16[4,256,640]{2,1,0:T(...) custom-call(f32[1024,1]{1,0:T(8,128)} %fusion.20.ok_ref, ...), custom_call_target="tpu_custom_call" | custom-call | flops 16106127360 | bytes 8388608 | tf_op jit(solution)/shard_map/cross_forward/pallas_call | solution.py:727
  297.5 51.7 %feed_forward.1 = (f32[640,1024]{1,0:T(8,128)}, f32[640,1024]{1,0:T(8,128)}, bf16[640,1024]{1,0:T(8,128)(2,1)}, f32[8,1024]{1,0:T(8,128)}, bf16[2,1024,1024]{2,1...) custom-call(bf16[640,1024]{1,0:T(8,128)(2,1)} %get-tuple-element.56.x_ref, ...), custom_call_target="tpu_custom_call" | custom-call | flops 32212254720 | bytes 41943040 | tf_op jit(solution)/shard_map/feed_forward/pallas_call | solution.py:864
  349.9 85.2 %cross_backward.1 = (f32[640,1024]{1,0:T(8,128)}, bf16[1024,1024]{1,0:T(8,128)(2,1)}, bf16[2,1024,1024]{2,1,0:T(8,128)(2,1)}, f32[4,1,256]{2,1,0:T(1,128)}, f32[...) custom-call(f32[1024,1]{1,0:T(8,128)} %fusion.20.ok_ref, ...), custom_call_target="tpu_custom_call" | custom-call | flops 32212254720 | bytes 16777216 | tf_op jit(solution)/shard_map/cross_backward/pallas_call | solution.py:1023
  436.5 2.8 multiply_reduce_fusion
  445.1 2.2 constant_dynamic-slice_fusion.5
  449.3 23.5 %collective-permute-done.18 = f32[104,128]{1,0:T(8,128)S(1)} collective-permute-done((f32[104,128]{1,0:T(8,128)S(1)}, f32[104,128]{1,0:T(8,128)S(1)}, u32[]{:S(2)}, u32[]{:S(2)}) %collective-permute-start.18) | collective-permute-done | bytes 53280 | tf_op jit(solution)/shard_map/ppermute | solution.py:1082
  474.0 3.9 collective-permute-done.19
  480.6 1.5 collective-permute-done.20
  482.1 1.8 collective-permute-start.21
  487.0 12.6 %collective-permute-done.11 = bf16[256,1024]{1,0:T(8,128)(2,1)S(1)} collective-permute-done((bf16[256,1024]{1,0:T(8,128)(2,1)S(1)}, bf16[256,1024]{1,0:T(8,128)(2,1)S(1)}, u32[]{:S(2)}, u32[]{:S(2)}) %collective-permute-start.11) | collective-permute-done | bytes 524320 | tf_op jit(solution)/shard_map/ppermute | solution.py:1082
  499.6 2.3 convert_add_fusion.5
  503.3 1.6 constant_dynamic-update-slice_fusion.1
  505.1 4.1 bitcast_multiply_fusion
  509.2 2.1 copy.57
  511.3 2.6 bitcast_reduce_fusion.dl_ref
  513.9 62.0 %self_backward.1 = (bf16[256,2560]{1,0:T(8,128)(2,1)}, bf16[2560,256]{1,0:T(8,128)(2,1)}, bf16[2560,256]{1,0:T(8,128)(2,1)}, f32[128,1024]{1,0:T(8,128)}, f32[12...) custom-call(s32[1,2]{1,0:T(1,128)} %b_ref.3, bf16[2560,256]{1,0:T(8,128)(2,1)} %get-tuple-element.126.q_ref, ...), custom_call_target="tpu_custom_call" | custom-call | flops 40265318400 | bytes 10485760 | tf_op jit(solution)/shard_map/self_backward/pallas_call | solution.py:598
  575.9 1.7 copy.59
  577.6 2.0 convert_reduce_fusion
  580.0 4.7 convolution_convert_fusion.1
  584.7 10.1 %convolution_convert_fusion.3 = bf16[1024,768]{0,1:T(8,128)(2,1)} fusion(bf16[2560,1024]{1,0:T(8,128)(2,1)} %get-tuple-element.49, bf16[2560,256]{1,0:T(8,128)(2,1)S(1)} %copy-done.22, bf16[2560,256]{1,0:T(8,128)(2,1)S(1)} %copy-done.21, bf16[2560,256]{1,0:T(8,128)(2,1)S(1)} %bitcast.122), kind=kOutput, calls=%fused_computation.41 | convolution fusion | flops 4039114752 | bytes 10747904 | tf_op jit(solution)/shard_map/dot_general | solution.py:28
  594.9 2.3 convolution_convert_fusion.4
  597.2 1.8 constant_dynamic-slice_fusion.7
  601.4 2.5 pad_maximum_fusion.1
  603.9 3.2 reshape.212
  607.2 5.6 constant_dynamic-slice_fusion.3
  613.9 1.5 collective-permute-start.22
  616.7 2.2 copy.71
  618.9 2.0 copy.67
  620.9 1.9 broadcast_multiply_fusion
  624.2 1.5 collective-permute-start.26
  625.7 13.6 %collective-permute-done.22 = bf16[2,2,128,1024]{2,3,0,1:T(8,128)(2,1)} collective-permute-done((bf16[2,2,128,1024]{2,3,0,1:T(8,128)(2,1)}, bf16[2,2,128,1024]{2,3,0,1:T(8,128)(2,1)}, u32[]{:S(2)}, u32[]{:S(2)}) %collective-permute-start.22) | collective-permute-done | bytes 1048608 | tf_op jit(solution)/shard_map/ppermute | solution.py:1082
  639.3 1.4 fusion.14
  640.8 1.8 collective-permute-start.23
  642.7 3.3 add_convert_fusion
  647.1 6.8 collective-permute-done.23
  655.6 1.9 collective-permute-start.24
  659.7 9.2 %collective-permute-done.24 = bf16[128,1024]{0,1:T(8,128)(2,1)} collective-permute-done((bf16[128,1024]{0,1:T(8,128)(2,1)}, bf16[128,1024]{0,1:T(8,128)(2,1)}, u32[]{:S(2)}, u32[]{:S(2)}) %collective-permute-start.24) | collective-permute-done | bytes 262176 | tf_op jit(solution)/shard_map/ppermute | solution.py:1082
  670.9 4.8 collective-permute-done.8
  675.7 3.1 fusion.8
  679.6 1.9 copy.64
  682.5 2.8 collective-permute-done.13
  686.3 3.5 fusion.32
  690.9 3.1 collective-permute-done.15
  694.9 2.0 add_add_fusion.2
  699.0 1.5 copy.108
  (238 shorter events, 49.1 us)
Async XLA Ops:
  0.6 5.5 copy-start.2
  0.7 4.2 copy-start.42
  0.7 4.2 copy-start.28
  0.7 4.6 copy-start.29
  0.7 4.6 copy-start.37
  0.7 4.7 copy-start.38
  0.7 4.8 copy-start.41
  2.4 5.3 copy-start.30
  2.4 5.3 copy-start.36
  4.9 81.0 %copy-start.32 = (f32[640]{0:T(1024)}, f32[640]{0:T(1024)S(1)}, u32[]{:S(2)}) copy-start(f32[640]{0:T(1024)S(1)} %fusion.27) | copy-start | bytes 7684
  4.9 81.0 %copy-start.34 = (f32[1,1,1024]{2,1,0:T(1,128)}, f32[1,1,1024]{2,1,0:T(1,128)S(1)}, u32[]{:S(2)}) copy-start(f32[1,1,1024]{2,1,0:T(1,128)S(1)} %get-tuple-element.161) | copy-start | bytes 12292
  92.5 3.1 copy-start.15
  103.5 3.2 copy-start.26
  103.5 3.3 copy-start.27
  105.2 56.1 %copy-start.16 = (bf16[2560,256]{0,1:T(8,128)(2,1)}, bf16[2560,256]{0,1:T(8,128)(2,1)S(1)}, u32[]{:S(2)}) copy-start(bf16[2560,256]{0,1:T(8,128)(2,1)S(1)} %copy.72) | copy-start | bytes 3932164
  170.1 11.9 %copy-start.43 = (f32[4096]{0:T(1024)S(1)}, f32[4096]{0:T(1024)}, u32[]{:S(2)}) copy-start(f32[4096]{0:T(1024)} %param.29) | copy-start | bytes 49156
  170.1 5.2 collective-permute-start.1
  170.1 14.0 %collective-permute-start = (bf16[640,1024]{1,0:T(8,128)(2,1)}, bf16[640,1024]{1,0:T(8,128)(2,1)S(1)}, u32[]{:S(2)}, u32[]{:S(2)}) collective-permute-start(bf16[640,1024]{1,0:T(8,128)(2,1)} %get-tuple-element.129), channel_id=1, source_target_pairs={{0,1},{1,0},{2,3},{3,2},{4,5},{5,4},{6,7},{7,6},{8,9},{9,8},{10,11... | collective-permute-start | bytes 3932168 | tf_op jit(solution)/shard_map/ppermute | solution.py:1082
  178.6 31.1 %collective-permute-start.2 = (bf16[640,1024]{1,0:T(8,128)(2,1)}, bf16[640,1024]{1,0:T(8,128)(2,1)}, u32[]{:S(2)}, u32[]{:S(2)}) collective-permute-start(bf16[640,1024]{1,0:T(8,128)(2,1)} %add_convert_fusion.2), channel_id=1, source_target_pairs={{0,2},{1,3},{2,0},{3,1},{4,6},{5,7},{6,4},{7,5},{8,10},{9,11},{10,... | collective-permute-start | bytes 3932168 | tf_op jit(solution)/shard_map/ppermute | solution.py:1082
  349.9 86.6 %copy-start.1 = (f32[640,1024]{1,0:T(8,128)S(1)}, f32[640,1024]{1,0:T(8,128)}, u32[]{:S(2)}) copy-start(f32[640,1024]{1,0:T(8,128)} %copy-done) | copy-start | bytes 7864324
  436.5 2.8 copy-start.44
  436.5 2.8 copy-start.7
  441.7 37.5 %copy-start.11 = (bf16[256,2560]{1,0:T(8,128)(2,1)S(1)}, bf16[256,2560]{1,0:T(8,128)(2,1)}, u32[]{:S(2)}) copy-start(bf16[256,2560]{1,0:T(8,128)(2,1)} %get-tuple-element.52) | copy-start | bytes 3932164
  441.7 42.3 %collective-permute-start.4 = (bf16[640,1024]{1,0:T(8,128)(2,1)S(1)}, bf16[640,1024]{1,0:T(8,128)(2,1)}, u32[]{:S(2)}, u32[]{:S(2)}) collective-permute-start(bf16[640,1024]{1,0:T(8,128)(2,1)S(1)} %get-tuple-element.118), channel_id=1, source_target_pairs={{0,2},{1,3},{2,0},{3,1},{4,6},{5,7},{6,4},{7,5},{8,10},{9,11},{10,... | collective-permute-start | bytes 3932168 | tf_op jit(solution)/shard_map/ppermute | solution.py:1082
  445.1 2.8 collective-permute-start.17
  447.4 36.6 %collective-permute-start.10 = (bf16[256,1024]{1,0:T(8,128)(2,1)}, bf16[256,1024]{1,0:T(8,128)(2,1)S(1)}, u32[]{:S(2)}, u32[]{:S(2)}) collective-permute-start(bf16[256,1024]{1,0:T(8,128)(2,1)} %get-tuple-element.134), channel_id=1, source_target_pairs={{0,1},{1,0},{2,3},{3,2},{4,5},{5,4},{6,7},{7,6},{8,9},{9,8},{10,11... | collective-permute-start | bytes 1572872 | tf_op jit(solution)/shard_map/ppermute | solution.py:1082
  447.9 24.9 %collective-permute-start.18 = (f32[104,128]{1,0:T(8,128)S(1)}, f32[104,128]{1,0:T(8,128)S(1)}, u32[]{:S(2)}, u32[]{:S(2)}) collective-permute-start(f32[104,128]{1,0:T(8,128)S(1)} %bitcast_add_fusion), channel_id=1, source_target_pairs={{0,2},{1,3},{2,0},{3,1},{4,6},{5,7},{6,4},{7,5},{8,10},{9,11},{10,... | collective-permute-start | bytes 159752 | tf_op jit(solution)/shard_map/ppermute | solution.py:1082
  449.3 52.6 %collective-permute-start.3 = (bf16[640,1024]{1,0:T(8,128)(2,1)S(1)}, bf16[640,1024]{1,0:T(8,128)(2,1)}, u32[]{:S(2)}, u32[]{:S(2)}) collective-permute-start(bf16[640,1024]{1,0:T(8,128)(2,1)S(1)} %get-tuple-element.118), channel_id=1, source_target_pairs={{0,1},{1,0},{2,3},{3,2},{4,5},{5,4},{6,7},{7,6},{8,9},{9,8},{10,11... | collective-permute-start | bytes 3932168 | tf_op jit(solution)/shard_map/ppermute | solution.py:1082
  472.8 5.1 collective-permute-start.19
  477.9 4.2 collective-permute-start.20
  480.6 6.4 collective-permute-start.9
  482.1 4.2 collective-permute-start.21
  483.9 20.9 %collective-permute-start.5 = (bf16[640,1024]{1,0:T(8,128)(2,1)}, bf16[640,1024]{1,0:T(8,128)(2,1)S(1)}, u32[]{:S(2)}, u32[]{:S(2)}) collective-permute-start(bf16[640,1024]{1,0:T(8,128)(2,1)} %collective-permute-done.4), channel_id=1, source_target_pairs={{0,1},{1,0},{2,3},{3,2},{4,5},{5,4},{6,7},{7,6},{8,9},{9,8},{10,11... | collective-permute-start | bytes 3932168 | tf_op jit(solution)/shard_map/ppermute | solution.py:1082
  485.2 14.4 %collective-permute-start.11 = (bf16[256,1024]{1,0:T(8,128)(2,1)S(1)}, bf16[256,1024]{1,0:T(8,128)(2,1)S(1)}, u32[]{:S(2)}, u32[]{:S(2)}) collective-permute-start(bf16[256,1024]{1,0:T(8,128)(2,1)S(1)} %add_convert_fusion.3), channel_id=1, source_target_pairs={{0,2},{1,3},{2,0},{3,1},{4,6},{5,7},{6,4},{7,5},{8,10},{9,11},{10,... | collective-permute-start | bytes 1572872 | tf_op jit(solution)/shard_map/ppermute | solution.py:1082
  505.1 4.1 copy-start.4
  577.6 2.4 copy-start.24
  577.6 17.2 %slice-start = ((s8[5242880]{0:T(1024)(128)(4,1)}), s8[4194304]{0:T(1024)(128)(4,1)S(1)}, s32[]{:S(2)}) async-start(s8[5242880]{0:T(1024)(128)(4,1)} %bitcast.117), calls=%async_computation | async-start | bytes 8388608
  580.0 14.9 %slice-start.1 = ((s8[5242880]{0:T(1024)(128)(4,1)}), s8[1048576]{0:T(1024)(128)(4,1)S(1)}, s32[]{:S(2)}) async-start(s8[5242880]{0:T(1024)(128)(4,1)} %bitcast.117), calls=%async_computation.1 | async-start | bytes 2097152
  584.7 12.5 %copy-start.13 = (bf16[2560,1024]{1,0:T(8,128)(2,1)}, bf16[2560,1024]{1,0:T(8,128)(2,1)S(1)}, u32[]{:S(2)}) copy-start(bf16[2560,1024]{1,0:T(8,128)(2,1)S(1)} %convolution_convert_fusion.1) | copy-start | bytes 15728644
  584.7 10.2 %copy-start.12 = (bf16[256,2560]{1,0:T(8,128)(2,1)S(1)}, bf16[256,2560]{1,0:T(8,128)(2,1)}, u32[]{:S(2)}) copy-start(bf16[256,2560]{1,0:T(8,128)(2,1)} %get-tuple-element.52) | copy-start | bytes 3932164
  599.0 2.4 copy-start.20
  599.0 43.7 %collective-permute-start.7 = (bf16[640,1024]{1,0:T(8,128)(2,1)}, bf16[640,1024]{1,0:T(8,128)(2,1)}, u32[]{:S(2)}, u32[]{:S(2)}) collective-permute-start(bf16[640,1024]{1,0:T(8,128)(2,1)} %get-tuple-element.128), channel_id=1, source_target_pairs={{0,1},{1,0},{2,3},{3,2},{4,5},{5,4},{6,7},{7,6},{8,9},{9,8},{10,11... | collective-permute-start | bytes 3932168 | tf_op jit(solution)/shard_map/ppermute | solution.py:1082
  599.0 71.9 %collective-permute-start.6 = (bf16[640,1024]{1,0:T(8,128)(2,1)}, bf16[640,1024]{1,0:T(8,128)(2,1)S(1)}, u32[]{:S(2)}, u32[]{:S(2)}) collective-permute-start(bf16[640,1024]{1,0:T(8,128)(2,1)} %get-tuple-element.127), channel_id=1, source_target_pairs={{0,1},{1,0},{2,3},{3,2},{4,5},{5,4},{6,7},{7,6},{8,9},{9,8},{10,11... | collective-permute-start | bytes 3932168 | tf_op jit(solution)/shard_map/ppermute | solution.py:1082
  601.4 21.5 %collective-permute-start.25 = (bf16[2,128,1024]{1,2,0:T(8,128)(2,1)}, bf16[2,128,1024]{1,2,0:T(8,128)(2,1)}, u32[]{:S(2)}, u32[]{:S(2)}) collective-permute-start(bf16[2,128,1024]{1,2,0:T(8,128)(2,1)} %bitcast.133), channel_id=1, source_target_pairs={{0,8},{4,12},{8,0},{12,4},{16,24},{20,28},{24,16},{28,20},{1,9},{5... | collective-permute-start | bytes 1572872 | tf_op jit(solution)/shard_map/ppermute | solution.py:1082
  612.8 2.7 copy-start.25
  613.9 25.4 %collective-permute-start.22 = (bf16[2,2,128,1024]{2,3,0,1:T(8,128)(2,1)}, bf16[2,2,128,1024]{2,3,0,1:T(8,128)(2,1)}, u32[]{:S(2)}, u32[]{:S(2)}) collective-permute-start(bf16[2,2,128,1024]{2,3,0,1:T(8,128)(2,1)} %bitcast.115), channel_id=1, source_target_pairs={{0,4},{4,0},{8,12},{12,8},{16,20},{20,16},{24,28},{28,24},{1,5},{5... | collective-permute-start | bytes 3145736 | tf_op jit(solution)/shard_map/ppermute | solution.py:1082
  616.7 22.6 %copy-start.10 = (bf16[2,2,1,128,1024]{3,2,1,0,4:T(2,128)(2,1)S(1)}, bf16[2,2,1,128,1024]{3,2,1,0,4:T(2,128)(2,1)}, u32[]{:S(2)}) copy-start(bf16[2,2,1,128,1024]{3,2,1,0,4:T(2,128)(2,1)} %get-tuple-element.131) | copy-start | bytes 3145732
  624.2 18.4 %collective-permute-start.26 = (bf16[128,1024]{0,1:T(8,128)(2,1)S(1)}, bf16[128,1024]{0,1:T(8,128)(2,1)S(1)}, u32[]{:S(2)}, u32[]{:S(2)}) collective-permute-start(bf16[128,1024]{0,1:T(8,128)(2,1)S(1)} %dynamic-slice_bitcast_fusion.1), channel_id=1, source_target_pairs={{0,16},{4,20},{8,24},{12,28},{16,0},{20,4},{24,8},{28,12},{1,17},{... | collective-permute-start | bytes 786440 | tf_op jit(solution)/shard_map/ppermute | solution.py:1082
  640.8 13.0 %collective-permute-start.23 = (bf16[2,128,1024]{1,2,0:T(8,128)(2,1)S(1)}, bf16[2,128,1024]{1,2,0:T(8,128)(2,1)S(1)}, u32[]{:S(2)}, u32[]{:S(2)}) collective-permute-start(bf16[2,128,1024]{1,2,0:T(8,128)(2,1)S(1)} %dynamic-slice_bitcast_fusion), channel_id=1, source_target_pairs={{0,8},{4,12},{8,0},{12,4},{16,24},{20,28},{24,16},{28,20},{1,9},{5... | collective-permute-start | bytes 1572872 | tf_op jit(solution)/shard_map/ppermute | solution.py:1082
  646.0 29.6 %copy-start.3 = (bf16[640,1024]{1,0:T(8,128)(2,1)S(1)}, bf16[640,1024]{1,0:T(8,128)(2,1)}, u32[]{:S(2)}) copy-start(bf16[640,1024]{1,0:T(8,128)(2,1)} %param.15) | copy-start | bytes 3932164
  646.0 29.6 %copy-start.31 = (f32[640]{0:T(1024)S(1)}, f32[640]{0:T(1024)}, u32[]{:S(2)}) copy-start(f32[640]{0:T(1024)} %copy-done.30) | copy-start | bytes 7684
  646.0 29.6 %copy-start.33 = (f32[640]{0:T(1024)S(1)}, f32[640]{0:T(1024)}, u32[]{:S(2)}) copy-start(f32[640]{0:T(1024)} %copy-done.32) | copy-start | bytes 7684
  646.0 29.6 %copy-start.35 = (f32[1,1,1024]{2,1,0:T(1,128)S(1)}, f32[1,1,1024]{2,1,0:T(1,128)}, u32[]{:S(2)}) copy-start(f32[1,1,1024]{2,1,0:T(1,128)} %copy-done.34) | copy-start | bytes 12292
  646.0 29.6 %collective-permute-start.8 = (bf16[640,1024]{1,0:T(8,128)(2,1)}, bf16[640,1024]{1,0:T(8,128)(2,1)}, u32[]{:S(2)}, u32[]{:S(2)}) collective-permute-start(bf16[640,1024]{1,0:T(8,128)(2,1)} %add_convert_fusion), channel_id=1, source_target_pairs={{0,2},{1,3},{2,0},{3,1},{4,6},{5,7},{6,4},{7,5},{8,10},{9,11},{10,... | collective-permute-start | bytes 3932168 | tf_op jit(solution)/shard_map/ppermute | solution.py:1082
  655.6 13.4 %collective-permute-start.24 = (bf16[128,1024]{0,1:T(8,128)(2,1)}, bf16[128,1024]{0,1:T(8,128)(2,1)}, u32[]{:S(2)}, u32[]{:S(2)}) collective-permute-start(bf16[128,1024]{0,1:T(8,128)(2,1)} %dynamic-slice_bitcast_fusion.2), channel_id=1, source_target_pairs={{0,16},{4,20},{8,24},{12,28},{16,0},{20,4},{24,8},{28,12},{1,17},{... | collective-permute-start | bytes 786440 | tf_op jit(solution)/shard_map/ppermute | solution.py:1082
  670.9 11.6 %copy-start.40 = (f32[640]{0:T(1024)S(1)}, f32[640]{0:T(1024)}, u32[]{:S(2)}) copy-start(f32[640]{0:T(1024)} %copy-done.39) | copy-start | bytes 7684
  678.8 2.7 collective-permute-start.12
  681.5 3.8 collective-permute-start.13
  685.3 9.6 %copy-start.6 = (f32[640,1024]{1,0:T(8,128)S(1)}, f32[640,1024]{1,0:T(8,128)}, u32[]{:S(2)}) copy-start(f32[640,1024]{1,0:T(8,128)} %copy-done.5) | copy-start | bytes 7864324
  685.3 9.6 %copy-start.9 = (f32[640,1024]{1,0:T(8,128)S(1)}, f32[640,1024]{1,0:T(8,128)}, u32[]{:S(2)}) copy-start(f32[640,1024]{1,0:T(8,128)} %get-tuple-element.60) | copy-start | bytes 7864324
  685.3 4.9 collective-permute-start.14
  690.2 3.7 collective-permute-start.15
  693.9 3.7 collective-permute-start.16
  694.9 4.2 copy-start.18
  (10 other events, 15.6 us)

commit v5 on v4

--- a/solution.py
+++ b/solution.py
@@ -297,6 +297,243 @@
                 copy.wait_send()
 
 
+class RowSum:
+    def __init__(self, links, terms, buffers):
+        self.near, self.far, self.got_near, self.got_far, self.got_x = buffers
+        count = self.near.shape[0]
+
+        def rows(distance):
+            start = pl.multiple_of((links.tensor ^ distance) * count, count)
+            return terms.at[pl.ds(start, count)]
+
+        self.loads = [links.local(rows(0), self.near), links.local(rows(2), self.far)]
+        self.core = [links.copy(rows(3), self.got_far, CORE), links.copy(rows(1), self.got_near, CORE)]
+        self.over_x = links.copy(self.far, self.got_x, X)
+
+    def start(self):
+        for copy in self.loads[::-1] + self.core:
+            copy.start()
+
+    def middle(self):
+        self.loads[1].wait()
+        self.core[0].wait_recv()
+
+        def add(rows):
+            self.far[rows, :] = (self.far[rows, :].astype(F32) + self.got_far[rows, :].astype(F32)).astype(BF16)
+
+        by_rows(self.far.shape[0], 64, add)
+        self.over_x.start()
+
+    def end(self):
+        self.loads[0].wait()
+        self.core[1].wait_recv()
+        self.over_x.wait_recv()
+        for copy in self.core + [self.over_x]:
+            copy.wait_send()
+
+    def total(self, rows):
+        return self.near[rows, :].astype(F32) + self.got_near[rows, :].astype(F32) + self.got_x[rows, :].astype(F32)
+
+
+def row_sum_scratch(count, width):
+    return [pltpu.VMEM((count, width), BF16)] * 5
+
+
+class Everywhere:
+    def __init__(self, links, held, slots, n):
+        self.held, self.slots = held, slots
+        ways = everywhere_ways(n)
+        self.copies = [links.copy(held.at[k], slots.at[k], way) for k, way in enumerate(ways)]
+
+    def start(self, step):
+        self.copies[step].start()
+
+    def finish(self, step):
+        self.copies[step].wait()
+        self.held[step + 1] = self.held[step] + self.slots[step]
+
+
+def everywhere_ways(n):
+    return [CORE, X, Y] + z_ways(n)
+
+
+def everywhere_scratch(k, c, n):
+    steps = len(everywhere_ways(n))
+    return [pltpu.VMEM((steps + 1, k, c), F32), pltpu.VMEM((steps, k, c), F32)]
+
+
+def middle_kernel(
+    back_ref, rows_ref, grad_ref, norm_ref, down_ref,
+    wide_out, grad_out, sums_ref, down_out,
+    low, column, slots, send_sems, recv_sems, local_sems, *, n
+):
+    links = Links(send_sems, recv_sems, local_sems)
+    count = low.shape[0]
+    load = links.local(down_ref, column)
+    load.start()
+    collect = Collect(links, column, slots)
+
+    def place(distance):
+        return wide_out.at[pl.ds(pl.multiple_of((links.tensor ^ distance) * count, count), count)]
+
+    own = links.local(low, place(0))
+    half = count // 2
+    parts = [pl.ds(0, half), pl.ds(half, half)]
+    over_x = [links.copy(low.at[part], place(0).at[part], X) for part in parts]
+    over_core = links.copy(low, place(0), CORE)
+    onward = [links.copy(place(2).at[part], place(2).at[part], CORE) for part in parts]
+    links.greet([CORE, X] + z_ways(n))
+    load.wait()
+    collect.start(0)
+    sums_ref[...] = jnp.zeros_like(sums_ref)
+
+    def norm_back(rows):
+        incoming = back_ref[rows, :]
+        rows_grad, gain_terms = norm_rows_back(rows_ref[rows, :], incoming, norm_ref[0:1, :])
+        rows_grad = rows_grad + grad_ref[rows, :]
+        rounded = rows_grad.astype(BF16)
+        grad_out[rows, :] = rows_grad
+        low[rows, :] = rounded
+        for k, terms in enumerate((gain_terms, incoming, rounded.astype(F32))):
+            sums_ref[k : k + 1, :] += jnp.sum(terms, axis=0, keepdims=True)
+
+    for part, copy in zip(parts, over_x):
+        by_rows(half, 64, lambda rows, part=part: norm_back(pl.ds(pl.multiple_of(part.start + rows.start, 64), 64)))
+        copy.start()
+    own.start()
+    over_core.start()
+    for step in range(len(collect.stages) - 1):
+        collect.finish(step)
+        collect.start(step + 1)
+    for copy, later in zip(over_x, onward):
+        copy.wait_recv()
+        later.start()
+    collect.finish(len(collect.stages) - 1)
+    down_out[...] = column[collect.z].astype(F32)
+    collect.drain()
+    own.wait()
+    for copy in over_x:
+        copy.wait_send()
+    over_core.wait()
+    for copy in onward:
+        copy.wait()
+
+
+def middle(back, rows, grad, norm, down_column):
+    n = lax.axis_size("dp")
+    count, width = rows.shape
+    m, r, c = down_column.shape
+    vmem = pl.BlockSpec(memory_space=pltpu.VMEM)
+    return pl.pallas_call(
+        functools.partial(middle_kernel, n=n),
+        in_specs=[vmem, vmem, vmem, vmem, ANY],
+        out_specs=[ANY, vmem, vmem, vmem],
+        out_shape=[
+            jax.ShapeDtypeStruct((4 * count, width), BF16),
+            jax.ShapeDtypeStruct((count, width), F32),
+            jax.ShapeDtypeStruct((8, width), F32),
+            jax.ShapeDtypeStruct((r, c), F32),
+        ],
+        scratch_shapes=[
+            pltpu.VMEM((count, width), BF16),
+            pltpu.VMEM((m, r, c), BF16),
+            pltpu.VMEM((m, r, c), BF16),
+        ]
+        + link_scratch(5 + m, 2),
+        compiler_params=pltpu.CompilerParams(
+            vmem_limit_bytes=VMEM_LIMIT, collective_id=6, has_side_effects=True
+        ),
+        cost_estimate=pl.CostEstimate(flops=0, bytes_accessed=100 * 2**20, transcendentals=0),
+        name="middle",
+    )(back, rows, grad, norm, down_column)
+
+
+def tail_kernel(
+    terms_ref, weights_ref, rows_ref, grad_ref, norm_ref, late_ref,
+    grad_out, weights_out, late_out, *scratch, n
+):
+    links = Links(*scratch[-3:])
+    rows_sum = RowSum(links, terms_ref, scratch[:5])
+    columns, gots, slots = scratch[5:7], scratch[7:9], scratch[9:11]
+    held, late_slots = scratch[11:13]
+    y = links.dp % 2
+    c = columns[0].shape[2]
+    loads, over_y, collects = [], [], []
+    for k, (column, got, slot) in enumerate(zip(columns, gots, slots)):
+        part = pl.ds(k * c, c)
+        loads.append(links.local(weights_ref.at[:, y, :, part], column))
+        over_y.append(links.copy(weights_ref.at[:, 1 - y, :, part], got, Y))
+        collects.append(Collect(links, column, slot))
+    late = Everywhere(links, held, late_slots, n)
+    links.greet(everywhere_ways(n))
+    rows_sum.start()
+    over_y[0].start()
+    for load in loads:
+        load.start()
+    rows_sum.middle()
+    for k in range(2):
+        loads[k].wait()
+        over_y[k].wait_recv()
+        if k == 0:
+            over_y[1].start()
+        add_to(columns[k], gots[k])
+        collects[k].start(0)
+    stages = len(collects[0].stages)
+    for step in range(stages):
+        for k in range(2):
+            collects[k].finish(step)
+            if step < stages - 1:
+                collects[k].start(step + 1)
+    for k in range(2):
+        weights_out[:, k * c : (k + 1) * c] = columns[k][collects[k].z].astype(F32)
+    rows_sum.end()
+    held[0] = late_ref[...]
+
+    def norm_back(rows):
+        incoming = rows_sum.total(rows)
+        rows_grad, gain_terms = norm_rows_back(rows_ref[rows, :].astype(F32), incoming, norm_ref[0:1, :])
+        grad_out[rows, :] = rows_grad + grad_ref[rows, :]
+        held[0, 0:1, :] += jnp.sum(gain_terms, axis=0, keepdims=True)
+        held[0, 1:2, :] += jnp.sum(incoming, axis=0, keepdims=True)
+
+    by_rows(grad_out.shape[0], 64, norm_back)
+    steps = len(late.copies)
+    for step in range(steps):
+        late.start(step)
+        late.finish(step)
+    late_out[...] = held[steps]
+    for k in range(2):
+        over_y[k].wait_send()
+        collects[k].drain()
+
+
+def tail(terms, weights, rows, grad, norm, late):
+    n = lax.axis_size("dp")
+    count, width = rows.shape
+    m, _, r, c = weights.shape
+    vmem = pl.BlockSpec(memory_space=pltpu.VMEM)
+    part = pltpu.VMEM((m, r, c // 2), BF16)
+    return pl.pallas_call(
+        functools.partial(tail_kernel, n=n),
+        in_specs=[ANY, ANY, vmem, vmem, vmem, vmem],
+        out_specs=[vmem, vmem, vmem],
+        out_shape=[
+            jax.ShapeDtypeStruct((count, width), F32),
+            jax.ShapeDtypeStruct((r, c), F32),
+            jax.ShapeDtypeStruct(late.shape, F32),
+        ],
+        scratch_shapes=row_sum_scratch(count, width)
+        + [part] * 6
+        + everywhere_scratch(*late.shape, n)
+        + link_scratch(5 + 2 * m + len(everywhere_ways(n)), 4),
+        compiler_params=pltpu.CompilerParams(
+            vmem_limit_bytes=VMEM_LIMIT, collective_id=7, has_side_effects=True
+        ),
+        cost_estimate=pl.CostEstimate(flops=0, bytes_accessed=100 * 2**20, transcendentals=0),
+        name="tail",
+    )(terms, weights, rows, grad, norm, late)
+
+
 def start_kernel(
     rows_ref, enc_ref, self_ref, cross_ref, rows_out, enc_out, self_out, cross_out, send_sems, recv_sems, local_sems, *, n
 ):
@@ -331,16 +568,20 @@
         go(links.copy(source, place(target, member, size), CORE))
     self_stages = column_stages(links, self_ref, self_out.at[:, y], n)
     cross_stages = column_stages(links, cross_ref, cross_out, n)
-    for self_stage, cross_stage in zip(self_stages, cross_stages):
+    for self_stage in self_stages:
         for copy, _ in self_stage:
-            go(copy)
-        for copy, _ in cross_stage:
             go(copy)
         for copy, index in self_stage:
             got(copy)
             go(links.copy(self_out.at[index, y], self_out.at[index, y], Y))
+        if self_stage is self_stages[0]:
+            for copy, _ in cross_stages[0]:
+                go(copy)
+    for cross_stage, later in zip(cross_stages, cross_stages[1:]):
         for copy, _ in cross_stage:
             got(copy)
+        for copy, _ in later:
+            go(copy)
     for copy, (_, target, size) in zip(along_x, groups):
         got(copy)
         there = place(target, member ^ 2, size)
@@ -496,37 +737,61 @@
 
 
 def self_backward_kernel(
-    b_ref, q_ref, k_ref, v_ref, kt_ref, do_ref, lse_ref, dl_ref, up_ref, down_ref, cross_ref,
-    dqt_ref, dk_ref, dv_ref, up_out, down_out, cross_out, dka, dva, dqa, *scratch, bk, heads, safe
+    b_ref, q_ref, k_ref, v_ref, kt_ref, do_ref, lse_ref, dl_ref, up_ref, cross_ref, enc_ref, early_ref,
+    dqt_ref, dk_ref, dv_ref, up_out, cross_out, enc_out, early_out, dka, dva, dqa, *scratch, bk, heads, safe, n
 ):
     i = pl.program_id(0)
-    links = Links(*scratch[11:])
-    columns = scratch[7:9]
-    collects = [Collect(links, column, slots) for column, slots in zip(columns, scratch[9:11])]
-    loads = [links.local(ref, column) for ref, column in zip((up_ref, down_ref), columns)]
+    last = pl.num_programs(0) - 1
+    links = Links(*scratch[-3:])
     cross = Gather(links, cross_ref.at[0], cross_ref.at[1], scratch[:7])
-    leave = links.local(cross.column, cross_out)
-    stages = len(collects[0].stages)
+    cross_z = Collect(links, cross.column, scratch[7])
+    up_column = scratch[8]
+    up_z = Collect(links, up_column, scratch[9])
+    load = links.local(up_ref, up_column)
+    enc = RowSum(links, enc_ref, scratch[10:15])
+    held = scratch[15]
+    early = Everywhere(links, held, scratch[16], n)
+    stages = len(up_z.stages)
+    steps = len(early.copies)
 
     @pl.when(i == 0)
     def _():
-        links.greet([X, Y] + z_ways(2 * columns[0].shape[0]))
+        links.greet(everywhere_ways(n))
         cross.start()
-        for copy in loads:
-            copy.start()
-        for copy in loads:
-            copy.wait()
-        for c in collects:
-            c.start(0)
+        enc.start()
+        load.start()
+        held[0] = early_ref[...]
+        early.start(0)
+        load.wait()
+        up_z.start(0)
+
+    @pl.when(i == 1)
+    def _():
+        enc.middle()
+        early.finish(0)
+        early.start(1)
+
+    @pl.when(i == 2)
+    def _():
+        cross.middle()
+        early.finish(1)
+        early.start(2)
 
     @pl.when(i == 3)
     def _():
-        cross.middle()
         for step in range(stages - 1):
-            for c in collects:
-                c.finish(step)
-            for c in collects:
-                c.start(step + 1)
+            up_z.finish(step)
+            up_z.start(step + 1)
+        early.finish(2)
+        early.start(3)
+
+    @pl.when(i == last)
+    def _():
+        cross.end()
+        cross_z.start(0)
+        for step in range(3, steps - 1):
+            early.finish(step)
+            early.start(step + 1)
 
     bq, width = q_ref.shape
     hd = width // heads
@@ -574,29 +839,39 @@
     def _():
         dk_ref[...] = dka[...].astype(BF16)
         dv_ref[...] = dva[...].astype(BF16)
-        cross.end()
-        leave.start()
-        for c, out in zip(collects, (up_out, down_out)):
-            c.finish(stages - 1)
-            out[...] = c.column[c.z].astype(F32)
-        for c in collects:
-            c.drain()
-        leave.wait()
+        up_z.finish(stages - 1)
+        up_out[...] = up_column[up_z.z].astype(F32)
+        for step in range(stages):
+            cross_z.finish(step)
+            if step < stages - 1:
+                cross_z.start(step + 1)
+        cross_out[...] = cross.column[cross_z.z].astype(F32)
+        enc.end()
+
+        def store(rows):
+            enc_out[rows, :] = enc.total(rows)
+
+        by_rows(enc_out.shape[0], 64, store)
+        early.finish(steps - 1)
+        early_out[...] = held[steps]
+        up_z.drain()
+        cross_z.drain()
 
 
 def self_backward(
-    bounds, queries, keys, values, keys_t, grads, lse, inner, up_column, down_column, cross_sum, heads, safe
+    bounds, queries, keys, values, keys_t, grads, lse, inner, up_column, cross_sum, enc_terms, early, heads, safe
 ):
     n, width = queries.shape
+    dp = lax.axis_size("dp")
     m, r, c = up_column.shape
     cross_c = cross_sum.shape[4]
-    done = pl.BlockSpec((r, c), lambda i: (0, 0))
+    enc_shape = (enc_terms.shape[0] // 4, enc_terms.shape[1])
     bq = bk = 512
     whole = pl.BlockSpec((n, width), lambda i: (0, 0))
     some = pl.BlockSpec((bq, width), lambda i: (i, 0))
     per_row = pl.BlockSpec((heads, bq), lambda i: (0, i))
     return pl.pallas_call(
-        functools.partial(self_backward_kernel, bk=bk, heads=heads, safe=safe),
+        functools.partial(self_backward_kernel, bk=bk, heads=heads, safe=safe, n=dp),
         grid=(n // bq,),
         in_specs=[
             pl.BlockSpec(memory_space=pltpu.SMEM),
@@ -608,15 +883,18 @@
             per_row,
             per_row,
         ]
-        + [ANY] * 3,
-        out_specs=[pl.BlockSpec((width, bq), lambda i: (0, i)), whole, whole, done, done, ANY],
+        + [ANY] * 3
+        + [const(early.shape)],
+        out_specs=[pl.BlockSpec((width, bq), lambda i: (0, i)), whole, whole]
+        + [const((r, c)), const((r, cross_c)), const(enc_shape), const(early.shape)],
         out_shape=[
             jax.ShapeDtypeStruct((width, n), BF16),
             jax.ShapeDtypeStruct((n, width), BF16),
             jax.ShapeDtypeStruct((n, width), BF16),
             jax.ShapeDtypeStruct((r, c), F32),
-            jax.ShapeDtypeStruct((r, c), F32),
-            jax.ShapeDtypeStruct((m, r, cross_c), BF16),
+            jax.ShapeDtypeStruct((r, cross_c), F32),
+            jax.ShapeDtypeStruct(enc_shape, F32),
+            jax.ShapeDtypeStruct(early.shape, F32),
         ],
         scratch_shapes=[
             pltpu.VMEM((n, width), F32),
@@ -624,9 +902,11 @@
             pltpu.VMEM((width, bq), F32),
         ]
         + gather_scratch(m, r, cross_c)
+        + [pltpu.VMEM((m, r, cross_c), BF16)]
         + [pltpu.VMEM((m, r, c), BF16)] * 2
-        + [pltpu.VMEM((m, r, c), BF16)] * 2
-        + link_scratch(4 + 2 * m, 6),
+        + row_sum_scratch(*enc_shape)
+        + everywhere_scratch(*early.shape, dp)
+        + link_scratch(7 + 2 * m + len(everywhere_ways(dp)), 6),
         compiler_params=pltpu.CompilerParams(
             vmem_limit_bytes=VMEM_LIMIT, collective_id=5, has_side_effects=True
         ),
@@ -634,7 +914,7 @@
             flops=24 * n * n * width, bytes_accessed=16 * n * width, transcendentals=n * n * heads // 2
         ),
         name="self_backward",
-    )(bounds, queries, keys, values, keys_t, grads, lse, inner, up_column, down_column, cross_sum)
+    )(bounds, queries, keys, values, keys_t, grads, lse, inner, up_column, cross_sum, enc_terms, early)
 
 
 def const(shape):
@@ -935,7 +1215,7 @@
         back_ref[...] = jnp.zeros_like(back_ref)
         enc_acc[...] = jnp.zeros_like(enc_acc)
 
-    @pl.when(i == 2)
+    @pl.when(i == 1)
     def _():
         for g in sums:
             g.middle()
@@ -1095,44 +1375,6 @@
     return (a.astype(F32) + b.astype(F32)).astype(BF16)
 
 
-def reduce_dp(total, distances, axes):
-    me = lax.axis_index("dp")
-    rows, columns = total.shape[0] // 2 ** len(axes), total.shape[1]
-    shape = [2] * len(axes) + [rows, columns]
-    axes = list(axes)
-    total = total.reshape(shape)
-    for step, distance in enumerate(distances):
-        axis = axes.index(distance)
-        axes.pop(axis)
-        mine = me // distance % 2
-        keep = lax.dynamic_index_in_dim(total, mine, axis, keepdims=False)
-        give = lax.dynamic_index_in_dim(total, 1 - mine, axis, keepdims=False)
-        got = swap(give, "dp", distance)
-        total = keep.astype(F32) + got.astype(F32)
-        if step < len(distances) - 1:
-            total = total.astype(BF16)
-    return total
-
-
-def sum_everywhere(value):
-    for distance in (1, 2):
-        value = value + swap(value, "tensor", distance)
-    for distance in dp_distances():
-        value = value + swap(value, "dp", distance)
-    return value
-
-
-def widen(rows_low):
-    member = lax.axis_index("tensor")
-    count, width = rows_low.shape
-    other = swap(rows_low, "tensor", 2)
-    parts = [rows_low, swap(rows_low, "tensor", 1), other, swap(other, "tensor", 1)]
-    out = jnp.zeros((4 * count, width), rows_low.dtype)
-    for distance, part in enumerate(parts):
-        out = lax.dynamic_update_slice(out, part, ((member ^ distance) * count, 0))
-    return out
-
-
 def narrow(rows_low):
     member = lax.axis_index("tensor")
     count = rows_low.shape[0] // 4
@@ -1183,10 +1425,6 @@
             out = lax.dynamic_update_slice_in_dim(out, part, (member ^ distance) * size, 0)
         return out
 
-    def norm_back(rows, incoming, which):
-        _, pull_rows = jax.vjp(layer_norm, rows, norm_params[which, 0], norm_params[which, 1])
-        return pull_rows(incoming)
-
     start_rows = block_in.astype(F32)
     first_in, enc_all, self_w, cross_column = start_gather(
         layer_norm(start_rows, norm_params[0, 0], norm_params[0, 1]).astype(BF16),
@@ -1248,7 +1486,6 @@
         biases[6:7],
         norm_params[2],
     )
-    gain_three, shift_three, bias_co_grad, bias_down_grad = (ffn_sums[k] for k in range(4))
 
     by_shard = (2, groups_count // 2, 2, w_rows, hidden_width)
     second_grad, enc_terms, cross_sum, bias_cq_parts, bias_cv_parts, up_column, down_column = cross_backward(
@@ -1266,15 +1503,22 @@
         down_sum.reshape(by_shard),
         heads,
     )
-    rows_two, gain_two, shift_two = norm_back(after_self, second_grad, 1)
-    self_rows_grad = cross_rows_grad + rows_two
-    self_low = self_rows_grad.astype(BF16)
-    bias_so_grad = jnp.sum(self_low.astype(F32), axis=0)
-    self_wide = widen(self_low)
-    encoder_grad = narrow(enc_terms)
+    self_wide, self_rows_grad, self_sums, summed_down = middle(
+        second_grad, after_self, cross_rows_grad, norm_params[1], down_column
+    )
     bias_cq_grad = blocks_placed([bias_cq_parts[d, 0] for d in range(4)])
     bias_cv_grad = blocks_placed([bias_cv_parts[d, 0] for d in range(4)])
     bias_up_grad = blocks_placed([bias_up_parts[d, 0] for d in range(4)])
+
+    early = jnp.concatenate(
+        [
+            self_sums[:3],
+            ffn_sums[:4],
+            jnp.stack([bias_cq_grad, bias_cv_grad]),
+            bias_up_grad.reshape(-1, model_width),
+        ]
+    )
+    early = jnp.pad(early, ((0, -early.shape[0] % 8), (0, 0)))
 
     self_mixed_grad = dot_nn(self_wide, self_out_w).astype(BF16)
     self_inner = jnp.sum(
@@ -1282,7 +1526,7 @@
         * self_mixed_grad.T.reshape(heads, width // heads, 4 * own_rows).astype(F32),
         axis=1,
     )
-    self_dq_t, self_dk, self_dv, summed_up, summed_down, cross_column = self_backward(
+    self_dq_t, self_dk, self_dv, summed_up, summed_cross, encoder_grad, early = self_backward(
         bounds,
         queries,
         key_rows,
@@ -1292,57 +1536,39 @@
         self_lse,
         self_inner,
         up_column,
-        down_column,
         cross_sum.reshape(2, groups_count // 2, 2, w_rows, 4 * width),
+        enc_terms,
+        early,
         heads,
         self_safe,
     )
-    summed_cross = reduce_dp(cross_column.reshape(-1, 4 * width), dp_distances()[-2::-1], dp_distances()[:-1])
     grad_so_t = lax.dot_general(
         self_wide, self_mixed_t, (((0,), (1,)), ((), ())), preferred_element_type=F32
     ).astype(BF16)
     qkv_grad = jnp.concatenate([self_dq_t.T, self_dk, self_dv], axis=1)
     first_terms = dot_nt(qkv_grad, self_w[:, : 3 * width]).astype(BF16)
-    first_grad = narrow(first_terms)
-    summed_self = reduce_dp(
-        jnp.concatenate([dot_tn(first_in, qkv_grad).astype(BF16), grad_so_t], axis=1),
-        dp_distances()[::-1],
-        dp_distances(),
-    )
+    self_grads = jnp.concatenate([dot_tn(first_in, qkv_grad).astype(BF16), grad_so_t], axis=1)
     column_sums = jnp.sum(qkv_grad.astype(F32), axis=0)
-    rows_one, gain_one, shift_one = norm_back(start_rows, first_grad, 0)
-    input_grad = self_rows_grad + rows_one
 
     def only_own(part):
         out = jnp.zeros((model_width,), F32)
         return lax.dynamic_update_slice_in_dim(out, part, member * width, 0)
 
-    early = sum_everywhere(
-        jnp.concatenate(
-            [
-                gain_two,
-                shift_two,
-                gain_three,
-                shift_three,
-                bias_so_grad,
-                bias_cq_grad,
-                bias_cv_grad,
-                bias_co_grad,
-                bias_down_grad,
-                bias_up_grad,
-            ]
-        ).reshape(-1, 128)
-    ).reshape(-1, model_width)
-    late = sum_everywhere(
-        jnp.concatenate(
-            [gain_one, shift_one, only_own(column_sums[:width]), only_own(column_sums[2 * width :])]
-        ).reshape(-1, 128)
-    ).reshape(-1, model_width)
-    norm_total = jnp.stack([late[0], late[1], early[0], early[1], early[2], early[3]]).reshape(
+    late = jnp.zeros((8, model_width), F32)
+    late = late.at[2].set(only_own(column_sums[:width])).at[3].set(only_own(column_sums[2 * width :]))
+    input_grad, summed_self, late = tail(
+        first_terms,
+        self_grads.reshape(groups_count // 2, 2, w_rows, 4 * width),
+        block_in,
+        self_rows_grad,
+        norm_params[0],
+        late,
+    )
+    norm_total = jnp.stack([late[0], late[1], early[0], early[1], early[3], early[4]]).reshape(
         norm_params.shape
     )
-    bias_total = jnp.stack([late[2], late[3], early[4], early[5], early[6], early[7], early[8]])
-    up_total = early[9:].reshape(-1)
+    bias_total = jnp.stack([late[2], late[3], early[2], early[7], early[8], early[5], early[6]])
+    up_total = early[9 : 9 + up_bias.shape[0] // model_width].reshape(-1)
     scale = 1.0 / groups
     return (
         output,

time: 710 us -> 689 us (0.970)
  Pallas kernels: 413 us -> 534 us
  waiting for transfers between devices: 113 us -> 26.7 us
  other arithmetic: 56.2 us -> 31 us
  starting transfers between devices: 21.3 us -> 2 us
  local copies, waits for them, and re-layouts: 61.3 us -> 50.6 us
    pallas_call x0 -> x2, Pallas kernels: none -> 103 us  [the longest x1 62.9 us: tail(): pl.pallas_call(functools.partial(tail_kernel, n=n), in_specs=[ANY, ANY, v...]
    ppermute x27 -> x3, waiting for transfers between devices: 113 us -> 26.7 us  [swap(): return lax.ppermute(value, axis, [(i, i ^ distance) for i in range(size)])]
    pallas_call x1, Pallas kernels: 62 us -> 86.3 us  [self_backward(): pl.pallas_call(functools.partial(self_backward_kernel, bk=bk, heads=heads...]
    ppermute x27 -> x3, starting transfers between devices: 21.3 us -> 2 us  [swap(): return lax.ppermute(value, axis, [(i, i ^ distance) for i in range(size)])]
    dynamic_slice x4 -> x0, local copies, waits for them, and re-layouts: 8.68 us -> none  [the longest x2 6.53 us: reduce_dp(): keep = lax.dynamic_index_in_dim(total, mine, axis, keepdims=False)]
    unnamed x115 -> x80, local copies, waits for them, and re-layouts: 18.7 us -> 16.7 us
  transfers between devices with their start and end apart: 27 -> 3, of which waited for: 14 -> 2; matrix products, arithmetic and copies ran while one was open for 9% -> 1% of each run, Pallas kernels for 0% -> 0%
where the time goes in v5:
time: 689 us; the launch traced here: 678 us
  Pallas kernels  534 us (78%)
  local copies, waits for them, and re-layouts  50.6 us (7%)
  matrix products  31.7 us (5%)
  other arithmetic  31 us (4%)
  waiting for transfers between devices  26.7 us (4%)
    pallas_call x1, Pallas kernels, self_backward(): pl.pallas_call(functools.partial(self_backward_kernel, bk=bk, heads=heads...  86.3 us
    pallas_call x1, Pallas kernels, cross_forward(): pl.pallas_call(functools.partial(cross_forward_kernel, heads=heads), grid...  83.2 us
    pallas_call x1, Pallas kernels, cross_backward(): pl.pallas_call(functools.partial(cross_backward_kernel, heads=heads, bk=2...  79.4 us
    pallas_call x1, Pallas kernels, start_gather(): pl.pallas_call(functools.partial(start_kernel, n=n), in_specs=[ANY] * 4,...  77.3 us
    pallas_call x1, Pallas kernels, tail(): pl.pallas_call(functools.partial(tail_kernel, n=n), in_specs=[ANY, ANY, v...  62.9 us
    pallas_call x1, Pallas kernels, self_forward(): pl.pallas_call(functools.partial(self_forward_kernel, bk=bk, heads=heads,...  53.1 us
    pallas_call x1, Pallas kernels, feed_forward(): pl.pallas_call(functools.partial(feed_forward_kernel, chunks=chunks), gri...  51.7 us
    pallas_call x1, Pallas kernels, middle(): pl.pallas_call(functools.partial(middle_kernel, n=n), in_specs=[vmem, vme...  39.8 us
  transfers between devices with their start and end apart: 3, of which 2 were waited for; matrix products, arithmetic and copies ran while one was open for 1% of the time, Pallas kernels for 0%

profile of v5, /device:TPU:0, one launch (start us, length us, event | category | flops | bytes accessed | tf_op | source)
XLA Modules:
  0.0 677.8 jit_solution(3900158663026708028)
XLA Ops:
  0.7 1.6 fusion.19
  2.4 0.8 fusion.20
  3.1 1.6 convert_reduce_fusion.1
  4.7 1.8 fusion.2
  7.2 1.6 fusion.5.rows_ref
  8.8 0.9 pad_maximum_fusion.3
  9.6 77.3 %start_gather.1 = (bf16[2560,1024]{1,0:T(8,128)(2,1)}, bf16[1024,1024]{1,0:T(8,128)(2,1)}, bf16[4,2,128,1024]{3,2,1,0:T(8,128)(2,1)}, bf16[4,128,1024]{2,1,0:T(8,128)(2,1)}) custom-call(bf16[640,1024]{1,0:T(8,128)(2,1)} %fusion.5.rows_ref, bf16[256,1024]{1,0:T(8,128)(2,1)} %enc_ref.1, bf16[128,1024]{1,0:T(8,128)(2,1)} %get-tuple-element.205.self_ref, ...), custom_call_target="tpu_custom_call" | custom-call | bytes 104857600 | tf_op jit(solution)/shard_map/start_gather/pallas_call | solution.py:601
  86.9 6.6 fusion.10
  93.6 3.0 copy-done.5
  96.6 1.2 slice.238
  97.8 4.0 fusion.7
  101.8 1.0 copy-done.7
  102.9 1.6 copy.52.vt_ref
  104.5 1.7 copy.67
  106.2 1.5 copy.51.k_ref
  107.8 0.8 pad_maximum_fusion.2.shard_ref
  108.7 53.1 %self_forward.1 = (bf16[256,2560]{1,0:T(8,128)(2,1)}, f32[4,2560]{1,0:T(4,128)}, bf16[4,4,2,128,1024]{4,3,2,1,0:T(8,128)(2,1)}, bf16[4,128,2048]{2,1,0:T(8,128)(2,1)}) custom-call(s32[1,2]{1,0:T(1,128)} %b_ref.3, bf16[2560,256]{1,0:T(8,128)(2,1)} %get-tuple-element.154.q_ref, bf16[2560,256]{1,0:T(8,128)(2,1)} %copy.51.k_ref, bf16[256,2560]{1,0:T(8,128)(2,1)} %copy.52.vt_ref, ...), custom_call_target="tpu_custom_call" | custom-call | flops 20132659200 | bytes 5242880 | tf_op jit(solution)/shard_map/self_forward/pallas_call | solution.py:701
  161.8 5.3 convolution_convert_fusion
  167.2 3.4 constant_dynamic-slice_fusion.9
  171.1 2.9 collective-permute-done.1
  174.0 3.3 add_convert_fusion.1
  177.2 1.5 collective-permute-start.2
  178.7 1.8 copy.55
  183.1 0.8 fusion.12.ok_ref
  184.5 23.8 %collective-permute-done.2 = bf16[640,1024]{1,0:T(8,128)(2,1)} collective-permute-done((bf16[640,1024]{1,0:T(8,128)(2,1)}, bf16[640,1024]{1,0:T(8,128)(2,1)}, u32[]{:S(2)}, u32[]{:S(2)}) %collective-permute-start.2) | collective-permute-done | bytes 1310752 | tf_op jit(solution)/shard_map/ppermute | solution.py:1362
  208.4 2.9 fusion.15
  211.7 1.6 add_convert_fusion.x_ref
  213.3 83.2 %cross_forward.1 = (bf16[4,640,256]{2,1,0:T(8,128)(2,1)}, bf16[4,1024,256]{2,1,0:T(8,128)(2,1)}, bf16[4,1024,256]{2,1,0:T(8,128)(2,1)}, bf16[4,256,640]{2,1,0:T(...) custom-call(f32[1024,1]{1,0:T(8,128)} %fusion.12.ok_ref, ...), custom_call_target="tpu_custom_call" | custom-call | flops 16106127360 | bytes 8388608 | tf_op jit(solution)/shard_map/cross_forward/pallas_call | solution.py:1007
  296.5 51.7 %feed_forward.1 = (f32[640,1024]{1,0:T(8,128)}, f32[640,1024]{1,0:T(8,128)}, bf16[640,1024]{1,0:T(8,128)(2,1)}, f32[8,1024]{1,0:T(8,128)}, bf16[2,1024,1024]{2,1...) custom-call(bf16[640,1024]{1,0:T(8,128)(2,1)} %get-tuple-element.88.x_ref, ...), custom_call_target="tpu_custom_call" | custom-call | flops 32212254720 | bytes 41943040 | tf_op jit(solution)/shard_map/feed_forward/pallas_call | solution.py:1144
  348.2 0.7 fusion.21
  350.0 79.4 %cross_backward.1 = (f32[640,1024]{1,0:T(8,128)}, bf16[1024,1024]{1,0:T(8,128)(2,1)}, bf16[2,1024,1024]{2,1,0:T(8,128)(2,1)}, f32[4,1,256]{2,1,0:T(1,128)}, f32[...) custom-call(f32[1024,1]{1,0:T(8,128)} %fusion.12.ok_ref, ...), custom_call_target="tpu_custom_call" | custom-call | flops 32212254720 | bytes 16777216 | tf_op jit(solution)/shard_map/cross_backward/pallas_call | solution.py:1303
  430.1 0.7 constant_dynamic-update-slice_fusion.4
  430.8 0.7 constant_dynamic-update-slice_fusion.3
  432.1 0.7 constant_dynamic-update-slice_fusion.9
  432.8 0.7 constant_dynamic-update-slice_fusion.8
  434.2 0.7 constant_dynamic-update-slice_fusion.6
  434.9 39.8 %middle.1 = (bf16[2560,1024]{1,0:T(8,128)(2,1)}, f32[640,1024]{1,0:T(8,128)}, f32[8,1024]{1,0:T(8,128)}, f32[128,1024]{1,0:T(8,128)}) custom-call(f32[640,1024]{1,0:T(8,128)} %get-tuple-element.100.back_ref, f32[640,1024]{1,0:T(8,128)} %copy-done, f32[640,1024]{1,0:T(8,128)} %get-tuple-element.101.grad_ref, f32[2,1024]{1,0:T(2,128)} %get-tuple-element.174.norm_ref, ...), custom_call_target="tpu_custom_call" | custom-call | bytes 104857600 | tf_op jit(solution)/shard_map/middle/pallas_call | solution.py:427
  474.7 0.8 slice.206
  475.4 5.2 bitcast_multiply_fusion
  480.6 2.1 copy.56
  482.7 2.6 bitcast_reduce_fusion.dl_ref
  486.0 86.3 %self_backward.1 = (bf16[256,2560]{1,0:T(8,128)(2,1)}, bf16[2560,256]{1,0:T(8,128)(2,1)}, bf16[2560,256]{1,0:T(8,128)(2,1)}, f32[128,1024]{1,0:T(8,128)}, f32[12...) custom-call(s32[1,2]{1,0:T(1,128)} %b_ref.3, bf16[2560,256]{1,0:T(8,128)(2,1)} %get-tuple-element.154.q_ref, ...), custom_call_target="tpu_custom_call" | custom-call | flops 40265318400 | bytes 10485760 | tf_op jit(solution)/shard_map/self_backward/pallas_call | solution.py:873
  572.4 1.7 copy.58
  574.1 2.1 convert_reduce_fusion
  576.3 6.9 %convolution_convert_fusion.3 = bf16[1024,768]{0,1:T(8,128)(2,1)S(1)} fusion(bf16[2560,1024]{1,0:T(8,128)(2,1)} %get-tuple-element.81, bf16[2560,256]{1,0:T(8,128)(2,1)S(1)} %copy-done.11, bf16[2560,256]{1,0:T(8,128)(2,1)S(1)} %copy-done.10, bf16[2560,256]{1,0:T(8,128)(2,1)S(1)} %bitcast.84), kind=kOutput, calls=%fused_computation.25 | convolution fusion | flops 4039114752 | bytes 10747904 | tf_op jit(solution)/shard_map/dot_general | solution.py:28
  583.2 1.5 convolution_convert_fusion.4
  584.8 6.0 convolution_convert_fusion.1.terms_ref
  592.3 2.6 copy.59
  595.6 62.9 %tail.1 = (f32[640,1024]{1,0:T(8,128)}, f32[128,1024]{1,0:T(8,128)}, f32[8,1024]{1,0:T(8,128)}) custom-call(bf16[2560,1024]{1,0:T(8,128)(2,1)} %convolution_convert_fusion.1.terms_ref, bf16[4,2,128,1024]{3,2,1,0:T(8,128)(2,1)} %bitcast.79, bf16[640,1024]{1,0:T(8,128)(2,1)} %rows_ref.1, f32[640,1024]{1,0:T(8,128)} %get-tuple-element.116.grad_ref, ...), custom_call_target="tpu_custom_call" | custom-call | bytes 104857600 | tf_op jit(solution)/shard_map/tail/pallas_call | solution.py:516
  658.5 1.0 slice_multiply_fusion
  659.6 0.9 multiply_bitcast_fusion.2
  660.5 0.7 multiply_bitcast_fusion.1
  661.2 1.4 fusion.18
  663.5 0.9 copy.61
  664.4 0.8 copy.62
  665.1 1.9 broadcast_multiply_fusion
  667.1 0.9 mul.212
  667.9 0.8 copy.63
  669.3 1.1 multiply_bitcast_fusion
  670.4 1.0 copy.64
  672.0 1.5 copy.93
  673.5 1.2 copy-done.9
  674.7 1.5 copy.94
  676.7 1.0 copy.95
  (119 shorter events, 12.7 us)
Async XLA Ops:
  0.6 6.5 copy-start.1
  0.7 5.9 copy-start.17
  0.7 6.2 copy-start.19
  0.7 6.3 copy-start.22
  0.7 6.4 copy-start.23
  4.7 4.1 copy-start.21
  93.6 3.1 copy-start.5
  101.8 1.0 copy-start.7
  104.5 3.2 copy-start.15
  104.5 3.3 copy-start.16
  106.1 55.7 %copy-start.6 = (bf16[2560,256]{0,1:T(8,128)(2,1)}, bf16[2560,256]{0,1:T(8,128)(2,1)S(1)}, u32[]{:S(2)}) copy-start(bf16[2560,256]{0,1:T(8,128)(2,1)S(1)} %copy.67) | copy-start | bytes 3932164
  170.6 8.2 %copy-start.2 = (bf16[256,2560]{1,0:T(8,128)(2,1)S(1)}, bf16[256,2560]{1,0:T(8,128)(2,1)}, u32[]{:S(2)}) copy-start(bf16[256,2560]{1,0:T(8,128)(2,1)} %get-tuple-element.84) | copy-start | bytes 3932164
  170.6 3.4 collective-permute-start.1
  170.6 14.0 %collective-permute-start = (bf16[640,1024]{1,0:T(8,128)(2,1)}, bf16[640,1024]{1,0:T(8,128)(2,1)}, u32[]{:S(2)}, u32[]{:S(2)}) collective-permute-start(bf16[640,1024]{1,0:T(8,128)(2,1)} %get-tuple-element.155), channel_id=1, source_target_pairs={{0,1},{1,0},{2,3},{3,2},{4,5},{5,4},{6,7},{7,6},{8,9},{9,8},{10,11... | collective-permute-start | bytes 3932168 | tf_op jit(solution)/shard_map/ppermute | solution.py:1362
  171.1 11.3 %copy-start.28 = (f32[4096]{0:T(1024)S(1)}, f32[4096]{0:T(1024)}, u32[]{:S(2)}) copy-start(f32[4096]{0:T(1024)} %param.33) | copy-start | bytes 49156
  177.2 6.7 copy-start.20
  177.2 31.1 %collective-permute-start.2 = (bf16[640,1024]{1,0:T(8,128)(2,1)}, bf16[640,1024]{1,0:T(8,128)(2,1)}, u32[]{:S(2)}, u32[]{:S(2)}) collective-permute-start(bf16[640,1024]{1,0:T(8,128)(2,1)} %add_convert_fusion.1), channel_id=1, source_target_pairs={{0,2},{1,3},{2,0},{3,1},{4,6},{5,7},{6,4},{7,5},{8,10},{9,11},{10,... | collective-permute-start | bytes 3932168 | tf_op jit(solution)/shard_map/ppermute | solution.py:1362
  211.3 2.0 copy-start
  434.9 40.6 %copy-start.30 = (f32[8,1024]{1,0:T(8,128)S(1)}, f32[8,1024]{1,0:T(8,128)}, u32[]{:S(2)}) copy-start(f32[8,1024]{1,0:T(8,128)} %get-tuple-element.109) | copy-start | bytes 98308
  434.9 40.6 %copy-start.4 = (bf16[256,2560]{0,1:T(8,128)(2,1)S(1)}, bf16[256,2560]{0,1:T(8,128)(2,1)}, u32[]{:S(2)}) copy-start(bf16[256,2560]{0,1:T(8,128)(2,1)} %copy.55) | copy-start | bytes 3932164
  572.3 1.7 copy-start.10
  574.1 2.2 copy-start.11
  574.1 9.1 %slice-start = ((s8[5242880]{0:T(1024)(128)(4,1)}), s8[4194304]{0:T(1024)(128)(4,1)S(1)}, s32[]{:S(2)}) async-start(s8[5242880]{0:T(1024)(128)(4,1)} %bitcast.80), calls=%async_computation | async-start | bytes 8388608
  576.2 7.0 %copy-start.3 = (bf16[256,2560]{1,0:T(8,128)(2,1)S(1)}, bf16[256,2560]{1,0:T(8,128)(2,1)}, u32[]{:S(2)}) copy-start(bf16[256,2560]{1,0:T(8,128)(2,1)} %get-tuple-element.84) | copy-start | bytes 3932164
  576.2 7.0 %slice-start.1 = ((s8[5242880]{0:T(1024)(128)(4,1)}), s8[1048576]{0:T(1024)(128)(4,1)S(1)}, s32[]{:S(2)}) async-start(s8[5242880]{0:T(1024)(128)(4,1)} %bitcast.80), calls=%async_computation.1 | async-start | bytes 2097152
  583.2 1.6 copy-start.13
  584.8 6.1 copy-start.24
  595.0 0.6 copy-start.18
  595.6 64.9 %copy-start.14 = (f32[128,1024]{1,0:T(8,128)S(1)}, f32[128,1024]{1,0:T(8,128)}, u32[]{:S(2)}) copy-start(f32[128,1024]{1,0:T(8,128)} %get-tuple-element.122) | copy-start | bytes 1572868
  663.5 8.6 %copy-start.8 = (f32[640,1024]{1,0:T(8,128)S(1)}, f32[640,1024]{1,0:T(8,128)}, u32[]{:S(2)}) copy-start(f32[640,1024]{1,0:T(8,128)} %get-tuple-element.220) | copy-start | bytes 7864324
  665.1 6.2 copy-start.25
  665.1 6.2 copy-start.26
  665.1 6.2 copy-start.27
  665.1 6.2 copy-start.29
  672.0 2.7 copy-start.9
  674.7 2.0 copy-start.12

commit v6 on v5

--- a/solution.py
+++ b/solution.py
@@ -54,10 +54,13 @@
     return bad
 
 
-def over_keys(i, bq, bk, safe, block):
+def over_keys(i, bq, bk, safe, block, between=()):
     diagonal = i * (bq // bk)
 
     def visit(j, c):
+        for at_i, at_j, action in between:
+            pl.when((i == at_i) & (j == at_j))(action)
+
         @pl.when(j < safe // bk)
         def _():
             block(j, "none")
@@ -262,6 +265,38 @@
     return [whole] * 3 + [half] * 2 + [whole] * 2
 
 
+class GatherLast:
+    def __init__(self, links, near, far, diagonal, buffers):
+        y = links.dp % 2
+        self.column, self.over_x, self.diagonal, self.sum_y, self.sum_x = buffers
+        self.loads = [
+            links.local(far.at[:, y], self.over_x),
+            links.local(diagonal, self.diagonal),
+            links.local(near.at[:, y], self.column),
+        ]
+        self.over_y = links.copy(near.at[:, 1 - y], self.sum_y, Y)
+        self.along_x = links.copy(self.over_x, self.sum_x, X)
+
+    def start(self):
+        self.over_y.start()
+        for copy in self.loads:
+            copy.start()
+
+    def middle(self):
+        for copy in self.loads:
+            copy.wait()
+        add_to(self.over_x, self.diagonal)
+        self.along_x.start()
+
+    def end(self):
+        self.over_y.wait_recv()
+        self.along_x.wait_recv()
+        add_to(self.column, self.sum_y)
+        add_to(self.column, self.sum_x)
+        self.over_y.wait_send()
+        self.along_x.wait_send()
+
+
 class Collect:
     def __init__(self, links, column, slots):
         z = links.dp // 2
@@ -363,8 +398,8 @@
 
 
 def middle_kernel(
-    back_ref, rows_ref, grad_ref, norm_ref, down_ref,
-    wide_out, grad_out, sums_ref, down_out,
+    back_ref, rows_ref, grad_ref, norm_ref, down_ref, cross_ref,
+    wide_out, grad_out, sums_ref, down_out, diagonal_out,
     low, column, slots, send_sems, recv_sems, local_sems, *, n
 ):
     links = Links(send_sems, recv_sems, local_sems)
@@ -382,7 +417,9 @@
     over_x = [links.copy(low.at[part], place(0).at[part], X) for part in parts]
     over_core = links.copy(low, place(0), CORE)
     onward = [links.copy(place(2).at[part], place(2).at[part], CORE) for part in parts]
-    links.greet([CORE, X] + z_ways(n))
+    over_y = links.copy(cross_ref.at[1, :, 1 - links.dp % 2], diagonal_out, Y)
+    links.greet([CORE, X, Y] + z_ways(n))
+    over_y.start()
     load.wait()
     collect.start(0)
     sums_ref[...] = jnp.zeros_like(sums_ref)
@@ -417,121 +454,177 @@
     over_core.wait()
     for copy in onward:
         copy.wait()
-
-
-def middle(back, rows, grad, norm, down_column):
+    over_y.wait()
+
+
+def middle(back, rows, grad, norm, down_column, cross_sum):
     n = lax.axis_size("dp")
     count, width = rows.shape
     m, r, c = down_column.shape
     vmem = pl.BlockSpec(memory_space=pltpu.VMEM)
     return pl.pallas_call(
         functools.partial(middle_kernel, n=n),
-        in_specs=[vmem, vmem, vmem, vmem, ANY],
-        out_specs=[ANY, vmem, vmem, vmem],
+        in_specs=[vmem, vmem, vmem, vmem, ANY, ANY],
+        out_specs=[ANY, vmem, vmem, vmem, ANY],
         out_shape=[
             jax.ShapeDtypeStruct((4 * count, width), BF16),
             jax.ShapeDtypeStruct((count, width), F32),
             jax.ShapeDtypeStruct((8, width), F32),
             jax.ShapeDtypeStruct((r, c), F32),
+            jax.ShapeDtypeStruct((m, r, cross_sum.shape[4]), BF16),
         ],
         scratch_shapes=[
             pltpu.VMEM((count, width), BF16),
             pltpu.VMEM((m, r, c), BF16),
             pltpu.VMEM((m, r, c), BF16),
         ]
-        + link_scratch(5 + m, 2),
+        + link_scratch(6 + m, 2),
         compiler_params=pltpu.CompilerParams(
             vmem_limit_bytes=VMEM_LIMIT, collective_id=6, has_side_effects=True
         ),
         cost_estimate=pl.CostEstimate(flops=0, bytes_accessed=100 * 2**20, transcendentals=0),
         name="middle",
-    )(back, rows, grad, norm, down_column)
+    )(back, rows, grad, norm, down_column, cross_sum)
 
 
 def tail_kernel(
-    terms_ref, weights_ref, rows_ref, grad_ref, norm_ref, late_ref,
-    grad_out, weights_out, late_out, *scratch, n
+    dq_ref, dk_ref, dv_ref, w_ref, first_ref, so_ref, rows_ref, grad_ref, norm_ref, late_ref,
+    grad_out, weights_out, late_out, give, acc, weights, *scratch, n, step_rows
 ):
     links = Links(*scratch[-3:])
-    rows_sum = RowSum(links, terms_ref, scratch[:5])
+    near, far, got_near, got_far, got_x = scratch[:5]
     columns, gots, slots = scratch[5:7], scratch[7:9], scratch[9:11]
     held, late_slots = scratch[11:13]
+    count, model = near.shape
+    width = dq_ref.shape[1]
     y = links.dp % 2
     c = columns[0].shape[2]
-    loads, over_y, collects = [], [], []
+    m, _, r, _ = weights.shape
+    half = count // 2
+    parts = [pl.ds(0, half), pl.ds(half, half)]
+    core_far = links.copy(give.at[0], got_far, CORE)
+    core_near = links.copy(give.at[1], got_near, CORE)
+    over_x = [links.copy(far.at[part], got_x.at[part], X) for part in parts]
+    over_y, collects = [], []
     for k, (column, got, slot) in enumerate(zip(columns, gots, slots)):
-        part = pl.ds(k * c, c)
-        loads.append(links.local(weights_ref.at[:, y, :, part], column))
-        over_y.append(links.copy(weights_ref.at[:, 1 - y, :, part], got, Y))
+        over_y.append(links.copy(weights.at[:, 1 - y, :, pl.ds(k * c, c)], got, Y))
         collects.append(Collect(links, column, slot))
     late = Everywhere(links, held, late_slots, n)
     links.greet(everywhere_ways(n))
-    rows_sum.start()
+
+    def terms(distance, target):
+        base = (links.tensor ^ distance) * count
+
+        def one(rows):
+            there = pl.ds(pl.multiple_of(base + rows.start, 128), 128)
+            total = dot_nt(dq_ref[there, :], w_ref[:, :width])
+            total = total + dot_nt(dk_ref[there, :], w_ref[:, width : 2 * width])
+            target[rows, :] = (total + dot_nt(dv_ref[there, :], w_ref[:, 2 * width : 3 * width])).astype(BF16)
+
+        by_rows(count, 128, one)
+
+    terms(3, give.at[0])
+    core_far.start()
+    terms(2, far)
+    core_far.wait_recv()
+    for part, copy in zip(parts, over_x):
+
+        def add(rows, part=part):
+            there = pl.ds(pl.multiple_of(part.start + rows.start, 64), 64)
+            far[there, :] = (far[there, :].astype(F32) + got_far[there, :].astype(F32)).astype(BF16)
+
+        by_rows(half, 64, add)
+        copy.start()
+
+    acc[...] = jnp.zeros_like(acc)
+
+    def products(rows):
+        source = first_ref[rows, :].T
+        for k, ref in enumerate((dq_ref, dk_ref, dv_ref)):
+            acc[:, k * width : (k + 1) * width] += dot_nn(source, ref[rows, :])
+
+    by_rows(dq_ref.shape[0], step_rows, products)
+    for k in range(2 * m):
+        span = slice(k * r, (k + 1) * r)
+        weights[k // 2, k % 2, :, : 3 * width] = acc[span, :].astype(BF16)
+        weights[k // 2, k % 2, :, 3 * width :] = so_ref[span, :]
     over_y[0].start()
-    for load in loads:
-        load.start()
-    rows_sum.middle()
+    terms(1, give.at[1])
+    core_near.start()
+    terms(0, near)
     for k in range(2):
-        loads[k].wait()
+        columns[k][...] = weights[:, y, :, k * c : (k + 1) * c]
+    for k in range(2):
         over_y[k].wait_recv()
         if k == 0:
             over_y[1].start()
         add_to(columns[k], gots[k])
         collects[k].start(0)
     stages = len(collects[0].stages)
-    for step in range(stages):
+    for step in range(stages - 1):
         for k in range(2):
             collects[k].finish(step)
-            if step < stages - 1:
-                collects[k].start(step + 1)
-    for k in range(2):
-        weights_out[:, k * c : (k + 1) * c] = columns[k][collects[k].z].astype(F32)
-    rows_sum.end()
+            collects[k].start(step + 1)
     held[0] = late_ref[...]
-
-    def norm_back(rows):
-        incoming = rows_sum.total(rows)
-        rows_grad, gain_terms = norm_rows_back(rows_ref[rows, :].astype(F32), incoming, norm_ref[0:1, :])
-        grad_out[rows, :] = rows_grad + grad_ref[rows, :]
-        held[0, 0:1, :] += jnp.sum(gain_terms, axis=0, keepdims=True)
-        held[0, 1:2, :] += jnp.sum(incoming, axis=0, keepdims=True)
-
-    by_rows(grad_out.shape[0], 64, norm_back)
+    core_near.wait_recv()
+    for part, copy in zip(parts, over_x):
+        copy.wait_recv()
+
+        def norm_back(rows, part=part):
+            rows = pl.ds(pl.multiple_of(part.start + rows.start, 64), 64)
+            incoming = near[rows, :].astype(F32) + got_near[rows, :].astype(F32) + got_x[rows, :].astype(F32)
+            rows_grad, gain_terms = norm_rows_back(rows_ref[rows, :].astype(F32), incoming, norm_ref[0:1, :])
+            grad_out[rows, :] = rows_grad + grad_ref[rows, :]
+            held[0, 0:1, :] += jnp.sum(gain_terms, axis=0, keepdims=True)
+            held[0, 1:2, :] += jnp.sum(incoming, axis=0, keepdims=True)
+
+        by_rows(half, 64, norm_back)
     steps = len(late.copies)
     for step in range(steps):
         late.start(step)
+        if step == 0:
+            for k in range(2):
+                collects[k].finish(stages - 1)
+                weights_out[:, k * c : (k + 1) * c] = columns[k][collects[k].z].astype(F32)
         late.finish(step)
     late_out[...] = held[steps]
-    for k in range(2):
-        over_y[k].wait_send()
-        collects[k].drain()
-
-
-def tail(terms, weights, rows, grad, norm, late):
+    for copy in over_x + over_y + [core_near, core_far]:
+        copy.wait_send()
+    for collect in collects:
+        collect.drain()
+
+
+def tail(dq, dk, dv, w, first, so_grad, rows, grad, norm, late):
     n = lax.axis_size("dp")
-    count, width = rows.shape
-    m, _, r, c = weights.shape
+    count, model = rows.shape
+    total, width = dq.shape
+    m, r, c = n // 2, model // n, 4 * width
     vmem = pl.BlockSpec(memory_space=pltpu.VMEM)
     part = pltpu.VMEM((m, r, c // 2), BF16)
     return pl.pallas_call(
-        functools.partial(tail_kernel, n=n),
-        in_specs=[ANY, ANY, vmem, vmem, vmem, vmem],
+        functools.partial(tail_kernel, n=n, step_rows=512),
+        in_specs=[vmem] * 10,
         out_specs=[vmem, vmem, vmem],
         out_shape=[
-            jax.ShapeDtypeStruct((count, width), F32),
+            jax.ShapeDtypeStruct((count, model), F32),
             jax.ShapeDtypeStruct((r, c), F32),
             jax.ShapeDtypeStruct(late.shape, F32),
         ],
-        scratch_shapes=row_sum_scratch(count, width)
+        scratch_shapes=[
+            pltpu.VMEM((2, count, model), BF16),
+            pltpu.VMEM((model, 3 * width), F32),
+            pltpu.VMEM((m, 2, r, c), BF16),
+        ]
+        + row_sum_scratch(count, model)
         + [part] * 6
         + everywhere_scratch(*late.shape, n)
-        + link_scratch(5 + 2 * m + len(everywhere_ways(n)), 4),
+        + link_scratch(6 + 2 * m + len(everywhere_ways(n)), 1),
         compiler_params=pltpu.CompilerParams(
             vmem_limit_bytes=VMEM_LIMIT, collective_id=7, has_side_effects=True
         ),
         cost_estimate=pl.CostEstimate(flops=0, bytes_accessed=100 * 2**20, transcendentals=0),
         name="tail",
-    )(terms, weights, rows, grad, norm, late)
+    )(dq, dk, dv, w, first, so_grad, rows, grad, norm, late)
 
 
 def start_kernel(
@@ -737,22 +830,27 @@
 
 
 def self_backward_kernel(
-    b_ref, q_ref, k_ref, v_ref, kt_ref, do_ref, lse_ref, dl_ref, up_ref, cross_ref, enc_ref, early_ref,
-    dqt_ref, dk_ref, dv_ref, up_out, cross_out, enc_out, early_out, dka, dva, dqa, *scratch, bk, heads, safe, n
+    b_ref, q_ref, k_ref, v_ref, kt_ref, wide_ref, w_ref, mt_ref, lse_ref,
+    up_ref, cross_ref, diagonal_ref, enc_ref, early_ref,
+    dq_ref, dk_ref, dv_ref, up_out, cross_out, enc_out, early_out, dka, dva, dqa, *scratch, bk, heads, safe, n
 ):
     i = pl.program_id(0)
     last = pl.num_programs(0) - 1
     links = Links(*scratch[-3:])
-    cross = Gather(links, cross_ref.at[0], cross_ref.at[1], scratch[:7])
-    cross_z = Collect(links, cross.column, scratch[7])
-    up_column = scratch[8]
-    up_z = Collect(links, up_column, scratch[9])
+    cross = GatherLast(links, cross_ref.at[0], cross_ref.at[1], diagonal_ref, scratch[:5])
+    cross_z = Collect(links, cross.column, scratch[5])
+    up_column = scratch[6]
+    up_z = Collect(links, up_column, scratch[7])
     load = links.local(up_ref, up_column)
-    enc = RowSum(links, enc_ref, scratch[10:15])
-    held = scratch[15]
-    early = Everywhere(links, held, scratch[16], n)
+    enc = RowSum(links, enc_ref, scratch[8:13])
+    held = scratch[13]
+    early = Everywhere(links, held, scratch[14], n)
     stages = len(up_z.stages)
     steps = len(early.copies)
+
+    def next_early(step):
+        early.finish(step)
+        early.start(step + 1)
 
     @pl.when(i == 0)
     def _():
@@ -764,50 +862,50 @@
         early.start(0)
         load.wait()
         up_z.start(0)
+        dka[...] = jnp.zeros_like(dka)
+        dva[...] = jnp.zeros_like(dva)
 
     @pl.when(i == 1)
     def _():
-        enc.middle()
-        early.finish(0)
-        early.start(1)
+        cross.middle()
+        next_early(0)
 
     @pl.when(i == 2)
-    def _():
-        cross.middle()
-        early.finish(1)
-        early.start(2)
-
-    @pl.when(i == 3)
     def _():
         for step in range(stages - 1):
             up_z.finish(step)
             up_z.start(step + 1)
-        early.finish(2)
-        early.start(3)
+        next_early(1)
+
+    @pl.when(i == 3)
+    def _():
+        next_early(2)
 
     @pl.when(i == last)
     def _():
+        for step in range(3, steps - 1):
+            next_early(step)
+
+    def sum_cross():
         cross.end()
         cross_z.start(0)
-        for step in range(3, steps - 1):
-            early.finish(step)
-            early.start(step + 1)
+        enc.middle()
+
+    def next_cross():
+        for step in range(stages - 1):
+            cross_z.finish(step)
+            cross_z.start(step + 1)
 
     bq, width = q_ref.shape
     hd = width // heads
     scale = 1.0 / math.sqrt(hd)
-
-    @pl.when(i == 0)
-    def _():
-        dka[...] = jnp.zeros_like(dka)
-        dva[...] = jnp.zeros_like(dva)
-
+    grads = dot_nn(wide_ref[...], w_ref[...]).astype(BF16)
+    products = grads.T.astype(F32) * mt_ref[...].astype(F32)
+    inner = [jnp.sum(products[h * hd : (h + 1) * hd, :], axis=0, keepdims=True) for h in range(heads)]
     scaled = q_ref[...] * jnp.asarray(scale, BF16)
-    grads = do_ref[...]
     q_heads = [head_only(scaled, h, hd) for h in range(heads)]
     d_heads = [head_only(grads, h, hd) for h in range(heads)]
     lse = lse_ref[...]
-    inner = dl_ref[...]
     dqa[...] = jnp.zeros_like(dqa)
 
     def block(j, mode):
@@ -823,7 +921,7 @@
         for h in range(heads):
             part = slice(h * hd, (h + 1) * hd)
             probs = jnp.exp(scores[h] - lse[h : h + 1, :])
-            ds = (probs * (dprobs[h] - inner[h : h + 1, :])).astype(BF16)
+            ds = (probs * (dprobs[h] - inner[h])).astype(BF16)
             dv_h = dot_nn(probs.astype(BF16), d_heads[h])
             dk_h = dot_nn(ds, q_heads[h])
             dv_sum = dv_h if dv_sum is None else dv_sum + dv_h
@@ -832,8 +930,8 @@
         dva[rows, :] += dv_sum
         dka[rows, :] += dk_sum
 
-    over_keys(i, bq, bk, safe, block)
-    dqt_ref[...] = (dqa[...] * scale).astype(BF16)
+    over_keys(i, bq, bk, safe, block, [(3, 2, sum_cross), (4, 2, next_cross)])
+    dq_ref[...] = (dqa[...] * scale).astype(BF16).T
 
     @pl.when(i == pl.num_programs(0) - 1)
     def _():
@@ -841,10 +939,7 @@
         dv_ref[...] = dva[...].astype(BF16)
         up_z.finish(stages - 1)
         up_out[...] = up_column[up_z.z].astype(F32)
-        for step in range(stages):
-            cross_z.finish(step)
-            if step < stages - 1:
-                cross_z.start(step + 1)
+        cross_z.finish(stages - 1)
         cross_out[...] = cross.column[cross_z.z].astype(F32)
         enc.end()
 
@@ -859,36 +954,37 @@
 
 
 def self_backward(
-    bounds, queries, keys, values, keys_t, grads, lse, inner, up_column, cross_sum, enc_terms, early, heads, safe
+    bounds, queries, keys, values, keys_t, wide, w_out, mixed_t, lse,
+    up_column, cross_sum, diagonal, enc_terms, early, heads, safe
 ):
     n, width = queries.shape
+    model = wide.shape[1]
     dp = lax.axis_size("dp")
     m, r, c = up_column.shape
     cross_c = cross_sum.shape[4]
     enc_shape = (enc_terms.shape[0] // 4, enc_terms.shape[1])
     bq = bk = 512
-    whole = pl.BlockSpec((n, width), lambda i: (0, 0))
     some = pl.BlockSpec((bq, width), lambda i: (i, 0))
-    per_row = pl.BlockSpec((heads, bq), lambda i: (0, i))
     return pl.pallas_call(
         functools.partial(self_backward_kernel, bk=bk, heads=heads, safe=safe, n=dp),
         grid=(n // bq,),
         in_specs=[
             pl.BlockSpec(memory_space=pltpu.SMEM),
             some,
-            whole,
-            whole,
-            pl.BlockSpec((width, n), lambda i: (0, 0)),
-            some,
-            per_row,
-            per_row,
+            const((n, width)),
+            const((n, width)),
+            const((width, n)),
+            pl.BlockSpec((bq, model), lambda i: (i, 0)),
+            const((model, width)),
+            pl.BlockSpec((width, bq), lambda i: (0, i)),
+            pl.BlockSpec((heads, bq), lambda i: (0, i)),
         ]
-        + [ANY] * 3
+        + [ANY] * 4
         + [const(early.shape)],
-        out_specs=[pl.BlockSpec((width, bq), lambda i: (0, i)), whole, whole]
+        out_specs=[some, const((n, width)), const((n, width))]
         + [const((r, c)), const((r, cross_c)), const(enc_shape), const(early.shape)],
         out_shape=[
-            jax.ShapeDtypeStruct((width, n), BF16),
+            jax.ShapeDtypeStruct((n, width), BF16),
             jax.ShapeDtypeStruct((n, width), BF16),
             jax.ShapeDtypeStruct((n, width), BF16),
             jax.ShapeDtypeStruct((r, c), F32),
@@ -901,12 +997,11 @@
             pltpu.VMEM((n, width), F32),
             pltpu.VMEM((width, bq), F32),
         ]
-        + gather_scratch(m, r, cross_c)
-        + [pltpu.VMEM((m, r, cross_c), BF16)]
+        + [pltpu.VMEM((m, r, cross_c), BF16)] * 6
         + [pltpu.VMEM((m, r, c), BF16)] * 2
         + row_sum_scratch(*enc_shape)
         + everywhere_scratch(*early.shape, dp)
-        + link_scratch(7 + 2 * m + len(everywhere_ways(dp)), 6),
+        + link_scratch(5 + 2 * m + len(everywhere_ways(dp)), 6),
         compiler_params=pltpu.CompilerParams(
             vmem_limit_bytes=VMEM_LIMIT, collective_id=5, has_side_effects=True
         ),
@@ -914,7 +1009,7 @@
             flops=24 * n * n * width, bytes_accessed=16 * n * width, transcendentals=n * n * heads // 2
         ),
         name="self_backward",
-    )(bounds, queries, keys, values, keys_t, grads, lse, inner, up_column, cross_sum, enc_terms, early)
+    )(bounds, queries, keys, values, keys_t, wide, w_out, mixed_t, lse, up_column, cross_sum, diagonal, enc_terms, early)
 
 
 def const(shape):
@@ -1503,8 +1598,9 @@
         down_sum.reshape(by_shard),
         heads,
     )
-    self_wide, self_rows_grad, self_sums, summed_down = middle(
-        second_grad, after_self, cross_rows_grad, norm_params[1], down_column
+    cross_sum = cross_sum.reshape(2, groups_count // 2, 2, w_rows, 4 * width)
+    self_wide, self_rows_grad, self_sums, summed_down, diagonal = middle(
+        second_grad, after_self, cross_rows_grad, norm_params[1], down_column, cross_sum
     )
     bias_cq_grad = blocks_placed([bias_cq_parts[d, 0] for d in range(4)])
     bias_cv_grad = blocks_placed([bias_cv_parts[d, 0] for d in range(4)])
@@ -1520,23 +1616,19 @@
     )
     early = jnp.pad(early, ((0, -early.shape[0] % 8), (0, 0)))
 
-    self_mixed_grad = dot_nn(self_wide, self_out_w).astype(BF16)
-    self_inner = jnp.sum(
-        self_mixed_t.reshape(heads, width // heads, 4 * own_rows).astype(F32)
-        * self_mixed_grad.T.reshape(heads, width // heads, 4 * own_rows).astype(F32),
-        axis=1,
-    )
-    self_dq_t, self_dk, self_dv, summed_up, summed_cross, encoder_grad, early = self_backward(
+    self_dq, self_dk, self_dv, summed_up, summed_cross, encoder_grad, early = self_backward(
         bounds,
         queries,
         key_rows,
         value_rows,
         key_rows.T,
-        self_mixed_grad,
+        self_wide,
+        self_out_w,
+        self_mixed_t,
         self_lse,
-        self_inner,
         up_column,
-        cross_sum.reshape(2, groups_count // 2, 2, w_rows, 4 * width),
+        cross_sum,
+        diagonal,
         enc_terms,
         early,
         heads,
@@ -1545,20 +1637,21 @@
     grad_so_t = lax.dot_general(
         self_wide, self_mixed_t, (((0,), (1,)), ((), ())), preferred_element_type=F32
     ).astype(BF16)
-    qkv_grad = jnp.concatenate([self_dq_t.T, self_dk, self_dv], axis=1)
-    first_terms = dot_nt(qkv_grad, self_w[:, : 3 * width]).astype(BF16)
-    self_grads = jnp.concatenate([dot_tn(first_in, qkv_grad).astype(BF16), grad_so_t], axis=1)
-    column_sums = jnp.sum(qkv_grad.astype(F32), axis=0)
 
     def only_own(part):
         out = jnp.zeros((model_width,), F32)
         return lax.dynamic_update_slice_in_dim(out, part, member * width, 0)
 
     late = jnp.zeros((8, model_width), F32)
-    late = late.at[2].set(only_own(column_sums[:width])).at[3].set(only_own(column_sums[2 * width :]))
+    late = late.at[2].set(only_own(jnp.sum(self_dq.astype(F32), axis=0)))
+    late = late.at[3].set(only_own(jnp.sum(self_dv.astype(F32), axis=0)))
     input_grad, summed_self, late = tail(
-        first_terms,
-        self_grads.reshape(groups_count // 2, 2, w_rows, 4 * width),
+        self_dq,
+        self_dk,
+        self_dv,
+        self_w,
+        first_in,
+        grad_so_t,
         block_in,
         self_rows_grad,
         norm_params[0],

time: 689 us -> 685 us (level)
  Pallas kernels: 534 us -> 551 us
  matrix products: 31.7 us -> 16.8 us
    dot_general x2 -> x0, matrix products: 13 us -> none  [the longest x1 6.93 us: dot_tn(): lax.dot_general(a, b, (((0,), (0,)), ((), ())), preferred_element_type=F32)]
    pallas_call x1, Pallas kernels: 62.9 us -> 74.2 us  [tail(): pl.pallas_call(functools.partial(tail_kernel, n=n, step_rows=512), in_spe...]
    pallas_call x1, Pallas kernels: 79.4 us -> 89.2 us  [cross_backward(): pl.pallas_call(functools.partial(cross_backward_kernel, heads=heads, bk=2...]
    unnamed x80 -> x64, local copies, waits for them, and re-layouts: 16.7 us -> 16.6 us
where the time goes in v6:
time: 685 us; the launch traced here: 676 us
  Pallas kernels  551 us (80%)
  local copies, waits for them, and re-layouts  45.8 us (7%)
  other arithmetic  29.8 us (4%)
  waiting for transfers between devices  28.4 us (4%)
  matrix products  16.8 us (2%)
    pallas_call x1, Pallas kernels, cross_backward(): pl.pallas_call(functools.partial(cross_backward_kernel, heads=heads, bk=2...  89.2 us
    pallas_call x1, Pallas kernels, cross_forward(): pl.pallas_call(functools.partial(cross_forward_kernel, heads=heads), grid...  83.1 us
    pallas_call x1, Pallas kernels, self_backward(): pl.pallas_call(functools.partial(self_backward_kernel, bk=bk, heads=heads...  82.4 us
    pallas_call x1, Pallas kernels, start_gather(): pl.pallas_call(functools.partial(start_kernel, n=n), in_specs=[ANY] * 4,...  77.3 us
    pallas_call x1, Pallas kernels, tail(): pl.pallas_call(functools.partial(tail_kernel, n=n, step_rows=512), in_spe...  74.2 us
    pallas_call x1, Pallas kernels, self_forward(): pl.pallas_call(functools.partial(self_forward_kernel, bk=bk, heads=heads,...  53.4 us
    pallas_call x1, Pallas kernels, feed_forward(): pl.pallas_call(functools.partial(feed_forward_kernel, chunks=chunks), gri...  51.7 us
    pallas_call x1, Pallas kernels, middle(): pl.pallas_call(functools.partial(middle_kernel, n=n), in_specs=[vmem, vme...  39.8 us
  transfers between devices with their start and end apart: 3, of which 2 were waited for; matrix products, arithmetic and copies ran while one was open for 1% of the time, Pallas kernels for 0%

profile of v6, /device:TPU:0, one launch (start us, length us, event | category | flops | bytes accessed | tf_op | source)
XLA Modules:
  0.0 676.1 jit_solution(7860483992858901099)
XLA Ops:
  0.7 1.6 fusion.17
  2.4 0.8 fusion.18
  3.1 1.6 convert_reduce_fusion
  4.7 1.8 fusion.2
  7.2 1.6 fusion.5.rows_ref
  8.8 0.9 pad_maximum_fusion.1
  9.6 77.3 %start_gather.1 = (bf16[2560,1024]{1,0:T(8,128)(2,1)}, bf16[1024,1024]{1,0:T(8,128)(2,1)}, bf16[4,2,128,1024]{3,2,1,0:T(8,128)(2,1)}, bf16[4,128,1024]{2,1,0:T(8,128)(2,1)}) custom-call(bf16[640,1024]{1,0:T(8,128)(2,1)} %fusion.5.rows_ref, bf16[256,1024]{1,0:T(8,128)(2,1)} %enc_ref.1, bf16[128,1024]{1,0:T(8,128)(2,1)} %get-tuple-element.203.self_ref, ...), custom_call_target="tpu_custom_call" | custom-call | bytes 104857600 | tf_op jit(solution)/shard_map/start_gather/pallas_call | solution.py:694
  86.9 6.6 fusion.9
  93.6 3.1 copy-done.2
  96.6 1.2 slice.229
  97.8 4.0 fusion.7
  101.8 1.0 copy-done.4
  102.9 1.6 copy.48.vt_ref
  104.4 1.7 copy.57
  106.1 1.5 copy.47.k_ref
  107.8 0.8 pad_maximum_fusion.shard_ref
  108.6 53.4 %self_forward.1 = (bf16[256,2560]{1,0:T(8,128)(2,1)}, f32[4,2560]{1,0:T(4,128)}, bf16[4,4,2,128,1024]{4,3,2,1,0:T(8,128)(2,1)}, bf16[4,128,2048]{2,1,0:T(8,128)(2,1)}) custom-call(s32[1,2]{1,0:T(1,128)} %b_ref.3, bf16[2560,256]{1,0:T(8,128)(2,1)} %get-tuple-element.156.q_ref, bf16[2560,256]{1,0:T(8,128)(2,1)} %copy.47.k_ref, bf16[256,2560]{1,0:T(8,128)(2,1)} %copy.48.vt_ref, ...), custom_call_target="tpu_custom_call" | custom-call | flops 20132659200 | bytes 5242880 | tf_op jit(solution)/shard_map/self_forward/pallas_call | solution.py:794
  162.0 5.4 convolution_convert_fusion
  167.4 3.4 constant_dynamic-slice_fusion.9
  171.3 4.7 collective-permute-done.1
  176.0 3.3 add_convert_fusion.1
  179.3 1.5 collective-permute-start.2
  180.8 1.9 slice.231.w_ref
  185.3 0.8 fusion.11.ok_ref
  186.7 23.7 %collective-permute-done.2 = bf16[640,1024]{1,0:T(8,128)(2,1)} collective-permute-done((bf16[640,1024]{1,0:T(8,128)(2,1)}, bf16[640,1024]{1,0:T(8,128)(2,1)}, u32[]{:S(2)}, u32[]{:S(2)}) %collective-permute-start.2) | collective-permute-done | bytes 1310752 | tf_op jit(solution)/shard_map/ppermute | solution.py:1457
  210.4 2.5 fusion.13
  213.4 1.5 add_convert_fusion.x_ref
  214.9 83.1 %cross_forward.1 = (bf16[4,640,256]{2,1,0:T(8,128)(2,1)}, bf16[4,1024,256]{2,1,0:T(8,128)(2,1)}, bf16[4,1024,256]{2,1,0:T(8,128)(2,1)}, bf16[4,256,640]{2,1,0:T(...) custom-call(f32[1024,1]{1,0:T(8,128)} %fusion.11.ok_ref, ...), custom_call_target="tpu_custom_call" | custom-call | flops 16106127360 | bytes 8388608 | tf_op jit(solution)/shard_map/cross_forward/pallas_call | solution.py:1102
  298.0 51.7 %feed_forward.1 = (f32[640,1024]{1,0:T(8,128)}, f32[640,1024]{1,0:T(8,128)}, bf16[640,1024]{1,0:T(8,128)(2,1)}, f32[8,1024]{1,0:T(8,128)}, bf16[2,1024,1024]{2,1...) custom-call(bf16[640,1024]{1,0:T(8,128)(2,1)} %get-tuple-element.89.x_ref, ...), custom_call_target="tpu_custom_call" | custom-call | flops 32212254720 | bytes 41943040 | tf_op jit(solution)/shard_map/feed_forward/pallas_call | solution.py:1239
  349.8 0.7 fusion.19
  351.6 89.2 %cross_backward.1 = (f32[640,1024]{1,0:T(8,128)}, bf16[1024,1024]{1,0:T(8,128)(2,1)}, bf16[2,1024,1024]{2,1,0:T(8,128)(2,1)}, f32[4,1,256]{2,1,0:T(1,128)}, f32[...) custom-call(f32[1024,1]{1,0:T(8,128)} %fusion.11.ok_ref, ...), custom_call_target="tpu_custom_call" | custom-call | flops 32212254720 | bytes 16777216 | tf_op jit(solution)/shard_map/cross_backward/pallas_call | solution.py:1398
  440.8 0.6 constant_dynamic-update-slice_fusion.5
  441.4 0.7 constant_dynamic-update-slice_fusion.4
  442.1 0.7 constant_dynamic-update-slice_fusion.3
  443.4 0.7 constant_dynamic-update-slice_fusion.9
  444.1 0.7 constant_dynamic-update-slice_fusion.8
  444.7 0.7 constant_dynamic-update-slice_fusion.7
  446.1 39.8 %middle.1 = (bf16[2560,1024]{1,0:T(8,128)(2,1)}, f32[640,1024]{1,0:T(8,128)}, f32[8,1024]{1,0:T(8,128)}, f32[128,1024]{1,0:T(8,128)}, bf16[4,128,1024]{2,1,0:T(8,128)(2,1)}) custom-call(f32[640,1024]{1,0:T(8,128)} %get-tuple-element.101.back_ref, f32[640,1024]{1,0:T(8,128)} %copy-done, f32[640,1024]{1,0:T(8,128)} %get-tuple-element.102.grad_ref, ...), custom_call_target="tpu_custom_call" | custom-call | bytes 104857600 | tf_op jit(solution)/shard_map/middle/pallas_call | solution.py:465
  485.8 0.8 slice.199
  486.6 4.8 convolution_convert_fusion.1.so_ref
  491.5 0.6 pad.9.early_ref
  492.2 82.4 %self_backward.1 = (bf16[2560,256]{1,0:T(8,128)(2,1)}, bf16[2560,256]{1,0:T(8,128)(2,1)}, bf16[2560,256]{1,0:T(8,128)(2,1)}, f32[128,1024]{1,0:T(8,128)}, f32[12...) custom-call(s32[1,2]{1,0:T(1,128)} %b_ref.3, bf16[2560,256]{1,0:T(8,128)(2,1)} %get-tuple-element.156.q_ref, ...), custom_call_target="tpu_custom_call" | custom-call | flops 40265318400 | bytes 10485760 | tf_op jit(solution)/shard_map/self_backward/pallas_call | solution.py:968
  574.6 1.5 fusion.15
  576.1 1.4 slice.223
  577.5 1.7 convert_reduce_fusion.2
  579.1 1.7 convert_reduce_fusion.1
  581.6 74.2 %tail.1 = (f32[640,1024]{1,0:T(8,128)}, f32[128,1024]{1,0:T(8,128)}, f32[8,1024]{1,0:T(8,128)}) custom-call(bf16[2560,256]{1,0:T(8,128)(2,1)} %get-tuple-element.115.dq_ref, bf16[2560,256]{1,0:T(8,128)(2,1)} %get-tuple-element.116.dk_ref, bf16[2560,256]{1,0:T(8,128)(2,1)} %get-tuple-element.117.dv_ref, bf16[1024,1024]{1,0:T(8,128)(2,1)} %bitcast.76, ...), custom_call_target="tpu_custom_call" | custom-call | bytes 104857600 | tf_op jit(solution)/shard_map/tail/pallas_call | solution.py:604
  655.8 1.0 slice_multiply_fusion
  656.9 0.9 multiply_bitcast_fusion.2
  657.8 0.7 multiply_bitcast_fusion.1
  658.5 0.8 multiply_bitcast_fusion.3
  659.3 1.4 fusion.16
  661.5 0.9 copy.52
  662.4 0.8 copy.53
  663.2 1.9 broadcast_multiply_fusion
  665.1 0.9 mul.204
  666.0 0.8 copy.54
  667.4 1.1 multiply_bitcast_fusion
  668.4 1.0 copy.55
  669.4 0.6 maximum_multiply_fusion.1
  670.1 1.5 copy.83
  671.6 1.2 copy-done.7
  672.8 1.5 copy.84
  674.7 1.0 copy.85
  (94 shorter events, 9.3 us)
Async XLA Ops:
  0.6 6.5 copy-start.1
  0.7 5.9 copy-start.12
  0.7 6.2 copy-start.14
  0.7 6.3 copy-start.17
  0.7 6.4 copy-start.18
  4.7 4.1 copy-start.16
  93.6 3.1 copy-start.2
  101.8 1.0 copy-start.4
  104.4 3.2 copy-start.10
  104.4 3.3 copy-start.11
  106.1 55.9 %copy-start.3 = (bf16[2560,256]{0,1:T(8,128)(2,1)}, bf16[2560,256]{0,1:T(8,128)(2,1)S(1)}, u32[]{:S(2)}) copy-start(bf16[2560,256]{0,1:T(8,128)(2,1)S(1)} %copy.57) | copy-start | bytes 3932164
  170.8 13.8 %copy-start.22 = (f32[4096]{0:T(1024)S(1)}, f32[4096]{0:T(1024)}, u32[]{:S(2)}) copy-start(f32[4096]{0:T(1024)} %param.33) | copy-start | bytes 49156
  170.8 5.2 collective-permute-start.1
  170.8 15.9 %collective-permute-start = (bf16[640,1024]{1,0:T(8,128)(2,1)}, bf16[640,1024]{1,0:T(8,128)(2,1)S(1)}, u32[]{:S(2)}, u32[]{:S(2)}) collective-permute-start(bf16[640,1024]{1,0:T(8,128)(2,1)} %get-tuple-element.157), channel_id=1, source_target_pairs={{0,1},{1,0},{2,3},{3,2},{4,5},{5,4},{6,7},{7,6},{8,9},{9,8},{10,11... | collective-permute-start | bytes 3932168 | tf_op jit(solution)/shard_map/ppermute | solution.py:1457
  171.3 14.8 %copy-start.15 = (f32[3,2,1024]{2,1,0:T(2,128)S(1)}, f32[3,2,1024]{2,1,0:T(2,128)}, u32[]{:S(2)}) copy-start(f32[3,2,1024]{2,1,0:T(2,128)} %param.24) | copy-start | bytes 73732
  179.3 31.1 %collective-permute-start.2 = (bf16[640,1024]{1,0:T(8,128)(2,1)}, bf16[640,1024]{1,0:T(8,128)(2,1)}, u32[]{:S(2)}, u32[]{:S(2)}) collective-permute-start(bf16[640,1024]{1,0:T(8,128)(2,1)} %add_convert_fusion.1), channel_id=1, source_target_pairs={{0,2},{1,3},{2,0},{3,1},{4,6},{5,7},{6,4},{7,5},{8,10},{9,11},{10,... | collective-permute-start | bytes 3932168 | tf_op jit(solution)/shard_map/ppermute | solution.py:1457
  213.0 2.0 copy-start
  446.0 40.6 %copy-start.24 = (f32[8,1024]{1,0:T(8,128)S(1)}, f32[8,1024]{1,0:T(8,128)}, u32[]{:S(2)}) copy-start(f32[8,1024]{1,0:T(8,128)} %get-tuple-element.111) | copy-start | bytes 98308
  446.1 40.6 %copy-start.5 = (bf16[256,2560]{1,0:T(8,128)(2,1)S(1)}, bf16[256,2560]{1,0:T(8,128)(2,1)}, u32[]{:S(2)}) copy-start(bf16[256,2560]{1,0:T(8,128)(2,1)} %get-tuple-element.85.mt_ref) | copy-start | bytes 3932164
  581.0 0.6 copy-start.13
  581.6 76.2 %copy-start.9 = (f32[128,1024]{1,0:T(8,128)S(1)}, f32[128,1024]{1,0:T(8,128)}, u32[]{:S(2)}) copy-start(f32[128,1024]{1,0:T(8,128)} %get-tuple-element.124) | copy-start | bytes 1572868
  661.5 8.6 %copy-start.6 = (f32[640,1024]{1,0:T(8,128)S(1)}, f32[640,1024]{1,0:T(8,128)}, u32[]{:S(2)}) copy-start(f32[640,1024]{1,0:T(8,128)} %get-tuple-element.218) | copy-start | bytes 7864324
  663.2 6.3 copy-start.19
  663.2 6.3 copy-start.20
  663.2 6.3 copy-start.21
  663.2 6.3 copy-start.23
  670.1 2.7 copy-start.7
  672.8 2.0 copy-start.8

commit v7 on v6

--- a/solution.py
+++ b/solution.py
@@ -215,43 +215,41 @@
 
 
 class Gather:
-    def __init__(self, links, near, far, buffers):
+    def __init__(self, links, near, far, from_x, from_y, buffers):
         y = links.dp % 2
-        self.column, self.over_y, self.over_x, self.got_y, self.got_x, self.sum_y, self.sum_x = buffers
+        self.column, self.over_y, self.over_x, self.add_y, self.add_x, self.sum_y, self.sum_x = buffers
         m = self.column.shape[0]
-        low, high = pl.ds(0, m // 2), pl.ds(m // 2, m // 2)
-        self.low, self.high = low, high
+        low, high = pl.ds(0, m // 2), pl.ds(m // 2, m - m // 2)
         self.loads = [
+            links.local(near.at[low, 1 - y], self.over_y),
+            links.local(far.at[high, y], self.over_x),
+            links.local(from_x, self.add_y),
+            links.local(from_y, self.add_x),
             links.local(near.at[:, y], self.column),
-            links.local(near.at[:, 1 - y], self.over_y),
-            links.local(far.at[:, y], self.over_x),
         ]
-        diagonal = far.at[:, 1 - y]
         self.first = [
-            links.copy(diagonal.at[low], self.got_y, X),
-            links.copy(diagonal.at[high], self.got_x, Y),
+            links.copy(far.at[low, y], self.sum_x.at[low], X),
+            links.copy(near.at[high, 1 - y], self.sum_y.at[high], Y),
         ]
         self.second = [
-            links.copy(self.over_x, self.sum_x, X),
-            links.copy(self.over_y, self.sum_y, Y),
+            links.copy(self.over_x, self.sum_x.at[high], X),
+            links.copy(self.over_y, self.sum_y.at[low], Y),
         ]
 
     def start(self):
-        for copy in self.loads + self.first:
+        for copy in self.first + self.loads:
             copy.start()
 
     def middle(self):
         for copy in self.loads:
             copy.wait()
-        for copy in self.first:
-            copy.wait_recv()
-        add_to(self.over_y.at[self.low], self.got_y)
-        add_to(self.over_x.at[self.high], self.got_x)
+        add_to(self.over_x, self.add_x)
+        add_to(self.over_y, self.add_y)
         for copy in self.second:
             copy.start()
 
     def end(self):
-        for copy in self.second:
+        for copy in self.first + self.second:
             copy.wait_recv()
         add_to(self.column, self.sum_y)
         add_to(self.column, self.sum_x)
@@ -262,7 +260,7 @@
 def gather_scratch(m, r, c):
     whole = pltpu.VMEM((m, r, c), BF16)
     half = pltpu.VMEM((m // 2, r, c), BF16)
-    return [whole] * 3 + [half] * 2 + [whole] * 2
+    return [whole] + [half] * 4 + [whole] * 2
 
 
 class GatherLast:
@@ -561,10 +559,6 @@
         add_to(columns[k], gots[k])
         collects[k].start(0)
     stages = len(collects[0].stages)
-    for step in range(stages - 1):
-        for k in range(2):
-            collects[k].finish(step)
-            collects[k].start(step + 1)
     held[0] = late_ref[...]
     core_near.wait_recv()
     for part, copy in zip(parts, over_x):
@@ -579,10 +573,15 @@
             held[0, 1:2, :] += jnp.sum(incoming, axis=0, keepdims=True)
 
         by_rows(half, 64, norm_back)
+        if part is parts[0]:
+            for step in range(stages - 1):
+                for k in range(2):
+                    collects[k].finish(step)
+                    collects[k].start(step + 1)
     steps = len(late.copies)
     for step in range(steps):
         late.start(step)
-        if step == 0:
+        if step == 1:
             for k in range(2):
                 collects[k].finish(stages - 1)
                 weights_out[:, k * c : (k + 1) * c] = columns[k][collects[k].z].astype(F32)
@@ -831,11 +830,10 @@
 
 def self_backward_kernel(
     b_ref, q_ref, k_ref, v_ref, kt_ref, wide_ref, w_ref, mt_ref, lse_ref,
-    up_ref, cross_ref, diagonal_ref, enc_ref, early_ref,
-    dq_ref, dk_ref, dv_ref, up_out, cross_out, enc_out, early_out, dka, dva, dqa, *scratch, bk, heads, safe, n
+    up_ref, cross_ref, diagonal_ref, enc_ref,
+    dq_ref, dk_ref, dv_ref, up_out, cross_out, enc_out, dka, dva, dqa, *scratch, bk, heads, safe, n
 ):
     i = pl.program_id(0)
-    last = pl.num_programs(0) - 1
     links = Links(*scratch[-3:])
     cross = GatherLast(links, cross_ref.at[0], cross_ref.at[1], diagonal_ref, scratch[:5])
     cross_z = Collect(links, cross.column, scratch[5])
@@ -843,14 +841,7 @@
     up_z = Collect(links, up_column, scratch[7])
     load = links.local(up_ref, up_column)
     enc = RowSum(links, enc_ref, scratch[8:13])
-    held = scratch[13]
-    early = Everywhere(links, held, scratch[14], n)
     stages = len(up_z.stages)
-    steps = len(early.copies)
-
-    def next_early(step):
-        early.finish(step)
-        early.start(step + 1)
 
     @pl.when(i == 0)
     def _():
@@ -858,8 +849,6 @@
         cross.start()
         enc.start()
         load.start()
-        held[0] = early_ref[...]
-        early.start(0)
         load.wait()
         up_z.start(0)
         dka[...] = jnp.zeros_like(dka)
@@ -868,23 +857,12 @@
     @pl.when(i == 1)
     def _():
         cross.middle()
-        next_early(0)
 
     @pl.when(i == 2)
     def _():
         for step in range(stages - 1):
             up_z.finish(step)
             up_z.start(step + 1)
-        next_early(1)
-
-    @pl.when(i == 3)
-    def _():
-        next_early(2)
-
-    @pl.when(i == last)
-    def _():
-        for step in range(3, steps - 1):
-            next_early(step)
 
     def sum_cross():
         cross.end()
@@ -947,15 +925,13 @@
             enc_out[rows, :] = enc.total(rows)
 
         by_rows(enc_out.shape[0], 64, store)
-        early.finish(steps - 1)
-        early_out[...] = held[steps]
         up_z.drain()
         cross_z.drain()
 
 
 def self_backward(
     bounds, queries, keys, values, keys_t, wide, w_out, mixed_t, lse,
-    up_column, cross_sum, diagonal, enc_terms, early, heads, safe
+    up_column, cross_sum, diagonal, enc_terms, heads, safe
 ):
     n, width = queries.shape
     model = wide.shape[1]
@@ -979,10 +955,9 @@
             pl.BlockSpec((width, bq), lambda i: (0, i)),
             pl.BlockSpec((heads, bq), lambda i: (0, i)),
         ]
-        + [ANY] * 4
-        + [const(early.shape)],
+        + [ANY] * 4,
         out_specs=[some, const((n, width)), const((n, width))]
-        + [const((r, c)), const((r, cross_c)), const(enc_shape), const(early.shape)],
+        + [const((r, c)), const((r, cross_c)), const(enc_shape)],
         out_shape=[
             jax.ShapeDtypeStruct((n, width), BF16),
             jax.ShapeDtypeStruct((n, width), BF16),
@@ -990,7 +965,6 @@
             jax.ShapeDtypeStruct((r, c), F32),
             jax.ShapeDtypeStruct((r, cross_c), F32),
             jax.ShapeDtypeStruct(enc_shape, F32),
-            jax.ShapeDtypeStruct(early.shape, F32),
         ],
         scratch_shapes=[
             pltpu.VMEM((n, width), F32),
@@ -1000,8 +974,7 @@
         + [pltpu.VMEM((m, r, cross_c), BF16)] * 6
         + [pltpu.VMEM((m, r, c), BF16)] * 2
         + row_sum_scratch(*enc_shape)
-        + everywhere_scratch(*early.shape, dp)
-        + link_scratch(5 + 2 * m + len(everywhere_ways(dp)), 6),
+        + link_scratch(5 + 2 * m, 6),
         compiler_params=pltpu.CompilerParams(
             vmem_limit_bytes=VMEM_LIMIT, collective_id=5, has_side_effects=True
         ),
@@ -1009,7 +982,7 @@
             flops=24 * n * n * width, bytes_accessed=16 * n * width, transcendentals=n * n * heads // 2
         ),
         name="self_backward",
-    )(bounds, queries, keys, values, keys_t, wide, w_out, mixed_t, lse, up_column, cross_sum, diagonal, enc_terms, early)
+    )(bounds, queries, keys, values, keys_t, wide, w_out, mixed_t, lse, up_column, cross_sum, diagonal, enc_terms)
 
 
 def const(shape):
@@ -1149,8 +1122,8 @@
 
 def feed_forward_kernel(
     x_ref, dy_ref, up_ref, down_ref, b_ref, after_ref, shift_ref, norm_ref,
-    out_ref, rows_out, low_out, sums_ref, gup_ref, gdown_ref, bias_ref,
-    xt_ref, dyt_ref, back_ref, give, got, send_sems, recv_sems, local_sems, *, chunks
+    out_ref, rows_out, low_out, sums_ref, gup_ref, gdown_ref, bias_ref, from_x, from_y,
+    xt_ref, dyt_ref, back_ref, give, got, diagonal, send_sems, recv_sems, local_sems, *, chunks
 ):
     s = pl.program_id(0)
     links = Links(send_sems, recv_sems, local_sems)
@@ -1159,6 +1132,14 @@
     pair = turn // 2
     slot = pair * chunks + chunk
     theirs = turn % 2 == 0
+    y = links.dp % 2
+    m, r = diagonal.shape[1], diagonal.shape[2]
+    low, high = pl.ds(0, m // 2), pl.ds(m // 2, m - m // 2)
+    links.used = 2 * chunks
+    across = [
+        links.copy(diagonal.at[:, low], from_x, X),
+        links.copy(diagonal.at[:, high], from_y, Y),
+    ]
     to_core = pltpu.make_async_remote_copy(
         src_ref=give.at[chunk],
         dst_ref=got.at[slot],
@@ -1170,7 +1151,7 @@
 
     @pl.when(s == 0)
     def _():
-        links.greet([CORE])
+        links.greet([CORE, X, Y])
         out_ref[...] = after_ref[...] + shift_ref[...]
         back_ref[...] = jnp.zeros_like(back_ref)
         xt_ref[...] = x_ref[...].T
@@ -1203,6 +1184,22 @@
         to_core.wait_recv()
         gup_ref[0] = (give[chunk, 0].astype(F32) + got[slot, 0].astype(F32)).astype(BF16)
         gdown_ref[0] = (give[chunk, 1].astype(F32) + got[slot, 1].astype(F32)).astype(BF16)
+
+    for k in range(chunks):
+
+        @pl.when(s == chunks + k)
+        def _():
+            def keep(z, carry):
+                rows = pl.ds(pl.multiple_of((2 * z + 1 - y) * r, r), r)
+                size = gup_ref.shape[2]
+                diagonal[0, z, :, k * size : (k + 1) * size] = gup_ref[0, rows, :]
+                diagonal[1, z, :, k * size : (k + 1) * size] = gdown_ref[0, rows, :]
+                return carry
+
+            lax.fori_loop(0, m, keep, 0)
+            if k == chunks - 1:
+                for copy in across:
+                    copy.start()
 
     @pl.when(s == pl.num_programs(0) - 1)
     def _():
@@ -1218,6 +1215,8 @@
                 sums_ref[k : k + 1, :] += jnp.sum(terms, axis=0, keepdims=True)
 
         by_rows(x_ref.shape[0], 128, norm_back)
+        for copy in across:
+            copy.wait()
 
 
 def feed_forward(x, dy, weights, bias, after, shift, norm):
@@ -1226,12 +1225,15 @@
     size = min(512, hidden)
     chunks = hidden // size
 
+    n = lax.axis_size("dp")
+    m, r = n // 2, width // n
+
     def block(s):
-        return (s // chunks) ^ 1
+        return 3 - s // chunks
 
     def placed(s):
         turn = s // chunks
-        return (turn // 2, 0, (s % chunks) * (turn % 2))
+        return (1 - turn // 2, 0, (s % chunks) * (turn % 2))
 
     rows_spec = const((rows, width))
     grad_spec = pl.BlockSpec((1, width, size), placed)
@@ -1249,7 +1251,7 @@
             const((1, width)),
             const((2, width)),
         ],
-        out_specs=[rows_spec, rows_spec, rows_spec, const((8, width)), grad_spec, grad_spec, bias_spec],
+        out_specs=[rows_spec, rows_spec, rows_spec, const((8, width)), grad_spec, grad_spec, bias_spec, ANY, ANY],
         out_shape=[
             jax.ShapeDtypeStruct((rows, width), F32),
             jax.ShapeDtypeStruct((rows, width), F32),
@@ -1258,6 +1260,8 @@
             jax.ShapeDtypeStruct((2, width, hidden), BF16),
             jax.ShapeDtypeStruct((2, width, hidden), BF16),
             jax.ShapeDtypeStruct((4, 1, hidden), F32),
+            jax.ShapeDtypeStruct((2, m // 2, r, hidden), BF16),
+            jax.ShapeDtypeStruct((2, m - m // 2, r, hidden), BF16),
         ],
         scratch_shapes=[
             pltpu.VMEM((width, rows), BF16),
@@ -1265,8 +1269,9 @@
             pltpu.VMEM((rows, width), F32),
             pltpu.VMEM((chunks, 2, width, size), BF16),
             pltpu.VMEM((2 * chunks, 2, width, size), BF16),
+            pltpu.VMEM((2, m, r, hidden), BF16),
         ]
-        + link_scratch(2 * chunks, 1),
+        + link_scratch(2 * chunks + 2, 1),
         compiler_params=pltpu.CompilerParams(
             vmem_limit_bytes=VMEM_LIMIT, collective_id=3, has_side_effects=True
         ),
@@ -1278,7 +1283,7 @@
 
 
 def cross_backward_kernel(
-    ok_ref, low_ref, x_ref, enc_ref, w_ref, q_ref, k_ref, v_ref, mt_ref, lse_ref, up_ref, down_ref,
+    ok_ref, low_ref, x_ref, enc_ref, w_ref, q_ref, k_ref, v_ref, mt_ref, lse_ref, up_ref, down_ref, from_x, from_y,
     back_ref, enc_out, grad_ref, bq_ref, bv_ref, up_out, down_out,
     low_t, x_t, enc_t, enc_acc, give, got, *scratch, heads, bk
 ):
@@ -1286,7 +1291,8 @@
     last = pl.num_programs(0) - 1
     links = Links(*scratch[14:])
     sums = [
-        Gather(links, ref.at[0], ref.at[1], scratch[7 * k : 7 * k + 7]) for k, ref in enumerate((up_ref, down_ref))
+        Gather(links, ref.at[0], ref.at[1], from_x.at[k], from_y.at[k], scratch[7 * k : 7 * k + 7])
+        for k, ref in enumerate((up_ref, down_ref))
     ]
     leave = [links.local(g.column, out) for g, out in zip(sums, (up_out, down_out))]
     pair = i // 2
@@ -1385,7 +1391,9 @@
             copy.wait()
 
 
-def cross_backward(ok, low, x, encoder, weights, queries, keys, values, mixed_t, lse, up_sum, down_sum, heads):
+def cross_backward(
+    ok, low, x, encoder, weights, queries, keys, values, mixed_t, lse, up_sum, down_sum, from_x, from_y, heads
+):
     count, model = x.shape
     n = encoder.shape[0]
     parts, _, columns = weights.shape
@@ -1409,6 +1417,8 @@
             by_part(n, width),
             by_part(width, count),
             by_part(heads, count),
+            ANY,
+            ANY,
             ANY,
             ANY,
         ],
@@ -1439,7 +1449,7 @@
             pltpu.VMEM((2, model, columns), BF16),
         ]
         + gather_scratch(m, r, c) * 2
-        + link_scratch(10, 8),
+        + link_scratch(10, 12),
         compiler_params=pltpu.CompilerParams(
             vmem_limit_bytes=60 * 2**20, collective_id=4, has_side_effects=True
         ),
@@ -1449,7 +1459,7 @@
             transcendentals=parts * count * n * heads,
         ),
         name="cross_backward",
-    )(ok, low, x, encoder, weights, queries, keys, values, mixed_t, lse, up_sum, down_sum)
+    )(ok, low, x, encoder, weights, queries, keys, values, mixed_t, lse, up_sum, down_sum, from_x, from_y)
 
 
 def swap(value, axis, distance):
@@ -1572,7 +1582,7 @@
         heads,
     )
 
-    output, cross_rows_grad, cross_low, ffn_sums, up_sum, down_sum, bias_up_parts = feed_forward(
+    output, cross_rows_grad, cross_low, ffn_sums, up_sum, down_sum, bias_up_parts, from_x, from_y = feed_forward(
         third_in,
         out_grad,
         ffn_w.reshape(4, model_width, 2 * hidden_width),
@@ -1596,6 +1606,8 @@
         cross_lse,
         up_sum.reshape(by_shard),
         down_sum.reshape(by_shard),
+        from_x,
+        from_y,
         heads,
     )
     cross_sum = cross_sum.reshape(2, groups_count // 2, 2, w_rows, 4 * width)
@@ -1606,17 +1618,7 @@
     bias_cv_grad = blocks_placed([bias_cv_parts[d, 0] for d in range(4)])
     bias_up_grad = blocks_placed([bias_up_parts[d, 0] for d in range(4)])
 
-    early = jnp.concatenate(
-        [
-            self_sums[:3],
-            ffn_sums[:4],
-            jnp.stack([bias_cq_grad, bias_cv_grad]),
-            bias_up_grad.reshape(-1, model_width),
-        ]
-    )
-    early = jnp.pad(early, ((0, -early.shape[0] % 8), (0, 0)))
-
-    self_dq, self_dk, self_dv, summed_up, summed_cross, encoder_grad, early = self_backward(
+    self_dq, self_dk, self_dv, summed_up, summed_cross, encoder_grad = self_backward(
         bounds,
         queries,
         key_rows,
@@ -1630,7 +1632,6 @@
         cross_sum,
         diagonal,
         enc_terms,
-        early,
         heads,
         self_safe,
     )
@@ -1642,10 +1643,27 @@
         out = jnp.zeros((model_width,), F32)
         return lax.dynamic_update_slice_in_dim(out, part, member * width, 0)
 
-    late = jnp.zeros((8, model_width), F32)
-    late = late.at[2].set(only_own(jnp.sum(self_dq.astype(F32), axis=0)))
-    late = late.at[3].set(only_own(jnp.sum(self_dv.astype(F32), axis=0)))
-    input_grad, summed_self, late = tail(
+    vectors = jnp.concatenate(
+        [
+            jnp.zeros((2, model_width), F32),
+            self_sums[:2],
+            ffn_sums[:2],
+            jnp.stack(
+                [
+                    only_own(jnp.sum(self_dq.astype(F32), axis=0)),
+                    only_own(jnp.sum(self_dv.astype(F32), axis=0)),
+                    self_sums[2],
+                    bias_cq_grad,
+                    bias_cv_grad,
+                    ffn_sums[2],
+                    ffn_sums[3],
+                ]
+            ),
+            bias_up_grad.reshape(-1, model_width),
+        ]
+    )
+    vectors = jnp.pad(vectors, ((0, -vectors.shape[0] % 8), (0, 0)))
+    input_grad, summed_self, vectors = tail(
         self_dq,
         self_dk,
         self_dv,
@@ -1655,13 +1673,11 @@
         block_in,
         self_rows_grad,
         norm_params[0],
-        late,
+        vectors,
     )
-    norm_total = jnp.stack([late[0], late[1], early[0], early[1], early[3], early[4]]).reshape(
-        norm_params.shape
-    )
-    bias_total = jnp.stack([late[2], late[3], early[2], early[7], early[8], early[5], early[6]])
-    up_total = early[9 : 9 + up_bias.shape[0] // model_width].reshape(-1)
+    norm_total = vectors[:6].reshape(norm_params.shape)
+    bias_total = vectors[6:13]
+    up_total = vectors[13 : 13 + up_bias.shape[0] // model_width].reshape(-1)
     scale = 1.0 / groups
     return (
         output,

time: 685 us -> 648 us (0.946)
  Pallas kernels: 551 us -> 524 us
  local copies, waits for them, and re-layouts: 45.8 us -> 36.9 us
    pallas_call x1, Pallas kernels: 82.4 us -> 65.6 us  [self_backward(): pl.pallas_call(functools.partial(self_backward_kernel, bk=bk, heads=heads...]
    pallas_call x1, Pallas kernels: 89.2 us -> 73.9 us  [cross_backward(): pl.pallas_call(functools.partial(cross_backward_kernel, heads=heads, bk=2...]
    unnamed x64 -> x62, local copies, waits for them, and re-layouts: 16.6 us -> 17 us
where the time goes in v7:
time: 648 us; the launch traced here: 639 us
  Pallas kernels  524 us (81%)
  local copies, waits for them, and re-layouts  36.9 us (6%)
  other arithmetic  29.4 us (5%)
  waiting for transfers between devices  28.4 us (4%)
  matrix products  16.8 us (3%)
    pallas_call x1, Pallas kernels, cross_forward(): pl.pallas_call(functools.partial(cross_forward_kernel, heads=heads), grid...  83.1 us
    pallas_call x1, Pallas kernels, start_gather(): pl.pallas_call(functools.partial(start_kernel, n=n), in_specs=[ANY] * 4,...  77.3 us
    pallas_call x1, Pallas kernels, tail(): pl.pallas_call(functools.partial(tail_kernel, n=n, step_rows=512), in_spe...  76 us
    pallas_call x1, Pallas kernels, cross_backward(): pl.pallas_call(functools.partial(cross_backward_kernel, heads=heads, bk=2...  73.9 us
    pallas_call x1, Pallas kernels, self_backward(): pl.pallas_call(functools.partial(self_backward_kernel, bk=bk, heads=heads...  65.6 us
    pallas_call x1, Pallas kernels, feed_forward(): pl.pallas_call(functools.partial(feed_forward_kernel, chunks=chunks), gri...  54.2 us
    pallas_call x1, Pallas kernels, self_forward(): pl.pallas_call(functools.partial(self_forward_kernel, bk=bk, heads=heads,...  53.4 us
    pallas_call x1, Pallas kernels, middle(): pl.pallas_call(functools.partial(middle_kernel, n=n), in_specs=[vmem, vme...  40.2 us
  transfers between devices with their start and end apart: 3, of which 2 were waited for; matrix products, arithmetic and copies ran while one was open for 1% of the time, Pallas kernels for 0%

profile of v7, /device:TPU:0, one launch (start us, length us, event | category | flops | bytes accessed | tf_op | source)
XLA Modules:
  0.0 639.5 jit_solution(4098944052359244987)
XLA Ops:
  0.7 1.6 fusion.16
  2.4 0.8 fusion.17
  3.1 1.6 convert_reduce_fusion
  4.7 1.8 fusion.2
  7.2 1.6 fusion.5.rows_ref
  8.8 0.9 pad_maximum_fusion.1
  9.6 77.3 %start_gather.1 = (bf16[2560,1024]{1,0:T(8,128)(2,1)}, bf16[1024,1024]{1,0:T(8,128)(2,1)}, bf16[4,2,128,1024]{3,2,1,0:T(8,128)(2,1)}, bf16[4,128,1024]{2,1,0:T(8,128)(2,1)}) custom-call(bf16[640,1024]{1,0:T(8,128)(2,1)} %fusion.5.rows_ref, bf16[256,1024]{1,0:T(8,128)(2,1)} %enc_ref.1, bf16[128,1024]{1,0:T(8,128)(2,1)} %get-tuple-element.177.self_ref, ...), custom_call_target="tpu_custom_call" | custom-call | bytes 104857600 | tf_op jit(solution)/shard_map/start_gather/pallas_call | solution.py:693
  86.9 6.6 %fusion.9 = f32[2560,768]{1,0:T(8,128)S(1)} fusion(bf16[2560,1024]{1,0:T(8,128)(2,1)} %get-tuple-element.59.first_ref, bf16[1024,1024]{1,0:T(8,128)(2,1)} %bitcast.73), kind=kOutput, calls=%fused_computation.20 | convolution fusion | flops 4026531840 | bytes 14680064 | tf_op jit(solution)/shard_map/dot_general | solution.py:24
  93.6 3.1 copy-done.2
  96.6 1.2 slice.178
  97.8 4.0 fusion.7
  101.8 1.0 copy-done.4
  102.9 1.6 copy.48.vt_ref
  104.4 1.7 copy.57
  106.1 1.5 copy.47.k_ref
  107.7 0.8 pad_maximum_fusion.shard_ref
  108.6 53.4 %self_forward.1 = (bf16[256,2560]{1,0:T(8,128)(2,1)}, f32[4,2560]{1,0:T(4,128)}, bf16[4,4,2,128,1024]{4,3,2,1,0:T(8,128)(2,1)}, bf16[4,128,2048]{2,1,0:T(8,128)(2,1)}) custom-call(s32[1,2]{1,0:T(1,128)} %b_ref.3, bf16[2560,256]{1,0:T(8,128)(2,1)} %get-tuple-element.134.q_ref, bf16[2560,256]{1,0:T(8,128)(2,1)} %copy.47.k_ref, bf16[256,2560]{1,0:T(8,128)(2,1)} %copy.48.vt_ref, ...), custom_call_target="tpu_custom_call" | custom-call | flops 20132659200 | bytes 5242880 | tf_op jit(solution)/shard_map/self_forward/pallas_call | solution.py:793
  162.0 5.4 convolution_convert_fusion
  167.3 3.4 constant_dynamic-slice_fusion.9
  170.8 0.5 collective-permute-start
  171.3 4.7 collective-permute-done.1
  176.0 3.3 add_convert_fusion.1
  179.3 1.5 collective-permute-start.2
  180.8 1.9 slice.180.w_ref
  182.7 0.6 broadcast_in_dim.10.bq_ref
  183.3 0.6 broadcast_in_dim.11.bv_ref
  184.6 0.6 broadcast_in_dim.24.b_ref
  185.3 0.8 fusion.11.ok_ref
  186.1 0.6 slice_bitcast_fusion
  186.7 23.7 %collective-permute-done.2 = bf16[640,1024]{1,0:T(8,128)(2,1)} collective-permute-done((bf16[640,1024]{1,0:T(8,128)(2,1)}, bf16[640,1024]{1,0:T(8,128)(2,1)}, u32[]{:S(2)}, u32[]{:S(2)}) %collective-permute-start.2) | collective-permute-done | bytes 1310752 | tf_op jit(solution)/shard_map/ppermute | solution.py:1467
  210.4 2.5 fusion.13
  213.0 0.4 multiply_reduce_fusion
  213.4 1.5 add_convert_fusion.x_ref
  214.9 83.1 %cross_forward.1 = (bf16[4,640,256]{2,1,0:T(8,128)(2,1)}, bf16[4,1024,256]{2,1,0:T(8,128)(2,1)}, bf16[4,1024,256]{2,1,0:T(8,128)(2,1)}, bf16[4,256,640]{2,1,0:T(...) custom-call(f32[1024,1]{1,0:T(8,128)} %fusion.11.ok_ref, ...), custom_call_target="tpu_custom_call" | custom-call | flops 16106127360 | bytes 8388608 | tf_op jit(solution)/shard_map/cross_forward/pallas_call | solution.py:1075
  298.0 54.2 %feed_forward.1 = (f32[640,1024]{1,0:T(8,128)}, f32[640,1024]{1,0:T(8,128)}, bf16[640,1024]{1,0:T(8,128)(2,1)}, f32[8,1024]{1,0:T(8,128)}, bf16[2,1024,1024]{2,1...) custom-call(bf16[640,1024]{1,0:T(8,128)(2,1)} %get-tuple-element.66., ...), custom_call_target="tpu_custom_call" | custom-call | flops 32212254720 | bytes 41943040 | tf_op jit(solution)/shard_map/feed_forward/pallas_call | solution.py:1241
  352.2 73.9 %cross_backward.1 = (f32[640,1024]{1,0:T(8,128)}, bf16[1024,1024]{1,0:T(8,128)(2,1)}, bf16[2,1024,1024]{2,1,0:T(8,128)(2,1)}, f32[4,1,256]{2,1,0:T(1,128)}, f32[...) custom-call(f32[1024,1]{1,0:T(8,128)} %fusion.11.ok_ref, ...), custom_call_target="tpu_custom_call" | custom-call | flops 32212254720 | bytes 16777216 | tf_op jit(solution)/shard_map/cross_backward/pallas_call | solution.py:1406
  426.2 40.2 %middle.1 = (bf16[2560,1024]{1,0:T(8,128)(2,1)}, f32[640,1024]{1,0:T(8,128)}, f32[8,1024]{1,0:T(8,128)}, f32[128,1024]{1,0:T(8,128)}, bf16[4,128,1024]{2,1,0:T(8,128)(2,1)}) custom-call(f32[640,1024]{1,0:T(8,128)} %get-tuple-element.80.back_ref, f32[640,1024]{1,0:T(8,128)} %copy-done, f32[640,1024]{1,0:T(8,128)} %get-tuple-element.81.grad_ref, ...), custom_call_target="tpu_custom_call" | custom-call | bytes 104857600 | tf_op jit(solution)/shard_map/middle/pallas_call | solution.py:463
  466.4 0.8 slice.152
  467.1 0.8 slice.154
  467.9 0.3 dynamic_update_slice.62
  469.2 4.8 convolution_convert_fusion.1.so_ref
  474.1 65.6 %self_backward.1 = (bf16[2560,256]{1,0:T(8,128)(2,1)}, bf16[2560,256]{1,0:T(8,128)(2,1)}, bf16[2560,256]{1,0:T(8,128)(2,1)}, f32[128,1024]{1,0:T(8,128)}, f32[128,1024]{1,0:T(8,128)}, /*index=5*/f32[256,1024]{1,0:T(8,128)}) custom-call(s32[1,2]{1,0:T(1,128)} %b_ref.3, bf16[2560,256]{1,0:T(8,128)(2,1)} %get-tuple-element.134.q_ref, ...), custom_call_target="tpu_custom_call" | custom-call | flops 40265318400 | bytes 10485760 | tf_op jit(solution)/shard_map/self_backward/pallas_call | solution.py:944
  539.7 1.7 convert_reduce_fusion.1
  541.3 1.7 convert_reduce_fusion.2
  543.3 0.7 pad.4.late_ref
  544.0 76.0 %tail.1 = (f32[640,1024]{1,0:T(8,128)}, f32[128,1024]{1,0:T(8,128)}, f32[24,1024]{1,0:T(8,128)}) custom-call(bf16[2560,256]{1,0:T(8,128)(2,1)} %get-tuple-element.89.dq_ref, bf16[2560,256]{1,0:T(8,128)(2,1)} %get-tuple-element.90.dk_ref, bf16[2560,256]{1,0:T(8,128)(2,1)} %get-tuple-element.91.dv_ref, bf16[1024,1024]{1,0:T(8,128)(2,1)} %bitcast.76, ...), custom_call_target="tpu_custom_call" | custom-call | bytes 104857600 | tf_op jit(solution)/shard_map/tail/pallas_call | solution.py:603
  620.0 1.1 slice_multiply_fusion
  621.1 1.0 multiply_bitcast_fusion.2
  622.0 0.8 slice_multiply_fusion.4
  622.8 0.8 multiply_bitcast_fusion.3
  623.7 1.5 slice_multiply_fusion.3
  625.1 0.7 multiply_bitcast_fusion.1
  626.0 0.9 copy.52
  626.9 0.8 copy.53
  627.7 0.6 mul.195
  628.3 0.6 copy.61
  628.9 0.8 broadcast_multiply_fusion
  629.7 0.9 mul.204
  630.6 0.8 copy.54
  631.4 1.0 copy.55
  632.4 3.7 copy.81
  636.1 1.5 copy.82
  637.6 0.5 copy-done.7
  638.1 1.0 copy.83
  (89 shorter events, 2.3 us)
Async XLA Ops:
  0.6 6.5 %copy-start.1 = (bf16[640,1024]{1,0:T(8,128)(2,1)S(1)}, bf16[640,1024]{1,0:T(8,128)(2,1)}, u32[]{:S(2)}) copy-start(bf16[640,1024]{1,0:T(8,128)(2,1)} %rows_ref.1) | copy-start | bytes 3932164
  0.7 5.9 copy-start.13
  0.7 6.2 copy-start.14
  0.7 6.3 copy-start.17
  0.7 6.4 copy-start.18
  4.7 4.1 copy-start.16
  93.6 3.1 copy-start.2
  101.8 1.0 copy-start.4
  104.4 3.1 copy-start.11
  104.4 3.3 copy-start.12
  106.1 55.9 %copy-start.3 = (bf16[2560,256]{0,1:T(8,128)(2,1)}, bf16[2560,256]{0,1:T(8,128)(2,1)S(1)}, u32[]{:S(2)}) copy-start(bf16[2560,256]{0,1:T(8,128)(2,1)S(1)} %copy.57) | copy-start | bytes 3932164
  170.8 13.8 %copy-start.19 = (f32[4096]{0:T(1024)S(1)}, f32[4096]{0:T(1024)}, u32[]{:S(2)}) copy-start(f32[4096]{0:T(1024)} %param.29) | copy-start | bytes 49156
  170.8 5.2 collective-permute-start.1
  170.8 15.9 %collective-permute-start = (bf16[640,1024]{1,0:T(8,128)(2,1)}, bf16[640,1024]{1,0:T(8,128)(2,1)S(1)}, u32[]{:S(2)}, u32[]{:S(2)}) collective-permute-start(bf16[640,1024]{1,0:T(8,128)(2,1)} %get-tuple-element.135), channel_id=1, source_target_pairs={{0,1},{1,0},{2,3},{3,2},{4,5},{5,4},{6,7},{7,6},{8,9},{9,8},{10,11... | collective-permute-start | bytes 3932168 | tf_op jit(solution)/shard_map/ppermute | solution.py:1467
  171.3 14.8 %copy-start.15 = (f32[3,2,1024]{2,1,0:T(2,128)S(1)}, f32[3,2,1024]{2,1,0:T(2,128)}, u32[]{:S(2)}) copy-start(f32[3,2,1024]{2,1,0:T(2,128)} %param.20) | copy-start | bytes 73732
  179.3 31.1 %collective-permute-start.2 = (bf16[640,1024]{1,0:T(8,128)(2,1)}, bf16[640,1024]{1,0:T(8,128)(2,1)}, u32[]{:S(2)}, u32[]{:S(2)}) collective-permute-start(bf16[640,1024]{1,0:T(8,128)(2,1)} %add_convert_fusion.1), channel_id=1, source_target_pairs={{0,2},{1,3},{2,0},{3,1},{4,6},{5,7},{6,4},{7,5},{8,10},{9,11},{10,... | collective-permute-start | bytes 3932168 | tf_op jit(solution)/shard_map/ppermute | solution.py:1467
  213.0 2.0 copy-start
  426.1 41.8 %copy-start.20 = (f32[4,1,1024]{2,1,0:T(1,128)S(1)}, f32[4,1,1024]{2,1,0:T(1,128)}, u32[]{:S(2)}) copy-start(f32[4,1,1024]{2,1,0:T(1,128)} %get-tuple-element.97) | copy-start | bytes 49156
  426.1 42.9 %copy-start.23 = (f32[4,1,256]{2,1,0:T(1,128)S(1)}, f32[4,1,256]{2,1,0:T(1,128)}, u32[]{:S(2)}) copy-start(f32[4,1,256]{2,1,0:T(1,128)} %get-tuple-element.96) | copy-start | bytes 12292
  426.1 43.0 %copy-start.22 = (f32[4,1,256]{2,1,0:T(1,128)S(1)}, f32[4,1,256]{2,1,0:T(1,128)}, u32[]{:S(2)}) copy-start(f32[4,1,256]{2,1,0:T(1,128)} %get-tuple-element.95) | copy-start | bytes 12292
  426.1 43.1 %copy-start.5 = (bf16[256,2560]{1,0:T(8,128)(2,1)S(1)}, bf16[256,2560]{1,0:T(8,128)(2,1)}, u32[]{:S(2)}) copy-start(bf16[256,2560]{1,0:T(8,128)(2,1)} %get-tuple-element.62.mt_ref) | copy-start | bytes 3932164
  539.7 3.4 copy-start.21
  544.0 81.2 %copy-start.10 = (f32[128,1024]{1,0:T(8,128)S(1)}, f32[128,1024]{1,0:T(8,128)}, u32[]{:S(2)}) copy-start(f32[128,1024]{1,0:T(8,128)} %get-tuple-element.102) | copy-start | bytes 1572868
  620.0 8.9 %copy-start.9 = (f32[128,1024]{1,0:T(8,128)S(1)}, f32[128,1024]{1,0:T(8,128)}, u32[]{:S(2)}) copy-start(f32[128,1024]{1,0:T(8,128)} %get-tuple-element.103) | copy-start | bytes 1572868
  621.1 10.3 %copy-start.8 = (f32[128,1024]{1,0:T(8,128)S(1)}, f32[128,1024]{1,0:T(8,128)}, u32[]{:S(2)}) copy-start(f32[128,1024]{1,0:T(8,128)} %get-tuple-element.104) | copy-start | bytes 1572868
  632.4 3.7 copy-start.6
  636.1 2.0 copy-start.7

commit v8 on v7

--- a/solution.py
+++ b/solution.py
@@ -328,6 +328,44 @@
         for stage in self.stages:
             for copy, _, _ in stage:
                 copy.wait_send()
+
+
+class SpreadFar:
+    def __init__(self, links, column, near, near_core, whole):
+        y = links.dp % 2
+        far, far_core = whole.at[2], whole.at[3]
+        m, _, c = column.shape
+        step = max(m // 4, 1)
+        self.local = [links.local(near, whole.at[0]), links.local(near_core, whole.at[1])]
+        self.over_x, self.over_y, self.core_x, self.core_y = [], [], [], []
+        for k in range(m // step):
+            for h in range(2):
+                z, part = pl.ds(k * step, step), pl.ds(h * (c // 2), c // 2)
+                own = far.at[z, y, :, part]
+                other = far.at[z, 1 - y, :, part]
+                self.over_x.append(links.copy(column.at[z, :, part], own, X))
+                self.over_y.append(links.copy(own, own, Y))
+                self.core_x.append(links.copy(own, far_core.at[z, y, :, part], CORE))
+                self.core_y.append(links.copy(other, far_core.at[z, 1 - y, :, part], CORE))
+
+    def start(self):
+        for copy in self.over_x + self.local:
+            copy.start()
+
+    def onward(self, k):
+        self.over_x[k].wait_recv()
+        self.over_y[k].start()
+        self.core_x[k].start()
+
+    def last(self, k):
+        self.over_y[k].wait_recv()
+        self.core_y[k].start()
+
+    def end(self):
+        for copy in self.over_x + self.over_y:
+            copy.wait_send()
+        for copy in self.local + self.core_x + self.core_y:
+            copy.wait()
 
 
 class RowSum:
@@ -626,122 +664,132 @@
     )(dq, dk, dv, w, first, so_grad, rows, grad, norm, late)
 
 
-def start_kernel(
-    rows_ref, enc_ref, self_ref, cross_ref, rows_out, enc_out, self_out, cross_out, send_sems, recv_sems, local_sems, *, n
-):
+def start_kernel(rows_ref, self_ref, cross_ref, rows_out, self_out, cross_out, send_sems, recv_sems, local_sems, *, n):
     links = Links(send_sems, recv_sems, local_sems)
     member, z, y = links.tensor, links.dp // 2, links.dp % 2
-    links.greet([CORE, X, Y] + z_ways(n))
-
-    def place(ref, index, size):
-        return ref.at[pl.ds(pl.multiple_of(index * size, size), size)]
-
-    groups = [(rows_ref, rows_out, rows_ref.shape[0]), (enc_ref, enc_out, enc_ref.shape[0])]
-    local, started, arrived = [], [], []
-    for source, target, size in groups:
-        local.append(links.local(source, place(target, member, size)))
-    local.append(links.local(self_ref, self_out.at[z, y]))
-    local.append(links.local(cross_ref, cross_out.at[z]))
-    for copy in local:
-        copy.start()
-
-    def go(copy):
-        copy.start()
-        started.append(copy)
-        return copy
-
-    def got(copy):
-        copy.wait_recv()
-        arrived.append(copy)
-
-    along_x = [go(links.copy(source, place(target, member, size), X)) for source, target, size in groups]
-    go(links.copy(self_ref, self_out.at[z, y], Y))
-    for source, target, size in groups:
-        go(links.copy(source, place(target, member, size), CORE))
+    count = rows_ref.shape[0]
+    half = count // 2
+    parts = [pl.ds(0, half), pl.ds(half, half)]
+
+    def place(distance):
+        return rows_out.at[pl.ds(pl.multiple_of((member ^ distance) * count, count), count)]
+
+    over_x = [links.copy(rows_ref.at[part], place(0).at[part], X) for part in parts]
+    over_core = [links.copy(rows_ref, place(0), CORE)]
+    over_core += [links.copy(place(2).at[part], place(2).at[part], CORE) for part in parts]
     self_stages = column_stages(links, self_ref, self_out.at[:, y], n)
     cross_stages = column_stages(links, cross_ref, cross_out, n)
+    over_y = [links.copy(self_ref, self_out.at[z, y], Y)]
+    local = [
+        links.local(rows_ref, place(0)),
+        links.local(self_ref, self_out.at[z, y]),
+        links.local(cross_ref, cross_out.at[z]),
+    ]
+    links.greet([CORE, X, Y] + z_ways(n))
+    for copy in over_x + over_y + over_core[:1] + local:
+        copy.start()
     for self_stage in self_stages:
         for copy, _ in self_stage:
-            go(copy)
+            copy.start()
         for copy, index in self_stage:
-            got(copy)
-            go(links.copy(self_out.at[index, y], self_out.at[index, y], Y))
+            copy.wait_recv()
+            onward = links.copy(self_out.at[index, y], self_out.at[index, y], Y)
+            onward.start()
+            over_y.append(onward)
         if self_stage is self_stages[0]:
             for copy, _ in cross_stages[0]:
-                go(copy)
-    for cross_stage, later in zip(cross_stages, cross_stages[1:]):
+                copy.start()
+    for cross_stage, later in zip(cross_stages, cross_stages[1:] + [[]]):
         for copy, _ in cross_stage:
-            got(copy)
+            copy.wait_recv()
         for copy, _ in later:
-            go(copy)
-    for copy, (_, target, size) in zip(along_x, groups):
-        got(copy)
-        there = place(target, member ^ 2, size)
-        go(links.copy(there, there, CORE))
-    for copy in local:
+            copy.start()
+    for copy, onward in zip(over_x, over_core[1:]):
+        copy.wait_recv()
+        onward.start()
+    for copy in local + over_y + over_core:
         copy.wait()
-    for copy in started:
+    for copy in over_x:
         copy.wait_send()
-        if not any(copy is other for other in arrived):
-            copy.wait_recv()
-
-
-def start_gather(rows_low, enc_low, self_shard, cross_shard):
+    for stage in self_stages + cross_stages:
+        for copy, _ in stage:
+            copy.wait_send()
+
+
+def start_gather(rows_low, self_shard, cross_shard):
     n = lax.axis_size("dp")
     r, c = self_shard.shape
-    copies = 3 * n + 8
     return pl.pallas_call(
         functools.partial(start_kernel, n=n),
-        in_specs=[ANY] * 4,
-        out_specs=[ANY] * 4,
+        in_specs=[ANY] * 3,
+        out_specs=[ANY] * 3,
         out_shape=[
             jax.ShapeDtypeStruct((4 * rows_low.shape[0], rows_low.shape[1]), BF16),
-            jax.ShapeDtypeStruct((4 * enc_low.shape[0], enc_low.shape[1]), BF16),
             jax.ShapeDtypeStruct((n // 2, 2, r, c), BF16),
             jax.ShapeDtypeStruct((n // 2,) + cross_shard.shape, BF16),
         ],
-        scratch_shapes=link_scratch(copies, 4),
+        scratch_shapes=link_scratch(2 * n + 8, 3),
         compiler_params=pltpu.CompilerParams(collective_id=0, has_side_effects=True),
         cost_estimate=pl.CostEstimate(flops=0, bytes_accessed=100 * 2**20, transcendentals=0),
         name="start_gather",
-    )(rows_low, enc_low, self_shard, cross_shard)
+    )(rows_low, self_shard, cross_shard)
 
 
 def self_forward_kernel(
-    b_ref, q_ref, k_ref, vt_ref, column_ref, shard_ref,
-    ot_ref, lse_ref, whole, next_column,
-    m_s, l_s, acc, send_sems, recv_sems, local_sems, *, bk, heads, safe, n
+    b_ref, x_ref, w_ref, bq_ref, bv_ref, column_ref, shard_ref, enc_ref,
+    q_out, k_ref, v_out, kt_out, ot_ref, lse_ref, terms_ref, whole, next_column, enc_out,
+    vt_ref, m_s, l_s, acc, send_sems, recv_sems, local_sems, *, bk, heads, safe, n
 ):
     i = pl.program_id(0)
     last = pl.num_programs(0) - 1
-    bq, width = q_ref.shape
+    bq, width = q_out.shape
     links = Links(send_sems, recv_sems, local_sems)
     spread = Spread(links, column_ref, whole)
-    keep = links.local(shard_ref, next_column.at[links.dp // 2])
     stages = column_stages(links, shard_ref, next_column, n)
+    enc_count = enc_ref.shape[0]
+
+    def place(distance):
+        return enc_out.at[pl.ds(pl.multiple_of((links.tensor ^ distance) * enc_count, enc_count), enc_count)]
+
+    enc_x = links.copy(enc_ref, place(0), X)
+    enc_core = [links.copy(enc_ref, place(0), CORE), links.copy(place(2), place(2), CORE)]
+    local = [links.local(shard_ref, next_column.at[links.dp // 2]), links.local(enc_ref, place(0))]
 
     @pl.when(i == 0)
     def _():
         links.greet([CORE, X, Y] + z_ways(n))
         spread.start()
-        keep.start()
+        for copy in local + enc_core[:1]:
+            copy.start()
         for copy, _ in stages[0]:
             copy.start()
 
     @pl.when(i == last)
     def _():
         spread.middle()
+        enc_x.start()
         for k in range(1, len(stages)):
             for copy, _ in stages[k - 1]:
                 copy.wait_recv()
             for copy, _ in stages[k]:
                 copy.start()
 
-    hd = width // heads
+    projected = dot_nn(x_ref[...], w_ref[:, : 3 * width])
+    query = (projected[:, :width] + bq_ref[...]).astype(BF16)
+    key = projected[:, width : 2 * width].astype(BF16)
+    value = (projected[:, 2 * width :] + bv_ref[...]).astype(BF16)
+    here = pl.ds(pl.multiple_of(i * bq, bq), bq)
+    q_out[...] = query
+    v_out[...] = value
+    kt_out[...] = key.T
+    k_ref[here, :] = key
+    vt_ref[:, here] = value.T
+
     m_s[...] = jnp.full_like(m_s, NEGATIVE)
     l_s[...] = jnp.zeros_like(l_s)
     acc[...] = jnp.zeros_like(acc)
-    scaled = q_ref[...] * jnp.asarray(1.0 / math.sqrt(hd), BF16)
+    hd = width // heads
+    scaled = query * jnp.asarray(1.0 / math.sqrt(hd), BF16)
     q_heads = [head_only(scaled, h, hd) for h in range(heads)]
 
     def block(j, mode):
@@ -773,51 +821,76 @@
         part = slice(h * hd, (h + 1) * hd)
         ot_ref[part, :] = (acc[part, :] * inverse[h : h + 1, :]).astype(BF16)
     lse_ref[...] = m_s[...] + jnp.log(l_s[...])
+    terms_ref[...] = dot_nt(ot_ref[...].T, w_ref[:, 3 * width :]).astype(BF16)
 
     @pl.when(i == last)
     def _():
         spread.end()
-        keep.wait()
+        enc_x.wait_recv()
+        enc_core[1].start()
         for k, stage in enumerate(stages):
             for copy, _ in stage:
                 copy.wait_send()
                 if k == len(stages) - 1:
                     copy.wait_recv()
-
-
-def self_forward(bounds, queries, keys, values_t, column, shard, heads, safe):
-    n, width = queries.shape
+        enc_x.wait_send()
+        for copy in local + enc_core:
+            copy.wait()
+
+
+def self_forward(bounds, x, w, q_shift, v_shift, column, shard, encoder, heads, safe):
+    n, model = x.shape
+    width = w.shape[1] // 4
     bq = bk = 512
     dp = lax.axis_size("dp")
     m, r, c = column.shape
+    enc_count = encoder.shape[0]
+    by_rows_spec = pl.BlockSpec((bq, width), lambda i: (i, 0))
+    by_columns_spec = pl.BlockSpec((width, bq), lambda i: (0, i))
     return pl.pallas_call(
         functools.partial(self_forward_kernel, bk=bk, heads=heads, safe=safe, n=dp),
         grid=(n // bq,),
         in_specs=[
             pl.BlockSpec(memory_space=pltpu.SMEM),
-            pl.BlockSpec((bq, width), lambda i: (i, 0)),
-            pl.BlockSpec((n, width), lambda i: (0, 0)),
-            pl.BlockSpec((width, n), lambda i: (0, 0)),
+            pl.BlockSpec((bq, model), lambda i: (i, 0)),
+            const((model, 4 * width)),
+            const((1, width)),
+            const((1, width)),
+            ANY,
             ANY,
             ANY,
         ],
         out_specs=[
-            pl.BlockSpec((width, bq), lambda i: (0, i)),
+            by_rows_spec,
+            const((n, width)),
+            by_rows_spec,
+            by_columns_spec,
+            by_columns_spec,
             pl.BlockSpec((heads, bq), lambda i: (0, i)),
-        ]
-        + [ANY] * 2,
+            pl.BlockSpec((bq, model), lambda i: (i, 0)),
+            ANY,
+            ANY,
+            ANY,
+        ],
         out_shape=[
+            jax.ShapeDtypeStruct((n, width), BF16),
+            jax.ShapeDtypeStruct((n, width), BF16),
+            jax.ShapeDtypeStruct((n, width), BF16),
+            jax.ShapeDtypeStruct((width, n), BF16),
             jax.ShapeDtypeStruct((width, n), BF16),
             jax.ShapeDtypeStruct((heads, n), F32),
-        ]
-        + [jax.ShapeDtypeStruct((4, m, 2, r, c), BF16)]
-        + [jax.ShapeDtypeStruct((m,) + shard.shape, BF16)],
+            jax.ShapeDtypeStruct((n, model), BF16),
+            jax.ShapeDtypeStruct((4, m, 2, r, c), BF16),
+            jax.ShapeDtypeStruct((m,) + shard.shape, BF16),
+            jax.ShapeDtypeStruct((4 * enc_count, model), BF16),
+        ],
         scratch_shapes=[
+            pltpu.VMEM((width, n), BF16),
             pltpu.VMEM((heads, bq), F32),
             pltpu.VMEM((heads, bq), F32),
             pltpu.VMEM((width, bq), F32),
         ]
-        + link_scratch(8 + m, 2),
+        + link_scratch(11 + m, 3),
         compiler_params=pltpu.CompilerParams(
             vmem_limit_bytes=VMEM_LIMIT, collective_id=1, has_side_effects=True
         ),
@@ -825,7 +898,66 @@
             flops=12 * n * n * width, bytes_accessed=8 * n * width, transcendentals=n * n * heads // 2
         ),
         name="self_forward",
-    )(bounds, queries, keys, values_t, column, shard)
+    )(bounds, x, w, q_shift, v_shift, column, shard, encoder)
+
+
+def after_self_kernel(
+    terms_ref, rows_ref, shift_ref, norm_ref, column_ref,
+    after_out, second_out, near_out, core_out, *scratch
+):
+    links = Links(*scratch[-3:])
+    rows_sum = RowSum(links, terms_ref, scratch[:5])
+    y = links.dp % 2
+    own = links.local(column_ref, near_out.at[:, y])
+    over_y = links.copy(column_ref, near_out.at[:, y], Y)
+    over_core = [
+        links.copy(column_ref, core_out.at[:, y], CORE),
+        links.copy(near_out.at[:, 1 - y], core_out.at[:, 1 - y], CORE),
+    ]
+    links.greet([CORE, X, Y])
+    rows_sum.start()
+    over_y.start()
+    own.start()
+    rows_sum.middle()
+    over_core[0].start()
+    rows_sum.end()
+
+    def norm(rows):
+        after = rows_ref[rows, :].astype(F32) + rows_sum.total(rows) + shift_ref[...]
+        after_out[rows, :] = after
+        xhat, _ = normalized(after)
+        second_out[rows, :] = (xhat * norm_ref[0:1, :] + norm_ref[1:2, :]).astype(BF16)
+
+    by_rows(after_out.shape[0], 64, norm)
+    over_y.wait_recv()
+    over_core[1].start()
+    over_y.wait_send()
+    own.wait()
+    for copy in over_core:
+        copy.wait()
+
+
+def sum_after_self(terms, rows, shift, norm, column):
+    count, model = rows.shape
+    m, r, c = column.shape
+    vmem = pl.BlockSpec(memory_space=pltpu.VMEM)
+    return pl.pallas_call(
+        after_self_kernel,
+        in_specs=[ANY, vmem, vmem, vmem, ANY],
+        out_specs=[vmem, vmem, ANY, ANY],
+        out_shape=[
+            jax.ShapeDtypeStruct((count, model), F32),
+            jax.ShapeDtypeStruct((count, model), BF16),
+            jax.ShapeDtypeStruct((m, 2, r, c), BF16),
+            jax.ShapeDtypeStruct((m, 2, r, c), BF16),
+        ],
+        scratch_shapes=row_sum_scratch(count, model) + link_scratch(6, 3),
+        compiler_params=pltpu.CompilerParams(
+            vmem_limit_bytes=VMEM_LIMIT, collective_id=8, has_side_effects=True
+        ),
+        cost_estimate=pl.CostEstimate(flops=0, bytes_accessed=100 * 2**20, transcendentals=0),
+        name="sum_after_self",
+    )(terms, rows, shift, norm, column)
 
 
 def self_backward_kernel(
@@ -877,7 +1009,7 @@
     bq, width = q_ref.shape
     hd = width // heads
     scale = 1.0 / math.sqrt(hd)
-    grads = dot_nn(wide_ref[...], w_ref[...]).astype(BF16)
+    grads = dot_nn(wide_ref[...], w_ref[:, 3 * width :]).astype(BF16)
     products = grads.T.astype(F32) * mt_ref[...].astype(F32)
     inner = [jnp.sum(products[h * hd : (h + 1) * hd, :], axis=0, keepdims=True) for h in range(heads)]
     scaled = q_ref[...] * jnp.asarray(scale, BF16)
@@ -930,7 +1062,7 @@
 
 
 def self_backward(
-    bounds, queries, keys, values, keys_t, wide, w_out, mixed_t, lse,
+    bounds, queries, keys, values, keys_t, wide, w, mixed_t, lse,
     up_column, cross_sum, diagonal, enc_terms, heads, safe
 ):
     n, width = queries.shape
@@ -951,7 +1083,7 @@
             const((n, width)),
             const((width, n)),
             pl.BlockSpec((bq, model), lambda i: (i, 0)),
-            const((model, width)),
+            const((model, 4 * width)),
             pl.BlockSpec((width, bq), lambda i: (0, i)),
             pl.BlockSpec((heads, bq), lambda i: (0, i)),
         ]
@@ -982,7 +1114,7 @@
             flops=24 * n * n * width, bytes_accessed=16 * n * width, transcendentals=n * n * heads // 2
         ),
         name="self_backward",
-    )(bounds, queries, keys, values, keys_t, wide, w_out, mixed_t, lse, up_column, cross_sum, diagonal, enc_terms)
+    )(bounds, queries, keys, values, keys_t, wide, w, mixed_t, lse, up_column, cross_sum, diagonal, enc_terms)
 
 
 def const(shape):
@@ -1011,19 +1143,27 @@
 
 
 def cross_forward_kernel(
-    ok_ref, x_ref, enc_ref, w_ref, bq_ref, bv_ref, rows_ref, shift_ref, norm_ref, column_ref,
+    ok_ref, x_ref, enc_ref, w_ref, bq_ref, bv_ref, rows_ref, shift_ref, norm_ref, column_ref, near_ref, core_ref,
     q_out, k_out, v_out, ot_ref, lse_ref, after_ref, third_ref, whole, send_sems, recv_sems, local_sems, *, heads
 ):
     i = pl.program_id(0)
     last = pl.num_programs(0) - 1
     links = Links(send_sems, recv_sems, local_sems)
-    spread = Spread(links, column_ref, whole)
+    spread = SpreadFar(links, column_ref, near_ref, core_ref, whole)
+    pieces = len(spread.over_x)
 
     @pl.when(i == 0)
     def _():
         links.greet([CORE, X, Y])
         spread.start()
         after_ref[...] = rows_ref[...] + shift_ref[...]
+
+    for step, ready in ((1, (0,)), (2, (1, 2)), (3, (3,))):
+
+        @pl.when(i == step)
+        def _():
+            for k in ready:
+                spread.onward(k)
 
     width = q_out.shape[2]
     hd = width // heads
@@ -1052,17 +1192,19 @@
 
     @pl.when(i == last)
     def _():
-        spread.middle()
-
         def norm(rows):
             xhat, _ = normalized(after_ref[rows, :])
             third_ref[rows, :] = (xhat * norm_ref[0:1, :] + norm_ref[1:2, :]).astype(BF16)
 
         by_rows(after_ref.shape[0], 128, norm)
+        for k in range(4, pieces):
+            spread.onward(k)
+        for k in range(pieces):
+            spread.last(k)
         spread.end()
 
 
-def cross_forward(ok, x, encoder, weights, q_shift, v_shift, rows, shift, norm, column, heads):
+def cross_forward(ok, x, encoder, weights, q_shift, v_shift, rows, shift, norm, column, near, near_core, heads):
     count, model = x.shape
     n = encoder.shape[0]
     parts, _, columns = weights.shape
@@ -1085,6 +1227,8 @@
             const((count, model)),
             const((1, model)),
             const((2, model)),
+            ANY,
+            ANY,
             ANY,
         ],
         out_specs=[
@@ -1107,7 +1251,7 @@
             jax.ShapeDtypeStruct((count, model), BF16),
             jax.ShapeDtypeStruct((4, m, 2, r, c), BF16),
         ],
-        scratch_shapes=link_scratch(8, 1),
+        scratch_shapes=link_scratch(32, 2),
         compiler_params=pltpu.CompilerParams(
             vmem_limit_bytes=VMEM_LIMIT, collective_id=2, has_side_effects=True
         ),
@@ -1117,7 +1261,7 @@
             transcendentals=parts * count * n * heads,
         ),
         name="cross_forward",
-    )(ok, x, encoder, weights, q_shift, v_shift, rows, shift, norm, column)
+    )(ok, x, encoder, weights, q_shift, v_shift, rows, shift, norm, column, near, near_core)
 
 
 def feed_forward_kernel(
@@ -1462,37 +1606,6 @@
     )(ok, low, x, encoder, weights, queries, keys, values, mixed_t, lse, up_sum, down_sum, from_x, from_y)
 
 
-def swap(value, axis, distance):
-    size = lax.axis_size(axis)
-    return lax.ppermute(value, axis, [(i, i ^ distance) for i in range(size)])
-
-
-def dp_distances():
-    n = lax.axis_size("dp")
-    found = []
-    while n > 1:
-        n //= 2
-        found.append(n)
-    return found
-
-
-def add_low(a, b):
-    return (a.astype(F32) + b.astype(F32)).astype(BF16)
-
-
-def narrow(rows_low):
-    member = lax.axis_index("tensor")
-    count = rows_low.shape[0] // 4
-    parts = [
-        lax.dynamic_slice_in_dim(rows_low, (member ^ distance) * count, count, 0)
-        for distance in range(4)
-    ]
-    far = add_low(parts[2], swap(parts[3], "tensor", 1))
-    got = swap(far, "tensor", 2)
-    near = parts[0].astype(F32) + swap(parts[1], "tensor", 1).astype(F32)
-    return near + got.astype(F32)
-
-
 def on_device(
     block_in,
     encoder_out,
@@ -1530,40 +1643,32 @@
             out = lax.dynamic_update_slice_in_dim(out, part, (member ^ distance) * size, 0)
         return out
 
-    start_rows = block_in.astype(F32)
-    first_in, enc_all, self_w, cross_column = start_gather(
-        layer_norm(start_rows, norm_params[0, 0], norm_params[0, 1]).astype(BF16),
-        encoder_out,
+    first_in, self_w, cross_column = start_gather(
+        layer_norm(block_in.astype(F32), norm_params[0, 0], norm_params[0, 1]).astype(BF16),
         jnp.concatenate([w_qkv.reshape(w_rows, 3 * width), w_self_out.T], axis=1),
         jnp.concatenate([w_cross_q, w_cross_kv.reshape(w_rows, 2 * width), w_cross_out.T], axis=1),
     )
     self_w = self_w.reshape(model_width, 4 * width)
 
-    projected = dot_nn(first_in, self_w[:, : 3 * width])
-    queries = (projected[:, :width] + block_of(biases[0], width, 0)).astype(BF16)
-    key_rows = projected[:, width : 2 * width].astype(BF16)
-    value_rows = (projected[:, 2 * width :] + block_of(biases[1], width, 0)).astype(BF16)
     self_safe = 1024
-    self_mixed_t, self_lse, cross_w, ffn_column = self_forward(
+    queries, key_rows, value_rows, keys_t, self_mixed_t, self_lse, terms, cross_w, ffn_column, enc_all = self_forward(
         bounds,
-        queries,
-        key_rows,
-        value_rows.T,
+        first_in,
+        self_w,
+        block_of(biases[0], width, 0)[None],
+        block_of(biases[1], width, 0)[None],
         cross_column,
         jnp.concatenate([w_up, w_down.T], axis=1),
+        encoder_out,
         heads,
         self_safe,
     )
     cross_w = cross_w.reshape(4, model_width, 4 * width)
-    self_out_w = self_w[:, 3 * width :]
-    after_self = (
-        start_rows
-        + narrow(lax.dot_general(self_mixed_t, self_out_w, (((0,), (1,)), ((), ())), preferred_element_type=F32).astype(BF16))
-        + biases[2]
+    after_self, second_in, ffn_near, ffn_near_core = sum_after_self(
+        terms, block_in, biases[2:3], norm_params[1], ffn_column
     )
 
     ok = (jnp.arange(4 * enc_rows, dtype=jnp.int32) < enc_lengths[0]).astype(F32)[:, None]
-    second_in = layer_norm(after_self, norm_params[1, 0], norm_params[1, 1]).astype(BF16)
 
     def all_blocks(vector, size):
         return jnp.stack([block_of(vector, size, d) for d in range(4)])[:, None]
@@ -1579,6 +1684,8 @@
         biases[5:6],
         norm_params[2],
         ffn_column,
+        ffn_near,
+        ffn_near_core,
         heads,
     )
 
@@ -1623,9 +1730,9 @@
         queries,
         key_rows,
         value_rows,
-        key_rows.T,
+        keys_t,
         self_wide,
-        self_out_w,
+        self_w,
         self_mixed_t,
         self_lse,
         up_column,

time: 648 us -> 833 us (1.29)
  Pallas kernels: 524 us -> 774 us
  waiting for transfers between devices: 28.4 us -> 0 us
  other arithmetic: 29.4 us -> 17.4 us
  matrix products: 16.8 us -> 4.9 us
  local copies, waits for them, and re-layouts: 36.9 us -> 26.6 us
    pallas_call x1, Pallas kernels: 83.1 us -> 264 us  [cross_forward(): pl.pallas_call(functools.partial(cross_forward_kernel, heads=heads), grid...]
    pallas_call x1 -> x2, Pallas kernels: 77.3 us -> 131 us  [the longest x1 69.5 us: sum_after_self(): pl.pallas_call(after_self_kernel, in_specs=[ANY, vmem, vmem, vmem, ANY],...]
    ppermute x3 -> x0, waiting for transfers between devices: 28.4 us -> none  [swap(): return lax.ppermute(value, axis, [(i, i ^ distance) for i in range(size)])]
    pallas_call x1, Pallas kernels: 53.4 us -> 70.3 us  [self_forward(): pl.pallas_call(functools.partial(self_forward_kernel, bk=bk, heads=heads,...]
    dot_general x2 -> x0, matrix products: 12 us -> none  [the longest x1 6.64 us: dot_nn(): lax.dot_general(a, b, (((1,), (0,)), ((), ())), preferred_element_type=F32)]
    convert_element_type x4 -> x1, other arithmetic: 10.5 us -> 1.6 us  [on_device(): layer_norm(block_in.astype(F32), norm_params[0, 0], norm_params[0, 1])]
    unnamed x62 -> x47, local copies, waits for them, and re-layouts: 17 us -> 10.3 us
  transfers between devices with their start and end apart: 3 -> 0, of which waited for: 2 -> 0; matrix products, arithmetic and copies ran while one was open for 1% -> 0% of each run, Pallas kernels for 0% -> 0%
where the time goes in v8:
time: 833 us; the launch traced here: 825 us
  Pallas kernels  774 us (93%)
  local copies, waits for them, and re-layouts  26.6 us (3%)
  other arithmetic  17.4 us (2%)
    pallas_call x1, Pallas kernels, cross_forward(): pl.pallas_call(functools.partial(cross_forward_kernel, heads=heads), grid...  264 us
    pallas_call x1, Pallas kernels, tail(): pl.pallas_call(functools.partial(tail_kernel, n=n, step_rows=512), in_spe...  75.6 us
    pallas_call x1, Pallas kernels, cross_backward(): pl.pallas_call(functools.partial(cross_backward_kernel, heads=heads, bk=2...  74.9 us
    pallas_call x1, Pallas kernels, self_forward(): pl.pallas_call(functools.partial(self_forward_kernel, bk=bk, heads=heads,...  70.3 us
    pallas_call x1, Pallas kernels, sum_after_self(): pl.pallas_call(after_self_kernel, in_specs=[ANY, vmem, vmem, vmem, ANY],...  69.5 us
    pallas_call x1, Pallas kernels, self_backward(): pl.pallas_call(functools.partial(self_backward_kernel, bk=bk, heads=heads...  66.3 us
    pallas_call x1, Pallas kernels, start_gather(): pl.pallas_call(functools.partial(start_kernel, n=n), in_specs=[ANY] * 3,...  61.2 us
    pallas_call x1, Pallas kernels, feed_forward(): pl.pallas_call(functools.partial(feed_forward_kernel, chunks=chunks), gri...  53.1 us

profile of v8, /device:TPU:0, one launch (start us, length us, event | category | flops | bytes accessed | tf_op | source)
XLA Modules:
  0.0 825.4 jit_solution(16607020215311090174)
XLA Ops:
  0.7 1.6 fusion.8
  2.4 0.6 broadcast_in_dim.20.bq_ref
  3.0 0.6 broadcast_in_dim.21.bv_ref
  3.6 0.6 constant_dynamic-slice_fusion.8
  4.1 1.6 convert_reduce_fusion
  5.8 1.9 fusion.2
  7.7 1.6 fusion.5.rows_ref
  9.3 0.2 copy.36
  9.5 0.2 copy.38
  9.7 0.1 copy.37
  9.9 0.9 pad_maximum_fusion.1
  10.8 61.2 %start_gather.1 = (bf16[2560,1024]{1,0:T(8,128)(2,1)}, bf16[4,2,128,1024]{3,2,1,0:T(8,128)(2,1)}, bf16[4,128,1024]{2,1,0:T(8,128)(2,1)}) custom-call(bf16[640,1024]{1,0:T(8,128)(2,1)} %fusion.5.rows_ref, bf16[128,1024]{1,0:T(8,128)(2,1)} %get-tuple-element.181.self_ref, bf16[128,1024]{1,0:T(8,128)(2,1)} %get-tuple-element.182.cross_ref), custom_call_target="tpu_custom_call" | custom-call | bytes 104857600 | tf_op jit(solution)/shard_map/start_gather/pallas_call | solution.py:722
  72.0 0.1 copy.40
  72.2 0.8 pad_maximum_fusion.shard_ref
  73.0 70.3 %self_forward.1 = (bf16[2560,256]{1,0:T(8,128)(2,1)}, bf16[2560,256]{1,0:T(8,128)(2,1)}, bf16[2560,256]{1,0:T(8,128)(2,1)}, bf16[256,2560]{1,0:T(8,128)(2,1)}, b...) custom-call(s32[1,2]{1,0:T(1,128)} %b_ref.3, ...), custom_call_target="tpu_custom_call" | custom-call | flops 20132659200 | bytes 5242880 | tf_op jit(solution)/shard_map/self_forward/pallas_call | solution.py:850
  143.3 0.6 slice_bitcast_fusion
  143.9 69.5 %sum_after_self.1 = (f32[640,1024]{1,0:T(8,128)}, bf16[640,1024]{1,0:T(8,128)(2,1)}, bf16[4,2,128,2048]{3,2,1,0:T(8,128)(2,1)}, bf16[4,2,128,2048]{3,2,1,0:T(8,128)(2,1)}) custom-call(bf16[2560,1024]{1,0:T(8,128)(2,1)} %get-tuple-element.71.terms_ref, bf16[640,1024]{1,0:T(8,128)(2,1)} %rows_ref.3, f32[1,1024]{1,0:T(1,128)} %get-tuple-element.156.shift_ref, ...), custom_call_target="tpu_custom_call" | custom-call | bytes 104857600 | tf_op jit(solution)/shard_map/sum_after_self/pallas_call | solution.py:944
  214.1 0.8 fusion.6.ok_ref
  214.9 263.6 %cross_forward.1 = (bf16[4,640,256]{2,1,0:T(8,128)(2,1)}, bf16[4,1024,256]{2,1,0:T(8,128)(2,1)}, bf16[4,1024,256]{2,1,0:T(8,128)(2,1)}, bf16[4,256,640]{2,1,0:T(...) custom-call(f32[1024,1]{1,0:T(8,128)} %fusion.6.ok_ref, ...), custom_call_target="tpu_custom_call" | custom-call | flops 16106127360 | bytes 8388608 | tf_op jit(solution)/shard_map/cross_forward/pallas_call | solution.py:1217
  478.6 0.6 broadcast_in_dim.22.b_ref
  479.3 53.1 %feed_forward.1 = (f32[640,1024]{1,0:T(8,128)}, f32[640,1024]{1,0:T(8,128)}, bf16[640,1024]{1,0:T(8,128)(2,1)}, f32[8,1024]{1,0:T(8,128)}, bf16[2,1024,1024]{2,1...) custom-call(bf16[640,1024]{1,0:T(8,128)(2,1)} %get-tuple-element.79., ...), custom_call_target="tpu_custom_call" | custom-call | flops 32212254720 | bytes 41943040 | tf_op jit(solution)/shard_map/feed_forward/pallas_call | solution.py:1385
  532.4 0.7 fusion.10
  533.1 0.3 dynamic_update_slice.62
  533.3 0.3 dynamic_update_slice.63
  533.6 0.3 dynamic_update_slice.64
  533.9 0.3 dynamic_update_slice.65
  534.2 74.9 %cross_backward.1 = (f32[640,1024]{1,0:T(8,128)}, bf16[1024,1024]{1,0:T(8,128)(2,1)}, bf16[2,1024,1024]{2,1,0:T(8,128)(2,1)}, f32[4,1,256]{2,1,0:T(1,128)}, f32[...) custom-call(f32[1024,1]{1,0:T(8,128)} %fusion.6.ok_ref, ...), custom_call_target="tpu_custom_call" | custom-call | flops 32212254720 | bytes 16777216 | tf_op jit(solution)/shard_map/cross_backward/pallas_call | solution.py:1550
  609.1 0.6 constant_dynamic-update-slice_fusion.3
  609.8 0.7 constant_dynamic-update-slice_fusion.2
  610.4 0.7 constant_dynamic-update-slice_fusion.1
  611.1 0.7 constant_dynamic-update-slice_fusion
  611.8 0.7 constant_dynamic-update-slice_fusion.7
  612.5 0.7 constant_dynamic-update-slice_fusion.6
  613.1 0.7 constant_dynamic-update-slice_fusion.5
  613.8 0.7 constant_dynamic-update-slice_fusion.4
  614.5 39.7 %middle.1 = (bf16[2560,1024]{1,0:T(8,128)(2,1)}, f32[640,1024]{1,0:T(8,128)}, f32[8,1024]{1,0:T(8,128)}, f32[128,1024]{1,0:T(8,128)}, bf16[4,128,1024]{2,1,0:T(8,128)(2,1)}) custom-call(f32[640,1024]{1,0:T(8,128)} %get-tuple-element.97.back_ref, f32[640,1024]{1,0:T(8,128)} %get-tuple-element.76.rows_ref, f32[640,1024]{1,0:T(8,128)} %get-tuple-element.98.grad_ref, ...), custom_call_target="tpu_custom_call" | custom-call | bytes 104857600 | tf_op jit(solution)/shard_map/middle/pallas_call | solution.py:501
  654.3 66.3 %self_backward.1 = (bf16[2560,256]{1,0:T(8,128)(2,1)}, bf16[2560,256]{1,0:T(8,128)(2,1)}, bf16[2560,256]{1,0:T(8,128)(2,1)}, f32[128,1024]{1,0:T(8,128)}, f32[128,1024]{1,0:T(8,128)}, /*index=5*/f32[256,1024]{1,0:T(8,128)}) custom-call(s32[1,2]{1,0:T(1,128)} %b_ref.3, bf16[2560,256]{1,0:T(8,128)(2,1)} %get-tuple-element.83.q_ref, ...), custom_call_target="tpu_custom_call" | custom-call | flops 40265318400 | bytes 10485760 | tf_op jit(solution)/shard_map/self_backward/pallas_call | solution.py:1076
  720.6 1.8 convert_reduce_fusion.1
  722.4 1.7 convert_reduce_fusion.2
  724.1 0.8 slice.124
  724.9 0.8 slice.126
  725.7 0.4 concatenate.16
  726.1 0.7 pad.4.late_ref
  726.8 4.9 convolution_convert_fusion.so_ref
  731.7 75.6 %tail.1 = (f32[640,1024]{1,0:T(8,128)}, f32[128,1024]{1,0:T(8,128)}, f32[24,1024]{1,0:T(8,128)}) custom-call(bf16[2560,256]{1,0:T(8,128)(2,1)} %get-tuple-element.107.dq_ref, bf16[2560,256]{1,0:T(8,128)(2,1)} %get-tuple-element.108.dk_ref, bf16[2560,256]{1,0:T(8,128)(2,1)} %get-tuple-element.109.dv_ref, bf16[1024,1024]{1,0:T(8,128)(2,1)} %bitcast.66, ...), custom_call_target="tpu_custom_call" | custom-call | bytes 104857600 | tf_op jit(solution)/shard_map/tail/pallas_call | solution.py:641
  807.4 1.1 slice_multiply_fusion
  808.5 0.2 copy.41
  808.6 0.9 copy.42
  809.5 0.9 multiply_bitcast_fusion.2
  810.5 0.8 copy.43
  811.2 0.6 mul.152
  811.9 0.6 copy.49
  812.5 0.6 slice_multiply_fusion.3
  813.1 1.9 broadcast_multiply_fusion
  815.0 0.9 mul.161
  815.9 0.7 multiply_bitcast_fusion.1
  816.5 0.8 copy.44
  817.3 1.1 multiply_bitcast_fusion
  818.4 1.0 copy.45
  819.4 1.5 copy.69
  820.9 1.2 copy-done.2
  822.1 1.5 copy.70
  823.6 0.5 copy-done.3
  824.0 1.0 copy.71
  (55 shorter events, 0.4 us)
Async XLA Ops:
  0.6 7.1 copy-start
  0.7 7.0 copy-start.13
  4.1 5.2 copy-start.7
  5.7 3.9 copy-start.8
  5.7 3.9 copy-start.11
  5.8 4.0 copy-start.12
  5.8 4.1 copy-start.10
  9.3 62.7 %copy-start.5 = (bf16[1024,128]{1,0:T(8,128)(2,1)S(1)}, bf16[1024,128]{1,0:T(8,128)(2,1)}, u32[]{:S(2)}) copy-start(bf16[1024,128]{1,0:T(8,128)(2,1)} %param.27) | copy-start | bytes 786436
  9.3 62.9 %copy-start.6 = (bf16[128,1024]{1,0:T(8,128)(2,1)S(1)}, bf16[128,1024]{1,0:T(8,128)(2,1)}, u32[]{:S(2)}) copy-start(bf16[128,1024]{1,0:T(8,128)(2,1)} %param.26) | copy-start | bytes 786436
  214.9 263.7 %copy-start.14 = (f32[4096]{0:T(1024)S(1)}, f32[4096]{0:T(1024)}, u32[]{:S(2)}) copy-start(f32[4096]{0:T(1024)} %param.29) | copy-start | bytes 49156
  720.6 5.0 copy-start.15
  720.6 6.2 copy-start.16
  807.3 3.9 copy-start.9
  807.4 7.6 copy-start.4
  811.2 8.2 copy-start.1
  819.4 2.7 copy-start.2
  822.1 2.0 copy-start.3

commit v9 on v8

--- a/solution.py
+++ b/solution.py
@@ -162,11 +162,12 @@
 
 
 class Spread:
-    def __init__(self, links, column, whole):
+    def __init__(self, links, source, column, whole):
         y = links.dp % 2
         half = column.shape[0] // 2
         low, high = pl.ds(0, half), pl.ds(half, half)
         near, near_core, far, far_core = (whole.at[k] for k in range(4))
+        self.load = links.local(source, column)
         self.own = links.local(column, near.at[:, y])
         self.first = [
             links.copy(column, near.at[:, y], Y),
@@ -184,8 +185,9 @@
         self.core_third = [links.copy(far.at[:, 1 - y], far_core.at[:, 1 - y], CORE)]
 
     def start(self):
-        self.own.start()
-        for copy in self.first + self.core:
+        self.load.start()
+        self.load.wait()
+        for copy in self.first + self.core + [self.own]:
             copy.start()
 
     def middle(self):
@@ -331,12 +333,11 @@
 
 
 class SpreadFar:
-    def __init__(self, links, column, near, near_core, whole):
+    def __init__(self, links, column, whole):
         y = links.dp % 2
-        far, far_core = whole.at[2], whole.at[3]
+        far, far_core = whole.at[0], whole.at[1]
         m, _, c = column.shape
         step = max(m // 4, 1)
-        self.local = [links.local(near, whole.at[0]), links.local(near_core, whole.at[1])]
         self.over_x, self.over_y, self.core_x, self.core_y = [], [], [], []
         for k in range(m // step):
             for h in range(2):
@@ -349,7 +350,7 @@
                 self.core_y.append(links.copy(other, far_core.at[z, 1 - y, :, part], CORE))
 
     def start(self):
-        for copy in self.over_x + self.local:
+        for copy in self.over_x:
             copy.start()
 
     def onward(self, k):
@@ -364,7 +365,7 @@
     def end(self):
         for copy in self.over_x + self.over_y:
             copy.wait_send()
-        for copy in self.local + self.core_x + self.core_y:
+        for copy in self.core_x + self.core_y:
             copy.wait()
 
 
@@ -721,7 +722,7 @@
     r, c = self_shard.shape
     return pl.pallas_call(
         functools.partial(start_kernel, n=n),
-        in_specs=[ANY] * 3,
+        in_specs=[pl.BlockSpec(memory_space=pltpu.VMEM)] * 3,
         out_specs=[ANY] * 3,
         out_shape=[
             jax.ShapeDtypeStruct((4 * rows_low.shape[0], rows_low.shape[1]), BF16),
@@ -738,13 +739,13 @@
 def self_forward_kernel(
     b_ref, x_ref, w_ref, bq_ref, bv_ref, column_ref, shard_ref, enc_ref,
     q_out, k_ref, v_out, kt_out, ot_ref, lse_ref, terms_ref, whole, next_column, enc_out,
-    vt_ref, m_s, l_s, acc, send_sems, recv_sems, local_sems, *, bk, heads, safe, n
+    vt_ref, m_s, l_s, acc, column, send_sems, recv_sems, local_sems, *, bk, heads, safe, n
 ):
     i = pl.program_id(0)
     last = pl.num_programs(0) - 1
     bq, width = q_out.shape
     links = Links(send_sems, recv_sems, local_sems)
-    spread = Spread(links, column_ref, whole)
+    spread = Spread(links, column_ref, column, whole)
     stages = column_stages(links, shard_ref, next_column, n)
     enc_count = enc_ref.shape[0]
 
@@ -857,8 +858,8 @@
             const((1, width)),
             const((1, width)),
             ANY,
-            ANY,
-            ANY,
+            const(shard.shape),
+            const(encoder.shape),
         ],
         out_specs=[
             by_rows_spec,
@@ -889,8 +890,9 @@
             pltpu.VMEM((heads, bq), F32),
             pltpu.VMEM((heads, bq), F32),
             pltpu.VMEM((width, bq), F32),
+            pltpu.VMEM((m, r, c), BF16),
         ]
-        + link_scratch(11 + m, 3),
+        + link_scratch(11 + m, 4),
         compiler_params=pltpu.CompilerParams(
             vmem_limit_bytes=VMEM_LIMIT, collective_id=1, has_side_effects=True
         ),
@@ -903,19 +905,24 @@
 
 def after_self_kernel(
     terms_ref, rows_ref, shift_ref, norm_ref, column_ref,
-    after_out, second_out, near_out, core_out, *scratch
+    after_out, second_out, whole_out, *scratch
 ):
     links = Links(*scratch[-3:])
     rows_sum = RowSum(links, terms_ref, scratch[:5])
+    column = scratch[5]
     y = links.dp % 2
-    own = links.local(column_ref, near_out.at[:, y])
-    over_y = links.copy(column_ref, near_out.at[:, y], Y)
+    near_out, core_out = whole_out.at[0], whole_out.at[1]
+    load = links.local(column_ref, column)
+    own = links.local(column, near_out.at[:, y])
+    over_y = links.copy(column, near_out.at[:, y], Y)
     over_core = [
-        links.copy(column_ref, core_out.at[:, y], CORE),
+        links.copy(column, core_out.at[:, y], CORE),
         links.copy(near_out.at[:, 1 - y], core_out.at[:, 1 - y], CORE),
     ]
     links.greet([CORE, X, Y])
     rows_sum.start()
+    load.start()
+    load.wait()
     over_y.start()
     own.start()
     rows_sum.middle()
@@ -944,14 +951,13 @@
     return pl.pallas_call(
         after_self_kernel,
         in_specs=[ANY, vmem, vmem, vmem, ANY],
-        out_specs=[vmem, vmem, ANY, ANY],
+        out_specs=[vmem, vmem, ANY],
         out_shape=[
             jax.ShapeDtypeStruct((count, model), F32),
             jax.ShapeDtypeStruct((count, model), BF16),
-            jax.ShapeDtypeStruct((m, 2, r, c), BF16),
-            jax.ShapeDtypeStruct((m, 2, r, c), BF16),
+            jax.ShapeDtypeStruct((2, m, 2, r, c), BF16),
         ],
-        scratch_shapes=row_sum_scratch(count, model) + link_scratch(6, 3),
+        scratch_shapes=row_sum_scratch(count, model) + [pltpu.VMEM((m, r, c), BF16)] + link_scratch(6, 4),
         compiler_params=pltpu.CompilerParams(
             vmem_limit_bytes=VMEM_LIMIT, collective_id=8, has_side_effects=True
         ),
@@ -1143,13 +1149,13 @@
 
 
 def cross_forward_kernel(
-    ok_ref, x_ref, enc_ref, w_ref, bq_ref, bv_ref, rows_ref, shift_ref, norm_ref, column_ref, near_ref, core_ref,
+    ok_ref, x_ref, enc_ref, w_ref, bq_ref, bv_ref, rows_ref, shift_ref, norm_ref, column_ref,
     q_out, k_out, v_out, ot_ref, lse_ref, after_ref, third_ref, whole, send_sems, recv_sems, local_sems, *, heads
 ):
     i = pl.program_id(0)
     last = pl.num_programs(0) - 1
     links = Links(send_sems, recv_sems, local_sems)
-    spread = SpreadFar(links, column_ref, near_ref, core_ref, whole)
+    spread = SpreadFar(links, column_ref, whole)
     pieces = len(spread.over_x)
 
     @pl.when(i == 0)
@@ -1204,7 +1210,7 @@
         spread.end()
 
 
-def cross_forward(ok, x, encoder, weights, q_shift, v_shift, rows, shift, norm, column, near, near_core, heads):
+def cross_forward(ok, x, encoder, weights, q_shift, v_shift, rows, shift, norm, column, heads):
     count, model = x.shape
     n = encoder.shape[0]
     parts, _, columns = weights.shape
@@ -1227,8 +1233,6 @@
             const((count, model)),
             const((1, model)),
             const((2, model)),
-            ANY,
-            ANY,
             ANY,
         ],
         out_specs=[
@@ -1249,9 +1253,9 @@
             jax.ShapeDtypeStruct((parts, heads, count), F32),
             jax.ShapeDtypeStruct((count, model), F32),
             jax.ShapeDtypeStruct((count, model), BF16),
-            jax.ShapeDtypeStruct((4, m, 2, r, c), BF16),
+            jax.ShapeDtypeStruct((2, m, 2, r, c), BF16),
         ],
-        scratch_shapes=link_scratch(32, 2),
+        scratch_shapes=link_scratch(32, 1),
         compiler_params=pltpu.CompilerParams(
             vmem_limit_bytes=VMEM_LIMIT, collective_id=2, has_side_effects=True
         ),
@@ -1261,13 +1265,13 @@
             transcendentals=parts * count * n * heads,
         ),
         name="cross_forward",
-    )(ok, x, encoder, weights, q_shift, v_shift, rows, shift, norm, column, near, near_core)
+    )(ok, x, encoder, weights, q_shift, v_shift, rows, shift, norm, column)
 
 
 def feed_forward_kernel(
-    x_ref, dy_ref, up_ref, down_ref, b_ref, after_ref, shift_ref, norm_ref,
+    x_ref, dy_ref, near_ref, far_ref, b_ref, after_ref, shift_ref, norm_ref,
     out_ref, rows_out, low_out, sums_ref, gup_ref, gdown_ref, bias_ref, from_x, from_y,
-    xt_ref, dyt_ref, back_ref, give, got, diagonal, send_sems, recv_sems, local_sems, *, chunks
+    xt_ref, dyt_ref, back_ref, give, got, diagonal, loaded, load_sems, send_sems, recv_sems, local_sems, *, chunks
 ):
     s = pl.program_id(0)
     links = Links(send_sems, recv_sems, local_sems)
@@ -1293,8 +1297,29 @@
         device_id_type=pl.DeviceIdType.MESH,
     )
 
+    size = loaded.shape[3]
+
+    def fetch(step, act):
+        block = 3 - step // chunks
+        slot = step % 2
+        first = (step % chunks) * size
+
+        def both(source):
+            for k in range(2):
+                columns = pl.ds(pl.multiple_of(first + k * chunks * size, size), size)
+                act(pltpu.make_async_copy(source.at[:, columns], loaded.at[slot, k], load_sems.at[slot, k]))
+
+        @pl.when(block >= 2)
+        def _():
+            both(far_ref.at[block - 2])
+
+        @pl.when(block < 2)
+        def _():
+            both(near_ref.at[block])
+
     @pl.when(s == 0)
     def _():
+        fetch(0, lambda copy: copy.start())
         links.greet([CORE, X, Y])
         out_ref[...] = after_ref[...] + shift_ref[...]
         back_ref[...] = jnp.zeros_like(back_ref)
@@ -1302,8 +1327,15 @@
         dyt_ref[...] = dy_ref[...].T
         sums_ref[...] = jnp.zeros_like(sums_ref)
 
-    pre_act = dot_nn(x_ref[...], up_ref[0]) + b_ref[0]
-    hidden_grad = dot_nn(dy_ref[...], down_ref[0])
+    fetch(s, lambda copy: copy.wait())
+
+    @pl.when(s + 1 < pl.num_programs(0))
+    def _():
+        fetch(s + 1, lambda copy: copy.start())
+
+    up_ref, down_ref = loaded.at[s % 2, 0], loaded.at[s % 2, 1]
+    pre_act = dot_nn(x_ref[...], up_ref[...]) + b_ref[0]
+    hidden_grad = dot_nn(dy_ref[...], down_ref[...])
     normal_cdf = 0.5 * (1.0 + lax.erf(pre_act * (1.0 / math.sqrt(2.0))))
     density = jnp.exp(-0.5 * pre_act * pre_act) * (1.0 / math.sqrt(2.0 * math.pi))
     hidden = (pre_act * normal_cdf).astype(BF16)
@@ -1316,8 +1348,8 @@
 
     give[chunk, 0] = dot_nn(xt_ref[...], pre_grad).astype(BF16)
     give[chunk, 1] = dot_nn(dyt_ref[...], hidden).astype(BF16)
-    out_ref[...] += dot_nt(hidden, down_ref[0])
-    back_ref[...] += dot_nt(pre_grad, up_ref[0])
+    out_ref[...] += dot_nt(hidden, down_ref[...])
+    back_ref[...] += dot_nt(pre_grad, up_ref[...])
 
     @pl.when(theirs)
     def _():
@@ -1363,9 +1395,9 @@
             copy.wait()
 
 
-def feed_forward(x, dy, weights, bias, after, shift, norm):
+def feed_forward(x, dy, near, far, bias, after, shift, norm):
     rows, width = x.shape
-    hidden = weights.shape[2] // 2
+    hidden = near.shape[2] // 2
     size = min(512, hidden)
     chunks = hidden // size
 
@@ -1388,8 +1420,8 @@
         in_specs=[
             rows_spec,
             rows_spec,
-            pl.BlockSpec((1, width, size), lambda s: (block(s), 0, s % chunks)),
-            pl.BlockSpec((1, width, size), lambda s: (block(s), 0, chunks + s % chunks)),
+            ANY,
+            ANY,
             bias_spec,
             rows_spec,
             const((1, width)),
@@ -1414,6 +1446,8 @@
             pltpu.VMEM((chunks, 2, width, size), BF16),
             pltpu.VMEM((2 * chunks, 2, width, size), BF16),
             pltpu.VMEM((2, m, r, hidden), BF16),
+            pltpu.VMEM((2, 2, width, size), BF16),
+            pltpu.SemaphoreType.DMA((2, 2)),
         ]
         + link_scratch(2 * chunks + 2, 1),
         compiler_params=pltpu.CompilerParams(
@@ -1423,7 +1457,7 @@
             flops=48 * rows * width * hidden, bytes_accessed=40 * 2**20, transcendentals=8 * rows * hidden
         ),
         name="feed_forward",
-    )(x, dy, weights, weights, bias, after, shift, norm)
+    )(x, dy, near, far, bias, after, shift, norm)
 
 
 def cross_backward_kernel(
@@ -1664,7 +1698,7 @@
         self_safe,
     )
     cross_w = cross_w.reshape(4, model_width, 4 * width)
-    after_self, second_in, ffn_near, ffn_near_core = sum_after_self(
+    after_self, second_in, ffn_near = sum_after_self(
         terms, block_in, biases[2:3], norm_params[1], ffn_column
     )
 
@@ -1673,7 +1707,7 @@
     def all_blocks(vector, size):
         return jnp.stack([block_of(vector, size, d) for d in range(4)])[:, None]
 
-    cross_q, cross_k, cross_v, cross_mixed_t, cross_lse, after_cross, third_in, ffn_w = cross_forward(
+    cross_q, cross_k, cross_v, cross_mixed_t, cross_lse, after_cross, third_in, ffn_far = cross_forward(
         ok,
         second_in,
         enc_all,
@@ -1684,15 +1718,14 @@
         biases[5:6],
         norm_params[2],
         ffn_column,
-        ffn_near,
-        ffn_near_core,
         heads,
     )
 
     output, cross_rows_grad, cross_low, ffn_sums, up_sum, down_sum, bias_up_parts, from_x, from_y = feed_forward(
         third_in,
         out_grad,
-        ffn_w.reshape(4, model_width, 2 * hidden_width),
+        ffn_near.reshape(2, model_width, 2 * hidden_width),
+        ffn_far.reshape(2, model_width, 2 * hidden_width),
         all_blocks(up_bias, hidden_width),
         after_cross,
         biases[6:7],

time: 833 us -> 606 us (0.73)
  Pallas kernels: 774 us -> 547 us
    pallas_call x1, Pallas kernels: 264 us -> 66.2 us  [cross_forward(): pl.pallas_call(functools.partial(cross_forward_kernel, heads=heads), grid...]
    pallas_call x1, Pallas kernels: 69.5 us -> 57.9 us  [sum_after_self(): pl.pallas_call(after_self_kernel, in_specs=[ANY, vmem, vmem, vmem, ANY],...]
    pallas_call x1, Pallas kernels: 61.2 us -> 50.7 us  [start_gather(): pl.pallas_call(functools.partial(start_kernel, n=n), in_specs=[pl.BlockSp...]
    pallas_call x1, Pallas kernels: 70.3 us -> 61.9 us  [self_forward(): pl.pallas_call(functools.partial(self_forward_kernel, bk=bk, heads=heads,...]
where the time goes in v9:
time: 606 us; the launch traced here: 598 us
  Pallas kernels  547 us (90%)
  local copies, waits for them, and re-layouts  26.6 us (4%)
  other arithmetic  17.4 us (3%)
    pallas_call x1, Pallas kernels, tail(): pl.pallas_call(functools.partial(tail_kernel, n=n, step_rows=512), in_spe...  75.8 us
    pallas_call x1, Pallas kernels, cross_backward(): pl.pallas_call(functools.partial(cross_backward_kernel, heads=heads, bk=2...  74.3 us
    pallas_call x1, Pallas kernels, self_backward(): pl.pallas_call(functools.partial(self_backward_kernel, bk=bk, heads=heads...  66.4 us
    pallas_call x1, Pallas kernels, cross_forward(): pl.pallas_call(functools.partial(cross_forward_kernel, heads=heads), grid...  66.2 us
    pallas_call x1, Pallas kernels, self_forward(): pl.pallas_call(functools.partial(self_forward_kernel, bk=bk, heads=heads,...  61.9 us
    pallas_call x1, Pallas kernels, sum_after_self(): pl.pallas_call(after_self_kernel, in_specs=[ANY, vmem, vmem, vmem, ANY],...  57.9 us
    pallas_call x1, Pallas kernels, feed_forward(): pl.pallas_call(functools.partial(feed_forward_kernel, chunks=chunks), gri...  53.2 us
    pallas_call x1, Pallas kernels, start_gather(): pl.pallas_call(functools.partial(start_kernel, n=n), in_specs=[pl.BlockSp...  50.7 us

profile of v9, /device:TPU:0, one launch (start us, length us, event | category | flops | bytes accessed | tf_op | source)
XLA Modules:
  0.0 598.1 jit_solution(13293795632424495247)
XLA Ops:
  0.7 1.6 fusion.8
  2.4 0.6 broadcast_in_dim.20.bq_ref
  3.0 0.6 broadcast_in_dim.21.bv_ref
  3.6 0.6 constant_dynamic-slice_fusion.8
  4.1 1.6 convert_reduce_fusion
  5.8 1.9 fusion.2
  7.7 1.6 fusion.5.rows_ref
  9.3 0.2 copy.36
  9.5 0.2 copy.38
  9.7 0.1 copy.37
  9.9 0.9 pad_maximum_fusion.1
  10.8 50.7 %start_gather.1 = (bf16[2560,1024]{1,0:T(8,128)(2,1)}, bf16[4,2,128,1024]{3,2,1,0:T(8,128)(2,1)}, bf16[4,128,1024]{2,1,0:T(8,128)(2,1)}) custom-call(bf16[640,1024]{1,0:T(8,128)(2,1)} %fusion.5.rows_ref, bf16[128,1024]{1,0:T(8,128)(2,1)} %get-tuple-element.179.self_ref, bf16[128,1024]{1,0:T(8,128)(2,1)} %get-tuple-element.180.cross_ref), custom_call_target="tpu_custom_call" | custom-call | bytes 104857600 | tf_op jit(solution)/shard_map/start_gather/pallas_call | solution.py:723
  61.5 0.1 copy.40
  61.7 0.8 pad_maximum_fusion.shard_ref
  62.5 61.9 %self_forward.1 = (bf16[2560,256]{1,0:T(8,128)(2,1)}, bf16[2560,256]{1,0:T(8,128)(2,1)}, bf16[2560,256]{1,0:T(8,128)(2,1)}, bf16[256,2560]{1,0:T(8,128)(2,1)}, b...) custom-call(s32[1,2]{1,0:T(1,128)} %b_ref.3, ...), custom_call_target="tpu_custom_call" | custom-call | flops 20132659200 | bytes 5242880 | tf_op jit(solution)/shard_map/self_forward/pallas_call | solution.py:851
  124.5 0.6 slice_bitcast_fusion
  125.1 57.9 %sum_after_self.1 = (f32[640,1024]{1,0:T(8,128)}, bf16[640,1024]{1,0:T(8,128)(2,1)}, bf16[2,4,2,128,2048]{4,3,2,1,0:T(8,128)(2,1)}) custom-call(bf16[2560,1024]{1,0:T(8,128)(2,1)} %get-tuple-element.70.terms_ref, bf16[640,1024]{1,0:T(8,128)(2,1)} %rows_ref.3, f32[1,1024]{1,0:T(1,128)} %get-tuple-element.154.shift_ref, ...), custom_call_target="tpu_custom_call" | custom-call | bytes 104857600 | tf_op jit(solution)/shard_map/sum_after_self/pallas_call | solution.py:951
  183.6 0.8 fusion.6.ok_ref
  184.5 66.2 %cross_forward.1 = (bf16[4,640,256]{2,1,0:T(8,128)(2,1)}, bf16[4,1024,256]{2,1,0:T(8,128)(2,1)}, bf16[4,1024,256]{2,1,0:T(8,128)(2,1)}, bf16[4,256,640]{2,1,0:T(...) custom-call(f32[1024,1]{1,0:T(8,128)} %fusion.6.ok_ref, ...), custom_call_target="tpu_custom_call" | custom-call | flops 16106127360 | bytes 8388608 | tf_op jit(solution)/shard_map/cross_forward/pallas_call | solution.py:1223
  250.8 0.6 broadcast_in_dim.22.b_ref
  251.4 53.2 %feed_forward.1 = (f32[640,1024]{1,0:T(8,128)}, f32[640,1024]{1,0:T(8,128)}, bf16[640,1024]{1,0:T(8,128)(2,1)}, f32[8,1024]{1,0:T(8,128)}, bf16[2,1024,1024]{2,1...) custom-call(bf16[640,1024]{1,0:T(8,128)(2,1)} %get-tuple-element.76., ...), custom_call_target="tpu_custom_call" | custom-call | flops 32212254720 | bytes 41943040 | tf_op jit(solution)/shard_map/feed_forward/pallas_call | solution.py:1417
  304.6 0.7 fusion.10
  305.3 0.3 dynamic_update_slice.62
  305.6 0.3 dynamic_update_slice.63
  305.9 0.3 dynamic_update_slice.64
  306.1 0.3 dynamic_update_slice.65
  306.4 74.3 %cross_backward.1 = (f32[640,1024]{1,0:T(8,128)}, bf16[1024,1024]{1,0:T(8,128)(2,1)}, bf16[2,1024,1024]{2,1,0:T(8,128)(2,1)}, f32[4,1,256]{2,1,0:T(1,128)}, f32[...) custom-call(f32[1024,1]{1,0:T(8,128)} %fusion.6.ok_ref, ...), custom_call_target="tpu_custom_call" | custom-call | flops 32212254720 | bytes 16777216 | tf_op jit(solution)/shard_map/cross_backward/pallas_call | solution.py:1584
  380.8 0.6 constant_dynamic-update-slice_fusion.3
  381.4 0.7 constant_dynamic-update-slice_fusion.2
  382.1 0.7 constant_dynamic-update-slice_fusion.1
  382.7 0.7 constant_dynamic-update-slice_fusion
  383.4 0.7 constant_dynamic-update-slice_fusion.7
  384.1 0.7 constant_dynamic-update-slice_fusion.6
  384.8 0.7 constant_dynamic-update-slice_fusion.5
  385.5 0.7 constant_dynamic-update-slice_fusion.4
  386.1 40.6 %middle.1 = (bf16[2560,1024]{1,0:T(8,128)(2,1)}, f32[640,1024]{1,0:T(8,128)}, f32[8,1024]{1,0:T(8,128)}, f32[128,1024]{1,0:T(8,128)}, bf16[4,128,1024]{2,1,0:T(8,128)(2,1)}) custom-call(f32[640,1024]{1,0:T(8,128)} %get-tuple-element.95.back_ref, f32[640,1024]{1,0:T(8,128)} %get-tuple-element.75.rows_ref, f32[640,1024]{1,0:T(8,128)} %get-tuple-element.96.grad_ref, ...), custom_call_target="tpu_custom_call" | custom-call | bytes 104857600 | tf_op jit(solution)/shard_map/middle/pallas_call | solution.py:502
  426.8 66.4 %self_backward.1 = (bf16[2560,256]{1,0:T(8,128)(2,1)}, bf16[2560,256]{1,0:T(8,128)(2,1)}, bf16[2560,256]{1,0:T(8,128)(2,1)}, f32[128,1024]{1,0:T(8,128)}, f32[128,1024]{1,0:T(8,128)}, /*index=5*/f32[256,1024]{1,0:T(8,128)}) custom-call(s32[1,2]{1,0:T(1,128)} %b_ref.3, bf16[2560,256]{1,0:T(8,128)(2,1)} %get-tuple-element.81.q_ref, ...), custom_call_target="tpu_custom_call" | custom-call | flops 40265318400 | bytes 10485760 | tf_op jit(solution)/shard_map/self_backward/pallas_call | solution.py:1082
  493.2 1.8 convert_reduce_fusion.1
  495.0 1.7 convert_reduce_fusion.2
  496.7 0.8 slice.124
  497.4 0.8 slice.126
  498.2 0.4 concatenate.16
  498.7 0.7 pad.4.late_ref
  499.3 4.9 convolution_convert_fusion.so_ref
  504.2 75.8 %tail.1 = (f32[640,1024]{1,0:T(8,128)}, f32[128,1024]{1,0:T(8,128)}, f32[24,1024]{1,0:T(8,128)}) custom-call(bf16[2560,256]{1,0:T(8,128)(2,1)} %get-tuple-element.105.dq_ref, bf16[2560,256]{1,0:T(8,128)(2,1)} %get-tuple-element.106.dk_ref, bf16[2560,256]{1,0:T(8,128)(2,1)} %get-tuple-element.107.dv_ref, bf16[1024,1024]{1,0:T(8,128)(2,1)} %bitcast.67, ...), custom_call_target="tpu_custom_call" | custom-call | bytes 104857600 | tf_op jit(solution)/shard_map/tail/pallas_call | solution.py:642
  580.0 1.1 slice_multiply_fusion
  581.1 0.2 copy.41
  581.2 0.9 copy.42
  582.2 0.9 multiply_bitcast_fusion.2
  583.1 0.8 copy.43
  583.9 0.6 mul.152
  584.5 0.6 copy.49
  585.1 0.6 slice_multiply_fusion.3
  585.7 1.9 broadcast_multiply_fusion
  587.6 0.9 mul.161
  588.5 0.7 multiply_bitcast_fusion.1
  589.2 0.8 copy.44
  589.9 1.1 multiply_bitcast_fusion
  591.0 1.0 copy.45
  592.0 1.5 copy.69
  593.5 1.2 copy-done.2
  594.7 1.5 copy.70
  596.2 0.5 copy-done.3
  596.7 1.0 copy.71
  (55 shorter events, 0.4 us)
Async XLA Ops:
  0.6 7.1 %copy-start = (bf16[640,1024]{1,0:T(8,128)(2,1)S(1)}, bf16[640,1024]{1,0:T(8,128)(2,1)}, u32[]{:S(2)}) copy-start(bf16[640,1024]{1,0:T(8,128)(2,1)} %rows_ref.3) | copy-start | bytes 3932164
  0.7 7.0 %copy-start.13 = (f32[3,2,1024]{2,1,0:T(2,128)S(1)}, f32[3,2,1024]{2,1,0:T(2,128)}, u32[]{:S(2)}) copy-start(f32[3,2,1024]{2,1,0:T(2,128)} %param.20) | copy-start | bytes 73732
  4.1 5.2 copy-start.7
  5.7 3.9 copy-start.8
  5.7 3.9 copy-start.11
  5.8 4.0 copy-start.12
  5.8 4.1 copy-start.10
  9.3 52.2 %copy-start.5 = (bf16[1024,128]{1,0:T(8,128)(2,1)S(1)}, bf16[1024,128]{1,0:T(8,128)(2,1)}, u32[]{:S(2)}) copy-start(bf16[1024,128]{1,0:T(8,128)(2,1)} %param.27) | copy-start | bytes 786436
  9.3 52.4 %copy-start.6 = (bf16[128,1024]{1,0:T(8,128)(2,1)S(1)}, bf16[128,1024]{1,0:T(8,128)(2,1)}, u32[]{:S(2)}) copy-start(bf16[128,1024]{1,0:T(8,128)(2,1)} %param.26) | copy-start | bytes 786436
  184.5 66.3 %copy-start.14 = (f32[4096]{0:T(1024)S(1)}, f32[4096]{0:T(1024)}, u32[]{:S(2)}) copy-start(f32[4096]{0:T(1024)} %param.29) | copy-start | bytes 49156
  493.1 5.0 copy-start.15
  493.1 6.2 %copy-start.16 = (bf16[256,2560]{1,0:T(8,128)(2,1)S(1)}, bf16[256,2560]{1,0:T(8,128)(2,1)}, u32[]{:S(2)}) copy-start(bf16[256,2560]{1,0:T(8,128)(2,1)} %get-tuple-element.100.mt_ref) | copy-start | bytes 3932164
  580.0 3.9 copy-start.9
  580.0 7.6 %copy-start.4 = (f32[128,1024]{1,0:T(8,128)S(1)}, f32[128,1024]{1,0:T(8,128)}, u32[]{:S(2)}) copy-start(f32[128,1024]{1,0:T(8,128)} %get-tuple-element.118) | copy-start | bytes 1572868
  583.8 8.2 %copy-start.1 = (f32[640,1024]{1,0:T(8,128)S(1)}, f32[640,1024]{1,0:T(8,128)}, u32[]{:S(2)}) copy-start(f32[640,1024]{1,0:T(8,128)} %get-tuple-element.200) | copy-start | bytes 7864324
  592.0 2.7 copy-start.2
  594.7 2.0 copy-start.3

commit v10 on v9

--- a/solution.py
+++ b/solution.py
@@ -26,18 +26,6 @@
 
 def dot_tn(a, b):
     return lax.dot_general(a, b, (((0,), (0,)), ((), ())), preferred_element_type=F32)
-
-
-def layer_norm(inputs, gain_row, shift_row):
-    center = inputs - jnp.mean(inputs, axis=-1, keepdims=True)
-    spread = jnp.mean(center * center, axis=-1, keepdims=True)
-    return center * lax.rsqrt(spread + EPSILON) * gain_row + shift_row
-
-
-def gelu_slope(values_in):
-    normal_cdf = 0.5 * (1.0 + lax.erf(values_in * (1.0 / math.sqrt(2.0))))
-    density = jnp.exp(-0.5 * values_in * values_in) * (1.0 / math.sqrt(2.0 * math.pi))
-    return normal_cdf + values_in * density
 
 
 def head_only(x, h, size):
@@ -463,7 +451,7 @@
 
     def norm_back(rows):
         incoming = back_ref[rows, :]
-        rows_grad, gain_terms = norm_rows_back(rows_ref[rows, :], incoming, norm_ref[0:1, :])
+        rows_grad, gain_terms = norm_rows_back(rows_ref[rows, :], incoming, norm_ref[1, 0:1, :])
         rows_grad = rows_grad + grad_ref[rows, :]
         rounded = rows_grad.astype(BF16)
         grad_out[rows, :] = rows_grad
@@ -525,10 +513,12 @@
 
 
 def tail_kernel(
-    dq_ref, dk_ref, dv_ref, w_ref, first_ref, so_ref, rows_ref, grad_ref, norm_ref, late_ref,
+    dq_ref, dk_ref, dv_ref, w_ref, first_ref, wide_ref, mt_ref, rows_ref, grad_ref, norm_ref,
+    self_ref, ffn_ref, cq_ref, cv_ref, up_ref,
     grad_out, weights_out, late_out, give, acc, weights, *scratch, n, step_rows
 ):
     links = Links(*scratch[-3:])
+    member = links.tensor
     near, far, got_near, got_far, got_x = scratch[:5]
     columns, gots, slots = scratch[5:7], scratch[7:9], scratch[9:11]
     held, late_slots = scratch[11:13]
@@ -546,11 +536,13 @@
     for k, (column, got, slot) in enumerate(zip(columns, gots, slots)):
         over_y.append(links.copy(weights.at[:, 1 - y, :, pl.ds(k * c, c)], got, Y))
         collects.append(Collect(links, column, slot))
+    stages = len(collects[0].stages)
     late = Everywhere(links, held, late_slots, n)
+    steps = len(late.copies)
     links.greet(everywhere_ways(n))
 
     def terms(distance, target):
-        base = (links.tensor ^ distance) * count
+        base = (member ^ distance) * count
 
         def one(rows):
             there = pl.ds(pl.multiple_of(base + rows.start, 128), 128)
@@ -560,6 +552,12 @@
 
         by_rows(count, 128, one)
 
+    def packed(k):
+        for block in range(2 * m):
+            span = slice(block * r, (block + 1) * r)
+            weights[block // 2, block % 2, :, k * c : (k + 1) * c] = acc[span, k * c : (k + 1) * c].astype(BF16)
+        columns[k][...] = weights[:, y, :, k * c : (k + 1) * c]
+
     terms(3, give.at[0])
     core_far.start()
     terms(2, far)
@@ -581,50 +579,82 @@
             acc[:, k * width : (k + 1) * width] += dot_nn(source, ref[rows, :])
 
     by_rows(dq_ref.shape[0], step_rows, products)
-    for k in range(2 * m):
-        span = slice(k * r, (k + 1) * r)
-        weights[k // 2, k % 2, :, : 3 * width] = acc[span, :].astype(BF16)
-        weights[k // 2, k % 2, :, 3 * width :] = so_ref[span, :]
+    packed(0)
     over_y[0].start()
     terms(1, give.at[1])
     core_near.start()
     terms(0, near)
-    for k in range(2):
-        columns[k][...] = weights[:, y, :, k * c : (k + 1) * c]
-    for k in range(2):
-        over_y[k].wait_recv()
-        if k == 0:
-            over_y[1].start()
-        add_to(columns[k], gots[k])
-        collects[k].start(0)
-    stages = len(collects[0].stages)
-    held[0] = late_ref[...]
-    core_near.wait_recv()
-    for part, copy in zip(parts, over_x):
-        copy.wait_recv()
-
-        def norm_back(rows, part=part):
+
+    def products_out(rows):
+        acc[:, 3 * width :] += dot_nn(wide_ref[rows, :].T, mt_ref[:, rows].T)
+
+    by_rows(dq_ref.shape[0], step_rows, products_out)
+    packed(1)
+
+    held[0] = jnp.zeros(held.shape[1:], F32)
+    held[0, 2:4, :] = self_ref[0:2, :]
+    held[0, 4:6, :] = ffn_ref[0:2, :]
+    held[0, 8:9, :] = self_ref[2:3, :]
+    held[0, 11:13, :] = ffn_ref[2:4, :]
+    for distance in range(4):
+        there = pl.ds(pl.multiple_of((member ^ distance) * width, width), width)
+        held[0, 9:10, there] = cq_ref[distance]
+        held[0, 10:11, there] = cv_ref[distance]
+        held[0, pl.ds(13 + (member ^ distance), 1), :] = up_ref[distance]
+    here = pl.ds(pl.multiple_of(member * width, width), width)
+
+    def column_sums(rows):
+        held[0, 6:7, here] += jnp.sum(dq_ref[rows, :].astype(F32), axis=0, keepdims=True)
+        held[0, 7:8, here] += jnp.sum(dv_ref[rows, :].astype(F32), axis=0, keepdims=True)
+
+    by_rows(dq_ref.shape[0], step_rows, column_sums)
+
+    def norm_back(part):
+        def one(rows):
             rows = pl.ds(pl.multiple_of(part.start + rows.start, 64), 64)
             incoming = near[rows, :].astype(F32) + got_near[rows, :].astype(F32) + got_x[rows, :].astype(F32)
-            rows_grad, gain_terms = norm_rows_back(rows_ref[rows, :].astype(F32), incoming, norm_ref[0:1, :])
+            rows_grad, gain_terms = norm_rows_back(rows_ref[rows, :].astype(F32), incoming, norm_ref[0, 0:1, :])
             grad_out[rows, :] = rows_grad + grad_ref[rows, :]
             held[0, 0:1, :] += jnp.sum(gain_terms, axis=0, keepdims=True)
             held[0, 1:2, :] += jnp.sum(incoming, axis=0, keepdims=True)
 
-        by_rows(half, 64, norm_back)
-        if part is parts[0]:
-            for step in range(stages - 1):
-                for k in range(2):
-                    collects[k].finish(step)
-                    collects[k].start(step + 1)
-    steps = len(late.copies)
-    for step in range(steps):
+        by_rows(half, 64, one)
+
+    def summed_y(k):
+        over_y[k].wait_recv()
+        add_to(columns[k], gots[k])
+        collects[k].start(0)
+
+    def next_z(k):
+        for step in range(stages - 1):
+            collects[k].finish(step)
+            collects[k].start(step + 1)
+
+    def last_z(k):
+        collects[k].finish(stages - 1)
+        weights_out[:, k * c : (k + 1) * c] = columns[k][collects[k].z].astype(F32)
+
+    summed_y(0)
+    over_y[1].start()
+    core_near.wait_recv()
+    over_x[0].wait_recv()
+    norm_back(parts[0])
+    next_z(0)
+    over_x[1].wait_recv()
+    norm_back(parts[1])
+    late.start(0)
+    summed_y(1)
+    late.finish(0)
+    late.start(1)
+    last_z(0)
+    late.finish(1)
+    late.start(2)
+    next_z(1)
+    late.finish(2)
+    for step in range(3, steps):
         late.start(step)
-        if step == 1:
-            for k in range(2):
-                collects[k].finish(stages - 1)
-                weights_out[:, k * c : (k + 1) * c] = columns[k][collects[k].z].astype(F32)
         late.finish(step)
+    last_z(1)
     late_out[...] = held[steps]
     for copy in over_x + over_y + [core_near, core_far]:
         copy.wait_send()
@@ -632,40 +662,87 @@
         collect.drain()
 
 
-def tail(dq, dk, dv, w, first, so_grad, rows, grad, norm, late):
+def tail(dq, dk, dv, w, first, wide, mixed_t, rows, grad, norm, self_sums, ffn_sums, cq_sums, cv_sums, up_sums):
     n = lax.axis_size("dp")
     count, model = rows.shape
-    total, width = dq.shape
+    width = dq.shape[1]
     m, r, c = n // 2, model // n, 4 * width
+    vectors = (24, model)
     vmem = pl.BlockSpec(memory_space=pltpu.VMEM)
     part = pltpu.VMEM((m, r, c // 2), BF16)
     return pl.pallas_call(
         functools.partial(tail_kernel, n=n, step_rows=512),
-        in_specs=[vmem] * 10,
+        in_specs=[vmem] * 15,
         out_specs=[vmem, vmem, vmem],
         out_shape=[
             jax.ShapeDtypeStruct((count, model), F32),
             jax.ShapeDtypeStruct((r, c), F32),
-            jax.ShapeDtypeStruct(late.shape, F32),
+            jax.ShapeDtypeStruct(vectors, F32),
         ],
         scratch_shapes=[
             pltpu.VMEM((2, count, model), BF16),
-            pltpu.VMEM((model, 3 * width), F32),
+            pltpu.VMEM((model, c), F32),
             pltpu.VMEM((m, 2, r, c), BF16),
         ]
         + row_sum_scratch(count, model)
         + [part] * 6
-        + everywhere_scratch(*late.shape, n)
+        + everywhere_scratch(*vectors, n)
         + link_scratch(6 + 2 * m + len(everywhere_ways(n)), 1),
         compiler_params=pltpu.CompilerParams(
             vmem_limit_bytes=VMEM_LIMIT, collective_id=7, has_side_effects=True
         ),
         cost_estimate=pl.CostEstimate(flops=0, bytes_accessed=100 * 2**20, transcendentals=0),
         name="tail",
-    )(dq, dk, dv, w, first, so_grad, rows, grad, norm, late)
-
-
-def start_kernel(rows_ref, self_ref, cross_ref, rows_out, self_out, cross_out, send_sems, recv_sems, local_sems, *, n):
+    )(dq, dk, dv, w, first, wide, mixed_t, rows, grad, norm, self_sums, ffn_sums, cq_sums, cv_sums, up_sums)
+
+
+def results_kernel(
+    output_ref, grad_ref, enc_ref, self_ref, cross_ref, up_ref, down_ref,
+    output_out, grad_out, enc_out, qkv_out, so_out, cq_out, ckv_out, co_out, up_out, down_out, *, scale
+):
+    output_out[...] = output_ref[...]
+    grad_out[...] = grad_ref[...]
+    enc_out[...] = enc_ref[...]
+    width = cq_out.shape[1]
+
+    @pl.when(pl.program_id(0) == 0)
+    def _():
+        for k in range(3):
+            qkv_out[:, k, :] = self_ref[:, k * width : (k + 1) * width] * scale
+        so_out[...] = self_ref[:, 3 * width :] * scale
+        cq_out[...] = cross_ref[:, :width] * scale
+        for k in range(2):
+            ckv_out[:, k, :] = cross_ref[:, (k + 1) * width : (k + 2) * width] * scale
+        co_out[...] = cross_ref[:, 3 * width :] * scale
+        up_out[...] = up_ref[...] * scale
+        down_out[...] = down_ref[...] * scale
+
+
+def results(output, grad, encoder, self_w, cross_w, up, down, scale):
+    r, c = self_w.shape
+    width = c // 4
+    steps = 4
+
+    def rows(value):
+        return pl.BlockSpec((value.shape[0] // steps, value.shape[1]), lambda i: (i, 0))
+
+    shapes = [(r, 3, width), (r, width), (r, width), (r, 2, width), (r, width), up.shape, down.shape]
+    return pl.pallas_call(
+        functools.partial(results_kernel, scale=scale),
+        grid=(steps,),
+        in_specs=[rows(output), rows(grad), rows(encoder)] + [const(v.shape) for v in (self_w, cross_w, up, down)],
+        out_specs=[rows(output), rows(grad), rows(encoder)] + [const(shape) for shape in shapes],
+        out_shape=[jax.ShapeDtypeStruct(v.shape, F32) for v in (output, grad, encoder)]
+        + [jax.ShapeDtypeStruct(shape, F32) for shape in shapes],
+        compiler_params=pltpu.CompilerParams(vmem_limit_bytes=VMEM_LIMIT),
+        cost_estimate=pl.CostEstimate(flops=0, bytes_accessed=20 * 2**20, transcendentals=0),
+        name="results",
+    )(output, grad, encoder, self_w, cross_w, up, down)
+
+
+def start_kernel(
+    in_ref, norm_ref, self_ref, cross_ref, rows_out, self_out, cross_out, rows_ref, send_sems, recv_sems, local_sems, *, n
+):
     links = Links(send_sems, recv_sems, local_sems)
     member, z, y = links.tensor, links.dp // 2, links.dp % 2
     count = rows_ref.shape[0]
@@ -687,11 +764,25 @@
         links.local(cross_ref, cross_out.at[z]),
     ]
     links.greet([CORE, X, Y] + z_ways(n))
-    for copy in over_x + over_y + over_core[:1] + local:
+    for copy in over_y + local[1:]:
+        copy.start()
+    for copy, _ in self_stages[0]:
+        copy.start()
+    for part, copy in zip(parts, over_x):
+
+        def norm(rows, part=part):
+            rows = pl.ds(pl.multiple_of(part.start + rows.start, 64), 64)
+            xhat, _ = normalized(in_ref[rows, :].astype(F32))
+            rows_ref[rows, :] = (xhat * norm_ref[0, 0:1, :] + norm_ref[0, 1:2, :]).astype(BF16)
+
+        by_rows(half, 64, norm)
+        copy.start()
+    for copy in local[:1] + over_core[:1]:
         copy.start()
     for self_stage in self_stages:
-        for copy, _ in self_stage:
-            copy.start()
+        if self_stage is not self_stages[0]:
+            for copy, _ in self_stage:
+                copy.start()
         for copy, index in self_stage:
             copy.wait_recv()
             onward = links.copy(self_out.at[index, y], self_out.at[index, y], Y)
@@ -717,27 +808,29 @@
             copy.wait_send()
 
 
-def start_gather(rows_low, self_shard, cross_shard):
+def start_gather(rows, norm, self_shard, cross_shard):
     n = lax.axis_size("dp")
     r, c = self_shard.shape
     return pl.pallas_call(
         functools.partial(start_kernel, n=n),
-        in_specs=[pl.BlockSpec(memory_space=pltpu.VMEM)] * 3,
+        in_specs=[pl.BlockSpec(memory_space=pltpu.VMEM)] * 4,
         out_specs=[ANY] * 3,
         out_shape=[
-            jax.ShapeDtypeStruct((4 * rows_low.shape[0], rows_low.shape[1]), BF16),
+            jax.ShapeDtypeStruct((4 * rows.shape[0], rows.shape[1]), BF16),
             jax.ShapeDtypeStruct((n // 2, 2, r, c), BF16),
             jax.ShapeDtypeStruct((n // 2,) + cross_shard.shape, BF16),
         ],
-        scratch_shapes=link_scratch(2 * n + 8, 3),
-        compiler_params=pltpu.CompilerParams(collective_id=0, has_side_effects=True),
+        scratch_shapes=[pltpu.VMEM(rows.shape, BF16)] + link_scratch(2 * n + 8, 3),
+        compiler_params=pltpu.CompilerParams(
+            vmem_limit_bytes=VMEM_LIMIT, collective_id=0, has_side_effects=True
+        ),
         cost_estimate=pl.CostEstimate(flops=0, bytes_accessed=100 * 2**20, transcendentals=0),
         name="start_gather",
-    )(rows_low, self_shard, cross_shard)
+    )(rows, norm, self_shard, cross_shard)
 
 
 def self_forward_kernel(
-    b_ref, x_ref, w_ref, bq_ref, bv_ref, column_ref, shard_ref, enc_ref,
+    b_ref, x_ref, w_ref, biases_ref, column_ref, shard_ref, enc_ref,
     q_out, k_ref, v_out, kt_out, ot_ref, lse_ref, terms_ref, whole, next_column, enc_out,
     vt_ref, m_s, l_s, acc, column, send_sems, recv_sems, local_sems, *, bk, heads, safe, n
 ):
@@ -765,8 +858,7 @@
         for copy, _ in stages[0]:
             copy.start()
 
-    @pl.when(i == last)
-    def _():
+    def onward():
         spread.middle()
         enc_x.start()
         for k in range(1, len(stages)):
@@ -775,10 +867,11 @@
             for copy, _ in stages[k]:
                 copy.start()
 
+    mine = pl.ds(pl.multiple_of(links.tensor * width, width), width)
     projected = dot_nn(x_ref[...], w_ref[:, : 3 * width])
-    query = (projected[:, :width] + bq_ref[...]).astype(BF16)
+    query = (projected[:, :width] + biases_ref[0:1, mine]).astype(BF16)
     key = projected[:, width : 2 * width].astype(BF16)
-    value = (projected[:, 2 * width :] + bv_ref[...]).astype(BF16)
+    value = (projected[:, 2 * width :] + biases_ref[1:2, mine]).astype(BF16)
     here = pl.ds(pl.multiple_of(i * bq, bq), bq)
     q_out[...] = query
     v_out[...] = value
@@ -816,7 +909,7 @@
         for h in range(heads):
             acc[h * hd : (h + 1) * hd, :] = a_out[h]
 
-    over_keys(i, bq, bk, safe, block)
+    over_keys(i, bq, bk, safe, block, [(3, 2, onward)])
     inverse = 1.0 / l_s[...]
     for h in range(heads):
         part = slice(h * hd, (h + 1) * hd)
@@ -839,7 +932,7 @@
             copy.wait()
 
 
-def self_forward(bounds, x, w, q_shift, v_shift, column, shard, encoder, heads, safe):
+def self_forward(bounds, x, w, biases, column, shard, encoder, heads, safe):
     n, model = x.shape
     width = w.shape[1] // 4
     bq = bk = 512
@@ -855,8 +948,7 @@
             pl.BlockSpec(memory_space=pltpu.SMEM),
             pl.BlockSpec((bq, model), lambda i: (i, 0)),
             const((model, 4 * width)),
-            const((1, width)),
-            const((1, width)),
+            const(biases.shape),
             ANY,
             const(shard.shape),
             const(encoder.shape),
@@ -900,11 +992,11 @@
             flops=12 * n * n * width, bytes_accessed=8 * n * width, transcendentals=n * n * heads // 2
         ),
         name="self_forward",
-    )(bounds, x, w, q_shift, v_shift, column, shard, encoder)
+    )(bounds, x, w, biases, column, shard, encoder)
 
 
 def after_self_kernel(
-    terms_ref, rows_ref, shift_ref, norm_ref, column_ref,
+    terms_ref, rows_ref, biases_ref, norm_ref, column_ref,
     after_out, second_out, whole_out, *scratch
 ):
     links = Links(*scratch[-3:])
@@ -930,10 +1022,10 @@
     rows_sum.end()
 
     def norm(rows):
-        after = rows_ref[rows, :].astype(F32) + rows_sum.total(rows) + shift_ref[...]
+        after = rows_ref[rows, :].astype(F32) + rows_sum.total(rows) + biases_ref[2:3, :]
         after_out[rows, :] = after
         xhat, _ = normalized(after)
-        second_out[rows, :] = (xhat * norm_ref[0:1, :] + norm_ref[1:2, :]).astype(BF16)
+        second_out[rows, :] = (xhat * norm_ref[1, 0:1, :] + norm_ref[1, 1:2, :]).astype(BF16)
 
     by_rows(after_out.shape[0], 64, norm)
     over_y.wait_recv()
@@ -944,7 +1036,7 @@
         copy.wait()
 
 
-def sum_after_self(terms, rows, shift, norm, column):
+def sum_after_self(terms, rows, biases, norm, column):
     count, model = rows.shape
     m, r, c = column.shape
     vmem = pl.BlockSpec(memory_space=pltpu.VMEM)
@@ -963,7 +1055,7 @@
         ),
         cost_estimate=pl.CostEstimate(flops=0, bytes_accessed=100 * 2**20, transcendentals=0),
         name="sum_after_self",
-    )(terms, rows, shift, norm, column)
+    )(terms, rows, biases, norm, column)
 
 
 def self_backward_kernel(
@@ -1149,7 +1241,7 @@
 
 
 def cross_forward_kernel(
-    ok_ref, x_ref, enc_ref, w_ref, bq_ref, bv_ref, rows_ref, shift_ref, norm_ref, column_ref,
+    len_ref, x_ref, enc_ref, w_ref, biases_ref, rows_ref, norm_ref, column_ref,
     q_out, k_out, v_out, ot_ref, lse_ref, after_ref, third_ref, whole, send_sems, recv_sems, local_sems, *, heads
 ):
     i = pl.program_id(0)
@@ -1162,7 +1254,7 @@
     def _():
         links.greet([CORE, X, Y])
         spread.start()
-        after_ref[...] = rows_ref[...] + shift_ref[...]
+        after_ref[...] = rows_ref[...] + biases_ref[5:6, :]
 
     for step, ready in ((1, (0,)), (2, (1, 2)), (3, (3,))):
 
@@ -1173,16 +1265,17 @@
 
     width = q_out.shape[2]
     hd = width // heads
-    query = (dot_nn(x_ref[...], w_ref[0, :, :width]) + bq_ref[0]).astype(BF16)
+    mine = pl.ds(pl.multiple_of((links.tensor ^ i) * width, width), width)
+    query = (dot_nn(x_ref[...], w_ref[0, :, :width]) + biases_ref[3:4, mine]).astype(BF16)
     key_value = dot_nn(enc_ref[...], w_ref[0, :, width : 3 * width])
     keys = key_value[:, :width].astype(BF16)
-    values = (key_value[:, width:] + bv_ref[0]).astype(BF16)
+    values = (key_value[:, width:] + biases_ref[4:5, mine]).astype(BF16)
     q_out[0] = query
     k_out[0] = keys
     v_out[0] = values
     values_t = values.T
     scaled = query * jnp.asarray(1.0 / math.sqrt(hd), BF16)
-    ok = ok_ref[...] > 0.0
+    ok = lax.broadcasted_iota(jnp.int32, (keys.shape[0], 1), 0) < len_ref[0]
     scores = [dot_nt(keys, head_only(scaled, h, hd)) for h in range(heads)]
     mixed = []
     for h in range(heads):
@@ -1200,7 +1293,7 @@
     def _():
         def norm(rows):
             xhat, _ = normalized(after_ref[rows, :])
-            third_ref[rows, :] = (xhat * norm_ref[0:1, :] + norm_ref[1:2, :]).astype(BF16)
+            third_ref[rows, :] = (xhat * norm_ref[2, 0:1, :] + norm_ref[2, 1:2, :]).astype(BF16)
 
         by_rows(after_ref.shape[0], 128, norm)
         for k in range(4, pieces):
@@ -1210,7 +1303,7 @@
         spread.end()
 
 
-def cross_forward(ok, x, encoder, weights, q_shift, v_shift, rows, shift, norm, column, heads):
+def cross_forward(lengths, x, encoder, weights, biases, rows, norm, column, heads):
     count, model = x.shape
     n = encoder.shape[0]
     parts, _, columns = weights.shape
@@ -1224,15 +1317,13 @@
         functools.partial(cross_forward_kernel, heads=heads),
         grid=(parts,),
         in_specs=[
-            const((n, 1)),
+            pl.BlockSpec(memory_space=pltpu.SMEM),
             const((count, model)),
             const((n, model)),
             by_part(model, columns),
-            by_part(1, width),
-            by_part(1, width),
+            const(biases.shape),
             const((count, model)),
-            const((1, model)),
-            const((2, model)),
+            const(norm.shape),
             ANY,
         ],
         out_specs=[
@@ -1265,11 +1356,11 @@
             transcendentals=parts * count * n * heads,
         ),
         name="cross_forward",
-    )(ok, x, encoder, weights, q_shift, v_shift, rows, shift, norm, column)
+    )(lengths, x, encoder, weights, biases, rows, norm, column)
 
 
 def feed_forward_kernel(
-    x_ref, dy_ref, near_ref, far_ref, b_ref, after_ref, shift_ref, norm_ref,
+    x_ref, dy_ref, near_ref, far_ref, b_ref, after_ref, biases_ref, norm_ref,
     out_ref, rows_out, low_out, sums_ref, gup_ref, gdown_ref, bias_ref, from_x, from_y,
     xt_ref, dyt_ref, back_ref, give, got, diagonal, loaded, load_sems, send_sems, recv_sems, local_sems, *, chunks
 ):
@@ -1321,7 +1412,7 @@
     def _():
         fetch(0, lambda copy: copy.start())
         links.greet([CORE, X, Y])
-        out_ref[...] = after_ref[...] + shift_ref[...]
+        out_ref[...] = after_ref[...] + biases_ref[6:7, :]
         back_ref[...] = jnp.zeros_like(back_ref)
         xt_ref[...] = x_ref[...].T
         dyt_ref[...] = dy_ref[...].T
@@ -1334,7 +1425,8 @@
         fetch(s + 1, lambda copy: copy.start())
 
     up_ref, down_ref = loaded.at[s % 2, 0], loaded.at[s % 2, 1]
-    pre_act = dot_nn(x_ref[...], up_ref[...]) + b_ref[0]
+    shift = b_ref[pl.ds(links.tensor ^ (3 - turn), 1), pl.ds(pl.multiple_of(chunk * size, size), size)]
+    pre_act = dot_nn(x_ref[...], up_ref[...]) + shift
     hidden_grad = dot_nn(dy_ref[...], down_ref[...])
     normal_cdf = 0.5 * (1.0 + lax.erf(pre_act * (1.0 / math.sqrt(2.0))))
     density = jnp.exp(-0.5 * pre_act * pre_act) * (1.0 / math.sqrt(2.0 * math.pi))
@@ -1382,7 +1474,7 @@
         def norm_back(rows):
             third = back_ref[rows, :]
             upstream = dy_ref[rows, :].astype(F32)
-            rows_grad, gain_terms = norm_rows_back(after_ref[rows, :], third, norm_ref[0:1, :])
+            rows_grad, gain_terms = norm_rows_back(after_ref[rows, :], third, norm_ref[2, 0:1, :])
             rows_grad = rows_grad + upstream
             low = rows_grad.astype(BF16)
             rows_out[rows, :] = rows_grad
@@ -1395,7 +1487,7 @@
             copy.wait()
 
 
-def feed_forward(x, dy, near, far, bias, after, shift, norm):
+def feed_forward(x, dy, near, far, bias, after, biases, norm):
     rows, width = x.shape
     hidden = near.shape[2] // 2
     size = min(512, hidden)
@@ -1422,10 +1514,10 @@
             rows_spec,
             ANY,
             ANY,
-            bias_spec,
+            const(bias.shape),
             rows_spec,
-            const((1, width)),
-            const((2, width)),
+            const(biases.shape),
+            const(norm.shape),
         ],
         out_specs=[rows_spec, rows_spec, rows_spec, const((8, width)), grad_spec, grad_spec, bias_spec, ANY, ANY],
         out_shape=[
@@ -1457,11 +1549,11 @@
             flops=48 * rows * width * hidden, bytes_accessed=40 * 2**20, transcendentals=8 * rows * hidden
         ),
         name="feed_forward",
-    )(x, dy, near, far, bias, after, shift, norm)
+    )(x, dy, near, far, bias, after, biases, norm)
 
 
 def cross_backward_kernel(
-    ok_ref, low_ref, x_ref, enc_ref, w_ref, q_ref, k_ref, v_ref, mt_ref, lse_ref, up_ref, down_ref, from_x, from_y,
+    len_ref, low_ref, x_ref, enc_ref, w_ref, q_ref, k_ref, v_ref, mt_ref, lse_ref, up_ref, down_ref, from_x, from_y,
     back_ref, enc_out, grad_ref, bq_ref, bv_ref, up_out, down_out,
     low_t, x_t, enc_t, enc_acc, give, got, *scratch, heads, bk
 ):
@@ -1519,7 +1611,7 @@
         span = slice(j * bk, (j + 1) * bk)
         keys = k_ref[0, span, :]
         values = v_ref[0, span, :]
-        ok = ok_ref[span, :] > 0.0
+        ok = j * bk + lax.broadcasted_iota(jnp.int32, (bk, 1), 0) < len_ref[0]
         scores = [dot_nt(keys, q_heads[h]) for h in range(heads)]
         dprobs = [dot_nt(values, d_heads[h]) for h in range(heads)]
         dv_sum, dk_sum = None, None
@@ -1570,7 +1662,7 @@
 
 
 def cross_backward(
-    ok, low, x, encoder, weights, queries, keys, values, mixed_t, lse, up_sum, down_sum, from_x, from_y, heads
+    lengths, low, x, encoder, weights, queries, keys, values, mixed_t, lse, up_sum, down_sum, from_x, from_y, heads
 ):
     count, model = x.shape
     n = encoder.shape[0]
@@ -1585,7 +1677,7 @@
         functools.partial(cross_backward_kernel, heads=heads, bk=256),
         grid=(parts,),
         in_specs=[
-            const((n, 1)),
+            pl.BlockSpec(memory_space=pltpu.SMEM),
             const((count, model)),
             const((count, model)),
             const((n, model)),
@@ -1637,7 +1729,7 @@
             transcendentals=parts * count * n * heads,
         ),
         name="cross_backward",
-    )(ok, low, x, encoder, weights, queries, keys, values, mixed_t, lse, up_sum, down_sum, from_x, from_y)
+    )(lengths, low, x, encoder, weights, queries, keys, values, mixed_t, lse, up_sum, down_sum, from_x, from_y)
 
 
 def on_device(
@@ -1657,28 +1749,16 @@
     biases,
     up_bias,
 ):
-    member = lax.axis_index("tensor")
     groups_count = lax.axis_size("dp")
-    groups = float(groups_count)
     width = w_cross_q.shape[1]
     hidden_width = w_up.shape[1]
     heads = H // 4
     own_rows, model_width = block_in.shape
-    enc_rows = encoder_out.shape[0]
     w_rows = w_cross_q.shape[0]
 
-    def block_of(vector, size, distance):
-        return lax.dynamic_slice_in_dim(vector, (member ^ distance) * size, size)
-
-    def blocks_placed(parts):
-        size = parts[0].shape[0]
-        out = jnp.zeros((4 * size,), F32)
-        for distance, part in enumerate(parts):
-            out = lax.dynamic_update_slice_in_dim(out, part, (member ^ distance) * size, 0)
-        return out
-
     first_in, self_w, cross_column = start_gather(
-        layer_norm(block_in.astype(F32), norm_params[0, 0], norm_params[0, 1]).astype(BF16),
+        block_in,
+        norm_params,
         jnp.concatenate([w_qkv.reshape(w_rows, 3 * width), w_self_out.T], axis=1),
         jnp.concatenate([w_cross_q, w_cross_kv.reshape(w_rows, 2 * width), w_cross_out.T], axis=1),
     )
@@ -1689,8 +1769,7 @@
         bounds,
         first_in,
         self_w,
-        block_of(biases[0], width, 0)[None],
-        block_of(biases[1], width, 0)[None],
+        biases,
         cross_column,
         jnp.concatenate([w_up, w_down.T], axis=1),
         encoder_out,
@@ -1699,24 +1778,17 @@
     )
     cross_w = cross_w.reshape(4, model_width, 4 * width)
     after_self, second_in, ffn_near = sum_after_self(
-        terms, block_in, biases[2:3], norm_params[1], ffn_column
+        terms, block_in, biases, norm_params, ffn_column
     )
 
-    ok = (jnp.arange(4 * enc_rows, dtype=jnp.int32) < enc_lengths[0]).astype(F32)[:, None]
-
-    def all_blocks(vector, size):
-        return jnp.stack([block_of(vector, size, d) for d in range(4)])[:, None]
-
     cross_q, cross_k, cross_v, cross_mixed_t, cross_lse, after_cross, third_in, ffn_far = cross_forward(
-        ok,
+        enc_lengths,
         second_in,
         enc_all,
         cross_w,
-        all_blocks(biases[3], width),
-        all_blocks(biases[4], width),
+        biases,
         after_self,
-        biases[5:6],
-        norm_params[2],
+        norm_params,
         ffn_column,
         heads,
     )
@@ -1726,15 +1798,15 @@
         out_grad,
         ffn_near.reshape(2, model_width, 2 * hidden_width),
         ffn_far.reshape(2, model_width, 2 * hidden_width),
-        all_blocks(up_bias, hidden_width),
+        up_bias.reshape(4, hidden_width),
         after_cross,
-        biases[6:7],
-        norm_params[2],
+        biases,
+        norm_params,
     )
 
     by_shard = (2, groups_count // 2, 2, w_rows, hidden_width)
     second_grad, enc_terms, cross_sum, bias_cq_parts, bias_cv_parts, up_column, down_column = cross_backward(
-        ok,
+        enc_lengths,
         cross_low,
         second_in,
         enc_all,
@@ -1752,12 +1824,8 @@
     )
     cross_sum = cross_sum.reshape(2, groups_count // 2, 2, w_rows, 4 * width)
     self_wide, self_rows_grad, self_sums, summed_down, diagonal = middle(
-        second_grad, after_self, cross_rows_grad, norm_params[1], down_column, cross_sum
+        second_grad, after_self, cross_rows_grad, norm_params, down_column, cross_sum
     )
-    bias_cq_grad = blocks_placed([bias_cq_parts[d, 0] for d in range(4)])
-    bias_cv_grad = blocks_placed([bias_cv_parts[d, 0] for d in range(4)])
-    bias_up_grad = blocks_placed([bias_up_parts[d, 0] for d in range(4)])
-
     self_dq, self_dk, self_dv, summed_up, summed_cross, encoder_grad = self_backward(
         bounds,
         queries,
@@ -1775,64 +1843,42 @@
         heads,
         self_safe,
     )
-    grad_so_t = lax.dot_general(
-        self_wide, self_mixed_t, (((0,), (1,)), ((), ())), preferred_element_type=F32
-    ).astype(BF16)
-
-    def only_own(part):
-        out = jnp.zeros((model_width,), F32)
-        return lax.dynamic_update_slice_in_dim(out, part, member * width, 0)
-
-    vectors = jnp.concatenate(
-        [
-            jnp.zeros((2, model_width), F32),
-            self_sums[:2],
-            ffn_sums[:2],
-            jnp.stack(
-                [
-                    only_own(jnp.sum(self_dq.astype(F32), axis=0)),
-                    only_own(jnp.sum(self_dv.astype(F32), axis=0)),
-                    self_sums[2],
-                    bias_cq_grad,
-                    bias_cv_grad,
-                    ffn_sums[2],
-                    ffn_sums[3],
-                ]
-            ),
-            bias_up_grad.reshape(-1, model_width),
-        ]
-    )
-    vectors = jnp.pad(vectors, ((0, -vectors.shape[0] % 8), (0, 0)))
     input_grad, summed_self, vectors = tail(
         self_dq,
         self_dk,
         self_dv,
         self_w,
         first_in,
-        grad_so_t,
+        self_wide,
+        self_mixed_t,
         block_in,
         self_rows_grad,
-        norm_params[0],
-        vectors,
+        norm_params,
+        self_sums,
+        ffn_sums,
+        bias_cq_parts,
+        bias_cv_parts,
+        bias_up_parts,
     )
-    norm_total = vectors[:6].reshape(norm_params.shape)
-    bias_total = vectors[6:13]
-    up_total = vectors[13 : 13 + up_bias.shape[0] // model_width].reshape(-1)
-    scale = 1.0 / groups
+    scale = 1.0 / groups_count
+    output, input_grad, encoder_grad, g_qkv, g_so, g_cq, g_ckv, g_co, g_up, g_down = results(
+        output, input_grad, encoder_grad, summed_self, summed_cross, summed_up, summed_down, scale
+    )
+    vectors = vectors * scale
     return (
         output,
         input_grad,
         encoder_grad,
-        norm_total * scale,
-        summed_self[:, : 3 * width].reshape(w_qkv.shape) * scale,
-        summed_self[:, 3 * width :].T * scale,
-        summed_cross[:, :width] * scale,
-        summed_cross[:, width : 3 * width].reshape(w_cross_kv.shape) * scale,
-        summed_cross[:, 3 * width :].T * scale,
-        summed_up * scale,
-        summed_down.T * scale,
-        bias_total * scale,
-        up_total * scale,
+        vectors[:6].reshape(norm_params.shape),
+        g_qkv,
+        g_so.T,
+        g_cq,
+        g_ckv,
+        g_co.T,
+        g_up,
+        g_down.T,
+        vectors[6:13],
+        vectors[13:17].reshape(-1),
     )
 
 

time: 606 us -> 562 us (0.927)
  other arithmetic: 17.4 us -> 3.43 us
  local copies, waits for them, and re-layouts: 26.6 us -> 14.6 us
  Pallas kernels: 547 us -> 536 us
    pallas_call x1, Pallas kernels: 74.3 us -> 64.9 us  [cross_backward(): pl.pallas_call(functools.partial(cross_backward_kernel, heads=heads, bk=2...]
    pallas_call x0 -> x1, Pallas kernels: none -> 7.62 us  [results(): pl.pallas_call(functools.partial(results_kernel, scale=scale), grid=(step...]
    pallas_call x1, Pallas kernels: 75.8 us -> 68.6 us  [tail(): pl.pallas_call(functools.partial(tail_kernel, n=n, step_rows=512), in_spe...]
    reduce_sum x4 -> x0, other arithmetic: 6.91 us -> none  [the longest x1 1.87 us: layer_norm(): spread = jnp.mean(center * center, axis=-1, keepdims=True)]
    dynamic_update_slice x14 -> x0, local copies, waits for them, and re-layouts: 6.48 us -> none  [the longest x12 6.46 us: blocks_placed(): lax.dynamic_update_slice_in_dim(out, part, (member ^ distance) * size, 0)]
where the time goes in v10:
time: 562 us; the launch traced here: 555 us
  Pallas kernels  536 us (95%)
  local copies, waits for them, and re-layouts  14.6 us (3%)
    pallas_call x1, Pallas kernels, tail(): pl.pallas_call(functools.partial(tail_kernel, n=n, step_rows=512), in_spe...  68.6 us
    pallas_call x1, Pallas kernels, self_backward(): pl.pallas_call(functools.partial(self_backward_kernel, bk=bk, heads=heads...  66.3 us
    pallas_call x1, Pallas kernels, cross_forward(): pl.pallas_call(functools.partial(cross_forward_kernel, heads=heads), grid...  64.9 us
    pallas_call x1, Pallas kernels, cross_backward(): pl.pallas_call(functools.partial(cross_backward_kernel, heads=heads, bk=2...  64.9 us
    pallas_call x1, Pallas kernels, self_forward(): pl.pallas_call(functools.partial(self_forward_kernel, bk=bk, heads=heads,...  60.6 us
    pallas_call x1, Pallas kernels, sum_after_self(): pl.pallas_call(after_self_kernel, in_specs=[ANY, vmem, vmem, vmem, ANY],...  57.9 us
    pallas_call x1, Pallas kernels, feed_forward(): pl.pallas_call(functools.partial(feed_forward_kernel, chunks=chunks), gri...  53.5 us
    pallas_call x1, Pallas kernels, start_gather(): pl.pallas_call(functools.partial(start_kernel, n=n), in_specs=[pl.BlockSp...  50.7 us

profile of v10, /device:TPU:0, one launch (start us, length us, event | category | flops | bytes accessed | tf_op | source)
XLA Modules:
  0.0 555.3 jit_solution(8427804953441855279)
XLA Ops:
  0.6 0.0 copy-start
  0.7 0.0 copy-start.1
  1.4 1.3 reshape.68.b_ref
  2.7 0.9 copy.37
  3.6 0.9 copy.39
  4.6 0.9 copy.45
  5.5 1.1 copy.36
  6.6 0.2 copy.38
  6.8 1.7 pad_maximum_fusion.1
  8.5 0.0 copy-done
  8.5 0.1 copy.40
  8.6 0.0 copy-done.1
  8.6 0.8 pad_maximum_fusion.shard_ref
  9.4 50.7 %start_gather.1 = (bf16[2560,1024]{1,0:T(8,128)(2,1)}, bf16[4,2,128,1024]{3,2,1,0:T(8,128)(2,1)}, bf16[4,128,1024]{2,1,0:T(8,128)(2,1)}) custom-call(bf16[640,1024]{1,0:T(8,128)(2,1)} %rows_ref.3, f32[3,2,1024]{2,1,0:T(2,128)} %norm_ref.11, bf16[128,1024]{1,0:T(8,128)(2,1)} %get-tuple-element.167.self_ref, bf16[128,1024]{1,0:T(8,128)(2,1)} %get-tuple-element.168.cross_ref), custom_call_target="tpu_custom_call" | custom-call | bytes 104857600 | tf_op jit(solution)/shard_map/start_gather/pallas_call | solution.py:814
  60.2 60.6 %self_forward.1 = (bf16[2560,256]{1,0:T(8,128)(2,1)}, bf16[2560,256]{1,0:T(8,128)(2,1)}, bf16[2560,256]{1,0:T(8,128)(2,1)}, bf16[256,2560]{1,0:T(8,128)(2,1)}, b...) custom-call(s32[1,2]{1,0:T(1,128)} %b_ref.3, ...), custom_call_target="tpu_custom_call" | custom-call | flops 20132659200 | bytes 5242880 | tf_op jit(solution)/shard_map/self_forward/pallas_call | solution.py:944
  120.8 57.9 %sum_after_self.1 = (f32[640,1024]{1,0:T(8,128)}, bf16[640,1024]{1,0:T(8,128)(2,1)}, bf16[2,4,2,128,2048]{4,3,2,1,0:T(8,128)(2,1)}) custom-call(bf16[2560,1024]{1,0:T(8,128)(2,1)} %get-tuple-element.80.terms_ref, bf16[640,1024]{1,0:T(8,128)(2,1)} %rows_ref.3, f32[7,1024]{1,0:T(8,128)} %biases_ref.7, f32[3,2,1024]{2,1,0:T(2,128)} %norm_ref.11, ...), custom_call_target="tpu_custom_call" | custom-call | bytes 104857600 | tf_op jit(solution)/shard_map/sum_after_self/pallas_call | solution.py:1043
  178.7 64.9 %cross_forward.1 = (bf16[4,640,256]{2,1,0:T(8,128)(2,1)}, bf16[4,1024,256]{2,1,0:T(8,128)(2,1)}, bf16[4,1024,256]{2,1,0:T(8,128)(2,1)}, bf16[4,256,640]{2,1,0:T(...) custom-call(s32[1]{0:T(128)S(6)} %copy.49.len_ref, ...), custom_call_target="tpu_custom_call" | custom-call | flops 16106127360 | bytes 8388608 | tf_op jit(solution)/shard_map/cross_forward/pallas_call | solution.py:1316
  243.6 53.5 %feed_forward.1 = (f32[640,1024]{1,0:T(8,128)}, f32[640,1024]{1,0:T(8,128)}, bf16[640,1024]{1,0:T(8,128)(2,1)}, f32[8,1024]{1,0:T(8,128)}, bf16[2,1024,1024]{2,1...) custom-call(bf16[640,1024]{1,0:T(8,128)(2,1)} %get-tuple-element.86., ...), custom_call_target="tpu_custom_call" | custom-call | flops 32212254720 | bytes 41943040 | tf_op jit(solution)/shard_map/feed_forward/pallas_call | solution.py:1509
  297.1 64.9 %cross_backward.1 = (f32[640,1024]{1,0:T(8,128)}, bf16[1024,1024]{1,0:T(8,128)(2,1)}, bf16[2,1024,1024]{2,1,0:T(8,128)(2,1)}, f32[4,1,256]{2,1,0:T(1,128)}, f32[...) custom-call(s32[1]{0:T(128)S(6)} %copy.49.len_ref, ...), custom_call_target="tpu_custom_call" | custom-call | flops 32212254720 | bytes 16777216 | tf_op jit(solution)/shard_map/cross_backward/pallas_call | solution.py:1676
  362.0 40.6 %middle.1 = (bf16[2560,1024]{1,0:T(8,128)(2,1)}, f32[640,1024]{1,0:T(8,128)}, f32[8,1024]{1,0:T(8,128)}, f32[128,1024]{1,0:T(8,128)}, bf16[4,128,1024]{2,1,0:T(8,128)(2,1)}) custom-call(f32[640,1024]{1,0:T(8,128)} %get-tuple-element.105.back_ref, f32[640,1024]{1,0:T(8,128)} %get-tuple-element.85.rows_ref, f32[640,1024]{1,0:T(8,128)} %get-tuple-element.106.grad_ref, ...), custom_call_target="tpu_custom_call" | custom-call | bytes 104857600 | tf_op jit(solution)/shard_map/middle/pallas_call | solution.py:490
  402.6 66.3 %self_backward.1 = (bf16[2560,256]{1,0:T(8,128)(2,1)}, bf16[2560,256]{1,0:T(8,128)(2,1)}, bf16[2560,256]{1,0:T(8,128)(2,1)}, f32[128,1024]{1,0:T(8,128)}, f32[128,1024]{1,0:T(8,128)}, /*index=5*/f32[256,1024]{1,0:T(8,128)}) custom-call(s32[1,2]{1,0:T(1,128)} %b_ref.3, bf16[2560,256]{1,0:T(8,128)(2,1)} %get-tuple-element.91.q_ref, ...), custom_call_target="tpu_custom_call" | custom-call | flops 40265318400 | bytes 10485760 | tf_op jit(solution)/shard_map/self_backward/pallas_call | solution.py:1174
  468.9 68.6 %tail.1 = (f32[640,1024]{1,0:T(8,128)}, f32[128,1024]{1,0:T(8,128)}, f32[24,1024]{1,0:T(8,128)}) custom-call(bf16[2560,256]{1,0:T(8,128)(2,1)} %get-tuple-element.115.dq_ref, bf16[2560,256]{1,0:T(8,128)(2,1)} %get-tuple-element.116.dk_ref, bf16[2560,256]{1,0:T(8,128)(2,1)} %get-tuple-element.117.dv_ref, bf16[1024,1024]{1,0:T(8,128)(2,1)} %bitcast.25, ...), custom_call_target="tpu_custom_call" | custom-call | bytes 104857600 | tf_op jit(solution)/shard_map/tail/pallas_call | solution.py:673
  537.5 0.9 broadcast_multiply_fusion
  538.4 0.6 copy.48
  539.0 0.6 slice.13
  539.6 0.6 reshape.72
  540.3 7.6 %results.1 = (f32[640,1024]{1,0:T(8,128)}, f32[640,1024]{1,0:T(8,128)}, f32[256,1024]{1,0:T(8,128)}, f32[128,3,256]{2,1,0:T(4,128)}, f32[128,256]{1,0:T(8,128)},...) custom-call(f32[640,1024]{1,0:T(8,128)} %get-tuple-element.90.output, ...), custom_call_target="tpu_custom_call" | custom-call | bytes 20971520 | tf_op jit(solution)/shard_map/results/pallas_call | solution.py:730
  547.9 1.7 copy.42
  549.5 1.7 copy.43
  551.2 1.9 copy.41
  553.1 2.0 copy.44
  (2 shorter events, 0.0 us)
Async XLA Ops:
  0.6 7.8 %copy-start = (bf16[1024,128]{1,0:T(8,128)(2,1)S(1)}, bf16[1024,128]{1,0:T(8,128)(2,1)}, u32[]{:S(2)}) copy-start(bf16[1024,128]{1,0:T(8,128)(2,1)} %param.27) | copy-start | bytes 786436
  0.7 8.0 %copy-start.1 = (bf16[128,1024]{1,0:T(8,128)(2,1)S(1)}, bf16[128,1024]{1,0:T(8,128)(2,1)}, u32[]{:S(2)}) copy-start(bf16[128,1024]{1,0:T(8,128)(2,1)} %param.26) | copy-start | bytes 786436

commit v11 on v10

--- a/solution.py
+++ b/solution.py
@@ -28,9 +28,22 @@
     return lax.dot_general(a, b, (((0,), (0,)), ((), ())), preferred_element_type=F32)
 
 
+LANES = 128
+
+
+def lanes_of(h, size):
+    group = h * size // LANES
+    return group, slice(group * LANES, (group + 1) * LANES)
+
+
 def head_only(x, h, size):
-    lane = lax.broadcasted_iota(jnp.int32, x.shape, 1)
-    return jnp.where((lane >= h * size) & (lane < (h + 1) * size), x, jnp.zeros_like(x))
+    group, part = lanes_of(h, size)
+    lane = group * LANES + lax.broadcasted_iota(jnp.int32, (x.shape[0], LANES), 1)
+    return jnp.where((lane >= h * size) & (lane < (h + 1) * size), x[:, part], jnp.zeros((), x.dtype))
+
+
+def add_group(sums, group, value):
+    sums[group] = value if group not in sums else sums[group] + value
 
 
 def self_bad(b_ref, q_start, k_start, bq, bk, causal):
@@ -42,26 +55,25 @@
     return bad
 
 
-def over_keys(i, bq, bk, safe, block, between=()):
-    diagonal = i * (bq // bk)
-
+def over_keys(i, bq, safe, block, between=()):
     def visit(j, c):
         for at_i, at_j, action in between:
             pl.when((i == at_i) & (j == at_j))(action)
 
-        @pl.when(j < safe // bk)
+        @pl.when(j < safe // bq)
         def _():
-            block(j, "none")
-
-        @pl.when(j >= safe // bk)
+            block(j * bq, bq, 0, "none")
+
+        @pl.when(j >= safe // bq)
         def _():
-            block(j, "segment")
+            block(j * bq, bq, 0, "segment")
 
         return c
 
-    lax.fori_loop(0, diagonal, visit, 0)
-    for step in range(bq // bk):
-        block(diagonal + step, "causal")
+    lax.fori_loop(0, i, visit, 0)
+    half = bq // 2
+    block(i * bq, half, 0, "causal")
+    block(i * bq + half, half, half, "causal")
 
 
 CORE = ("tensor", 1)
@@ -184,11 +196,13 @@
         for copy in self.second + self.core_second:
             copy.start()
 
-    def end(self):
+    def last(self):
         for copy in self.second:
             copy.wait_recv()
         for copy in self.core_third:
             copy.start()
+
+    def end(self):
         self.own.wait()
         for copy in self.first + self.second:
             copy.wait_send()
@@ -358,7 +372,8 @@
 
 
 class RowSum:
-    def __init__(self, links, terms, buffers):
+    def __init__(self, links, terms, buffers, left=False):
+        self.left = left
         self.near, self.far, self.got_near, self.got_far, self.got_x = buffers
         count = self.near.shape[0]
 
@@ -388,7 +403,7 @@
         self.loads[0].wait()
         self.core[1].wait_recv()
         self.over_x.wait_recv()
-        for copy in self.core + [self.over_x]:
+        for copy in self.core + ([] if self.left else [self.over_x]):
             copy.wait_send()
 
     def total(self, rows):
@@ -709,13 +724,13 @@
     def _():
         for k in range(3):
             qkv_out[:, k, :] = self_ref[:, k * width : (k + 1) * width] * scale
-        so_out[...] = self_ref[:, 3 * width :] * scale
+        so_out[...] = (self_ref[:, 3 * width :] * scale).T
         cq_out[...] = cross_ref[:, :width] * scale
         for k in range(2):
             ckv_out[:, k, :] = cross_ref[:, (k + 1) * width : (k + 2) * width] * scale
-        co_out[...] = cross_ref[:, 3 * width :] * scale
+        co_out[...] = (cross_ref[:, 3 * width :] * scale).T
         up_out[...] = up_ref[...] * scale
-        down_out[...] = down_ref[...] * scale
+        down_out[...] = (down_ref[...] * scale).T
 
 
 def results(output, grad, encoder, self_w, cross_w, up, down, scale):
@@ -726,7 +741,7 @@
     def rows(value):
         return pl.BlockSpec((value.shape[0] // steps, value.shape[1]), lambda i: (i, 0))
 
-    shapes = [(r, 3, width), (r, width), (r, width), (r, 2, width), (r, width), up.shape, down.shape]
+    shapes = [(r, 3, width), (width, r), (r, width), (r, 2, width), (width, r), up.shape, down.shape[::-1]]
     return pl.pallas_call(
         functools.partial(results_kernel, scale=scale),
         grid=(steps,),
@@ -741,7 +756,8 @@
 
 
 def start_kernel(
-    in_ref, norm_ref, self_ref, cross_ref, rows_out, self_out, cross_out, rows_ref, send_sems, recv_sems, local_sems, *, n
+    in_ref, norm_ref, qkv_ref, so_ref, cq_ref, ckv_ref, co_ref,
+    rows_out, self_out, cross_out, rows_ref, self_ref, cross_ref, send_sems, recv_sems, local_sems, *, n
 ):
     links = Links(send_sems, recv_sems, local_sems)
     member, z, y = links.tensor, links.dp // 2, links.dp % 2
@@ -763,6 +779,14 @@
         links.local(self_ref, self_out.at[z, y]),
         links.local(cross_ref, cross_out.at[z]),
     ]
+    width = cq_ref.shape[1]
+    for k in range(3):
+        self_ref[:, k * width : (k + 1) * width] = qkv_ref[:, k, :]
+    self_ref[:, 3 * width :] = so_ref[...].T
+    cross_ref[:, :width] = cq_ref[...]
+    for k in range(2):
+        cross_ref[:, (k + 1) * width : (k + 2) * width] = ckv_ref[:, k, :]
+    cross_ref[:, 3 * width :] = co_ref[...].T
     links.greet([CORE, X, Y] + z_ways(n))
     for copy in over_y + local[1:]:
         copy.start()
@@ -808,64 +832,70 @@
             copy.wait_send()
 
 
-def start_gather(rows, norm, self_shard, cross_shard):
+def start_gather(rows, norm, qkv, self_out, cross_q, cross_kv, cross_out):
     n = lax.axis_size("dp")
-    r, c = self_shard.shape
+    r, c = cross_q.shape[0], 4 * cross_q.shape[1]
     return pl.pallas_call(
         functools.partial(start_kernel, n=n),
-        in_specs=[pl.BlockSpec(memory_space=pltpu.VMEM)] * 4,
+        in_specs=[pl.BlockSpec(memory_space=pltpu.VMEM)] * 7,
         out_specs=[ANY] * 3,
         out_shape=[
             jax.ShapeDtypeStruct((4 * rows.shape[0], rows.shape[1]), BF16),
             jax.ShapeDtypeStruct((n // 2, 2, r, c), BF16),
-            jax.ShapeDtypeStruct((n // 2,) + cross_shard.shape, BF16),
+            jax.ShapeDtypeStruct((n // 2, r, c), BF16),
         ],
-        scratch_shapes=[pltpu.VMEM(rows.shape, BF16)] + link_scratch(2 * n + 8, 3),
+        scratch_shapes=[pltpu.VMEM(rows.shape, BF16)] + [pltpu.VMEM((r, c), BF16)] * 2 + link_scratch(2 * n + 8, 3),
         compiler_params=pltpu.CompilerParams(
             vmem_limit_bytes=VMEM_LIMIT, collective_id=0, has_side_effects=True
         ),
         cost_estimate=pl.CostEstimate(flops=0, bytes_accessed=100 * 2**20, transcendentals=0),
         name="start_gather",
-    )(rows, norm, self_shard, cross_shard)
+    )(rows, norm, qkv, self_out, cross_q, cross_kv, cross_out)
 
 
 def self_forward_kernel(
-    b_ref, x_ref, w_ref, biases_ref, column_ref, shard_ref, enc_ref,
-    q_out, k_ref, v_out, kt_out, ot_ref, lse_ref, terms_ref, whole, next_column, enc_out,
-    vt_ref, m_s, l_s, acc, column, send_sems, recv_sems, local_sems, *, bk, heads, safe, n
+    b_ref, x_ref, w_ref, biases_ref, column_ref, up_ref, down_ref,
+    q_out, k_ref, v_out, kt_out, ot_ref, lse_ref, terms_ref, whole, next_column,
+    vt_ref, m_s, l_s, acc, column, shard, send_sems, recv_sems, local_sems, *, heads, safe, n
 ):
     i = pl.program_id(0)
     last = pl.num_programs(0) - 1
     bq, width = q_out.shape
     links = Links(send_sems, recv_sems, local_sems)
     spread = Spread(links, column_ref, column, whole)
-    stages = column_stages(links, shard_ref, next_column, n)
-    enc_count = enc_ref.shape[0]
-
-    def place(distance):
-        return enc_out.at[pl.ds(pl.multiple_of((links.tensor ^ distance) * enc_count, enc_count), enc_count)]
-
-    enc_x = links.copy(enc_ref, place(0), X)
-    enc_core = [links.copy(enc_ref, place(0), CORE), links.copy(place(2), place(2), CORE)]
-    local = [links.local(shard_ref, next_column.at[links.dp // 2]), links.local(enc_ref, place(0))]
+    hidden = up_ref.shape[1]
+    halves = []
+    for k in range(2):
+        part = pl.ds(k * hidden, hidden)
+        halves.append(column_stages(links, shard.at[:, part], next_column.at[:, :, part], n))
+    keep = links.local(shard, next_column.at[links.dp // 2])
+
+    def start_stage(k, step):
+        for copy, _ in halves[k][step]:
+            copy.start()
+
+    def next_stage(k, step):
+        for copy, _ in halves[k][step]:
+            copy.wait_recv()
+        if step + 1 < len(halves[k]):
+            start_stage(k, step + 1)
 
     @pl.when(i == 0)
     def _():
+        shard[:, :hidden] = up_ref[...]
+        shard[:, hidden:] = down_ref[...].T
         links.greet([CORE, X, Y] + z_ways(n))
+        start_stage(0, 0)
         spread.start()
-        for copy in local + enc_core[:1]:
-            copy.start()
-        for copy, _ in stages[0]:
-            copy.start()
-
-    def onward():
-        spread.middle()
-        enc_x.start()
-        for k in range(1, len(stages)):
-            for copy, _ in stages[k - 1]:
-                copy.wait_recv()
-            for copy, _ in stages[k]:
-                copy.start()
+        keep.start()
+
+    def onward_one():
+        next_stage(0, 0)
+        start_stage(1, 0)
+
+    @pl.when(i == last)
+    def _():
+        next_stage(1, 0)
 
     mine = pl.ds(pl.multiple_of(links.tensor * width, width), width)
     projected = dot_nn(x_ref[...], w_ref[:, : 3 * width])
@@ -886,14 +916,13 @@
     scaled = query * jnp.asarray(1.0 / math.sqrt(hd), BF16)
     q_heads = [head_only(scaled, h, hd) for h in range(heads)]
 
-    def block(j, mode):
-        rows = pl.ds(pl.multiple_of(j * bk, bk), bk)
-        keys = k_ref[rows, :]
-        m_old = m_s[...]
-        l_old = l_s[...]
-        scores = [dot_nt(keys, q_heads[h]) for h in range(heads)]
+    def block(first, size, skip, mode):
+        rows = pl.ds(pl.multiple_of(first, size), size)
+        m_old = m_s[:, skip:]
+        l_old = l_s[:, skip:]
+        scores = [dot_nt(k_ref[rows, lanes_of(h, hd)[1]], q_heads[h][skip:]) for h in range(heads)]
         if mode != "none":
-            bad = self_bad(b_ref, i * bq, j * bk, bq, bk, mode == "causal")
+            bad = self_bad(b_ref, i * bq + skip, first, bq - skip, size, mode == "causal")
             scores = [jnp.where(bad, NEGATIVE, s) for s in scores]
         m_out, l_out, a_out = [], [], []
         for h in range(heads):
@@ -903,13 +932,13 @@
             expos = jnp.exp(scores[h] - m_new)
             l_out.append(l_old[h : h + 1, :] * shrink + jnp.sum(expos, axis=0, keepdims=True))
             m_out.append(m_new)
-            a_out.append(acc[part, :] * shrink + dot_nn(vt_ref[part, rows], expos.astype(BF16)))
-        m_s[...] = jnp.concatenate(m_out, 0)
-        l_s[...] = jnp.concatenate(l_out, 0)
+            a_out.append(acc[part, skip:] * shrink + dot_nn(vt_ref[part, rows], expos.astype(BF16)))
+        m_s[:, skip:] = jnp.concatenate(m_out, 0)
+        l_s[:, skip:] = jnp.concatenate(l_out, 0)
         for h in range(heads):
-            acc[h * hd : (h + 1) * hd, :] = a_out[h]
-
-    over_keys(i, bq, bk, safe, block, [(3, 2, onward)])
+            acc[h * hd : (h + 1) * hd, skip:] = a_out[h]
+
+    over_keys(i, bq, safe, block, [(2, 0, onward_one), (3, 2, spread.middle), (4, 3, spread.last)])
     inverse = 1.0 / l_s[...]
     for h in range(heads):
         part = slice(h * hd, (h + 1) * hd)
@@ -919,30 +948,28 @@
 
     @pl.when(i == last)
     def _():
+        for k in range(2):
+            for step in range(1, len(halves[k])):
+                next_stage(k, step)
         spread.end()
-        enc_x.wait_recv()
-        enc_core[1].start()
-        for k, stage in enumerate(stages):
-            for copy, _ in stage:
-                copy.wait_send()
-                if k == len(stages) - 1:
-                    copy.wait_recv()
-        enc_x.wait_send()
-        for copy in local + enc_core:
-            copy.wait()
-
-
-def self_forward(bounds, x, w, biases, column, shard, encoder, heads, safe):
+        for stages in halves:
+            for stage in stages:
+                for copy, _ in stage:
+                    copy.wait_send()
+        keep.wait()
+
+
+def self_forward(bounds, x, w, biases, column, up, down, heads, safe):
     n, model = x.shape
     width = w.shape[1] // 4
-    bq = bk = 512
+    bq = 512
     dp = lax.axis_size("dp")
     m, r, c = column.shape
-    enc_count = encoder.shape[0]
+    shard = (up.shape[0], 2 * up.shape[1])
     by_rows_spec = pl.BlockSpec((bq, width), lambda i: (i, 0))
     by_columns_spec = pl.BlockSpec((width, bq), lambda i: (0, i))
     return pl.pallas_call(
-        functools.partial(self_forward_kernel, bk=bk, heads=heads, safe=safe, n=dp),
+        functools.partial(self_forward_kernel, heads=heads, safe=safe, n=dp),
         grid=(n // bq,),
         in_specs=[
             pl.BlockSpec(memory_space=pltpu.SMEM),
@@ -950,8 +977,8 @@
             const((model, 4 * width)),
             const(biases.shape),
             ANY,
-            const(shard.shape),
-            const(encoder.shape),
+            const(up.shape),
+            const(down.shape),
         ],
         out_specs=[
             by_rows_spec,
@@ -961,7 +988,6 @@
             by_columns_spec,
             pl.BlockSpec((heads, bq), lambda i: (0, i)),
             pl.BlockSpec((bq, model), lambda i: (i, 0)),
-            ANY,
             ANY,
             ANY,
         ],
@@ -974,8 +1000,7 @@
             jax.ShapeDtypeStruct((heads, n), F32),
             jax.ShapeDtypeStruct((n, model), BF16),
             jax.ShapeDtypeStruct((4, m, 2, r, c), BF16),
-            jax.ShapeDtypeStruct((m,) + shard.shape, BF16),
-            jax.ShapeDtypeStruct((4 * enc_count, model), BF16),
+            jax.ShapeDtypeStruct((m,) + shard, BF16),
         ],
         scratch_shapes=[
             pltpu.VMEM((width, n), BF16),
@@ -983,8 +1008,9 @@
             pltpu.VMEM((heads, bq), F32),
             pltpu.VMEM((width, bq), F32),
             pltpu.VMEM((m, r, c), BF16),
+            pltpu.VMEM(shard, BF16),
         ]
-        + link_scratch(11 + m, 4),
+        + link_scratch(8 + 2 * m, 3),
         compiler_params=pltpu.CompilerParams(
             vmem_limit_bytes=VMEM_LIMIT, collective_id=1, has_side_effects=True
         ),
@@ -992,15 +1018,15 @@
             flops=12 * n * n * width, bytes_accessed=8 * n * width, transcendentals=n * n * heads // 2
         ),
         name="self_forward",
-    )(bounds, x, w, biases, column, shard, encoder)
+    )(bounds, x, w, biases, column, up, down)
 
 
 def after_self_kernel(
-    terms_ref, rows_ref, biases_ref, norm_ref, column_ref,
-    after_out, second_out, whole_out, *scratch
+    terms_ref, rows_ref, biases_ref, norm_ref, column_ref, enc_ref,
+    after_out, second_out, whole_out, enc_out, *scratch
 ):
     links = Links(*scratch[-3:])
-    rows_sum = RowSum(links, terms_ref, scratch[:5])
+    rows_sum = RowSum(links, terms_ref, scratch[:5], left=True)
     column = scratch[5]
     y = links.dp % 2
     near_out, core_out = whole_out.at[0], whole_out.at[1]
@@ -1011,14 +1037,26 @@
         links.copy(column, core_out.at[:, y], CORE),
         links.copy(near_out.at[:, 1 - y], core_out.at[:, 1 - y], CORE),
     ]
+    enc_count = enc_ref.shape[0]
+
+    def place(distance):
+        return enc_out.at[pl.ds(pl.multiple_of((links.tensor ^ distance) * enc_count, enc_count), enc_count)]
+
+    enc_x = links.copy(enc_ref, place(0), X)
+    enc_core = [links.copy(enc_ref, place(0), CORE), links.copy(place(2), place(2), CORE)]
+    enc_own = links.local(enc_ref, place(0))
     links.greet([CORE, X, Y])
     rows_sum.start()
     load.start()
     load.wait()
     over_y.start()
     own.start()
+    enc_own.start()
     rows_sum.middle()
     over_core[0].start()
+    enc_core[0].start()
+    rows_sum.over_x.wait_send()
+    enc_x.start()
     rows_sum.end()
 
     def norm(rows):
@@ -1028,40 +1066,43 @@
         second_out[rows, :] = (xhat * norm_ref[1, 0:1, :] + norm_ref[1, 1:2, :]).astype(BF16)
 
     by_rows(after_out.shape[0], 64, norm)
+    enc_x.wait_recv()
+    enc_core[1].start()
     over_y.wait_recv()
     over_core[1].start()
+    enc_x.wait_send()
     over_y.wait_send()
-    own.wait()
-    for copy in over_core:
+    for copy in [own, enc_own] + over_core + enc_core:
         copy.wait()
 
 
-def sum_after_self(terms, rows, biases, norm, column):
+def sum_after_self(terms, rows, biases, norm, column, encoder):
     count, model = rows.shape
     m, r, c = column.shape
     vmem = pl.BlockSpec(memory_space=pltpu.VMEM)
     return pl.pallas_call(
         after_self_kernel,
-        in_specs=[ANY, vmem, vmem, vmem, ANY],
-        out_specs=[vmem, vmem, ANY],
+        in_specs=[ANY, vmem, vmem, vmem, ANY, vmem],
+        out_specs=[vmem, vmem, ANY, ANY],
         out_shape=[
             jax.ShapeDtypeStruct((count, model), F32),
             jax.ShapeDtypeStruct((count, model), BF16),
             jax.ShapeDtypeStruct((2, m, 2, r, c), BF16),
+            jax.ShapeDtypeStruct((4 * encoder.shape[0], model), BF16),
         ],
-        scratch_shapes=row_sum_scratch(count, model) + [pltpu.VMEM((m, r, c), BF16)] + link_scratch(6, 4),
+        scratch_shapes=row_sum_scratch(count, model) + [pltpu.VMEM((m, r, c), BF16)] + link_scratch(9, 5),
         compiler_params=pltpu.CompilerParams(
             vmem_limit_bytes=VMEM_LIMIT, collective_id=8, has_side_effects=True
         ),
         cost_estimate=pl.CostEstimate(flops=0, bytes_accessed=100 * 2**20, transcendentals=0),
         name="sum_after_self",
-    )(terms, rows, biases, norm, column)
+    )(terms, rows, biases, norm, column, encoder)
 
 
 def self_backward_kernel(
     b_ref, q_ref, k_ref, v_ref, kt_ref, wide_ref, w_ref, mt_ref, lse_ref,
     up_ref, cross_ref, diagonal_ref, enc_ref,
-    dq_ref, dk_ref, dv_ref, up_out, cross_out, enc_out, dka, dva, dqa, *scratch, bk, heads, safe, n
+    dq_ref, dk_ref, dv_ref, up_out, cross_out, enc_out, dka, dva, dqa, *scratch, heads, safe, n
 ):
     i = pl.program_id(0)
     links = Links(*scratch[-3:])
@@ -1116,29 +1157,28 @@
     lse = lse_ref[...]
     dqa[...] = jnp.zeros_like(dqa)
 
-    def block(j, mode):
-        rows = pl.ds(pl.multiple_of(j * bk, bk), bk)
-        keys = k_ref[rows, :]
-        values = v_ref[rows, :]
-        scores = [dot_nt(keys, q_heads[h]) for h in range(heads)]
-        dprobs = [dot_nt(values, d_heads[h]) for h in range(heads)]
+    def block(first, size, skip, mode):
+        rows = pl.ds(pl.multiple_of(first, size), size)
+        scores = [dot_nt(k_ref[rows, lanes_of(h, hd)[1]], q_heads[h][skip:]) for h in range(heads)]
+        dprobs = [dot_nt(v_ref[rows, lanes_of(h, hd)[1]], d_heads[h][skip:]) for h in range(heads)]
         if mode != "none":
-            bad = self_bad(b_ref, i * bq, j * bk, bq, bk, mode == "causal")
+            bad = self_bad(b_ref, i * bq + skip, first, bq - skip, size, mode == "causal")
             scores = [jnp.where(bad, NEGATIVE, s) for s in scores]
-        dv_sum, dk_sum = None, None
+        dv_sums, dk_sums = {}, {}
         for h in range(heads):
             part = slice(h * hd, (h + 1) * hd)
-            probs = jnp.exp(scores[h] - lse[h : h + 1, :])
-            ds = (probs * (dprobs[h] - inner[h])).astype(BF16)
-            dv_h = dot_nn(probs.astype(BF16), d_heads[h])
-            dk_h = dot_nn(ds, q_heads[h])
-            dv_sum = dv_h if dv_sum is None else dv_sum + dv_h
-            dk_sum = dk_h if dk_sum is None else dk_sum + dk_h
-            dqa[part, :] += dot_nn(kt_ref[part, rows], ds)
-        dva[rows, :] += dv_sum
-        dka[rows, :] += dk_sum
-
-    over_keys(i, bq, bk, safe, block, [(3, 2, sum_cross), (4, 2, next_cross)])
+            group, _ = lanes_of(h, hd)
+            probs = jnp.exp(scores[h] - lse[h : h + 1, skip:])
+            ds = (probs * (dprobs[h] - inner[h][:, skip:])).astype(BF16)
+            add_group(dv_sums, group, dot_nn(probs.astype(BF16), d_heads[h][skip:]))
+            add_group(dk_sums, group, dot_nn(ds, q_heads[h][skip:]))
+            dqa[part, skip:] += dot_nn(kt_ref[part, rows], ds)
+        for group in dv_sums:
+            part = slice(group * LANES, (group + 1) * LANES)
+            dva[rows, part] += dv_sums[group]
+            dka[rows, part] += dk_sums[group]
+
+    over_keys(i, bq, safe, block, [(3, 2, sum_cross), (4, 2, next_cross)])
     dq_ref[...] = (dqa[...] * scale).astype(BF16).T
 
     @pl.when(i == pl.num_programs(0) - 1)
@@ -1169,10 +1209,10 @@
     m, r, c = up_column.shape
     cross_c = cross_sum.shape[4]
     enc_shape = (enc_terms.shape[0] // 4, enc_terms.shape[1])
-    bq = bk = 512
+    bq = 512
     some = pl.BlockSpec((bq, width), lambda i: (i, 0))
     return pl.pallas_call(
-        functools.partial(self_backward_kernel, bk=bk, heads=heads, safe=safe, n=dp),
+        functools.partial(self_backward_kernel, heads=heads, safe=safe, n=dp),
         grid=(n // bq,),
         in_specs=[
             pl.BlockSpec(memory_space=pltpu.SMEM),
@@ -1256,12 +1296,11 @@
         spread.start()
         after_ref[...] = rows_ref[...] + biases_ref[5:6, :]
 
-    for step, ready in ((1, (0,)), (2, (1, 2)), (3, (3,))):
-
-        @pl.when(i == step)
-        def _():
-            for k in ready:
-                spread.onward(k)
+    def onward(*when):
+        for step, k in when:
+            pl.when(i == step)(functools.partial(spread.onward, k))
+
+    onward((1, 0), (3, 3))
 
     width = q_out.shape[2]
     hd = width // heads
@@ -1276,7 +1315,7 @@
     values_t = values.T
     scaled = query * jnp.asarray(1.0 / math.sqrt(hd), BF16)
     ok = lax.broadcasted_iota(jnp.int32, (keys.shape[0], 1), 0) < len_ref[0]
-    scores = [dot_nt(keys, head_only(scaled, h, hd)) for h in range(heads)]
+    scores = [dot_nt(keys[:, lanes_of(h, hd)[1]], head_only(scaled, h, hd)) for h in range(heads)]
     mixed = []
     for h in range(heads):
         part = slice(h * hd, (h + 1) * hd)
@@ -1287,6 +1326,8 @@
         mixed.append((dot_nn(values_t[part, :], expos.astype(BF16)) * (1.0 / total)).astype(BF16))
         ot_ref[0, part, :] = mixed[h]
         lse_ref[0, h : h + 1, :] = largest + jnp.log(total)
+        if h == heads // 2 - 1:
+            onward((1, 1), (2, 2), (3, 4))
     after_ref[...] += dot_nt(jnp.concatenate(mixed, 0).T, w_ref[0, :, 3 * width :])
 
     @pl.when(i == last)
@@ -1296,7 +1337,7 @@
             third_ref[rows, :] = (xhat * norm_ref[2, 0:1, :] + norm_ref[2, 1:2, :]).astype(BF16)
 
         by_rows(after_ref.shape[0], 128, norm)
-        for k in range(4, pieces):
+        for k in range(5, pieces):
             spread.onward(k)
         for k in range(pieces):
             spread.last(k)
@@ -1425,7 +1466,9 @@
         fetch(s + 1, lambda copy: copy.start())
 
     up_ref, down_ref = loaded.at[s % 2, 0], loaded.at[s % 2, 1]
-    shift = b_ref[pl.ds(links.tensor ^ (3 - turn), 1), pl.ds(pl.multiple_of(chunk * size, size), size)]
+    lines = size // LANES
+    line = ((links.tensor ^ (3 - turn)) * chunks + chunk) * lines
+    shift = jnp.concatenate([b_ref[pl.ds(line + k, 1), :] for k in range(lines)], axis=1)
     pre_act = dot_nn(x_ref[...], up_ref[...]) + shift
     hidden_grad = dot_nn(dy_ref[...], down_ref[...])
     normal_cdf = 0.5 * (1.0 + lax.erf(pre_act * (1.0 / math.sqrt(2.0))))
@@ -1609,23 +1652,20 @@
     dkv = []
     for j in range(n // bk):
         span = slice(j * bk, (j + 1) * bk)
-        keys = k_ref[0, span, :]
-        values = v_ref[0, span, :]
         ok = j * bk + lax.broadcasted_iota(jnp.int32, (bk, 1), 0) < len_ref[0]
-        scores = [dot_nt(keys, q_heads[h]) for h in range(heads)]
-        dprobs = [dot_nt(values, d_heads[h]) for h in range(heads)]
-        dv_sum, dk_sum = None, None
+        scores = [dot_nt(k_ref[0, span, lanes_of(h, hd)[1]], q_heads[h]) for h in range(heads)]
+        dprobs = [dot_nt(v_ref[0, span, lanes_of(h, hd)[1]], d_heads[h]) for h in range(heads)]
+        dv_sums, dk_sums = {}, {}
         for h in range(heads):
             part = slice(h * hd, (h + 1) * hd)
+            group, _ = lanes_of(h, hd)
             probs = jnp.exp(jnp.where(ok, scores[h], NEGATIVE) - lse[h : h + 1, :])
             ds = (probs * (dprobs[h] - inner[h])).astype(BF16)
-            dv_h = dot_nn(probs.astype(BF16), d_heads[h])
-            dk_h = dot_nn(ds, q_heads[h])
-            dv_sum = dv_h if dv_sum is None else dv_sum + dv_h
-            dk_sum = dk_h if dk_sum is None else dk_sum + dk_h
+            add_group(dv_sums, group, dot_nn(probs.astype(BF16), d_heads[h]))
+            add_group(dk_sums, group, dot_nn(ds, q_heads[h]))
             dq_h = dot_nn(keys_t[part, span], ds)
             dq[h] = dq_h if dq[h] is None else dq[h] + dq_h
-        block = jnp.concatenate([dk_sum.astype(BF16), dv_sum.astype(BF16)], 1)
+        block = jnp.concatenate([sums_of[g].astype(BF16) for sums_of in (dk_sums, dv_sums) for g in sorted(sums_of)], 1)
         enc_acc[span, :] += dot_nt(block, w_keyval[...])
         dkv.append(block)
     dq = (jnp.concatenate(dq, 0) * scale).astype(BF16).T
@@ -1759,26 +1799,29 @@
     first_in, self_w, cross_column = start_gather(
         block_in,
         norm_params,
-        jnp.concatenate([w_qkv.reshape(w_rows, 3 * width), w_self_out.T], axis=1),
-        jnp.concatenate([w_cross_q, w_cross_kv.reshape(w_rows, 2 * width), w_cross_out.T], axis=1),
+        w_qkv,
+        w_self_out,
+        w_cross_q,
+        w_cross_kv,
+        w_cross_out,
     )
     self_w = self_w.reshape(model_width, 4 * width)
 
     self_safe = 1024
-    queries, key_rows, value_rows, keys_t, self_mixed_t, self_lse, terms, cross_w, ffn_column, enc_all = self_forward(
+    queries, key_rows, value_rows, keys_t, self_mixed_t, self_lse, terms, cross_w, ffn_column = self_forward(
         bounds,
         first_in,
         self_w,
         biases,
         cross_column,
-        jnp.concatenate([w_up, w_down.T], axis=1),
-        encoder_out,
+        w_up,
+        w_down,
         heads,
         self_safe,
     )
     cross_w = cross_w.reshape(4, model_width, 4 * width)
-    after_self, second_in, ffn_near = sum_after_self(
-        terms, block_in, biases, norm_params, ffn_column
+    after_self, second_in, ffn_near, enc_all = sum_after_self(
+        terms, block_in, biases, norm_params, ffn_column, encoder_out
     )
 
     cross_q, cross_k, cross_v, cross_mixed_t, cross_lse, after_cross, third_in, ffn_far = cross_forward(
@@ -1798,7 +1841,7 @@
         out_grad,
         ffn_near.reshape(2, model_width, 2 * hidden_width),
         ffn_far.reshape(2, model_width, 2 * hidden_width),
-        up_bias.reshape(4, hidden_width),
+        up_bias.reshape(-1, LANES),
         after_cross,
         biases,
         norm_params,
@@ -1871,12 +1914,12 @@
         encoder_grad,
         vectors[:6].reshape(norm_params.shape),
         g_qkv,
-        g_so.T,
+        g_so,
         g_cq,
         g_ckv,
-        g_co.T,
+        g_co,
         g_up,
-        g_down.T,
+        g_down,
         vectors[6:13],
         vectors[13:17].reshape(-1),
     )

time: 562 us -> 537 us (0.956)
  Pallas kernels: 536 us -> 522 us
  local copies, waits for them, and re-layouts: 14.6 us -> 5.53 us
    pallas_call x3, Pallas kernels: 185 us -> 177 us  [the longest x1 64.7 us: self_backward(): pl.pallas_call(functools.partial(self_backward_kernel, heads=heads, safe=...]
    unnamed x15 -> x4, local copies, waits for them, and re-layouts: 11.9 us -> 4.28 us
where the time goes in v11:
time: 537 us; the launch traced here: 530 us
  Pallas kernels  522 us (97%)
  local copies, waits for them, and re-layouts  5.53 us (1%)
    pallas_call x1, Pallas kernels, tail(): pl.pallas_call(functools.partial(tail_kernel, n=n, step_rows=512), in_spe...  68.6 us
    pallas_call x1, Pallas kernels, cross_forward(): pl.pallas_call(functools.partial(cross_forward_kernel, heads=heads), grid...  64.7 us
    pallas_call x1, Pallas kernels, self_backward(): pl.pallas_call(functools.partial(self_backward_kernel, heads=heads, safe=...  64.7 us
    pallas_call x1, Pallas kernels, cross_backward(): pl.pallas_call(functools.partial(cross_backward_kernel, heads=heads, bk=2...  59.6 us
    pallas_call x1, Pallas kernels, sum_after_self(): pl.pallas_call(after_self_kernel, in_specs=[ANY, vmem, vmem, vmem, ANY, v...  58 us
    pallas_call x1, Pallas kernels, self_forward(): pl.pallas_call(functools.partial(self_forward_kernel, heads=heads, safe=s...  53.9 us
    pallas_call x1, Pallas kernels, feed_forward(): pl.pallas_call(functools.partial(feed_forward_kernel, chunks=chunks), gri...  53.3 us
    pallas_call x1, Pallas kernels, start_gather(): pl.pallas_call(functools.partial(start_kernel, n=n), in_specs=[pl.BlockSp...  51.6 us

profile of v11, /device:TPU:0, one launch (start us, length us, event | category | flops | bytes accessed | tf_op | source)
XLA Modules:
  0.0 530.1 jit_solution(4801481443220728131)
XLA Ops:
  1.3 1.8 copy.28.qkv_ref
  3.1 51.6 %start_gather.1 = (bf16[2560,1024]{1,0:T(8,128)(2,1)}, bf16[4,2,128,1024]{3,2,1,0:T(8,128)(2,1)}, bf16[4,128,1024]{2,1,0:T(8,128)(2,1)}) custom-call(bf16[640,1024]{1,0:T(8,128)(2,1)} %rows_ref.3, f32[3,2,1024]{2,1,0:T(2,128)} %norm_ref.11, bf16[128,3,256]{2,1,0:T(4,128)(2,1)} %copy.28.qkv_ref, bf16[256,128]{1,0:T(8,128)(2,1)} %so_ref.1, ...), custom_call_target="tpu_custom_call" | custom-call | bytes 104857600 | tf_op jit(solution)/shard_map/start_gather/pallas_call | solution.py:838
  54.7 53.9 %self_forward.1 = (bf16[2560,256]{1,0:T(8,128)(2,1)}, bf16[2560,256]{1,0:T(8,128)(2,1)}, bf16[2560,256]{1,0:T(8,128)(2,1)}, bf16[256,2560]{1,0:T(8,128)(2,1)}, b...) custom-call(s32[1,2]{1,0:T(1,128)} %b_ref.3, ...), custom_call_target="tpu_custom_call" | custom-call | flops 20132659200 | bytes 5242880 | tf_op jit(solution)/shard_map/self_forward/pallas_call | solution.py:971
  108.7 58.0 %sum_after_self.1 = (f32[640,1024]{1,0:T(8,128)}, bf16[640,1024]{1,0:T(8,128)(2,1)}, bf16[2,4,2,128,2048]{4,3,2,1,0:T(8,128)(2,1)}, bf16[1024,1024]{1,0:T(8,128)(2,1)}) custom-call(bf16[2560,1024]{1,0:T(8,128)(2,1)} %get-tuple-element.80.terms_ref, bf16[640,1024]{1,0:T(8,128)(2,1)} %rows_ref.3, f32[7,1024]{1,0:T(8,128)} %biases_ref.7, ...), custom_call_target="tpu_custom_call" | custom-call | bytes 104857600 | tf_op jit(solution)/shard_map/sum_after_self/pallas_call | solution.py:1083
  166.7 64.7 %cross_forward.1 = (bf16[4,640,256]{2,1,0:T(8,128)(2,1)}, bf16[4,1024,256]{2,1,0:T(8,128)(2,1)}, bf16[4,1024,256]{2,1,0:T(8,128)(2,1)}, bf16[4,256,640]{2,1,0:T(...) custom-call(s32[1]{0:T(128)S(6)} %copy.33.len_ref, ...), custom_call_target="tpu_custom_call" | custom-call | flops 16106127360 | bytes 8388608 | tf_op jit(solution)/shard_map/cross_forward/pallas_call | solution.py:1357
  231.4 53.3 %feed_forward.1 = (f32[640,1024]{1,0:T(8,128)}, f32[640,1024]{1,0:T(8,128)}, bf16[640,1024]{1,0:T(8,128)(2,1)}, f32[8,1024]{1,0:T(8,128)}, bf16[2,1024,1024]{2,1...) custom-call(bf16[640,1024]{1,0:T(8,128)(2,1)} %get-tuple-element.86., ...), custom_call_target="tpu_custom_call" | custom-call | flops 32212254720 | bytes 41943040 | tf_op jit(solution)/shard_map/feed_forward/pallas_call | solution.py:1552
  284.7 59.6 %cross_backward.1 = (f32[640,1024]{1,0:T(8,128)}, bf16[1024,1024]{1,0:T(8,128)(2,1)}, bf16[2,1024,1024]{2,1,0:T(8,128)(2,1)}, f32[4,1,256]{2,1,0:T(1,128)}, f32[...) custom-call(s32[1]{0:T(128)S(6)} %copy.33.len_ref, ...), custom_call_target="tpu_custom_call" | custom-call | flops 32212254720 | bytes 16777216 | tf_op jit(solution)/shard_map/cross_backward/pallas_call | solution.py:1716
  344.3 39.8 %middle.1 = (bf16[2560,1024]{1,0:T(8,128)(2,1)}, f32[640,1024]{1,0:T(8,128)}, f32[8,1024]{1,0:T(8,128)}, f32[128,1024]{1,0:T(8,128)}, bf16[4,128,1024]{2,1,0:T(8,128)(2,1)}) custom-call(f32[640,1024]{1,0:T(8,128)} %get-tuple-element.105.back_ref, f32[640,1024]{1,0:T(8,128)} %get-tuple-element.85.rows_ref, f32[640,1024]{1,0:T(8,128)} %get-tuple-element.106.grad_ref, ...), custom_call_target="tpu_custom_call" | custom-call | bytes 104857600 | tf_op jit(solution)/shard_map/middle/pallas_call | solution.py:505
  384.1 64.7 %self_backward.1 = (bf16[2560,256]{1,0:T(8,128)(2,1)}, bf16[2560,256]{1,0:T(8,128)(2,1)}, bf16[2560,256]{1,0:T(8,128)(2,1)}, f32[128,1024]{1,0:T(8,128)}, f32[128,1024]{1,0:T(8,128)}, /*index=5*/f32[256,1024]{1,0:T(8,128)}) custom-call(s32[1,2]{1,0:T(1,128)} %b_ref.3, bf16[2560,256]{1,0:T(8,128)(2,1)} %get-tuple-element.91.q_ref, ...), custom_call_target="tpu_custom_call" | custom-call | flops 40265318400 | bytes 10485760 | tf_op jit(solution)/shard_map/self_backward/pallas_call | solution.py:1214
  448.9 68.6 %tail.1 = (f32[640,1024]{1,0:T(8,128)}, f32[128,1024]{1,0:T(8,128)}, f32[24,1024]{1,0:T(8,128)}) custom-call(bf16[2560,256]{1,0:T(8,128)(2,1)} %get-tuple-element.115.dq_ref, bf16[2560,256]{1,0:T(8,128)(2,1)} %get-tuple-element.116.dk_ref, bf16[2560,256]{1,0:T(8,128)(2,1)} %get-tuple-element.117.dv_ref, bf16[1024,1024]{1,0:T(8,128)(2,1)} %bitcast.17, ...), custom_call_target="tpu_custom_call" | custom-call | bytes 104857600 | tf_op jit(solution)/shard_map/tail/pallas_call | solution.py:688
  517.4 0.9 broadcast_multiply_fusion
  518.3 0.6 copy.32
  519.0 0.6 slice.13
  519.6 0.6 reshape.64
  520.2 7.8 %results.1 = (f32[640,1024]{1,0:T(8,128)}, f32[640,1024]{1,0:T(8,128)}, f32[256,1024]{1,0:T(8,128)}, f32[128,3,256]{2,1,0:T(4,128)}, f32[256,128]{1,0:T(8,128)},...) custom-call(f32[640,1024]{1,0:T(8,128)} %get-tuple-element.90.output, ...), custom_call_target="tpu_custom_call" | custom-call | bytes 20971520 | tf_op jit(solution)/shard_map/results/pallas_call | solution.py:745
  528.0 1.9 copy.29
  (2 shorter events, 0.0 us)

commit v12 on v11

--- a/solution.py
+++ b/solution.py
@@ -334,6 +334,81 @@
                 copy.wait_send()
 
 
+class Square:
+    def __init__(self, links, shard, out):
+        y = links.dp % 2
+        c = shard.shape[1]
+        low, high = pl.ds(0, c // 2), pl.ds(c // 2, c // 2)
+        self.own = links.local(shard, out.at[0, y])
+        self.first = [links.copy(shard, out.at[0, y], Y), links.copy(shard, out.at[1, y], X)]
+        self.second = [
+            links.copy(out.at[0, 1 - y, :, low], out.at[1, 1 - y, :, low], X),
+            links.copy(out.at[1, y, :, high], out.at[1, y, :, high], Y),
+        ]
+
+    def start(self):
+        for copy in self.first + [self.own]:
+            copy.start()
+
+    def middle(self):
+        for copy in self.first:
+            copy.wait_recv()
+        for copy in self.second:
+            copy.start()
+
+    def end(self):
+        for copy in self.first:
+            copy.wait_send()
+        for copy in self.second:
+            copy.wait()
+        self.own.wait()
+
+
+class SpreadZ:
+    def __init__(self, links, own, other, hold, whole, n):
+        z = links.dp // 2
+        distances = z_distances(n)
+        there = z ^ distances[0]
+        final, core = whole.at[0], whole.at[1]
+        self.loads = [links.local(own, hold.at[0]), links.local(other, hold.at[1])]
+        self.stores = [links.local(hold.at[0], final.at[z]), links.local(hold.at[1], final.at[there])]
+        self.core = [links.copy(hold.at[0], core.at[z], CORE), links.copy(hold.at[1], core.at[there], CORE)]
+        held = [(hold.at[0], z), (hold.at[1], there)]
+        self.stages, self.core_stages = [], []
+        for distance in distances[1:]:
+            came = [index ^ distance for _, index in held]
+            self.stages.append([links.copy(ref, final.at[index], ("dp", 2 * distance)) for ref, index in held])
+            self.core_stages.append([links.copy(final.at[index], core.at[index], CORE) for index in came])
+            held = held + [(final.at[index], index) for index in came]
+
+    def start(self):
+        for copy in self.loads:
+            copy.start()
+        for copy in self.loads:
+            copy.wait()
+        for copy in self.stages[0] + self.stores + self.core:
+            copy.start()
+
+    def end(self):
+        for step, (stage, core_stage) in enumerate(zip(self.stages, self.core_stages)):
+            for copy, onward in zip(stage, core_stage):
+                copy.wait_recv()
+                onward.start()
+            for copy in self.stages[step + 1] if step + 1 < len(self.stages) else []:
+                copy.start()
+        for copy in self.stores + self.core:
+            copy.wait()
+        for stage, core_stage in zip(self.stages, self.core_stages):
+            for copy in stage:
+                copy.wait_send()
+            for copy in core_stage:
+                copy.wait()
+
+
+def spread_z_copies(n):
+    return 2 * n
+
+
 class SpreadFar:
     def __init__(self, links, column, whole):
         y = links.dp % 2
@@ -415,9 +490,8 @@
 
 
 class Everywhere:
-    def __init__(self, links, held, slots, n):
+    def __init__(self, links, held, slots, ways):
         self.held, self.slots = held, slots
-        ways = everywhere_ways(n)
         self.copies = [links.copy(held.at[k], slots.at[k], way) for k, way in enumerate(ways)]
 
     def start(self, step):
@@ -528,15 +602,24 @@
 
 
 def tail_kernel(
-    dq_ref, dk_ref, dv_ref, w_ref, first_ref, wide_ref, mt_ref, rows_ref, grad_ref, norm_ref,
+    dq_ref, dk_ref, dv_ref, w_ref, first_hbm, wide_hbm, mt_hbm, rows_hbm, grad_hbm, norm_ref,
     self_ref, ffn_ref, cq_ref, cv_ref, up_ref,
-    grad_out, weights_out, late_out, give, acc, weights, *scratch, n, step_rows
+    grad_out, weights_out, late_out, give, acc, weights,
+    first_ref, wide_ref, mt_ref, rows_ref, grad_ref, *scratch, n, step_rows
 ):
     links = Links(*scratch[-3:])
+    loads = [
+        links.local(source, target)
+        for source, target in (
+            (first_hbm, first_ref), (wide_hbm, wide_ref), (mt_hbm, mt_ref), (rows_hbm, rows_ref), (grad_hbm, grad_ref)
+        )
+    ]
+    for copy in loads:
+        copy.start()
     member = links.tensor
     near, far, got_near, got_far, got_x = scratch[:5]
     columns, gots, slots = scratch[5:7], scratch[7:9], scratch[9:11]
-    held, late_slots = scratch[11:13]
+    held, late_slots, sums, early_slots = scratch[11:15]
     count, model = near.shape
     width = dq_ref.shape[1]
     y = links.dp % 2
@@ -552,7 +635,8 @@
         over_y.append(links.copy(weights.at[:, 1 - y, :, pl.ds(k * c, c)], got, Y))
         collects.append(Collect(links, column, slot))
     stages = len(collects[0].stages)
-    late = Everywhere(links, held, late_slots, n)
+    late = Everywhere(links, held, late_slots, everywhere_ways(n))
+    early = Everywhere(links, sums, early_slots, [CORE] + z_ways(n) + [Y, X])
     steps = len(late.copies)
     links.greet(everywhere_ways(n))
 
@@ -587,6 +671,8 @@
         copy.start()
 
     acc[...] = jnp.zeros_like(acc)
+    for copy in loads:
+        copy.wait()
 
     def products(rows):
         source = first_ref[rows, :].T
@@ -607,22 +693,24 @@
     packed(1)
 
     held[0] = jnp.zeros(held.shape[1:], F32)
-    held[0, 2:4, :] = self_ref[0:2, :]
-    held[0, 4:6, :] = ffn_ref[0:2, :]
-    held[0, 8:9, :] = self_ref[2:3, :]
-    held[0, 11:13, :] = ffn_ref[2:4, :]
+    sums[0] = jnp.zeros(sums.shape[1:], F32)
+    sums[0, 0:2, :] = self_ref[0:2, :]
+    sums[0, 2:4, :] = ffn_ref[0:2, :]
+    sums[0, 6:7, :] = self_ref[2:3, :]
+    sums[0, 9:11, :] = ffn_ref[2:4, :]
     for distance in range(4):
         there = pl.ds(pl.multiple_of((member ^ distance) * width, width), width)
-        held[0, 9:10, there] = cq_ref[distance]
-        held[0, 10:11, there] = cv_ref[distance]
-        held[0, pl.ds(13 + (member ^ distance), 1), :] = up_ref[distance]
+        sums[0, 7:8, there] = cq_ref[distance]
+        sums[0, 8:9, there] = cv_ref[distance]
+        sums[0, pl.ds(11 + (member ^ distance), 1), :] = up_ref[distance]
     here = pl.ds(pl.multiple_of(member * width, width), width)
 
     def column_sums(rows):
-        held[0, 6:7, here] += jnp.sum(dq_ref[rows, :].astype(F32), axis=0, keepdims=True)
-        held[0, 7:8, here] += jnp.sum(dv_ref[rows, :].astype(F32), axis=0, keepdims=True)
+        sums[0, 4:5, here] += jnp.sum(dq_ref[rows, :].astype(F32), axis=0, keepdims=True)
+        sums[0, 5:6, here] += jnp.sum(dv_ref[rows, :].astype(F32), axis=0, keepdims=True)
 
     by_rows(dq_ref.shape[0], step_rows, column_sums)
+    early.start(0)
 
     def norm_back(part):
         def one(rows):
@@ -651,26 +739,35 @@
 
     summed_y(0)
     over_y[1].start()
+    early.finish(0)
     core_near.wait_recv()
     over_x[0].wait_recv()
     norm_back(parts[0])
     next_z(0)
+    for step in range(1, steps - 2):
+        early.start(step)
+        early.finish(step)
     over_x[1].wait_recv()
     norm_back(parts[1])
     late.start(0)
     summed_y(1)
     late.finish(0)
     late.start(1)
+    early.start(steps - 2)
     last_z(0)
+    early.finish(steps - 2)
     late.finish(1)
     late.start(2)
+    early.start(steps - 1)
     next_z(1)
+    early.finish(steps - 1)
     late.finish(2)
+    late_out[2:, :] = sums[steps]
     for step in range(3, steps):
         late.start(step)
         late.finish(step)
     last_z(1)
-    late_out[...] = held[steps]
+    late_out[0:2, :] = held[steps, 0:2, :]
     for copy in over_x + over_y + [core_near, core_far]:
         copy.wait_send()
     for collect in collects:
@@ -682,27 +779,29 @@
     count, model = rows.shape
     width = dq.shape[1]
     m, r, c = n // 2, model // n, 4 * width
-    vectors = (24, model)
+    vectors = (16, model)
     vmem = pl.BlockSpec(memory_space=pltpu.VMEM)
     part = pltpu.VMEM((m, r, c // 2), BF16)
     return pl.pallas_call(
         functools.partial(tail_kernel, n=n, step_rows=512),
-        in_specs=[vmem] * 15,
+        in_specs=[vmem] * 4 + [ANY] * 5 + [vmem] * 6,
         out_specs=[vmem, vmem, vmem],
         out_shape=[
             jax.ShapeDtypeStruct((count, model), F32),
             jax.ShapeDtypeStruct((r, c), F32),
-            jax.ShapeDtypeStruct(vectors, F32),
+            jax.ShapeDtypeStruct((vectors[0] + 2, model), F32),
         ],
         scratch_shapes=[
             pltpu.VMEM((2, count, model), BF16),
             pltpu.VMEM((model, c), F32),
             pltpu.VMEM((m, 2, r, c), BF16),
         ]
+        + [pltpu.VMEM(v.shape, v.dtype) for v in (first, wide, mixed_t, rows, grad)]
         + row_sum_scratch(count, model)
         + [part] * 6
+        + everywhere_scratch(8, model, n)
         + everywhere_scratch(*vectors, n)
-        + link_scratch(6 + 2 * m + len(everywhere_ways(n)), 1),
+        + link_scratch(6 + 2 * m + 2 * len(everywhere_ways(n)), 5),
         compiler_params=pltpu.CompilerParams(
             vmem_limit_bytes=VMEM_LIMIT, collective_id=7, has_side_effects=True
         ),
@@ -756,8 +855,8 @@
 
 
 def start_kernel(
-    in_ref, norm_ref, qkv_ref, so_ref, cq_ref, ckv_ref, co_ref,
-    rows_out, self_out, cross_out, rows_ref, self_ref, cross_ref, send_sems, recv_sems, local_sems, *, n
+    in_ref, norm_ref, qkv_ref, so_ref, cq_ref, ckv_ref, co_ref, down_ref,
+    rows_out, self_out, cross_out, down_out, rows_ref, self_ref, cross_ref, shard_ref, send_sems, recv_sems, local_sems, *, n
 ):
     links = Links(send_sems, recv_sems, local_sems)
     member, z, y = links.tensor, links.dp // 2, links.dp % 2
@@ -787,6 +886,8 @@
     for k in range(2):
         cross_ref[:, (k + 1) * width : (k + 2) * width] = ckv_ref[:, k, :]
     cross_ref[:, 3 * width :] = co_ref[...].T
+    shard_ref[...] = down_ref[...].T
+    square = Square(links, shard_ref, down_out)
     links.greet([CORE, X, Y] + z_ways(n))
     for copy in over_y + local[1:]:
         copy.start()
@@ -803,6 +904,7 @@
         copy.start()
     for copy in local[:1] + over_core[:1]:
         copy.start()
+    square.start()
     for self_stage in self_stages:
         if self_stage is not self_stages[0]:
             for copy, _ in self_stage:
@@ -823,6 +925,8 @@
     for copy, onward in zip(over_x, over_core[1:]):
         copy.wait_recv()
         onward.start()
+    square.middle()
+    square.end()
     for copy in local + over_y + over_core:
         copy.wait()
     for copy in over_x:
@@ -832,70 +936,62 @@
             copy.wait_send()
 
 
-def start_gather(rows, norm, qkv, self_out, cross_q, cross_kv, cross_out):
+def start_gather(rows, norm, qkv, self_out, cross_q, cross_kv, cross_out, down):
     n = lax.axis_size("dp")
     r, c = cross_q.shape[0], 4 * cross_q.shape[1]
     return pl.pallas_call(
         functools.partial(start_kernel, n=n),
-        in_specs=[pl.BlockSpec(memory_space=pltpu.VMEM)] * 7,
-        out_specs=[ANY] * 3,
+        in_specs=[pl.BlockSpec(memory_space=pltpu.VMEM)] * 8,
+        out_specs=[ANY] * 4,
         out_shape=[
             jax.ShapeDtypeStruct((4 * rows.shape[0], rows.shape[1]), BF16),
             jax.ShapeDtypeStruct((n // 2, 2, r, c), BF16),
             jax.ShapeDtypeStruct((n // 2, r, c), BF16),
+            jax.ShapeDtypeStruct((2, 2, r, down.shape[0]), BF16),
         ],
-        scratch_shapes=[pltpu.VMEM(rows.shape, BF16)] + [pltpu.VMEM((r, c), BF16)] * 2 + link_scratch(2 * n + 8, 3),
+        scratch_shapes=[pltpu.VMEM(rows.shape, BF16)]
+        + [pltpu.VMEM((r, c), BF16)] * 2
+        + [pltpu.VMEM((r, down.shape[0]), BF16)]
+        + link_scratch(2 * n + 12, 4),
         compiler_params=pltpu.CompilerParams(
             vmem_limit_bytes=VMEM_LIMIT, collective_id=0, has_side_effects=True
         ),
         cost_estimate=pl.CostEstimate(flops=0, bytes_accessed=100 * 2**20, transcendentals=0),
         name="start_gather",
-    )(rows, norm, qkv, self_out, cross_q, cross_kv, cross_out)
+    )(rows, norm, qkv, self_out, cross_q, cross_kv, cross_out, down)
 
 
 def self_forward_kernel(
     b_ref, x_ref, w_ref, biases_ref, column_ref, up_ref, down_ref,
-    q_out, k_ref, v_out, kt_out, ot_ref, lse_ref, terms_ref, whole, next_column,
-    vt_ref, m_s, l_s, acc, column, shard, send_sems, recv_sems, local_sems, *, heads, safe, n
+    q_out, k_ref, v_out, kt_out, ot_ref, lse_ref, terms_ref, whole, next_column, far_down,
+    vt_ref, m_s, l_s, acc, column, send_sems, recv_sems, local_sems, *, heads, safe, n
 ):
     i = pl.program_id(0)
     last = pl.num_programs(0) - 1
     bq, width = q_out.shape
     links = Links(send_sems, recv_sems, local_sems)
     spread = Spread(links, column_ref, column, whole)
-    hidden = up_ref.shape[1]
-    halves = []
-    for k in range(2):
-        part = pl.ds(k * hidden, hidden)
-        halves.append(column_stages(links, shard.at[:, part], next_column.at[:, :, part], n))
-    keep = links.local(shard, next_column.at[links.dp // 2])
-
-    def start_stage(k, step):
-        for copy, _ in halves[k][step]:
+    stages = column_stages(links, up_ref, next_column, n)
+    keep = links.local(up_ref, next_column.at[links.dp // 2])
+    over_z = links.copy(down_ref.at[0], far_down, z_ways(n)[0])
+
+    def next_stage(step):
+        for copy, _ in stages[step]:
+            copy.wait_recv()
+        for copy, _ in stages[step + 1] if step + 1 < len(stages) else []:
             copy.start()
-
-    def next_stage(k, step):
-        for copy, _ in halves[k][step]:
-            copy.wait_recv()
-        if step + 1 < len(halves[k]):
-            start_stage(k, step + 1)
 
     @pl.when(i == 0)
     def _():
-        shard[:, :hidden] = up_ref[...]
-        shard[:, hidden:] = down_ref[...].T
         links.greet([CORE, X, Y] + z_ways(n))
-        start_stage(0, 0)
+        for copy, _ in stages[0]:
+            copy.start()
         spread.start()
         keep.start()
 
-    def onward_one():
-        next_stage(0, 0)
-        start_stage(1, 0)
-
-    @pl.when(i == last)
-    def _():
-        next_stage(1, 0)
+    def onward():
+        next_stage(0)
+        over_z.start()
 
     mine = pl.ds(pl.multiple_of(links.tensor * width, width), width)
     projected = dot_nn(x_ref[...], w_ref[:, : 3 * width])
@@ -938,7 +1034,7 @@
         for h in range(heads):
             acc[h * hd : (h + 1) * hd, skip:] = a_out[h]
 
-    over_keys(i, bq, safe, block, [(2, 0, onward_one), (3, 2, spread.middle), (4, 3, spread.last)])
+    over_keys(i, bq, safe, block, [(2, 0, onward), (3, 2, spread.middle), (4, 3, spread.last)])
     inverse = 1.0 / l_s[...]
     for h in range(heads):
         part = slice(h * hd, (h + 1) * hd)
@@ -948,14 +1044,13 @@
 
     @pl.when(i == last)
     def _():
-        for k in range(2):
-            for step in range(1, len(halves[k])):
-                next_stage(k, step)
+        for step in range(1, len(stages)):
+            next_stage(step)
+        over_z.wait()
         spread.end()
-        for stages in halves:
-            for stage in stages:
-                for copy, _ in stage:
-                    copy.wait_send()
+        for stage in stages:
+            for copy, _ in stage:
+                copy.wait_send()
         keep.wait()
 
 
@@ -965,7 +1060,6 @@
     bq = 512
     dp = lax.axis_size("dp")
     m, r, c = column.shape
-    shard = (up.shape[0], 2 * up.shape[1])
     by_rows_spec = pl.BlockSpec((bq, width), lambda i: (i, 0))
     by_columns_spec = pl.BlockSpec((width, bq), lambda i: (0, i))
     return pl.pallas_call(
@@ -978,7 +1072,7 @@
             const(biases.shape),
             ANY,
             const(up.shape),
-            const(down.shape),
+            ANY,
         ],
         out_specs=[
             by_rows_spec,
@@ -988,6 +1082,7 @@
             by_columns_spec,
             pl.BlockSpec((heads, bq), lambda i: (0, i)),
             pl.BlockSpec((bq, model), lambda i: (i, 0)),
+            ANY,
             ANY,
             ANY,
         ],
@@ -1000,7 +1095,8 @@
             jax.ShapeDtypeStruct((heads, n), F32),
             jax.ShapeDtypeStruct((n, model), BF16),
             jax.ShapeDtypeStruct((4, m, 2, r, c), BF16),
-            jax.ShapeDtypeStruct((m,) + shard, BF16),
+            jax.ShapeDtypeStruct((m,) + up.shape, BF16),
+            jax.ShapeDtypeStruct(down.shape[1:], BF16),
         ],
         scratch_shapes=[
             pltpu.VMEM((width, n), BF16),
@@ -1008,9 +1104,8 @@
             pltpu.VMEM((heads, bq), F32),
             pltpu.VMEM((width, bq), F32),
             pltpu.VMEM((m, r, c), BF16),
-            pltpu.VMEM(shard, BF16),
         ]
-        + link_scratch(8 + 2 * m, 3),
+        + link_scratch(9 + m, 3),
         compiler_params=pltpu.CompilerParams(
             vmem_limit_bytes=VMEM_LIMIT, collective_id=1, has_side_effects=True
         ),
@@ -1022,12 +1117,14 @@
 
 
 def after_self_kernel(
-    terms_ref, rows_ref, biases_ref, norm_ref, column_ref, enc_ref,
-    after_out, second_out, whole_out, enc_out, *scratch
+    terms_ref, rows_ref, biases_ref, norm_ref, column_ref, enc_ref, down_ref, from_z,
+    after_out, second_out, whole_out, enc_out, down_out, far_down, *scratch, n
 ):
     links = Links(*scratch[-3:])
     rows_sum = RowSum(links, terms_ref, scratch[:5], left=True)
     column = scratch[5]
+    spread = SpreadZ(links, down_ref.at[0], from_z, scratch[6], down_out, n)
+    over_z = links.copy(down_ref.at[1], far_down, z_ways(n)[0])
     y = links.dp % 2
     near_out, core_out = whole_out.at[0], whole_out.at[1]
     load = links.local(column_ref, column)
@@ -1045,13 +1142,15 @@
     enc_x = links.copy(enc_ref, place(0), X)
     enc_core = [links.copy(enc_ref, place(0), CORE), links.copy(place(2), place(2), CORE)]
     enc_own = links.local(enc_ref, place(0))
-    links.greet([CORE, X, Y])
+    links.greet([CORE, X, Y] + z_ways(n))
     rows_sum.start()
     load.start()
+    over_z.start()
     load.wait()
     over_y.start()
     own.start()
     enc_own.start()
+    spread.start()
     rows_sum.middle()
     over_core[0].start()
     enc_core[0].start()
@@ -1072,31 +1171,37 @@
     over_core[1].start()
     enc_x.wait_send()
     over_y.wait_send()
+    spread.end()
+    over_z.wait()
     for copy in [own, enc_own] + over_core + enc_core:
         copy.wait()
 
 
-def sum_after_self(terms, rows, biases, norm, column, encoder):
+def sum_after_self(terms, rows, biases, norm, column, encoder, down, from_z):
     count, model = rows.shape
     m, r, c = column.shape
     vmem = pl.BlockSpec(memory_space=pltpu.VMEM)
     return pl.pallas_call(
-        after_self_kernel,
-        in_specs=[ANY, vmem, vmem, vmem, ANY, vmem],
-        out_specs=[vmem, vmem, ANY, ANY],
+        functools.partial(after_self_kernel, n=2 * m),
+        in_specs=[ANY, vmem, vmem, vmem, ANY, vmem, ANY, ANY],
+        out_specs=[vmem, vmem, ANY, ANY, ANY, ANY],
         out_shape=[
             jax.ShapeDtypeStruct((count, model), F32),
             jax.ShapeDtypeStruct((count, model), BF16),
             jax.ShapeDtypeStruct((2, m, 2, r, c), BF16),
             jax.ShapeDtypeStruct((4 * encoder.shape[0], model), BF16),
+            jax.ShapeDtypeStruct((2, m, 2, r, c), BF16),
+            jax.ShapeDtypeStruct((2, r, c), BF16),
         ],
-        scratch_shapes=row_sum_scratch(count, model) + [pltpu.VMEM((m, r, c), BF16)] + link_scratch(9, 5),
+        scratch_shapes=row_sum_scratch(count, model)
+        + [pltpu.VMEM((m, r, c), BF16), pltpu.VMEM((2, 2, r, c), BF16)]
+        + link_scratch(10 + spread_z_copies(2 * m), 9),
         compiler_params=pltpu.CompilerParams(
             vmem_limit_bytes=VMEM_LIMIT, collective_id=8, has_side_effects=True
         ),
         cost_estimate=pl.CostEstimate(flops=0, bytes_accessed=100 * 2**20, transcendentals=0),
         name="sum_after_self",
-    )(terms, rows, biases, norm, column, encoder)
+    )(terms, rows, biases, norm, column, encoder, down, from_z)
 
 
 def self_backward_kernel(
@@ -1281,26 +1386,28 @@
 
 
 def cross_forward_kernel(
-    len_ref, x_ref, enc_ref, w_ref, biases_ref, rows_ref, norm_ref, column_ref,
-    q_out, k_out, v_out, ot_ref, lse_ref, after_ref, third_ref, whole, send_sems, recv_sems, local_sems, *, heads
+    len_ref, x_ref, enc_ref, w_ref, biases_ref, rows_ref, norm_ref, column_ref, down_ref, from_z,
+    q_out, k_out, v_out, ot_ref, lse_ref, after_ref, third_ref, whole, down_out, hold, send_sems, recv_sems, local_sems, *, heads, n
 ):
     i = pl.program_id(0)
     last = pl.num_programs(0) - 1
     links = Links(send_sems, recv_sems, local_sems)
     spread = SpreadFar(links, column_ref, whole)
     pieces = len(spread.over_x)
+    spread_z = SpreadZ(links, down_ref.at[1], from_z, hold, down_out, n)
 
     @pl.when(i == 0)
     def _():
-        links.greet([CORE, X, Y])
+        links.greet([CORE, X, Y] + z_ways(n))
         spread.start()
+        spread_z.start()
         after_ref[...] = rows_ref[...] + biases_ref[5:6, :]
 
     def onward(*when):
         for step, k in when:
             pl.when(i == step)(functools.partial(spread.onward, k))
 
-    onward((1, 0), (3, 3))
+    onward((1, 0), (1, 1), (2, 3), (3, 5))
 
     width = q_out.shape[2]
     hd = width // heads
@@ -1327,7 +1434,7 @@
         ot_ref[0, part, :] = mixed[h]
         lse_ref[0, h : h + 1, :] = largest + jnp.log(total)
         if h == heads // 2 - 1:
-            onward((1, 1), (2, 2), (3, 4))
+            onward((1, 2), (2, 4), (3, 6))
     after_ref[...] += dot_nt(jnp.concatenate(mixed, 0).T, w_ref[0, :, 3 * width :])
 
     @pl.when(i == last)
@@ -1337,14 +1444,15 @@
             third_ref[rows, :] = (xhat * norm_ref[2, 0:1, :] + norm_ref[2, 1:2, :]).astype(BF16)
 
         by_rows(after_ref.shape[0], 128, norm)
-        for k in range(5, pieces):
+        for k in range(7, pieces):
             spread.onward(k)
         for k in range(pieces):
             spread.last(k)
+        spread_z.end()
         spread.end()
 
 
-def cross_forward(lengths, x, encoder, weights, biases, rows, norm, column, heads):
+def cross_forward(lengths, x, encoder, weights, biases, rows, norm, column, down, from_z, heads):
     count, model = x.shape
     n = encoder.shape[0]
     parts, _, columns = weights.shape
@@ -1355,7 +1463,7 @@
         return pl.BlockSpec((1,) + shape, lambda i: (i,) + (0,) * len(shape))
 
     return pl.pallas_call(
-        functools.partial(cross_forward_kernel, heads=heads),
+        functools.partial(cross_forward_kernel, heads=heads, n=2 * m),
         grid=(parts,),
         in_specs=[
             pl.BlockSpec(memory_space=pltpu.SMEM),
@@ -1365,6 +1473,8 @@
             const(biases.shape),
             const((count, model)),
             const(norm.shape),
+            ANY,
+            ANY,
             ANY,
         ],
         out_specs=[
@@ -1376,6 +1486,7 @@
             const((count, model)),
             const((count, model)),
             ANY,
+            ANY,
         ],
         out_shape=[
             jax.ShapeDtypeStruct((parts, count, width), BF16),
@@ -1386,8 +1497,9 @@
             jax.ShapeDtypeStruct((count, model), F32),
             jax.ShapeDtypeStruct((count, model), BF16),
             jax.ShapeDtypeStruct((2, m, 2, r, c), BF16),
+            jax.ShapeDtypeStruct((2, m, 2, r, c), BF16),
         ],
-        scratch_shapes=link_scratch(32, 1),
+        scratch_shapes=[pltpu.VMEM((2, 2, r, c), BF16)] + link_scratch(32 + spread_z_copies(2 * m), 4),
         compiler_params=pltpu.CompilerParams(
             vmem_limit_bytes=VMEM_LIMIT, collective_id=2, has_side_effects=True
         ),
@@ -1397,11 +1509,11 @@
             transcendentals=parts * count * n * heads,
         ),
         name="cross_forward",
-    )(lengths, x, encoder, weights, biases, rows, norm, column)
+    )(lengths, x, encoder, weights, biases, rows, norm, column, down, from_z)
 
 
 def feed_forward_kernel(
-    x_ref, dy_ref, near_ref, far_ref, b_ref, after_ref, biases_ref, norm_ref,
+    x_ref, dy_ref, near_up, near_down, far_up, far_down, b_ref, after_ref, biases_ref, norm_ref,
     out_ref, rows_out, low_out, sums_ref, gup_ref, gdown_ref, bias_ref, from_x, from_y,
     xt_ref, dyt_ref, back_ref, give, got, diagonal, loaded, load_sems, send_sems, recv_sems, local_sems, *, chunks
 ):
@@ -1436,18 +1548,18 @@
         slot = step % 2
         first = (step % chunks) * size
 
-        def both(source):
-            for k in range(2):
-                columns = pl.ds(pl.multiple_of(first + k * chunks * size, size), size)
+        def both(*sources):
+            for k, source in enumerate(sources):
+                columns = pl.ds(pl.multiple_of(first, size), size)
                 act(pltpu.make_async_copy(source.at[:, columns], loaded.at[slot, k], load_sems.at[slot, k]))
 
         @pl.when(block >= 2)
         def _():
-            both(far_ref.at[block - 2])
+            both(far_up.at[block - 2], far_down.at[block - 2])
 
         @pl.when(block < 2)
         def _():
-            both(near_ref.at[block])
+            both(near_up.at[block], near_down.at[block])
 
     @pl.when(s == 0)
     def _():
@@ -1530,9 +1642,9 @@
             copy.wait()
 
 
-def feed_forward(x, dy, near, far, bias, after, biases, norm):
+def feed_forward(x, dy, weights, bias, after, biases, norm):
     rows, width = x.shape
-    hidden = near.shape[2] // 2
+    hidden = weights[0].shape[2]
     size = min(512, hidden)
     chunks = hidden // size
 
@@ -1555,6 +1667,8 @@
         in_specs=[
             rows_spec,
             rows_spec,
+            ANY,
+            ANY,
             ANY,
             ANY,
             const(bias.shape),
@@ -1592,7 +1706,7 @@
             flops=48 * rows * width * hidden, bytes_accessed=40 * 2**20, transcendentals=8 * rows * hidden
         ),
         name="feed_forward",
-    )(x, dy, near, far, bias, after, biases, norm)
+    )(x, dy, *weights, bias, after, biases, norm)
 
 
 def cross_backward_kernel(
@@ -1796,7 +1910,7 @@
     own_rows, model_width = block_in.shape
     w_rows = w_cross_q.shape[0]
 
-    first_in, self_w, cross_column = start_gather(
+    first_in, self_w, cross_column, down_square = start_gather(
         block_in,
         norm_params,
         w_qkv,
@@ -1804,27 +1918,28 @@
         w_cross_q,
         w_cross_kv,
         w_cross_out,
+        w_down,
     )
     self_w = self_w.reshape(model_width, 4 * width)
 
     self_safe = 1024
-    queries, key_rows, value_rows, keys_t, self_mixed_t, self_lse, terms, cross_w, ffn_column = self_forward(
+    queries, key_rows, value_rows, keys_t, self_mixed_t, self_lse, terms, cross_w, up_column, near_z = self_forward(
         bounds,
         first_in,
         self_w,
         biases,
         cross_column,
         w_up,
-        w_down,
+        down_square,
         heads,
         self_safe,
     )
     cross_w = cross_w.reshape(4, model_width, 4 * width)
-    after_self, second_in, ffn_near, enc_all = sum_after_self(
-        terms, block_in, biases, norm_params, ffn_column, encoder_out
+    after_self, second_in, near_up, enc_all, near_down, far_z = sum_after_self(
+        terms, block_in, biases, norm_params, up_column, encoder_out, down_square, near_z
     )
 
-    cross_q, cross_k, cross_v, cross_mixed_t, cross_lse, after_cross, third_in, ffn_far = cross_forward(
+    cross_q, cross_k, cross_v, cross_mixed_t, cross_lse, after_cross, third_in, far_up, far_down = cross_forward(
         enc_lengths,
         second_in,
         enc_all,
@@ -1832,15 +1947,16 @@
         biases,
         after_self,
         norm_params,
-        ffn_column,
+        up_column,
+        down_square,
+        far_z,
         heads,
     )
 
     output, cross_rows_grad, cross_low, ffn_sums, up_sum, down_sum, bias_up_parts, from_x, from_y = feed_forward(
         third_in,
         out_grad,
-        ffn_near.reshape(2, model_width, 2 * hidden_width),
-        ffn_far.reshape(2, model_width, 2 * hidden_width),
+        [w.reshape(2, model_width, hidden_width) for w in (near_up, near_down, far_up, far_down)],
         up_bias.reshape(-1, LANES),
         after_cross,
         biases,

time: 537 us -> 511 us (0.952)
  Pallas kernels: 522 us -> 496 us
    pallas_call x2, Pallas kernels: 123 us -> 101 us  [the longest x1 55.5 us: sum_after_self(): pl.pallas_call(functools.partial(after_self_kernel, n=2 * m), in_specs=[A...]
    pallas_call x1, Pallas kernels: 53.9 us -> 48.4 us  [self_forward(): pl.pallas_call(functools.partial(self_forward_kernel, heads=heads, safe=s...]
where the time goes in v12:
time: 511 us; the launch traced here: 504 us
  Pallas kernels  496 us (97%)
  local copies, waits for them, and re-layouts  5.53 us (1%)
    pallas_call x1, Pallas kernels, tail(): pl.pallas_call(functools.partial(tail_kernel, n=n, step_rows=512), in_spe...  67.8 us
    pallas_call x1, Pallas kernels, self_backward(): pl.pallas_call(functools.partial(self_backward_kernel, heads=heads, safe=...  64.6 us
    pallas_call x1, Pallas kernels, cross_backward(): pl.pallas_call(functools.partial(cross_backward_kernel, heads=heads, bk=2...  59.8 us
    pallas_call x1, Pallas kernels, sum_after_self(): pl.pallas_call(functools.partial(after_self_kernel, n=2 * m), in_specs=[A...  55.5 us
    pallas_call x1, Pallas kernels, start_gather(): pl.pallas_call(functools.partial(start_kernel, n=n), in_specs=[pl.BlockSp...  53.8 us
    pallas_call x1, Pallas kernels, feed_forward(): pl.pallas_call(functools.partial(feed_forward_kernel, chunks=chunks), gri...  53.3 us
    pallas_call x1, Pallas kernels, self_forward(): pl.pallas_call(functools.partial(self_forward_kernel, heads=heads, safe=s...  48.4 us
    pallas_call x1, Pallas kernels, cross_forward(): pl.pallas_call(functools.partial(cross_forward_kernel, heads=heads, n=2 *...  45.7 us

profile of v12, /device:TPU:0, one launch (start us, length us, event | category | flops | bytes accessed | tf_op | source)
XLA Modules:
  0.0 504.3 jit_solution(15942438555392567641)
XLA Ops:
  1.3 1.8 copy.28.qkv_ref
  3.1 53.8 %start_gather.1 = (bf16[2560,1024]{1,0:T(8,128)(2,1)}, bf16[4,2,128,1024]{3,2,1,0:T(8,128)(2,1)}, bf16[4,128,1024]{2,1,0:T(8,128)(2,1)}, bf16[2,2,128,1024]{3,2,1,0:T(8,128)(2,1)}) custom-call(bf16[640,1024]{1,0:T(8,128)(2,1)} %rows_hbm.1, f32[3,2,1024]{2,1,0:T(2,128)} %norm_ref.11, bf16[128,3,256]{2,1,0:T(4,128)(2,1)} %copy.28.qkv_ref, ...), custom_call_target="tpu_custom_call" | custom-call | bytes 104857600 | tf_op jit(solution)/shard_map/start_gather/pallas_call | solution.py:942
  56.9 48.4 %self_forward.1 = (bf16[2560,256]{1,0:T(8,128)(2,1)}, bf16[2560,256]{1,0:T(8,128)(2,1)}, bf16[2560,256]{1,0:T(8,128)(2,1)}, bf16[256,2560]{1,0:T(8,128)(2,1)}, b...) custom-call(s32[1,2]{1,0:T(1,128)} %b_ref.3, ...), custom_call_target="tpu_custom_call" | custom-call | flops 20132659200 | bytes 5242880 | tf_op jit(solution)/shard_map/self_forward/pallas_call | solution.py:1065
  105.2 55.5 %sum_after_self.1 = (f32[640,1024]{1,0:T(8,128)}, bf16[640,1024]{1,0:T(8,128)(2,1)}, bf16[2,4,2,128,1024]{4,3,2,1,0:T(8,128)(2,1)}, bf16[1024,1024]{1,0:T(8,128)...) custom-call(bf16[2560,1024]{1,0:T(8,128)(2,1)} %get-tuple-element.86.terms_ref, ...), custom_call_target="tpu_custom_call" | custom-call | bytes 104857600 | tf_op jit(solution)/shard_map/sum_after_self/pallas_call | solution.py:1184
  160.8 45.7 %cross_forward.1 = (bf16[4,640,256]{2,1,0:T(8,128)(2,1)}, bf16[4,1024,256]{2,1,0:T(8,128)(2,1)}, bf16[4,1024,256]{2,1,0:T(8,128)(2,1)}, bf16[4,256,640]{2,1,0:T(...) custom-call(s32[1]{0:T(128)S(6)} %copy.33.len_ref, ...), custom_call_target="tpu_custom_call" | custom-call | flops 16106127360 | bytes 8388608 | tf_op jit(solution)/shard_map/cross_forward/pallas_call | solution.py:1465
  206.4 53.3 %feed_forward.1 = (f32[640,1024]{1,0:T(8,128)}, f32[640,1024]{1,0:T(8,128)}, bf16[640,1024]{1,0:T(8,128)(2,1)}, f32[8,1024]{1,0:T(8,128)}, bf16[2,1024,1024]{2,1...) custom-call(bf16[640,1024]{1,0:T(8,128)(2,1)} %get-tuple-element.94., ...), custom_call_target="tpu_custom_call" | custom-call | flops 32212254720 | bytes 41943040 | tf_op jit(solution)/shard_map/feed_forward/pallas_call | solution.py:1664
  259.7 59.8 %cross_backward.1 = (f32[640,1024]{1,0:T(8,128)}, bf16[1024,1024]{1,0:T(8,128)(2,1)}, bf16[2,1024,1024]{2,1,0:T(8,128)(2,1)}, f32[4,1,256]{2,1,0:T(1,128)}, f32[...) custom-call(s32[1]{0:T(128)S(6)} %copy.33.len_ref, ...), custom_call_target="tpu_custom_call" | custom-call | flops 32212254720 | bytes 16777216 | tf_op jit(solution)/shard_map/cross_backward/pallas_call | solution.py:1830
  319.5 39.8 %middle.1 = (bf16[2560,1024]{1,0:T(8,128)(2,1)}, f32[640,1024]{1,0:T(8,128)}, f32[8,1024]{1,0:T(8,128)}, f32[128,1024]{1,0:T(8,128)}, bf16[4,128,1024]{2,1,0:T(8,128)(2,1)}) custom-call(f32[640,1024]{1,0:T(8,128)} %get-tuple-element.115.back_ref, f32[640,1024]{1,0:T(8,128)} %get-tuple-element.92.rows_ref, f32[640,1024]{1,0:T(8,128)} %get-tuple-element.116.grad_ref, ...), custom_call_target="tpu_custom_call" | custom-call | bytes 104857600 | tf_op jit(solution)/shard_map/middle/pallas_call | solution.py:579
  359.3 64.6 %self_backward.1 = (bf16[2560,256]{1,0:T(8,128)(2,1)}, bf16[2560,256]{1,0:T(8,128)(2,1)}, bf16[2560,256]{1,0:T(8,128)(2,1)}, f32[128,1024]{1,0:T(8,128)}, f32[128,1024]{1,0:T(8,128)}, /*index=5*/f32[256,1024]{1,0:T(8,128)}) custom-call(s32[1,2]{1,0:T(1,128)} %b_ref.3, bf16[2560,256]{1,0:T(8,128)(2,1)} %get-tuple-element.101.q_ref, ...), custom_call_target="tpu_custom_call" | custom-call | flops 40265318400 | bytes 10485760 | tf_op jit(solution)/shard_map/self_backward/pallas_call | solution.py:1319
  423.9 67.8 %tail.1 = (f32[640,1024]{1,0:T(8,128)}, f32[128,1024]{1,0:T(8,128)}, f32[18,1024]{1,0:T(8,128)}) custom-call(bf16[2560,256]{1,0:T(8,128)(2,1)} %get-tuple-element.125.dq_ref, bf16[2560,256]{1,0:T(8,128)(2,1)} %get-tuple-element.126.dk_ref, bf16[2560,256]{1,0:T(8,128)(2,1)} %get-tuple-element.127.dv_ref, bf16[1024,1024]{1,0:T(8,128)(2,1)} %bitcast.19, ...), custom_call_target="tpu_custom_call" | custom-call | bytes 104857600 | tf_op jit(solution)/shard_map/tail/pallas_call | solution.py:785
  491.7 0.9 broadcast_multiply_fusion
  492.6 0.6 copy.32
  493.2 0.6 slice.13
  493.8 0.6 reshape.72
  494.4 7.8 %results.1 = (f32[640,1024]{1,0:T(8,128)}, f32[640,1024]{1,0:T(8,128)}, f32[256,1024]{1,0:T(8,128)}, f32[128,3,256]{2,1,0:T(4,128)}, f32[256,128]{1,0:T(8,128)},...) custom-call(f32[640,1024]{1,0:T(8,128)} %get-tuple-element.100.outpu, ...), custom_call_target="tpu_custom_call" | custom-call | bytes 20971520 | tf_op jit(solution)/shard_map/results/pallas_call | solution.py:844
  502.2 1.9 copy.29
  (2 shorter events, 0.0 us)

commit v13 on v12

--- a/solution.py
+++ b/solution.py
@@ -268,21 +268,22 @@
 
 
 class GatherLast:
-    def __init__(self, links, near, far, diagonal, buffers):
+    def __init__(self, links, near, far, buffers):
         y = links.dp % 2
         self.column, self.over_x, self.diagonal, self.sum_y, self.sum_x = buffers
-        self.loads = [
-            links.local(far.at[:, y], self.over_x),
-            links.local(diagonal, self.diagonal),
-            links.local(near.at[:, y], self.column),
-        ]
+        self.loads = [links.local(far.at[:, y], self.over_x), links.local(near.at[:, y], self.column)]
+        self.first = links.copy(far.at[:, 1 - y], self.diagonal, Y)
         self.over_y = links.copy(near.at[:, 1 - y], self.sum_y, Y)
         self.along_x = links.copy(self.over_x, self.sum_x, X)
 
     def start(self):
-        self.over_y.start()
+        self.first.start()
         for copy in self.loads:
             copy.start()
+
+    def second(self):
+        self.first.wait_recv()
+        self.over_y.start()
 
     def middle(self):
         for copy in self.loads:
@@ -295,8 +296,8 @@
         self.along_x.wait_recv()
         add_to(self.column, self.sum_y)
         add_to(self.column, self.sum_x)
-        self.over_y.wait_send()
-        self.along_x.wait_send()
+        for copy in (self.first, self.over_y, self.along_x):
+            copy.wait_send()
 
 
 class Collect:
@@ -447,8 +448,7 @@
 
 
 class RowSum:
-    def __init__(self, links, terms, buffers, left=False):
-        self.left = left
+    def __init__(self, links, terms, buffers):
         self.near, self.far, self.got_near, self.got_far, self.got_x = buffers
         count = self.near.shape[0]
 
@@ -478,7 +478,7 @@
         self.loads[0].wait()
         self.core[1].wait_recv()
         self.over_x.wait_recv()
-        for copy in self.core + ([] if self.left else [self.over_x]):
+        for copy in self.core + [self.over_x]:
             copy.wait_send()
 
     def total(self, rows):
@@ -511,111 +511,23 @@
     return [pltpu.VMEM((steps + 1, k, c), F32), pltpu.VMEM((steps, k, c), F32)]
 
 
-def middle_kernel(
-    back_ref, rows_ref, grad_ref, norm_ref, down_ref, cross_ref,
-    wide_out, grad_out, sums_ref, down_out, diagonal_out,
-    low, column, slots, send_sems, recv_sems, local_sems, *, n
-):
-    links = Links(send_sems, recv_sems, local_sems)
-    count = low.shape[0]
-    load = links.local(down_ref, column)
-    load.start()
-    collect = Collect(links, column, slots)
-
-    def place(distance):
-        return wide_out.at[pl.ds(pl.multiple_of((links.tensor ^ distance) * count, count), count)]
-
-    own = links.local(low, place(0))
-    half = count // 2
-    parts = [pl.ds(0, half), pl.ds(half, half)]
-    over_x = [links.copy(low.at[part], place(0).at[part], X) for part in parts]
-    over_core = links.copy(low, place(0), CORE)
-    onward = [links.copy(place(2).at[part], place(2).at[part], CORE) for part in parts]
-    over_y = links.copy(cross_ref.at[1, :, 1 - links.dp % 2], diagonal_out, Y)
-    links.greet([CORE, X, Y] + z_ways(n))
-    over_y.start()
-    load.wait()
-    collect.start(0)
-    sums_ref[...] = jnp.zeros_like(sums_ref)
-
-    def norm_back(rows):
-        incoming = back_ref[rows, :]
-        rows_grad, gain_terms = norm_rows_back(rows_ref[rows, :], incoming, norm_ref[1, 0:1, :])
-        rows_grad = rows_grad + grad_ref[rows, :]
-        rounded = rows_grad.astype(BF16)
-        grad_out[rows, :] = rows_grad
-        low[rows, :] = rounded
-        for k, terms in enumerate((gain_terms, incoming, rounded.astype(F32))):
-            sums_ref[k : k + 1, :] += jnp.sum(terms, axis=0, keepdims=True)
-
-    for part, copy in zip(parts, over_x):
-        by_rows(half, 64, lambda rows, part=part: norm_back(pl.ds(pl.multiple_of(part.start + rows.start, 64), 64)))
-        copy.start()
-    own.start()
-    over_core.start()
-    for step in range(len(collect.stages) - 1):
-        collect.finish(step)
-        collect.start(step + 1)
-    for copy, later in zip(over_x, onward):
-        copy.wait_recv()
-        later.start()
-    collect.finish(len(collect.stages) - 1)
-    down_out[...] = column[collect.z].astype(F32)
-    collect.drain()
-    own.wait()
-    for copy in over_x:
-        copy.wait_send()
-    over_core.wait()
-    for copy in onward:
-        copy.wait()
-    over_y.wait()
-
-
-def middle(back, rows, grad, norm, down_column, cross_sum):
-    n = lax.axis_size("dp")
-    count, width = rows.shape
-    m, r, c = down_column.shape
-    vmem = pl.BlockSpec(memory_space=pltpu.VMEM)
-    return pl.pallas_call(
-        functools.partial(middle_kernel, n=n),
-        in_specs=[vmem, vmem, vmem, vmem, ANY, ANY],
-        out_specs=[ANY, vmem, vmem, vmem, ANY],
-        out_shape=[
-            jax.ShapeDtypeStruct((4 * count, width), BF16),
-            jax.ShapeDtypeStruct((count, width), F32),
-            jax.ShapeDtypeStruct((8, width), F32),
-            jax.ShapeDtypeStruct((r, c), F32),
-            jax.ShapeDtypeStruct((m, r, cross_sum.shape[4]), BF16),
-        ],
-        scratch_shapes=[
-            pltpu.VMEM((count, width), BF16),
-            pltpu.VMEM((m, r, c), BF16),
-            pltpu.VMEM((m, r, c), BF16),
-        ]
-        + link_scratch(6 + m, 2),
-        compiler_params=pltpu.CompilerParams(
-            vmem_limit_bytes=VMEM_LIMIT, collective_id=6, has_side_effects=True
-        ),
-        cost_estimate=pl.CostEstimate(flops=0, bytes_accessed=100 * 2**20, transcendentals=0),
-        name="middle",
-    )(back, rows, grad, norm, down_column, cross_sum)
-
-
 def tail_kernel(
-    dq_ref, dk_ref, dv_ref, w_ref, first_hbm, wide_hbm, mt_hbm, rows_hbm, grad_hbm, norm_ref,
+    dq_ref, dk_ref, dv_ref, w_ref, first_hbm, wide_hbm, mt_hbm, rows_hbm, grad_hbm, cross_hbm, norm_ref,
     self_ref, ffn_ref, cq_ref, cv_ref, up_ref,
-    grad_out, weights_out, late_out, give, acc, weights,
-    first_ref, wide_ref, mt_ref, rows_ref, grad_ref, *scratch, n, step_rows
+    grad_out, weights_out, late_out, cross_out, give, acc, weights,
+    first_ref, wide_ref, mt_ref, rows_ref, grad_ref, cross_ref, cross_slots, *scratch, n, step_rows
 ):
     links = Links(*scratch[-3:])
     loads = [
         links.local(source, target)
         for source, target in (
-            (first_hbm, first_ref), (wide_hbm, wide_ref), (mt_hbm, mt_ref), (rows_hbm, rows_ref), (grad_hbm, grad_ref)
+            (cross_hbm, cross_ref), (first_hbm, first_ref), (wide_hbm, wide_ref), (mt_hbm, mt_ref),
+            (rows_hbm, rows_ref), (grad_hbm, grad_ref),
         )
     ]
     for copy in loads:
         copy.start()
+    cross = Collect(links, cross_ref, cross_slots)
     member = links.tensor
     near, far, got_near, got_far, got_x = scratch[:5]
     columns, gots, slots = scratch[5:7], scratch[7:9], scratch[9:11]
@@ -657,6 +569,22 @@
             weights[block // 2, block % 2, :, k * c : (k + 1) * c] = acc[span, k * c : (k + 1) * c].astype(BF16)
         columns[k][...] = weights[:, y, :, k * c : (k + 1) * c]
 
+    loads[0].wait()
+    cross.start(0)
+    acc[...] = jnp.zeros_like(acc)
+    loads[1].wait()
+
+    def products(refs, at):
+        def one(rows):
+            source = first_ref[rows, :].T
+            for k, ref in enumerate(refs):
+                acc[:, (at + k) * width : (at + k + 1) * width] += dot_nn(source, ref[rows, :])
+
+        return one
+
+    by_rows(dq_ref.shape[0], step_rows, products((dq_ref, dk_ref), 0))
+    packed(0)
+    over_y[0].start()
     terms(3, give.at[0])
     core_far.start()
     terms(2, far)
@@ -669,28 +597,22 @@
 
         by_rows(half, 64, add)
         copy.start()
-
-    acc[...] = jnp.zeros_like(acc)
-    for copy in loads:
+    for copy in loads[2:]:
         copy.wait()
 
-    def products(rows):
-        source = first_ref[rows, :].T
-        for k, ref in enumerate((dq_ref, dk_ref, dv_ref)):
-            acc[:, k * width : (k + 1) * width] += dot_nn(source, ref[rows, :])
-
-    by_rows(dq_ref.shape[0], step_rows, products)
-    packed(0)
-    over_y[0].start()
+    def products_out(rows):
+        acc[:, 3 * width :] += dot_nn(wide_ref[rows, :].T, mt_ref[:, rows].T)
+
+    by_rows(dq_ref.shape[0], step_rows, products((dv_ref,), 2))
+    by_rows(dq_ref.shape[0], step_rows, products_out)
+    packed(1)
+    over_y[1].start()
     terms(1, give.at[1])
     core_near.start()
     terms(0, near)
-
-    def products_out(rows):
-        acc[:, 3 * width :] += dot_nn(wide_ref[rows, :].T, mt_ref[:, rows].T)
-
-    by_rows(dq_ref.shape[0], step_rows, products_out)
-    packed(1)
+    for step in range(stages - 1):
+        cross.finish(step)
+        cross.start(step + 1)
 
     held[0] = jnp.zeros(held.shape[1:], F32)
     sums[0] = jnp.zeros(sums.shape[1:], F32)
@@ -738,8 +660,9 @@
         weights_out[:, k * c : (k + 1) * c] = columns[k][collects[k].z].astype(F32)
 
     summed_y(0)
-    over_y[1].start()
     early.finish(0)
+    cross.finish(stages - 1)
+    cross_out[...] = cross_ref[cross.z].astype(F32)
     core_near.wait_recv()
     over_x[0].wait_recv()
     norm_back(parts[0])
@@ -770,11 +693,13 @@
     late_out[0:2, :] = held[steps, 0:2, :]
     for copy in over_x + over_y + [core_near, core_far]:
         copy.wait_send()
-    for collect in collects:
+    for collect in collects + [cross]:
         collect.drain()
 
 
-def tail(dq, dk, dv, w, first, wide, mixed_t, rows, grad, norm, self_sums, ffn_sums, cq_sums, cv_sums, up_sums):
+def tail(
+    dq, dk, dv, w, first, wide, mixed_t, rows, grad, cross_column, norm, self_sums, ffn_sums, cq_sums, cv_sums, up_sums
+):
     n = lax.axis_size("dp")
     count, model = rows.shape
     width = dq.shape[1]
@@ -784,35 +709,40 @@
     part = pltpu.VMEM((m, r, c // 2), BF16)
     return pl.pallas_call(
         functools.partial(tail_kernel, n=n, step_rows=512),
-        in_specs=[vmem] * 4 + [ANY] * 5 + [vmem] * 6,
-        out_specs=[vmem, vmem, vmem],
+        in_specs=[vmem] * 4 + [ANY] * 6 + [vmem] * 6,
+        out_specs=[vmem] * 4,
         out_shape=[
             jax.ShapeDtypeStruct((count, model), F32),
             jax.ShapeDtypeStruct((r, c), F32),
             jax.ShapeDtypeStruct((vectors[0] + 2, model), F32),
+            jax.ShapeDtypeStruct(cross_column.shape[1:], F32),
         ],
         scratch_shapes=[
             pltpu.VMEM((2, count, model), BF16),
             pltpu.VMEM((model, c), F32),
             pltpu.VMEM((m, 2, r, c), BF16),
         ]
-        + [pltpu.VMEM(v.shape, v.dtype) for v in (first, wide, mixed_t, rows, grad)]
+        + [pltpu.VMEM(v.shape, v.dtype) for v in (first, wide, mixed_t, rows, grad, cross_column, cross_column)]
         + row_sum_scratch(count, model)
         + [part] * 6
         + everywhere_scratch(8, model, n)
         + everywhere_scratch(*vectors, n)
-        + link_scratch(6 + 2 * m + 2 * len(everywhere_ways(n)), 5),
+        + link_scratch(6 + 3 * m + 2 * len(everywhere_ways(n)), 6),
         compiler_params=pltpu.CompilerParams(
             vmem_limit_bytes=VMEM_LIMIT, collective_id=7, has_side_effects=True
         ),
         cost_estimate=pl.CostEstimate(flops=0, bytes_accessed=100 * 2**20, transcendentals=0),
         name="tail",
-    )(dq, dk, dv, w, first, wide, mixed_t, rows, grad, norm, self_sums, ffn_sums, cq_sums, cv_sums, up_sums)
+    )(
+        dq, dk, dv, w, first, wide, mixed_t, rows, grad, cross_column, norm,
+        self_sums, ffn_sums, cq_sums, cv_sums, up_sums,
+    )
 
 
 def results_kernel(
-    output_ref, grad_ref, enc_ref, self_ref, cross_ref, up_ref, down_ref,
-    output_out, grad_out, enc_out, qkv_out, so_out, cq_out, ckv_out, co_out, up_out, down_out, *, scale
+    output_ref, grad_ref, enc_ref, self_ref, cross_ref, up_ref, down_ref, vectors_ref,
+    output_out, grad_out, enc_out, qkv_out, so_out, cq_out, ckv_out, co_out, up_out, down_out,
+    norm_out, biases_out, shift_out, *, scale
 ):
     output_out[...] = output_ref[...]
     grad_out[...] = grad_ref[...]
@@ -830,9 +760,17 @@
         co_out[...] = (cross_ref[:, 3 * width :] * scale).T
         up_out[...] = up_ref[...] * scale
         down_out[...] = (down_ref[...] * scale).T
-
-
-def results(output, grad, encoder, self_w, cross_w, up, down, scale):
+        vectors = vectors_ref[...] * scale
+        for k in range(3):
+            norm_out[k] = vectors[2 * k : 2 * k + 2, :]
+        biases_out[...] = vectors[6:13, :]
+        lines = vectors.shape[1] // LANES
+        for k in range(shift_out.shape[0]):
+            part = slice(k % lines * LANES, (k % lines + 1) * LANES)
+            shift_out[k : k + 1, :] = vectors[13 + k // lines : 14 + k // lines, part]
+
+
+def results(output, grad, encoder, self_w, cross_w, up, down, vectors, scale):
     r, c = self_w.shape
     width = c // 4
     steps = 4
@@ -841,17 +779,18 @@
         return pl.BlockSpec((value.shape[0] // steps, value.shape[1]), lambda i: (i, 0))
 
     shapes = [(r, 3, width), (width, r), (r, width), (r, 2, width), (width, r), up.shape, down.shape[::-1]]
+    shapes += [(3, 2, output.shape[1]), (7, output.shape[1]), (4 * up.shape[1] // LANES, LANES)]
     return pl.pallas_call(
         functools.partial(results_kernel, scale=scale),
         grid=(steps,),
-        in_specs=[rows(output), rows(grad), rows(encoder)] + [const(v.shape) for v in (self_w, cross_w, up, down)],
+        in_specs=[rows(output), rows(grad), rows(encoder)] + [const(v.shape) for v in (self_w, cross_w, up, down, vectors)],
         out_specs=[rows(output), rows(grad), rows(encoder)] + [const(shape) for shape in shapes],
         out_shape=[jax.ShapeDtypeStruct(v.shape, F32) for v in (output, grad, encoder)]
         + [jax.ShapeDtypeStruct(shape, F32) for shape in shapes],
         compiler_params=pltpu.CompilerParams(vmem_limit_bytes=VMEM_LIMIT),
         cost_estimate=pl.CostEstimate(flops=0, bytes_accessed=20 * 2**20, transcendentals=0),
         name="results",
-    )(output, grad, encoder, self_w, cross_w, up, down)
+    )(output, grad, encoder, self_w, cross_w, up, down, vectors)
 
 
 def start_kernel(
@@ -1121,7 +1060,7 @@
     after_out, second_out, whole_out, enc_out, down_out, far_down, *scratch, n
 ):
     links = Links(*scratch[-3:])
-    rows_sum = RowSum(links, terms_ref, scratch[:5], left=True)
+    rows_sum = RowSum(links, terms_ref, scratch[:5])
     column = scratch[5]
     spread = SpreadZ(links, down_ref.at[0], from_z, scratch[6], down_out, n)
     over_z = links.copy(down_ref.at[1], far_down, z_ways(n)[0])
@@ -1143,6 +1082,7 @@
     enc_core = [links.copy(enc_ref, place(0), CORE), links.copy(place(2), place(2), CORE)]
     enc_own = links.local(enc_ref, place(0))
     links.greet([CORE, X, Y] + z_ways(n))
+    enc_x.start()
     rows_sum.start()
     load.start()
     over_z.start()
@@ -1154,8 +1094,8 @@
     rows_sum.middle()
     over_core[0].start()
     enc_core[0].start()
-    rows_sum.over_x.wait_send()
-    enc_x.start()
+    enc_x.wait_recv()
+    enc_core[1].start()
     rows_sum.end()
 
     def norm(rows):
@@ -1165,8 +1105,6 @@
         second_out[rows, :] = (xhat * norm_ref[1, 0:1, :] + norm_ref[1, 1:2, :]).astype(BF16)
 
     by_rows(after_out.shape[0], 64, norm)
-    enc_x.wait_recv()
-    enc_core[1].start()
     over_y.wait_recv()
     over_core[1].start()
     enc_x.wait_send()
@@ -1205,61 +1143,106 @@
 
 
 def self_backward_kernel(
-    b_ref, q_ref, k_ref, v_ref, kt_ref, wide_ref, w_ref, mt_ref, lse_ref,
-    up_ref, cross_ref, diagonal_ref, enc_ref,
-    dq_ref, dk_ref, dv_ref, up_out, cross_out, enc_out, dka, dva, dqa, *scratch, heads, safe, n
+    b_ref, q_ref, k_ref, v_ref, kt_ref, w_ref, mt_ref, lse_ref, back_ref, rows_ref, above_ref, norm_ref,
+    up_ref, down_ref, cross_ref, enc_ref,
+    dq_ref, dk_ref, dv_ref, wide_out, grad_out, sums_ref, up_out, down_out, cross_out, enc_out,
+    dka, dva, dqa, wide, *scratch, bq, heads, safe, n
 ):
-    i = pl.program_id(0)
+    s = pl.program_id(0)
+    last = pl.num_programs(0) - 1
     links = Links(*scratch[-3:])
-    cross = GatherLast(links, cross_ref.at[0], cross_ref.at[1], diagonal_ref, scratch[:5])
-    cross_z = Collect(links, cross.column, scratch[5])
-    up_column = scratch[6]
-    up_z = Collect(links, up_column, scratch[7])
-    load = links.local(up_ref, up_column)
-    enc = RowSum(links, enc_ref, scratch[8:13])
-    stages = len(up_z.stages)
-
-    @pl.when(i == 0)
+    member = links.tensor
+    x = member // 2
+    later = (s // 2 + 1) // 2
+    i = s * (1 - x) + ((s + 3) * (1 - later) + (4 - s) * later) * x
+    cross = GatherLast(links, cross_ref.at[0], cross_ref.at[1], scratch[:5])
+    keep_cross = links.local(cross.column, cross_out)
+    columns, slots = scratch[5:7], scratch[7:9]
+    sums_z = [Collect(links, column, slot) for column, slot in zip(columns, slots)]
+    load_z = [links.local(ref, column) for ref, column in zip((up_ref, down_ref), columns)]
+    enc = RowSum(links, enc_ref, scratch[9:14])
+    stages = len(sums_z[0].stages)
+    count = grad_out.shape[0]
+    half = count // 2
+
+    def place(distance, k=None):
+        start = (member ^ distance) * count
+        if k is None:
+            return wide.at[pl.ds(pl.multiple_of(start, half), count)]
+        return wide.at[pl.ds(pl.multiple_of(start + k * half, half), half)]
+
+    over_x = [links.copy(place(0, k), place(0, k), X) for k in range(2)]
+    over_core = links.copy(place(0), place(0), CORE)
+    onward = [links.copy(place(2, k), place(2, k), CORE) for k in range(2)]
+    keep_wide = links.local(wide, wide_out)
+
+    def norm_back(k):
+        def one(rows):
+            rows = pl.ds(pl.multiple_of(k * half + rows.start, 64), 64)
+            incoming = back_ref[rows, :]
+            rows_grad, gain_terms = norm_rows_back(rows_ref[rows, :], incoming, norm_ref[1, 0:1, :])
+            rows_grad = rows_grad + above_ref[rows, :]
+            rounded = rows_grad.astype(BF16)
+            grad_out[rows, :] = rows_grad
+            wide[pl.ds(pl.multiple_of(member * count + rows.start, 64), 64), :] = rounded
+            for row, terms in enumerate((gain_terms, incoming, rounded.astype(F32))):
+                sums_ref[row : row + 1, :] += jnp.sum(terms, axis=0, keepdims=True)
+
+        by_rows(half, 64, one)
+
+    def arrive(k):
+        over_x[k].wait_recv()
+        onward[k].start()
+        onward[k].wait_recv()
+
+    @pl.when(s == 0)
     def _():
-        links.greet(everywhere_ways(n))
+        links.greet([CORE, X, Y] + z_ways(n))
+        for copy in load_z:
+            copy.start()
+        sums_ref[...] = jnp.zeros_like(sums_ref)
+        for k in range(2):
+            norm_back(k)
+            over_x[k].start()
+        over_core.start()
         cross.start()
         enc.start()
-        load.start()
-        load.wait()
-        up_z.start(0)
+        for copy, total in zip(load_z, sums_z):
+            copy.wait()
+            total.start(0)
         dka[...] = jnp.zeros_like(dka)
         dva[...] = jnp.zeros_like(dva)
-
-    @pl.when(i == 1)
+        over_core.wait_recv()
+
+    @pl.when(s == 2)
     def _():
+        arrive(0)
+        pl.when(x == 1)(functools.partial(arrive, 1))
+        cross.second()
+        enc.middle()
+        for step in range(stages - 1):
+            for total in sums_z:
+                total.finish(step)
+            for total in sums_z:
+                total.start(step + 1)
+
+    @pl.when(s == 3)
+    def _():
+        pl.when(x == 0)(functools.partial(arrive, 1))
         cross.middle()
-
-    @pl.when(i == 2)
-    def _():
-        for step in range(stages - 1):
-            up_z.finish(step)
-            up_z.start(step + 1)
-
-    def sum_cross():
-        cross.end()
-        cross_z.start(0)
-        enc.middle()
-
-    def next_cross():
-        for step in range(stages - 1):
-            cross_z.finish(step)
-            cross_z.start(step + 1)
-
-    bq, width = q_ref.shape
+        keep_wide.start()
+
+    width = k_ref.shape[1]
     hd = width // heads
     scale = 1.0 / math.sqrt(hd)
-    grads = dot_nn(wide_ref[...], w_ref[:, 3 * width :]).astype(BF16)
-    products = grads.T.astype(F32) * mt_ref[...].astype(F32)
+    here = pl.ds(pl.multiple_of(i * bq, bq), bq)
+    grads = dot_nn(wide[here, :], w_ref[:, 3 * width :]).astype(BF16)
+    products = grads.T.astype(F32) * mt_ref[:, here].astype(F32)
     inner = [jnp.sum(products[h * hd : (h + 1) * hd, :], axis=0, keepdims=True) for h in range(heads)]
-    scaled = q_ref[...] * jnp.asarray(scale, BF16)
+    scaled = q_ref[here, :] * jnp.asarray(scale, BF16)
     q_heads = [head_only(scaled, h, hd) for h in range(heads)]
     d_heads = [head_only(grads, h, hd) for h in range(heads)]
-    lse = lse_ref[...]
+    lse = lse_ref[:, here]
     dqa[...] = jnp.zeros_like(dqa)
 
     def block(first, size, skip, mode):
@@ -1283,81 +1266,93 @@
             dva[rows, part] += dv_sums[group]
             dka[rows, part] += dk_sums[group]
 
-    over_keys(i, bq, safe, block, [(3, 2, sum_cross), (4, 2, next_cross)])
-    dq_ref[...] = (dqa[...] * scale).astype(BF16).T
-
-    @pl.when(i == pl.num_programs(0) - 1)
+    over_keys(i, bq, safe, block)
+    dq_ref[here, :] = (dqa[...] * scale).astype(BF16).T
+
+    @pl.when(s == last)
     def _():
         dk_ref[...] = dka[...].astype(BF16)
         dv_ref[...] = dva[...].astype(BF16)
-        up_z.finish(stages - 1)
-        up_out[...] = up_column[up_z.z].astype(F32)
-        cross_z.finish(stages - 1)
-        cross_out[...] = cross.column[cross_z.z].astype(F32)
+        cross.end()
+        keep_cross.start()
+        for total, out in zip(sums_z, (up_out, down_out)):
+            total.finish(stages - 1)
+            out[...] = total.column[total.z].astype(F32)
+            total.drain()
         enc.end()
 
         def store(rows):
             enc_out[rows, :] = enc.total(rows)
 
         by_rows(enc_out.shape[0], 64, store)
-        up_z.drain()
-        cross_z.drain()
+        for copy in over_x + onward + [over_core]:
+            copy.wait_send()
+        keep_wide.wait()
+        keep_cross.wait()
 
 
 def self_backward(
-    bounds, queries, keys, values, keys_t, wide, w, mixed_t, lse,
-    up_column, cross_sum, diagonal, enc_terms, heads, safe
+    bounds, queries, keys, values, keys_t, w, mixed_t, lse, back, rows, above, norm,
+    up_column, down_column, cross_sum, enc_terms, heads, safe
 ):
     n, width = queries.shape
-    model = wide.shape[1]
+    count, model = rows.shape
     dp = lax.axis_size("dp")
     m, r, c = up_column.shape
     cross_c = cross_sum.shape[4]
     enc_shape = (enc_terms.shape[0] // 4, enc_terms.shape[1])
     bq = 512
-    some = pl.BlockSpec((bq, width), lambda i: (i, 0))
     return pl.pallas_call(
-        functools.partial(self_backward_kernel, heads=heads, safe=safe, n=dp),
+        functools.partial(self_backward_kernel, bq=bq, heads=heads, safe=safe, n=dp),
         grid=(n // bq,),
         in_specs=[
             pl.BlockSpec(memory_space=pltpu.SMEM),
-            some,
+            const((n, width)),
             const((n, width)),
             const((n, width)),
             const((width, n)),
-            pl.BlockSpec((bq, model), lambda i: (i, 0)),
             const((model, 4 * width)),
-            pl.BlockSpec((width, bq), lambda i: (0, i)),
-            pl.BlockSpec((heads, bq), lambda i: (0, i)),
+            const((width, n)),
+            const((heads, n)),
+            const((count, model)),
+            const((count, model)),
+            const((count, model)),
+            const(norm.shape),
         ]
         + [ANY] * 4,
-        out_specs=[some, const((n, width)), const((n, width))]
-        + [const((r, c)), const((r, cross_c)), const(enc_shape)],
-        out_shape=[
-            jax.ShapeDtypeStruct((n, width), BF16),
-            jax.ShapeDtypeStruct((n, width), BF16),
-            jax.ShapeDtypeStruct((n, width), BF16),
+        out_specs=[const((n, width))] * 3
+        + [ANY, const((count, model)), const((8, model)), const((r, c)), const((r, c)), ANY, const(enc_shape)],
+        out_shape=[jax.ShapeDtypeStruct((n, width), BF16)] * 3
+        + [
+            jax.ShapeDtypeStruct((n, model), BF16),
+            jax.ShapeDtypeStruct((count, model), F32),
+            jax.ShapeDtypeStruct((8, model), F32),
             jax.ShapeDtypeStruct((r, c), F32),
-            jax.ShapeDtypeStruct((r, cross_c), F32),
+            jax.ShapeDtypeStruct((r, c), F32),
+            jax.ShapeDtypeStruct((m, r, cross_c), BF16),
             jax.ShapeDtypeStruct(enc_shape, F32),
         ],
         scratch_shapes=[
             pltpu.VMEM((n, width), F32),
             pltpu.VMEM((n, width), F32),
             pltpu.VMEM((width, bq), F32),
+            pltpu.VMEM((n, model), BF16),
         ]
-        + [pltpu.VMEM((m, r, cross_c), BF16)] * 6
-        + [pltpu.VMEM((m, r, c), BF16)] * 2
+        + [pltpu.VMEM((m, r, cross_c), BF16)] * 5
+        + [pltpu.VMEM((m, r, c), BF16)] * 4
         + row_sum_scratch(*enc_shape)
-        + link_scratch(5 + 2 * m, 6),
+        + link_scratch(11 + 2 * m, 8),
         compiler_params=pltpu.CompilerParams(
-            vmem_limit_bytes=VMEM_LIMIT, collective_id=5, has_side_effects=True
+            vmem_limit_bytes=62 * 2**20, collective_id=5, has_side_effects=True
         ),
         cost_estimate=pl.CostEstimate(
             flops=24 * n * n * width, bytes_accessed=16 * n * width, transcendentals=n * n * heads // 2
         ),
         name="self_backward",
-    )(bounds, queries, keys, values, keys_t, wide, w, mixed_t, lse, up_column, cross_sum, diagonal, enc_terms)
+    )(
+        bounds, queries, keys, values, keys_t, w, mixed_t, lse, back, rows, above, norm,
+        up_column, down_column, cross_sum, enc_terms,
+    )
 
 
 def const(shape):
@@ -1982,27 +1977,31 @@
         heads,
     )
     cross_sum = cross_sum.reshape(2, groups_count // 2, 2, w_rows, 4 * width)
-    self_wide, self_rows_grad, self_sums, summed_down, diagonal = middle(
-        second_grad, after_self, cross_rows_grad, norm_params, down_column, cross_sum
-    )
-    self_dq, self_dk, self_dv, summed_up, summed_cross, encoder_grad = self_backward(
+
+    (
+        self_dq, self_dk, self_dv, self_wide, self_rows_grad, self_sums,
+        summed_up, summed_down, cross_column, encoder_grad,
+    ) = self_backward(
         bounds,
         queries,
         key_rows,
         value_rows,
         keys_t,
-        self_wide,
         self_w,
         self_mixed_t,
         self_lse,
+        second_grad,
+        after_self,
+        cross_rows_grad,
+        norm_params,
         up_column,
+        down_column,
         cross_sum,
-        diagonal,
         enc_terms,
         heads,
         self_safe,
     )
-    input_grad, summed_self, vectors = tail(
+    input_grad, summed_self, vectors, summed_cross = tail(
         self_dq,
         self_dk,
         self_dv,
@@ -2012,6 +2011,7 @@
         self_mixed_t,
         block_in,
         self_rows_grad,
+        cross_column,
         norm_params,
         self_sums,
         ffn_sums,
@@ -2019,16 +2019,15 @@
         bias_cv_parts,
         bias_up_parts,
     )
-    scale = 1.0 / groups_count
-    output, input_grad, encoder_grad, g_qkv, g_so, g_cq, g_ckv, g_co, g_up, g_down = results(
-        output, input_grad, encoder_grad, summed_self, summed_cross, summed_up, summed_down, scale
+    output, input_grad, encoder_grad, *weights_and_vectors = results(
+        output, input_grad, encoder_grad, summed_self, summed_cross, summed_up, summed_down, vectors, 1.0 / groups_count
     )
-    vectors = vectors * scale
+    g_qkv, g_so, g_cq, g_ckv, g_co, g_up, g_down, g_norm, g_biases, g_shift = weights_and_vectors
     return (
         output,
         input_grad,
         encoder_grad,
-        vectors[:6].reshape(norm_params.shape),
+        g_norm,
         g_qkv,
         g_so,
         g_cq,
@@ -2036,8 +2035,8 @@
         g_co,
         g_up,
         g_down,
-        vectors[6:13],
-        vectors[13:17].reshape(-1),
+        g_biases,
+        g_shift.reshape(-1),
     )
 
 

time: 511 us -> 493 us (0.965)
  Pallas kernels: 496 us -> 481 us
    pallas_call x2 -> x1, Pallas kernels: 104 us -> 85.9 us  [self_backward(): pl.pallas_call(functools.partial(self_backward_kernel, bq=bq, heads=heads...]
    pallas_call x1, Pallas kernels: 67.8 us -> 74.5 us  [tail(): pl.pallas_call(functools.partial(tail_kernel, n=n, step_rows=512), in_spe...]
where the time goes in v13:
time: 493 us; the launch traced here: 487 us
  Pallas kernels  481 us (98%)
    pallas_call x1, Pallas kernels, self_backward(): pl.pallas_call(functools.partial(self_backward_kernel, bq=bq, heads=heads...  85.9 us
    pallas_call x1, Pallas kernels, tail(): pl.pallas_call(functools.partial(tail_kernel, n=n, step_rows=512), in_spe...  74.5 us
    pallas_call x1, Pallas kernels, cross_backward(): pl.pallas_call(functools.partial(cross_backward_kernel, heads=heads, bk=2...  59.8 us
    pallas_call x1, Pallas kernels, start_gather(): pl.pallas_call(functools.partial(start_kernel, n=n), in_specs=[pl.BlockSp...  53.8 us
    pallas_call x1, Pallas kernels, feed_forward(): pl.pallas_call(functools.partial(feed_forward_kernel, chunks=chunks), gri...  53.3 us
    pallas_call x1, Pallas kernels, sum_after_self(): pl.pallas_call(functools.partial(after_self_kernel, n=2 * m), in_specs=[A...  52.3 us
    pallas_call x1, Pallas kernels, self_forward(): pl.pallas_call(functools.partial(self_forward_kernel, heads=heads, safe=s...  48.4 us
    pallas_call x1, Pallas kernels, cross_forward(): pl.pallas_call(functools.partial(cross_forward_kernel, heads=heads, n=2 *...  45.6 us

profile of v13, /device:TPU:0, one launch (start us, length us, event | category | flops | bytes accessed | tf_op | source)
XLA Modules:
  0.0 486.6 jit_solution(4515710813974730039)
XLA Ops:
  1.3 1.8 copy.28.qkv_ref
  3.1 53.8 %start_gather.1 = (bf16[2560,1024]{1,0:T(8,128)(2,1)}, bf16[4,2,128,1024]{3,2,1,0:T(8,128)(2,1)}, bf16[4,128,1024]{2,1,0:T(8,128)(2,1)}, bf16[2,2,128,1024]{3,2,1,0:T(8,128)(2,1)}) custom-call(bf16[640,1024]{1,0:T(8,128)(2,1)} %rows_hbm.1, f32[3,2,1024]{2,1,0:T(2,128)} %norm_ref.11, bf16[128,3,256]{2,1,0:T(4,128)(2,1)} %copy.28.qkv_ref, ...), custom_call_target="tpu_custom_call" | custom-call | bytes 104857600 | tf_op jit(solution)/shard_map/start_gather/pallas_call | solution.py:881
  56.9 48.4 %self_forward.1 = (bf16[2560,256]{1,0:T(8,128)(2,1)}, bf16[2560,256]{1,0:T(8,128)(2,1)}, bf16[2560,256]{1,0:T(8,128)(2,1)}, bf16[256,2560]{1,0:T(8,128)(2,1)}, b...) custom-call(s32[1,2]{1,0:T(1,128)} %b_ref.3, ...), custom_call_target="tpu_custom_call" | custom-call | flops 20132659200 | bytes 5242880 | tf_op jit(solution)/shard_map/self_forward/pallas_call | solution.py:1004
  105.2 52.3 %sum_after_self.1 = (f32[640,1024]{1,0:T(8,128)}, bf16[640,1024]{1,0:T(8,128)(2,1)}, bf16[2,4,2,128,1024]{4,3,2,1,0:T(8,128)(2,1)}, bf16[1024,1024]{1,0:T(8,128)...) custom-call(bf16[2560,1024]{1,0:T(8,128)(2,1)} %get-tuple-element.89.terms_ref, ...), custom_call_target="tpu_custom_call" | custom-call | bytes 104857600 | tf_op jit(solution)/shard_map/sum_after_self/pallas_call | solution.py:1122
  157.5 45.6 %cross_forward.1 = (bf16[4,640,256]{2,1,0:T(8,128)(2,1)}, bf16[4,1024,256]{2,1,0:T(8,128)(2,1)}, bf16[4,1024,256]{2,1,0:T(8,128)(2,1)}, bf16[4,256,640]{2,1,0:T(...) custom-call(s32[1]{0:T(128)S(6)} %copy.30.len_ref, ...), custom_call_target="tpu_custom_call" | custom-call | flops 16106127360 | bytes 8388608 | tf_op jit(solution)/shard_map/cross_forward/pallas_call | solution.py:1460
  203.1 53.3 %feed_forward.1 = (f32[640,1024]{1,0:T(8,128)}, f32[640,1024]{1,0:T(8,128)}, bf16[640,1024]{1,0:T(8,128)(2,1)}, f32[8,1024]{1,0:T(8,128)}, bf16[2,1024,1024]{2,1...) custom-call(bf16[640,1024]{1,0:T(8,128)(2,1)} %get-tuple-element.97., ...), custom_call_target="tpu_custom_call" | custom-call | flops 32212254720 | bytes 41943040 | tf_op jit(solution)/shard_map/feed_forward/pallas_call | solution.py:1659
  256.4 59.8 %cross_backward.1 = (f32[640,1024]{1,0:T(8,128)}, bf16[1024,1024]{1,0:T(8,128)(2,1)}, bf16[2,1024,1024]{2,1,0:T(8,128)(2,1)}, f32[4,1,256]{2,1,0:T(1,128)}, f32[...) custom-call(s32[1]{0:T(128)S(6)} %copy.30.len_ref, ...), custom_call_target="tpu_custom_call" | custom-call | flops 32212254720 | bytes 16777216 | tf_op jit(solution)/shard_map/cross_backward/pallas_call | solution.py:1825
  316.2 85.9 %self_backward.1 = (bf16[2560,256]{1,0:T(8,128)(2,1)}, bf16[2560,256]{1,0:T(8,128)(2,1)}, bf16[2560,256]{1,0:T(8,128)(2,1)}, bf16[2560,1024]{1,0:T(8,128)(2,1)},...) custom-call(s32[1,2]{1,0:T(1,128)} %b_ref.3, ...), custom_call_target="tpu_custom_call" | custom-call | flops 40265318400 | bytes 10485760 | tf_op jit(solution)/shard_map/self_backward/pallas_call | solution.py:1305
  402.1 74.5 %tail.1 = (f32[640,1024]{1,0:T(8,128)}, f32[128,1024]{1,0:T(8,128)}, f32[18,1024]{1,0:T(8,128)}, f32[128,1024]{1,0:T(8,128)}) custom-call(bf16[2560,256]{1,0:T(8,128)(2,1)} %get-tuple-element.126.dq_ref, bf16[2560,256]{1,0:T(8,128)(2,1)} %get-tuple-element.127.dk_ref, bf16[2560,256]{1,0:T(8,128)(2,1)} %get-tuple-element.128.dv_ref, ...), custom_call_target="tpu_custom_call" | custom-call | bytes 104857600 | tf_op jit(solution)/shard_map/tail/pallas_call | solution.py:710
  476.6 7.9 %results.1 = (f32[640,1024]{1,0:T(8,128)}, f32[640,1024]{1,0:T(8,128)}, f32[256,1024]{1,0:T(8,128)}, f32[128,3,256]{2,1,0:T(4,128)}, f32[256,128]{1,0:T(8,128)},...) custom-call(f32[640,1024]{1,0:T(8,128)} %get-tuple-element.103.outpu, ...), custom_call_target="tpu_custom_call" | custom-call | bytes 20971520 | tf_op jit(solution)/shard_map/results/pallas_call | solution.py:783
  484.5 1.9 copy.29

commit v14 on v13

--- a/solution.py
+++ b/solution.py
@@ -502,6 +502,34 @@
         self.held[step + 1] = self.held[step] + self.slots[step]
 
 
+class Direct:
+    def __init__(self, links, value, slots_tensor, slots_dp, n):
+        self.value = value
+        self.slots = (slots_tensor, slots_dp)
+        self.me = (links.tensor, links.dp)
+        self.copies = []
+        for slots, me, axis, size in zip(self.slots, self.me, ("tensor", "dp"), (4, n)):
+            self.copies.append([links.copy(value, slots.at[me], (axis, d)) for d in range(1, size)])
+
+    def start(self, phase):
+        for copy in self.copies[phase]:
+            copy.start()
+
+    def finish(self, phase):
+        slots = self.slots[phase]
+        slots[self.me[phase]] = self.value[...]
+        for copy in self.copies[phase]:
+            copy.wait()
+        total = slots[0]
+        for k in range(1, slots.shape[0]):
+            total = total + slots[k]
+        self.value[...] = total
+
+
+def direct_ways(n):
+    return [("tensor", d) for d in range(1, 4)] + [("dp", d) for d in range(1, n)]
+
+
 def everywhere_ways(n):
     return [CORE, X, Y] + z_ways(n)
 
@@ -531,7 +559,7 @@
     member = links.tensor
     near, far, got_near, got_far, got_x = scratch[:5]
     columns, gots, slots = scratch[5:7], scratch[7:9], scratch[9:11]
-    held, late_slots, sums, early_slots = scratch[11:15]
+    late_tensor, late_dp, sums, early_slots, held, compact = scratch[11:17]
     count, model = near.shape
     width = dq_ref.shape[1]
     y = links.dp % 2
@@ -547,10 +575,10 @@
         over_y.append(links.copy(weights.at[:, 1 - y, :, pl.ds(k * c, c)], got, Y))
         collects.append(Collect(links, column, slot))
     stages = len(collects[0].stages)
-    late = Everywhere(links, held, late_slots, everywhere_ways(n))
+    late = Direct(links, compact, late_tensor, late_dp, n)
     early = Everywhere(links, sums, early_slots, [CORE] + z_ways(n) + [Y, X])
-    steps = len(late.copies)
-    links.greet(everywhere_ways(n))
+    steps = len(early.copies)
+    links.greet(direct_ways(n))
 
     def terms(distance, target):
         base = (member ^ distance) * count
@@ -614,7 +642,7 @@
         cross.finish(step)
         cross.start(step + 1)
 
-    held[0] = jnp.zeros(held.shape[1:], F32)
+    held[...] = jnp.zeros_like(held)
     sums[0] = jnp.zeros(sums.shape[1:], F32)
     sums[0, 0:2, :] = self_ref[0:2, :]
     sums[0, 2:4, :] = ffn_ref[0:2, :]
@@ -640,8 +668,8 @@
             incoming = near[rows, :].astype(F32) + got_near[rows, :].astype(F32) + got_x[rows, :].astype(F32)
             rows_grad, gain_terms = norm_rows_back(rows_ref[rows, :].astype(F32), incoming, norm_ref[0, 0:1, :])
             grad_out[rows, :] = rows_grad + grad_ref[rows, :]
-            held[0, 0:1, :] += jnp.sum(gain_terms, axis=0, keepdims=True)
-            held[0, 1:2, :] += jnp.sum(incoming, axis=0, keepdims=True)
+            held[0:1, :] += jnp.sum(gain_terms, axis=0, keepdims=True)
+            held[1:2, :] += jnp.sum(incoming, axis=0, keepdims=True)
 
         by_rows(half, 64, one)
 
@@ -667,30 +695,27 @@
     over_x[0].wait_recv()
     norm_back(parts[0])
     next_z(0)
-    for step in range(1, steps - 2):
+    summed_y(1)
+    for step in range(1, steps - 1):
         early.start(step)
         early.finish(step)
+    next_z(1)
+    last_z(0)
     over_x[1].wait_recv()
     norm_back(parts[1])
+    lines = model // LANES
+    for k in range(2 * lines):
+        compact[k : k + 1, :] = held[k // lines : k // lines + 1, k % lines * LANES : (k % lines + 1) * LANES]
     late.start(0)
-    summed_y(1)
+    early.start(steps - 1)
+    last_z(1)
     late.finish(0)
     late.start(1)
-    early.start(steps - 2)
-    last_z(0)
-    early.finish(steps - 2)
+    early.finish(steps - 1)
+    late_out[2:, :] = sums[steps]
     late.finish(1)
-    late.start(2)
-    early.start(steps - 1)
-    next_z(1)
-    early.finish(steps - 1)
-    late.finish(2)
-    late_out[2:, :] = sums[steps]
-    for step in range(3, steps):
-        late.start(step)
-        late.finish(step)
-    last_z(1)
-    late_out[0:2, :] = held[steps, 0:2, :]
+    for k in range(2 * lines):
+        late_out[k // lines : k // lines + 1, k % lines * LANES : (k % lines + 1) * LANES] = compact[k : k + 1, :]
     for copy in over_x + over_y + [core_near, core_far]:
         copy.wait_send()
     for collect in collects + [cross]:
@@ -725,9 +750,10 @@
         + [pltpu.VMEM(v.shape, v.dtype) for v in (first, wide, mixed_t, rows, grad, cross_column, cross_column)]
         + row_sum_scratch(count, model)
         + [part] * 6
-        + everywhere_scratch(8, model, n)
+        + [pltpu.VMEM((size, 2 * model // LANES, LANES), F32) for size in (4, n)]
         + everywhere_scratch(*vectors, n)
-        + link_scratch(6 + 3 * m + 2 * len(everywhere_ways(n)), 6),
+        + [pltpu.VMEM((8, model), F32), pltpu.VMEM((2 * model // LANES, LANES), F32)]
+        + link_scratch(6 + 3 * m + len(everywhere_ways(n)) + len(direct_ways(n)), 6),
         compiler_params=pltpu.CompilerParams(
             vmem_limit_bytes=VMEM_LIMIT, collective_id=7, has_side_effects=True
         ),
@@ -794,8 +820,8 @@
 
 
 def start_kernel(
-    in_ref, norm_ref, qkv_ref, so_ref, cq_ref, ckv_ref, co_ref, down_ref,
-    rows_out, self_out, cross_out, down_out, rows_ref, self_ref, cross_ref, shard_ref, send_sems, recv_sems, local_sems, *, n
+    in_ref, norm_ref, qkv_ref, so_ref, cq_ref, ckv_ref, co_ref, down_ref, enc_ref,
+    rows_out, self_out, cross_out, down_out, enc_out, rows_ref, self_ref, cross_ref, shard_ref, send_sems, recv_sems, local_sems, *, n
 ):
     links = Links(send_sems, recv_sems, local_sems)
     member, z, y = links.tensor, links.dp // 2, links.dp % 2
@@ -827,6 +853,14 @@
     cross_ref[:, 3 * width :] = co_ref[...].T
     shard_ref[...] = down_ref[...].T
     square = Square(links, shard_ref, down_out)
+    enc_count = enc_ref.shape[0]
+
+    def enc_place(distance):
+        return enc_out.at[pl.ds(pl.multiple_of((member ^ distance) * enc_count, enc_count), enc_count)]
+
+    enc_x = links.copy(enc_ref, enc_place(0), X)
+    enc_core = [links.copy(enc_ref, enc_place(0), CORE), links.copy(enc_place(2), enc_place(2), CORE)]
+    local.append(links.local(enc_ref, enc_place(0)))
     links.greet([CORE, X, Y] + z_ways(n))
     for copy in over_y + local[1:]:
         copy.start()
@@ -844,6 +878,8 @@
     for copy in local[:1] + over_core[:1]:
         copy.start()
     square.start()
+    enc_x.start()
+    enc_core[0].start()
     for self_stage in self_stages:
         if self_stage is not self_stages[0]:
             for copy, _ in self_stage:
@@ -865,8 +901,11 @@
         copy.wait_recv()
         onward.start()
     square.middle()
+    enc_x.wait_recv()
+    enc_core[1].start()
+    enc_x.wait_send()
     square.end()
-    for copy in local + over_y + over_core:
+    for copy in local + over_y + over_core + enc_core:
         copy.wait()
     for copy in over_x:
         copy.wait_send()
@@ -875,29 +914,30 @@
             copy.wait_send()
 
 
-def start_gather(rows, norm, qkv, self_out, cross_q, cross_kv, cross_out, down):
+def start_gather(rows, norm, qkv, self_out, cross_q, cross_kv, cross_out, down, encoder):
     n = lax.axis_size("dp")
     r, c = cross_q.shape[0], 4 * cross_q.shape[1]
     return pl.pallas_call(
         functools.partial(start_kernel, n=n),
-        in_specs=[pl.BlockSpec(memory_space=pltpu.VMEM)] * 8,
-        out_specs=[ANY] * 4,
+        in_specs=[pl.BlockSpec(memory_space=pltpu.VMEM)] * 9,
+        out_specs=[ANY] * 5,
         out_shape=[
             jax.ShapeDtypeStruct((4 * rows.shape[0], rows.shape[1]), BF16),
             jax.ShapeDtypeStruct((n // 2, 2, r, c), BF16),
             jax.ShapeDtypeStruct((n // 2, r, c), BF16),
             jax.ShapeDtypeStruct((2, 2, r, down.shape[0]), BF16),
+            jax.ShapeDtypeStruct((4 * encoder.shape[0], encoder.shape[1]), BF16),
         ],
         scratch_shapes=[pltpu.VMEM(rows.shape, BF16)]
         + [pltpu.VMEM((r, c), BF16)] * 2
         + [pltpu.VMEM((r, down.shape[0]), BF16)]
-        + link_scratch(2 * n + 12, 4),
+        + link_scratch(2 * n + 15, 5),
         compiler_params=pltpu.CompilerParams(
             vmem_limit_bytes=VMEM_LIMIT, collective_id=0, has_side_effects=True
         ),
         cost_estimate=pl.CostEstimate(flops=0, bytes_accessed=100 * 2**20, transcendentals=0),
         name="start_gather",
-    )(rows, norm, qkv, self_out, cross_q, cross_kv, cross_out, down)
+    )(rows, norm, qkv, self_out, cross_q, cross_kv, cross_out, down, encoder)
 
 
 def self_forward_kernel(
@@ -1056,8 +1096,8 @@
 
 
 def after_self_kernel(
-    terms_ref, rows_ref, biases_ref, norm_ref, column_ref, enc_ref, down_ref, from_z,
-    after_out, second_out, whole_out, enc_out, down_out, far_down, *scratch, n
+    terms_ref, rows_ref, biases_ref, norm_ref, column_ref, down_ref, from_z,
+    after_out, second_out, whole_out, down_out, far_down, *scratch, n
 ):
     links = Links(*scratch[-3:])
     rows_sum = RowSum(links, terms_ref, scratch[:5])
@@ -1073,29 +1113,16 @@
         links.copy(column, core_out.at[:, y], CORE),
         links.copy(near_out.at[:, 1 - y], core_out.at[:, 1 - y], CORE),
     ]
-    enc_count = enc_ref.shape[0]
-
-    def place(distance):
-        return enc_out.at[pl.ds(pl.multiple_of((links.tensor ^ distance) * enc_count, enc_count), enc_count)]
-
-    enc_x = links.copy(enc_ref, place(0), X)
-    enc_core = [links.copy(enc_ref, place(0), CORE), links.copy(place(2), place(2), CORE)]
-    enc_own = links.local(enc_ref, place(0))
     links.greet([CORE, X, Y] + z_ways(n))
-    enc_x.start()
     rows_sum.start()
     load.start()
     over_z.start()
     load.wait()
     over_y.start()
     own.start()
-    enc_own.start()
+    rows_sum.middle()
     spread.start()
-    rows_sum.middle()
     over_core[0].start()
-    enc_core[0].start()
-    enc_x.wait_recv()
-    enc_core[1].start()
     rows_sum.end()
 
     def norm(rows):
@@ -1107,39 +1134,37 @@
     by_rows(after_out.shape[0], 64, norm)
     over_y.wait_recv()
     over_core[1].start()
-    enc_x.wait_send()
     over_y.wait_send()
     spread.end()
     over_z.wait()
-    for copy in [own, enc_own] + over_core + enc_core:
+    for copy in [own] + over_core:
         copy.wait()
 
 
-def sum_after_self(terms, rows, biases, norm, column, encoder, down, from_z):
+def sum_after_self(terms, rows, biases, norm, column, down, from_z):
     count, model = rows.shape
     m, r, c = column.shape
     vmem = pl.BlockSpec(memory_space=pltpu.VMEM)
     return pl.pallas_call(
         functools.partial(after_self_kernel, n=2 * m),
-        in_specs=[ANY, vmem, vmem, vmem, ANY, vmem, ANY, ANY],
-        out_specs=[vmem, vmem, ANY, ANY, ANY, ANY],
+        in_specs=[ANY, vmem, vmem, vmem, ANY, ANY, ANY],
+        out_specs=[vmem, vmem, ANY, ANY, ANY],
         out_shape=[
             jax.ShapeDtypeStruct((count, model), F32),
             jax.ShapeDtypeStruct((count, model), BF16),
             jax.ShapeDtypeStruct((2, m, 2, r, c), BF16),
-            jax.ShapeDtypeStruct((4 * encoder.shape[0], model), BF16),
             jax.ShapeDtypeStruct((2, m, 2, r, c), BF16),
             jax.ShapeDtypeStruct((2, r, c), BF16),
         ],
         scratch_shapes=row_sum_scratch(count, model)
         + [pltpu.VMEM((m, r, c), BF16), pltpu.VMEM((2, 2, r, c), BF16)]
-        + link_scratch(10 + spread_z_copies(2 * m), 9),
+        + link_scratch(7 + spread_z_copies(2 * m), 8),
         compiler_params=pltpu.CompilerParams(
             vmem_limit_bytes=VMEM_LIMIT, collective_id=8, has_side_effects=True
         ),
         cost_estimate=pl.CostEstimate(flops=0, bytes_accessed=100 * 2**20, transcendentals=0),
         name="sum_after_self",
-    )(terms, rows, biases, norm, column, encoder, down, from_z)
+    )(terms, rows, biases, norm, column, down, from_z)
 
 
 def self_backward_kernel(
@@ -1219,7 +1244,12 @@
         arrive(0)
         pl.when(x == 1)(functools.partial(arrive, 1))
         cross.second()
-        enc.middle()
+
+        @pl.when(x == 1)
+        def _():
+            cross.middle()
+            enc.middle()
+
         for step in range(stages - 1):
             for total in sums_z:
                 total.finish(step)
@@ -1228,8 +1258,12 @@
 
     @pl.when(s == 3)
     def _():
-        pl.when(x == 0)(functools.partial(arrive, 1))
-        cross.middle()
+        @pl.when(x == 0)
+        def _():
+            arrive(1)
+            cross.middle()
+            enc.middle()
+
         keep_wide.start()
 
     width = k_ref.shape[1]
@@ -1402,7 +1436,7 @@
         for step, k in when:
             pl.when(i == step)(functools.partial(spread.onward, k))
 
-    onward((1, 0), (1, 1), (2, 3), (3, 5))
+    onward((1, 0), (1, 1), (2, 4), (3, 6), (3, 7))
 
     width = q_out.shape[2]
     hd = width // heads
@@ -1429,7 +1463,12 @@
         ot_ref[0, part, :] = mixed[h]
         lse_ref[0, h : h + 1, :] = largest + jnp.log(total)
         if h == heads // 2 - 1:
-            onward((1, 2), (2, 4), (3, 6))
+            onward((1, 2), (1, 3), (2, 5))
+
+            @pl.when(i == last)
+            def _():
+                for k in range(pieces // 2):
+                    spread.last(k)
     after_ref[...] += dot_nt(jnp.concatenate(mixed, 0).T, w_ref[0, :, 3 * width :])
 
     @pl.when(i == last)
@@ -1439,9 +1478,7 @@
             third_ref[rows, :] = (xhat * norm_ref[2, 0:1, :] + norm_ref[2, 1:2, :]).astype(BF16)
 
         by_rows(after_ref.shape[0], 128, norm)
-        for k in range(7, pieces):
-            spread.onward(k)
-        for k in range(pieces):
+        for k in range(pieces // 2, pieces):
             spread.last(k)
         spread_z.end()
         spread.end()
@@ -1905,7 +1942,7 @@
     own_rows, model_width = block_in.shape
     w_rows = w_cross_q.shape[0]
 
-    first_in, self_w, cross_column, down_square = start_gather(
+    first_in, self_w, cross_column, down_square, enc_all = start_gather(
         block_in,
         norm_params,
         w_qkv,
@@ -1914,6 +1951,7 @@
         w_cross_kv,
         w_cross_out,
         w_down,
+        encoder_out,
     )
     self_w = self_w.reshape(model_width, 4 * width)
 
@@ -1930,8 +1968,8 @@
         self_safe,
     )
     cross_w = cross_w.reshape(4, model_width, 4 * width)
-    after_self, second_in, near_up, enc_all, near_down, far_z = sum_after_self(
-        terms, block_in, biases, norm_params, up_column, encoder_out, down_square, near_z
+    after_self, second_in, near_up, near_down, far_z = sum_after_self(
+        terms, block_in, biases, norm_params, up_column, down_square, near_z
     )
 
     cross_q, cross_k, cross_v, cross_mixed_t, cross_lse, after_cross, third_in, far_up, far_down = cross_forward(

time: 493 us -> 488 us (0.990)
    pallas_call x1, Pallas kernels: 52.3 us -> 46.1 us  [sum_after_self(): pl.pallas_call(functools.partial(after_self_kernel, n=2 * m), in_specs=[A...]
where the time goes in v14:
time: 488 us; the launch traced here: 482 us
  Pallas kernels  477 us (98%)
    pallas_call x1, Pallas kernels, self_backward(): pl.pallas_call(functools.partial(self_backward_kernel, bq=bq, heads=heads...  84.6 us
    pallas_call x1, Pallas kernels, tail(): pl.pallas_call(functools.partial(tail_kernel, n=n, step_rows=512), in_spe...  74.4 us
    pallas_call x1, Pallas kernels, cross_backward(): pl.pallas_call(functools.partial(cross_backward_kernel, heads=heads, bk=2...  60 us
    pallas_call x1, Pallas kernels, start_gather(): pl.pallas_call(functools.partial(start_kernel, n=n), in_specs=[pl.BlockSp...  58.3 us
    pallas_call x1, Pallas kernels, feed_forward(): pl.pallas_call(functools.partial(feed_forward_kernel, chunks=chunks), gri...  53.3 us
    pallas_call x1, Pallas kernels, self_forward(): pl.pallas_call(functools.partial(self_forward_kernel, heads=heads, safe=s...  48.6 us
    pallas_call x1, Pallas kernels, sum_after_self(): pl.pallas_call(functools.partial(after_self_kernel, n=2 * m), in_specs=[A...  46.1 us
    pallas_call x1, Pallas kernels, cross_forward(): pl.pallas_call(functools.partial(cross_forward_kernel, heads=heads, n=2 *...  43.4 us

profile of v14, /device:TPU:0, one launch (start us, length us, event | category | flops | bytes accessed | tf_op | source)
XLA Modules:
  0.0 481.9 jit_solution(12807620086370855140)
XLA Ops:
  1.3 1.8 copy.28.qkv_ref
  3.1 58.3 %start_gather.1 = (bf16[2560,1024]{1,0:T(8,128)(2,1)}, bf16[4,2,128,1024]{3,2,1,0:T(8,128)(2,1)}, bf16[4,128,1024]{2,1,0:T(8,128)(2,1)}, bf16[2,2,128,1024]{3,2,1,0:T(8,128)(2,1)}, bf16[1024,1024]{1,0:T(8,128)(2,1)}) custom-call(bf16[640,1024]{1,0:T(8,128)(2,1)} %rows_hbm.1, f32[3,2,1024]{2,1,0:T(2,128)} %norm_ref.11, bf16[128,3,256]{2,1,0:T(4,128)(2,1)} %copy.28.qkv_ref, ...), custom_call_target="tpu_custom_call" | custom-call | bytes 104857600 | tf_op jit(solution)/shard_map/start_gather/pallas_call | solution.py:920
  61.4 48.6 %self_forward.1 = (bf16[2560,256]{1,0:T(8,128)(2,1)}, bf16[2560,256]{1,0:T(8,128)(2,1)}, bf16[2560,256]{1,0:T(8,128)(2,1)}, bf16[256,2560]{1,0:T(8,128)(2,1)}, b...) custom-call(s32[1,2]{1,0:T(1,128)} %b_ref.3, ...), custom_call_target="tpu_custom_call" | custom-call | flops 20132659200 | bytes 5242880 | tf_op jit(solution)/shard_map/self_forward/pallas_call | solution.py:1044
  110.1 46.1 %sum_after_self.1 = (f32[640,1024]{1,0:T(8,128)}, bf16[640,1024]{1,0:T(8,128)(2,1)}, bf16[2,4,2,128,1024]{4,3,2,1,0:T(8,128)(2,1)}, bf16[2,4,2,128,1024]{4,3,2,1,0:T(8,128)(2,1)}, bf16[2,128,1024]{2,1,0:T(8,128)(2,1)}) custom-call(bf16[2560,1024]{1,0:T(8,128)(2,1)} %get-tuple-element.89.terms_ref, bf16[640,1024]{1,0:T(8,128)(2,1)} %rows_hbm.1, ...), custom_call_target="tpu_custom_call" | custom-call | bytes 104857600 | tf_op jit(solution)/shard_map/sum_after_self/pallas_call | solution.py:1148
  156.2 43.4 %cross_forward.1 = (bf16[4,640,256]{2,1,0:T(8,128)(2,1)}, bf16[4,1024,256]{2,1,0:T(8,128)(2,1)}, bf16[4,1024,256]{2,1,0:T(8,128)(2,1)}, bf16[4,256,640]{2,1,0:T(...) custom-call(s32[1]{0:T(128)S(6)} %copy.30.len_ref, ...), custom_call_target="tpu_custom_call" | custom-call | flops 16106127360 | bytes 8388608 | tf_op jit(solution)/shard_map/cross_forward/pallas_call | solution.py:1497
  199.6 53.3 %feed_forward.1 = (f32[640,1024]{1,0:T(8,128)}, f32[640,1024]{1,0:T(8,128)}, bf16[640,1024]{1,0:T(8,128)(2,1)}, f32[8,1024]{1,0:T(8,128)}, bf16[2,1024,1024]{2,1...) custom-call(bf16[640,1024]{1,0:T(8,128)(2,1)} %get-tuple-element.97., ...), custom_call_target="tpu_custom_call" | custom-call | flops 32212254720 | bytes 41943040 | tf_op jit(solution)/shard_map/feed_forward/pallas_call | solution.py:1696
  253.0 60.0 %cross_backward.1 = (f32[640,1024]{1,0:T(8,128)}, bf16[1024,1024]{1,0:T(8,128)(2,1)}, bf16[2,1024,1024]{2,1,0:T(8,128)(2,1)}, f32[4,1,256]{2,1,0:T(1,128)}, f32[...) custom-call(s32[1]{0:T(128)S(6)} %copy.30.len_ref, ...), custom_call_target="tpu_custom_call" | custom-call | flops 32212254720 | bytes 16777216 | tf_op jit(solution)/shard_map/cross_backward/pallas_call | solution.py:1862
  313.0 84.6 %self_backward.1 = (bf16[2560,256]{1,0:T(8,128)(2,1)}, bf16[2560,256]{1,0:T(8,128)(2,1)}, bf16[2560,256]{1,0:T(8,128)(2,1)}, bf16[2560,1024]{1,0:T(8,128)(2,1)},...) custom-call(s32[1,2]{1,0:T(1,128)} %b_ref.3, ...), custom_call_target="tpu_custom_call" | custom-call | flops 40265318400 | bytes 10485760 | tf_op jit(solution)/shard_map/self_backward/pallas_call | solution.py:1339
  397.6 74.4 %tail.1 = (f32[640,1024]{1,0:T(8,128)}, f32[128,1024]{1,0:T(8,128)}, f32[18,1024]{1,0:T(8,128)}, f32[128,1024]{1,0:T(8,128)}) custom-call(bf16[2560,256]{1,0:T(8,128)(2,1)} %get-tuple-element.126.dq_ref, bf16[2560,256]{1,0:T(8,128)(2,1)} %get-tuple-element.127.dk_ref, bf16[2560,256]{1,0:T(8,128)(2,1)} %get-tuple-element.128.dv_ref, ...), custom_call_target="tpu_custom_call" | custom-call | bytes 104857600 | tf_op jit(solution)/shard_map/tail/pallas_call | solution.py:735
  472.0 7.9 %results.1 = (f32[640,1024]{1,0:T(8,128)}, f32[640,1024]{1,0:T(8,128)}, f32[256,1024]{1,0:T(8,128)}, f32[128,3,256]{2,1,0:T(4,128)}, f32[256,128]{1,0:T(8,128)},...) custom-call(f32[640,1024]{1,0:T(8,128)} %get-tuple-element.103.outpu, ...), custom_call_target="tpu_custom_call" | custom-call | bytes 20971520 | tf_op jit(solution)/shard_map/results/pallas_call | solution.py:809
  479.9 1.9 copy.29

commit v15 on v14

--- a/solution.py
+++ b/solution.py
@@ -458,7 +458,7 @@
 
         self.loads = [links.local(rows(0), self.near), links.local(rows(2), self.far)]
         self.core = [links.copy(rows(3), self.got_far, CORE), links.copy(rows(1), self.got_near, CORE)]
-        self.over_x = links.copy(self.far, self.got_x, X)
+        self.over_x = None if self.got_x is None else links.copy(self.far, self.got_x, X)
 
     def start(self):
         for copy in self.loads[::-1] + self.core:
@@ -473,6 +473,10 @@
 
         by_rows(self.far.shape[0], 64, add)
         self.over_x.start()
+
+    def core_end(self):
+        for copy in self.loads + self.core:
+            copy.wait()
 
     def end(self):
         self.loads[0].wait()
@@ -541,8 +545,8 @@
 
 def tail_kernel(
     dq_ref, dk_ref, dv_ref, w_ref, first_hbm, wide_hbm, mt_hbm, rows_hbm, grad_hbm, cross_hbm, norm_ref,
-    self_ref, ffn_ref, cq_ref, cv_ref, up_ref,
-    grad_out, weights_out, late_out, cross_out, give, acc, weights,
+    self_ref, ffn_ref, cq_ref, cv_ref, up_ref, enc_near, enc_far,
+    grad_out, weights_out, late_out, cross_out, enc_out, enc_got, give, acc, weights,
     first_ref, wide_ref, mt_ref, rows_ref, grad_ref, cross_ref, cross_slots, *scratch, n, step_rows
 ):
     links = Links(*scratch[-3:])
@@ -578,7 +582,9 @@
     late = Direct(links, compact, late_tensor, late_dp, n)
     early = Everywhere(links, sums, early_slots, [CORE] + z_ways(n) + [Y, X])
     steps = len(early.copies)
+    enc_x = links.copy(enc_far, enc_got, X)
     links.greet(direct_ways(n))
+    enc_x.start()
 
     def terms(distance, target):
         base = (member ^ distance) * count
@@ -630,17 +636,6 @@
 
     def products_out(rows):
         acc[:, 3 * width :] += dot_nn(wide_ref[rows, :].T, mt_ref[:, rows].T)
-
-    by_rows(dq_ref.shape[0], step_rows, products((dv_ref,), 2))
-    by_rows(dq_ref.shape[0], step_rows, products_out)
-    packed(1)
-    over_y[1].start()
-    terms(1, give.at[1])
-    core_near.start()
-    terms(0, near)
-    for step in range(stages - 1):
-        cross.finish(step)
-        cross.start(step + 1)
 
     held[...] = jnp.zeros_like(held)
     sums[0] = jnp.zeros(sums.shape[1:], F32)
@@ -687,30 +682,44 @@
         collects[k].finish(stages - 1)
         weights_out[:, k * c : (k + 1) * c] = columns[k][collects[k].z].astype(F32)
 
+    for step in range(stages - 1):
+        cross.finish(step)
+        cross.start(step + 1)
+    by_rows(dq_ref.shape[0], step_rows, products((dv_ref,), 2))
+    by_rows(dq_ref.shape[0], step_rows, products_out)
+    packed(1)
+    over_y[1].start()
     summed_y(0)
     early.finish(0)
-    cross.finish(stages - 1)
-    cross_out[...] = cross_ref[cross.z].astype(F32)
+    terms(1, give.at[1])
+    core_near.start()
+    terms(0, near)
+    enc_x.wait_recv()
+    enc_out[...] = enc_near[...] + enc_got[...].astype(F32)
     core_near.wait_recv()
     over_x[0].wait_recv()
     norm_back(parts[0])
+    cross.finish(stages - 1)
+    cross_out[...] = cross_ref[cross.z].astype(F32)
     next_z(0)
     summed_y(1)
-    for step in range(1, steps - 1):
+    for step in range(1, steps - 2):
         early.start(step)
         early.finish(step)
-    next_z(1)
-    last_z(0)
     over_x[1].wait_recv()
     norm_back(parts[1])
+    next_z(1)
     lines = model // LANES
     for k in range(2 * lines):
         compact[k : k + 1, :] = held[k // lines : k // lines + 1, k % lines * LANES : (k % lines + 1) * LANES]
     late.start(0)
+    early.start(steps - 2)
+    last_z(0)
+    early.finish(steps - 2)
+    late.finish(0)
+    late.start(1)
     early.start(steps - 1)
     last_z(1)
-    late.finish(0)
-    late.start(1)
     early.finish(steps - 1)
     late_out[2:, :] = sums[steps]
     late.finish(1)
@@ -720,10 +729,12 @@
         copy.wait_send()
     for collect in collects + [cross]:
         collect.drain()
+    enc_x.wait_send()
 
 
 def tail(
-    dq, dk, dv, w, first, wide, mixed_t, rows, grad, cross_column, norm, self_sums, ffn_sums, cq_sums, cv_sums, up_sums
+    dq, dk, dv, w, first, wide, mixed_t, rows, grad, cross_column, norm, self_sums, ffn_sums, cq_sums, cv_sums, up_sums,
+    enc_near, enc_far,
 ):
     n = lax.axis_size("dp")
     count, model = rows.shape
@@ -734,15 +745,17 @@
     part = pltpu.VMEM((m, r, c // 2), BF16)
     return pl.pallas_call(
         functools.partial(tail_kernel, n=n, step_rows=512),
-        in_specs=[vmem] * 4 + [ANY] * 6 + [vmem] * 6,
-        out_specs=[vmem] * 4,
+        in_specs=[vmem] * 4 + [ANY] * 6 + [vmem] * 8,
+        out_specs=[vmem] * 5,
         out_shape=[
             jax.ShapeDtypeStruct((count, model), F32),
             jax.ShapeDtypeStruct((r, c), F32),
             jax.ShapeDtypeStruct((vectors[0] + 2, model), F32),
             jax.ShapeDtypeStruct(cross_column.shape[1:], F32),
+            jax.ShapeDtypeStruct(enc_near.shape, F32),
         ],
         scratch_shapes=[
+            pltpu.VMEM(enc_far.shape, BF16),
             pltpu.VMEM((2, count, model), BF16),
             pltpu.VMEM((model, c), F32),
             pltpu.VMEM((m, 2, r, c), BF16),
@@ -753,7 +766,7 @@
         + [pltpu.VMEM((size, 2 * model // LANES, LANES), F32) for size in (4, n)]
         + everywhere_scratch(*vectors, n)
         + [pltpu.VMEM((8, model), F32), pltpu.VMEM((2 * model // LANES, LANES), F32)]
-        + link_scratch(6 + 3 * m + len(everywhere_ways(n)) + len(direct_ways(n)), 6),
+        + link_scratch(7 + 3 * m + len(everywhere_ways(n)) + len(direct_ways(n)), 6),
         compiler_params=pltpu.CompilerParams(
             vmem_limit_bytes=VMEM_LIMIT, collective_id=7, has_side_effects=True
         ),
@@ -761,7 +774,7 @@
         name="tail",
     )(
         dq, dk, dv, w, first, wide, mixed_t, rows, grad, cross_column, norm,
-        self_sums, ffn_sums, cq_sums, cv_sums, up_sums,
+        self_sums, ffn_sums, cq_sums, cv_sums, up_sums, enc_near, enc_far,
     )
 
 
@@ -1170,7 +1183,7 @@
 def self_backward_kernel(
     b_ref, q_ref, k_ref, v_ref, kt_ref, w_ref, mt_ref, lse_ref, back_ref, rows_ref, above_ref, norm_ref,
     up_ref, down_ref, cross_ref, enc_ref,
-    dq_ref, dk_ref, dv_ref, wide_out, grad_out, sums_ref, up_out, down_out, cross_out, enc_out,
+    dq_ref, dk_ref, dv_ref, wide_out, grad_out, sums_ref, up_out, down_out, cross_out, enc_near, enc_far,
     dka, dva, dqa, wide, *scratch, bq, heads, safe, n
 ):
     s = pl.program_id(0)
@@ -1185,7 +1198,7 @@
     columns, slots = scratch[5:7], scratch[7:9]
     sums_z = [Collect(links, column, slot) for column, slot in zip(columns, slots)]
     load_z = [links.local(ref, column) for ref, column in zip((up_ref, down_ref), columns)]
-    enc = RowSum(links, enc_ref, scratch[9:14])
+    enc = RowSum(links, enc_ref, list(scratch[9:13]) + [None])
     stages = len(sums_z[0].stages)
     count = grad_out.shape[0]
     half = count // 2
@@ -1243,13 +1256,7 @@
     def _():
         arrive(0)
         pl.when(x == 1)(functools.partial(arrive, 1))
-        cross.second()
-
-        @pl.when(x == 1)
-        def _():
-            cross.middle()
-            enc.middle()
-
+        pl.when(x == 0)(cross.second)
         for step in range(stages - 1):
             for total in sums_z:
                 total.finish(step)
@@ -1262,9 +1269,14 @@
         def _():
             arrive(1)
             cross.middle()
-            enc.middle()
 
         keep_wide.start()
+
+    def cross_sums():
+        @pl.when(x == 1)
+        def _():
+            cross.second()
+            cross.middle()
 
     width = k_ref.shape[1]
     hd = width // heads
@@ -1300,7 +1312,7 @@
             dva[rows, part] += dv_sums[group]
             dka[rows, part] += dk_sums[group]
 
-    over_keys(i, bq, safe, block)
+    over_keys(i, bq, safe, block, [(4, 3, cross_sums)])
     dq_ref[here, :] = (dqa[...] * scale).astype(BF16).T
 
     @pl.when(s == last)
@@ -1313,12 +1325,13 @@
             total.finish(stages - 1)
             out[...] = total.column[total.z].astype(F32)
             total.drain()
-        enc.end()
+        enc.core_end()
 
         def store(rows):
-            enc_out[rows, :] = enc.total(rows)
-
-        by_rows(enc_out.shape[0], 64, store)
+            enc_near[rows, :] = enc.near[rows, :].astype(F32) + enc.got_near[rows, :].astype(F32)
+            enc_far[rows, :] = (enc.far[rows, :].astype(F32) + enc.got_far[rows, :].astype(F32)).astype(BF16)
+
+        by_rows(enc_near.shape[0], 64, store)
         for copy in over_x + onward + [over_core]:
             copy.wait_send()
         keep_wide.wait()
@@ -1355,7 +1368,8 @@
         ]
         + [ANY] * 4,
         out_specs=[const((n, width))] * 3
-        + [ANY, const((count, model)), const((8, model)), const((r, c)), const((r, c)), ANY, const(enc_shape)],
+        + [ANY, const((count, model)), const((8, model)), const((r, c)), const((r, c)), ANY]
+        + [const(enc_shape)] * 2,
         out_shape=[jax.ShapeDtypeStruct((n, width), BF16)] * 3
         + [
             jax.ShapeDtypeStruct((n, model), BF16),
@@ -1365,6 +1379,7 @@
             jax.ShapeDtypeStruct((r, c), F32),
             jax.ShapeDtypeStruct((m, r, cross_c), BF16),
             jax.ShapeDtypeStruct(enc_shape, F32),
+            jax.ShapeDtypeStruct(enc_shape, BF16),
         ],
         scratch_shapes=[
             pltpu.VMEM((n, width), F32),
@@ -1374,7 +1389,7 @@
         ]
         + [pltpu.VMEM((m, r, cross_c), BF16)] * 5
         + [pltpu.VMEM((m, r, c), BF16)] * 4
-        + row_sum_scratch(*enc_shape)
+        + row_sum_scratch(*enc_shape)[:4]
         + link_scratch(11 + 2 * m, 8),
         compiler_params=pltpu.CompilerParams(
             vmem_limit_bytes=62 * 2**20, collective_id=5, has_side_effects=True
@@ -2018,7 +2033,7 @@
 
     (
         self_dq, self_dk, self_dv, self_wide, self_rows_grad, self_sums,
-        summed_up, summed_down, cross_column, encoder_grad,
+        summed_up, summed_down, cross_column, enc_near, enc_far,
     ) = self_backward(
         bounds,
         queries,
@@ -2039,7 +2054,7 @@
         heads,
         self_safe,
     )
-    input_grad, summed_self, vectors, summed_cross = tail(
+    input_grad, summed_self, vectors, summed_cross, encoder_grad = tail(
         self_dq,
         self_dk,
         self_dv,
@@ -2056,6 +2071,8 @@
         bias_cq_parts,
         bias_cv_parts,
         bias_up_parts,
+        enc_near,
+        enc_far,
     )
     output, input_grad, encoder_grad, *weights_and_vectors = results(
         output, input_grad, encoder_grad, summed_self, summed_cross, summed_up, summed_down, vectors, 1.0 / groups_count

time: 488 us -> 476 us (0.975)
  Pallas kernels: 477 us -> 464 us
    pallas_call x1, Pallas kernels: 84.6 us -> 75.7 us  [self_backward(): pl.pallas_call(functools.partial(self_backward_kernel, bq=bq, heads=heads...]
where the time goes in v15:
time: 476 us; the launch traced here: 469 us
  Pallas kernels  464 us (97%)
    pallas_call x1, Pallas kernels, self_backward(): pl.pallas_call(functools.partial(self_backward_kernel, bq=bq, heads=heads...  75.7 us
    pallas_call x1, Pallas kernels, tail(): pl.pallas_call(functools.partial(tail_kernel, n=n, step_rows=512), in_spe...  70.8 us
    pallas_call x1, Pallas kernels, cross_backward(): pl.pallas_call(functools.partial(cross_backward_kernel, heads=heads, bk=2...  60 us
    pallas_call x1, Pallas kernels, start_gather(): pl.pallas_call(functools.partial(start_kernel, n=n), in_specs=[pl.BlockSp...  58.3 us
    pallas_call x1, Pallas kernels, feed_forward(): pl.pallas_call(functools.partial(feed_forward_kernel, chunks=chunks), gri...  53.3 us
    pallas_call x1, Pallas kernels, self_forward(): pl.pallas_call(functools.partial(self_forward_kernel, heads=heads, safe=s...  48.6 us
    pallas_call x1, Pallas kernels, sum_after_self(): pl.pallas_call(functools.partial(after_self_kernel, n=2 * m), in_specs=[A...  46.1 us
    pallas_call x1, Pallas kernels, cross_forward(): pl.pallas_call(functools.partial(cross_forward_kernel, heads=heads, n=2 *...  43.4 us

profile of v15, /device:TPU:0, one launch (start us, length us, event | category | flops | bytes accessed | tf_op | source)
XLA Modules:
  0.0 469.5 jit_solution(6875360711040483099)
XLA Ops:
  1.3 1.8 copy.28.qkv_ref
  3.1 58.3 %start_gather.1 = (bf16[2560,1024]{1,0:T(8,128)(2,1)}, bf16[4,2,128,1024]{3,2,1,0:T(8,128)(2,1)}, bf16[4,128,1024]{2,1,0:T(8,128)(2,1)}, bf16[2,2,128,1024]{3,2,1,0:T(8,128)(2,1)}, bf16[1024,1024]{1,0:T(8,128)(2,1)}) custom-call(bf16[640,1024]{1,0:T(8,128)(2,1)} %rows_hbm.1, f32[3,2,1024]{2,1,0:T(2,128)} %norm_ref.11, bf16[128,3,256]{2,1,0:T(4,128)(2,1)} %copy.28.qkv_ref, ...), custom_call_target="tpu_custom_call" | custom-call | bytes 104857600 | tf_op jit(solution)/shard_map/start_gather/pallas_call | solution.py:933
  61.4 48.6 %self_forward.1 = (bf16[2560,256]{1,0:T(8,128)(2,1)}, bf16[2560,256]{1,0:T(8,128)(2,1)}, bf16[2560,256]{1,0:T(8,128)(2,1)}, bf16[256,2560]{1,0:T(8,128)(2,1)}, b...) custom-call(s32[1,2]{1,0:T(1,128)} %b_ref.3, ...), custom_call_target="tpu_custom_call" | custom-call | flops 20132659200 | bytes 5242880 | tf_op jit(solution)/shard_map/self_forward/pallas_call | solution.py:1057
  110.1 46.1 %sum_after_self.1 = (f32[640,1024]{1,0:T(8,128)}, bf16[640,1024]{1,0:T(8,128)(2,1)}, bf16[2,4,2,128,1024]{4,3,2,1,0:T(8,128)(2,1)}, bf16[2,4,2,128,1024]{4,3,2,1,0:T(8,128)(2,1)}, bf16[2,128,1024]{2,1,0:T(8,128)(2,1)}) custom-call(bf16[2560,1024]{1,0:T(8,128)(2,1)} %get-tuple-element.91.terms_ref, bf16[640,1024]{1,0:T(8,128)(2,1)} %rows_hbm.1, ...), custom_call_target="tpu_custom_call" | custom-call | bytes 104857600 | tf_op jit(solution)/shard_map/sum_after_self/pallas_call | solution.py:1161
  156.2 43.4 %cross_forward.1 = (bf16[4,640,256]{2,1,0:T(8,128)(2,1)}, bf16[4,1024,256]{2,1,0:T(8,128)(2,1)}, bf16[4,1024,256]{2,1,0:T(8,128)(2,1)}, bf16[4,256,640]{2,1,0:T(...) custom-call(s32[1]{0:T(128)S(6)} %copy.30.len_ref, ...), custom_call_target="tpu_custom_call" | custom-call | flops 16106127360 | bytes 8388608 | tf_op jit(solution)/shard_map/cross_forward/pallas_call | solution.py:1512
  199.6 53.3 %feed_forward.1 = (f32[640,1024]{1,0:T(8,128)}, f32[640,1024]{1,0:T(8,128)}, bf16[640,1024]{1,0:T(8,128)(2,1)}, f32[8,1024]{1,0:T(8,128)}, bf16[2,1024,1024]{2,1...) custom-call(bf16[640,1024]{1,0:T(8,128)(2,1)} %get-tuple-element.99., ...), custom_call_target="tpu_custom_call" | custom-call | flops 32212254720 | bytes 41943040 | tf_op jit(solution)/shard_map/feed_forward/pallas_call | solution.py:1711
  253.0 60.0 %cross_backward.1 = (f32[640,1024]{1,0:T(8,128)}, bf16[1024,1024]{1,0:T(8,128)(2,1)}, bf16[2,1024,1024]{2,1,0:T(8,128)(2,1)}, f32[4,1,256]{2,1,0:T(1,128)}, f32[...) custom-call(s32[1]{0:T(128)S(6)} %copy.30.len_ref, ...), custom_call_target="tpu_custom_call" | custom-call | flops 32212254720 | bytes 16777216 | tf_op jit(solution)/shard_map/cross_backward/pallas_call | solution.py:1877
  313.0 75.7 %self_backward.1 = (bf16[2560,256]{1,0:T(8,128)(2,1)}, bf16[2560,256]{1,0:T(8,128)(2,1)}, bf16[2560,256]{1,0:T(8,128)(2,1)}, bf16[2560,1024]{1,0:T(8,128)(2,1)},...) custom-call(s32[1,2]{1,0:T(1,128)} %b_ref.3, ...), custom_call_target="tpu_custom_call" | custom-call | flops 40265318400 | bytes 10485760 | tf_op jit(solution)/shard_map/self_backward/pallas_call | solution.py:1352
  388.7 70.8 %tail.1 = (f32[640,1024]{1,0:T(8,128)}, f32[128,1024]{1,0:T(8,128)}, f32[18,1024]{1,0:T(8,128)}, f32[128,1024]{1,0:T(8,128)}, f32[256,1024]{1,0:T(8,128)}) custom-call(bf16[2560,256]{1,0:T(8,128)(2,1)} %get-tuple-element.128.dq_ref, bf16[2560,256]{1,0:T(8,128)(2,1)} %get-tuple-element.129.dk_ref, bf16[2560,256]{1,0:T(8,128)(2,1)} %get-tuple-element.130.dv_ref, ...), custom_call_target="tpu_custom_call" | custom-call | bytes 104857600 | tf_op jit(solution)/shard_map/tail/pallas_call | solution.py:746
  459.5 7.9 %results.1 = (f32[640,1024]{1,0:T(8,128)}, f32[640,1024]{1,0:T(8,128)}, f32[256,1024]{1,0:T(8,128)}, f32[128,3,256]{2,1,0:T(4,128)}, f32[256,128]{1,0:T(8,128)},...) custom-call(f32[640,1024]{1,0:T(8,128)} %get-tuple-element.105.outpu, ...), custom_call_target="tpu_custom_call" | custom-call | bytes 20971520 | tf_op jit(solution)/shard_map/results/pallas_call | solution.py:822
  467.4 1.9 copy.29

commit v16 on v15

--- a/solution.py
+++ b/solution.py
@@ -390,13 +390,15 @@
         for copy in self.stages[0] + self.stores + self.core:
             copy.start()
 
-    def end(self):
+    def onward(self):
         for step, (stage, core_stage) in enumerate(zip(self.stages, self.core_stages)):
             for copy, onward in zip(stage, core_stage):
                 copy.wait_recv()
                 onward.start()
             for copy in self.stages[step + 1] if step + 1 < len(self.stages) else []:
                 copy.start()
+
+    def end(self):
         for copy in self.stores + self.core:
             copy.wait()
         for stage, core_stage in zip(self.stages, self.core_stages):
@@ -812,7 +814,7 @@
 def results(output, grad, encoder, self_w, cross_w, up, down, vectors, scale):
     r, c = self_w.shape
     width = c // 4
-    steps = 4
+    steps = 2
 
     def rows(value):
         return pl.BlockSpec((value.shape[0] // steps, value.shape[1]), lambda i: (i, 0))
@@ -1136,7 +1138,10 @@
     rows_sum.middle()
     spread.start()
     over_core[0].start()
+    over_y.wait_recv()
+    over_core[1].start()
     rows_sum.end()
+    spread.onward()
 
     def norm(rows):
         after = rows_ref[rows, :].astype(F32) + rows_sum.total(rows) + biases_ref[2:3, :]
@@ -1145,8 +1150,6 @@
         second_out[rows, :] = (xhat * norm_ref[1, 0:1, :] + norm_ref[1, 1:2, :]).astype(BF16)
 
     by_rows(after_out.shape[0], 64, norm)
-    over_y.wait_recv()
-    over_core[1].start()
     over_y.wait_send()
     spread.end()
     over_z.wait()
@@ -1190,7 +1193,8 @@
     last = pl.num_programs(0) - 1
     links = Links(*scratch[-3:])
     member = links.tensor
-    x = member // 2
+    x, core = member // 2, member % 2
+    second_core = (x == 1) & (core == 1)
     later = (s // 2 + 1) // 2
     i = s * (1 - x) + ((s + 3) * (1 - later) + (4 - s) * later) * x
     cross = GatherLast(links, cross_ref.at[0], cross_ref.at[1], scratch[:5])
@@ -1241,7 +1245,7 @@
         sums_ref[...] = jnp.zeros_like(sums_ref)
         for k in range(2):
             norm_back(k)
-            over_x[k].start()
+            pl.when(jnp.logical_not(second_core))(over_x[k].start)
         over_core.start()
         cross.start()
         enc.start()
@@ -1252,25 +1256,66 @@
         dva[...] = jnp.zeros_like(dva)
         over_core.wait_recv()
 
-    @pl.when(s == 2)
-    def _():
-        arrive(0)
-        pl.when(x == 1)(functools.partial(arrive, 1))
-        pl.when(x == 0)(cross.second)
+    def next_z():
         for step in range(stages - 1):
             for total in sums_z:
                 total.finish(step)
             for total in sums_z:
                 total.start(step + 1)
 
-    @pl.when(s == 3)
-    def _():
-        @pl.when(x == 0)
+    @pl.when((s == 2) & (x == 0) & (core == 0))
+    def _():
+        over_x[0].wait_recv()
+        onward[0].start()
+
+    @pl.when((s == 2) & (x == 0) & (core == 1))
+    def _():
+        onward[0].wait_recv()
+
+    @pl.when((s == 2) & (x == 1))
+    def _():
+        arrive(0)
+        arrive(1)
+
+    @pl.when((s == 3) & (x == 0) & (core == 0))
+    def _():
+        over_x[1].wait_recv()
+        onward[1].start()
+        onward[0].wait_recv()
+
+    @pl.when((s == 3) & (x == 0) & (core == 1))
+    def _():
+        over_x[0].wait_recv()
+        onward[0].start()
+        onward[1].wait_recv()
+
+    @pl.when((s == 3) & (x == 0))
+    def _():
+        cross.second()
+        cross.middle()
+        next_z()
+
+    @pl.when((s == 4) & (x == 0) & (core == 0))
+    def _():
+        onward[1].wait_recv()
+
+    @pl.when((s == 4) & (x == 0) & (core == 1))
+    def _():
+        over_x[1].wait_recv()
+        onward[1].start()
+
+    @pl.when(s == 4)
+    def _():
+        keep_wide.start()
+
+    def send_second():
+        @pl.when(second_core)
         def _():
-            arrive(1)
-            cross.middle()
-
-        keep_wide.start()
+            for copy in over_x:
+                copy.start()
+
+    def z_sums():
+        pl.when(x == 1)(next_z)
 
     def cross_sums():
         @pl.when(x == 1)
@@ -1312,7 +1357,7 @@
             dva[rows, part] += dv_sums[group]
             dka[rows, part] += dk_sums[group]
 
-    over_keys(i, bq, safe, block, [(4, 3, cross_sums)])
+    over_keys(i, bq, safe, block, [(3, 2, send_second), (4, 1, z_sums), (4, 3, cross_sums)])
     dq_ref[here, :] = (dqa[...] * scale).astype(BF16).T
 
     @pl.when(s == last)
@@ -1484,17 +1529,19 @@
             def _():
                 for k in range(pieces // 2):
                     spread.last(k)
+                spread_z.onward()
     after_ref[...] += dot_nt(jnp.concatenate(mixed, 0).T, w_ref[0, :, 3 * width :])
 
     @pl.when(i == last)
     def _():
+        for k in range(pieces // 2, pieces):
+            spread.last(k)
+
         def norm(rows):
             xhat, _ = normalized(after_ref[rows, :])
             third_ref[rows, :] = (xhat * norm_ref[2, 0:1, :] + norm_ref[2, 1:2, :]).astype(BF16)
 
         by_rows(after_ref.shape[0], 128, norm)
-        for k in range(pieces // 2, pieces):
-            spread.last(k)
         spread_z.end()
         spread.end()
 

time: 476 us -> 465 us (0.977)
  Pallas kernels: 464 us -> 453 us
    pallas_call x1, Pallas kernels: 75.7 us -> 69.8 us  [self_backward(): pl.pallas_call(functools.partial(self_backward_kernel, bq=bq, heads=heads...]
where the time goes in v16:
time: 465 us; the launch traced here: 458 us
  Pallas kernels  453 us (97%)
    pallas_call x1, Pallas kernels, self_backward(): pl.pallas_call(functools.partial(self_backward_kernel, bq=bq, heads=heads...  69.8 us
    pallas_call x1, Pallas kernels, tail(): pl.pallas_call(functools.partial(tail_kernel, n=n, step_rows=512), in_spe...  67.5 us
    pallas_call x1, Pallas kernels, cross_backward(): pl.pallas_call(functools.partial(cross_backward_kernel, heads=heads, bk=2...  60 us
    pallas_call x1, Pallas kernels, start_gather(): pl.pallas_call(functools.partial(start_kernel, n=n), in_specs=[pl.BlockSp...  58.3 us
    pallas_call x1, Pallas kernels, feed_forward(): pl.pallas_call(functools.partial(feed_forward_kernel, chunks=chunks), gri...  53.2 us
    pallas_call x1, Pallas kernels, self_forward(): pl.pallas_call(functools.partial(self_forward_kernel, heads=heads, safe=s...  48.6 us
    pallas_call x1, Pallas kernels, sum_after_self(): pl.pallas_call(functools.partial(after_self_kernel, n=2 * m), in_specs=[A...  46.7 us
    pallas_call x1, Pallas kernels, cross_forward(): pl.pallas_call(functools.partial(cross_forward_kernel, heads=heads, n=2 *...  41.7 us

profile of v16, /device:TPU:0, one launch (start us, length us, event | category | flops | bytes accessed | tf_op | source)
XLA Modules:
  0.0 458.1 jit_solution(6053993352886466001)
XLA Ops:
  1.3 1.8 copy.28.qkv_ref
  3.1 58.3 %start_gather.1 = (bf16[2560,1024]{1,0:T(8,128)(2,1)}, bf16[4,2,128,1024]{3,2,1,0:T(8,128)(2,1)}, bf16[4,128,1024]{2,1,0:T(8,128)(2,1)}, bf16[2,2,128,1024]{3,2,1,0:T(8,128)(2,1)}, bf16[1024,1024]{1,0:T(8,128)(2,1)}) custom-call(bf16[640,1024]{1,0:T(8,128)(2,1)} %rows_hbm.1, f32[3,2,1024]{2,1,0:T(2,128)} %norm_ref.11, bf16[128,3,256]{2,1,0:T(4,128)(2,1)} %copy.28.qkv_ref, ...), custom_call_target="tpu_custom_call" | custom-call | bytes 104857600 | tf_op jit(solution)/shard_map/start_gather/pallas_call | solution.py:935
  61.4 48.6 %self_forward.1 = (bf16[2560,256]{1,0:T(8,128)(2,1)}, bf16[2560,256]{1,0:T(8,128)(2,1)}, bf16[2560,256]{1,0:T(8,128)(2,1)}, bf16[256,2560]{1,0:T(8,128)(2,1)}, b...) custom-call(s32[1,2]{1,0:T(1,128)} %b_ref.3, ...), custom_call_target="tpu_custom_call" | custom-call | flops 20132659200 | bytes 5242880 | tf_op jit(solution)/shard_map/self_forward/pallas_call | solution.py:1059
  110.1 46.7 %sum_after_self.1 = (f32[640,1024]{1,0:T(8,128)}, bf16[640,1024]{1,0:T(8,128)(2,1)}, bf16[2,4,2,128,1024]{4,3,2,1,0:T(8,128)(2,1)}, bf16[2,4,2,128,1024]{4,3,2,1,0:T(8,128)(2,1)}, bf16[2,128,1024]{2,1,0:T(8,128)(2,1)}) custom-call(bf16[2560,1024]{1,0:T(8,128)(2,1)} %get-tuple-element.91.terms_ref, bf16[640,1024]{1,0:T(8,128)(2,1)} %rows_hbm.1, ...), custom_call_target="tpu_custom_call" | custom-call | bytes 104857600 | tf_op jit(solution)/shard_map/sum_after_self/pallas_call | solution.py:1164
  156.8 41.7 %cross_forward.1 = (bf16[4,640,256]{2,1,0:T(8,128)(2,1)}, bf16[4,1024,256]{2,1,0:T(8,128)(2,1)}, bf16[4,1024,256]{2,1,0:T(8,128)(2,1)}, bf16[4,256,640]{2,1,0:T(...) custom-call(s32[1]{0:T(128)S(6)} %copy.30.len_ref, ...), custom_call_target="tpu_custom_call" | custom-call | flops 16106127360 | bytes 8388608 | tf_op jit(solution)/shard_map/cross_forward/pallas_call | solution.py:1559
  198.5 53.2 %feed_forward.1 = (f32[640,1024]{1,0:T(8,128)}, f32[640,1024]{1,0:T(8,128)}, bf16[640,1024]{1,0:T(8,128)(2,1)}, f32[8,1024]{1,0:T(8,128)}, bf16[2,1024,1024]{2,1...) custom-call(bf16[640,1024]{1,0:T(8,128)(2,1)} %get-tuple-element.99., ...), custom_call_target="tpu_custom_call" | custom-call | flops 32212254720 | bytes 41943040 | tf_op jit(solution)/shard_map/feed_forward/pallas_call | solution.py:1758
  251.7 60.0 %cross_backward.1 = (f32[640,1024]{1,0:T(8,128)}, bf16[1024,1024]{1,0:T(8,128)(2,1)}, bf16[2,1024,1024]{2,1,0:T(8,128)(2,1)}, f32[4,1,256]{2,1,0:T(1,128)}, f32[...) custom-call(s32[1]{0:T(128)S(6)} %copy.30.len_ref, ...), custom_call_target="tpu_custom_call" | custom-call | flops 32212254720 | bytes 16777216 | tf_op jit(solution)/shard_map/cross_backward/pallas_call | solution.py:1924
  311.7 69.8 %self_backward.1 = (bf16[2560,256]{1,0:T(8,128)(2,1)}, bf16[2560,256]{1,0:T(8,128)(2,1)}, bf16[2560,256]{1,0:T(8,128)(2,1)}, bf16[2560,1024]{1,0:T(8,128)(2,1)},...) custom-call(s32[1,2]{1,0:T(1,128)} %b_ref.3, ...), custom_call_target="tpu_custom_call" | custom-call | flops 40265318400 | bytes 10485760 | tf_op jit(solution)/shard_map/self_backward/pallas_call | solution.py:1397
  381.5 67.5 %tail.1 = (f32[640,1024]{1,0:T(8,128)}, f32[128,1024]{1,0:T(8,128)}, f32[18,1024]{1,0:T(8,128)}, f32[128,1024]{1,0:T(8,128)}, f32[256,1024]{1,0:T(8,128)}) custom-call(bf16[2560,256]{1,0:T(8,128)(2,1)} %get-tuple-element.128.dq_ref, bf16[2560,256]{1,0:T(8,128)(2,1)} %get-tuple-element.129.dk_ref, bf16[2560,256]{1,0:T(8,128)(2,1)} %get-tuple-element.130.dv_ref, ...), custom_call_target="tpu_custom_call" | custom-call | bytes 104857600 | tf_op jit(solution)/shard_map/tail/pallas_call | solution.py:748
  449.1 6.9 %results.1 = (f32[640,1024]{1,0:T(8,128)}, f32[640,1024]{1,0:T(8,128)}, f32[256,1024]{1,0:T(8,128)}, f32[128,3,256]{2,1,0:T(4,128)}, f32[256,128]{1,0:T(8,128)},...) custom-call(f32[640,1024]{1,0:T(8,128)} %get-tuple-element.105.outpu, ...), custom_call_target="tpu_custom_call" | custom-call | bytes 20971520 | tf_op jit(solution)/shard_map/results/pallas_call | solution.py:824
  456.0 1.9 copy.29

commit v17 on v16

--- a/solution.py
+++ b/solution.py
@@ -460,7 +460,11 @@
 
         self.loads = [links.local(rows(0), self.near), links.local(rows(2), self.far)]
         self.core = [links.copy(rows(3), self.got_far, CORE), links.copy(rows(1), self.got_near, CORE)]
-        self.over_x = None if self.got_x is None else links.copy(self.far, self.got_x, X)
+        half = count // 2
+        self.parts = [pl.ds(0, half), pl.ds(half, half)]
+        self.over_x = []
+        if self.got_x is not None:
+            self.over_x = [links.copy(self.far.at[part], self.got_x.at[part], X) for part in self.parts]
 
     def start(self):
         for copy in self.loads[::-1] + self.core:
@@ -470,21 +474,27 @@
         self.loads[1].wait()
         self.core[0].wait_recv()
 
-        def add(rows):
-            self.far[rows, :] = (self.far[rows, :].astype(F32) + self.got_far[rows, :].astype(F32)).astype(BF16)
-
-        by_rows(self.far.shape[0], 64, add)
-        self.over_x.start()
+        for part, copy in zip(self.parts, self.over_x):
+
+            def add(rows, part=part):
+                rows = pl.ds(pl.multiple_of(part.start + rows.start, 64), 64)
+                self.far[rows, :] = (self.far[rows, :].astype(F32) + self.got_far[rows, :].astype(F32)).astype(BF16)
+
+            by_rows(part.size, 64, add)
+            copy.start()
 
     def core_end(self):
         for copy in self.loads + self.core:
             copy.wait()
 
-    def end(self):
-        self.loads[0].wait()
-        self.core[1].wait_recv()
-        self.over_x.wait_recv()
-        for copy in self.core + [self.over_x]:
+    def end(self, k):
+        if k == 0:
+            self.loads[0].wait()
+            self.core[1].wait_recv()
+        self.over_x[k].wait_recv()
+
+    def drain(self):
+        for copy in self.core + self.over_x:
             copy.wait_send()
 
     def total(self, rows):
@@ -582,7 +592,7 @@
         collects.append(Collect(links, column, slot))
     stages = len(collects[0].stages)
     late = Direct(links, compact, late_tensor, late_dp, n)
-    early = Everywhere(links, sums, early_slots, [CORE] + z_ways(n) + [Y, X])
+    early = Everywhere(links, sums, early_slots, [CORE, Y, X] + z_ways(n))
     steps = len(early.copies)
     enc_x = links.copy(enc_far, enc_got, X)
     links.greet(direct_ways(n))
@@ -705,26 +715,28 @@
     cross_out[...] = cross_ref[cross.z].astype(F32)
     next_z(0)
     summed_y(1)
-    for step in range(1, steps - 2):
-        early.start(step)
-        early.finish(step)
+    early.start(1)
+    next_z(1)
+    early.finish(1)
     over_x[1].wait_recv()
     norm_back(parts[1])
-    next_z(1)
     lines = model // LANES
     for k in range(2 * lines):
         compact[k : k + 1, :] = held[k // lines : k // lines + 1, k % lines * LANES : (k % lines + 1) * LANES]
     late.start(0)
-    early.start(steps - 2)
+    early.start(2)
     last_z(0)
-    early.finish(steps - 2)
+    early.finish(2)
     late.finish(0)
     late.start(1)
-    early.start(steps - 1)
+    early.start(3)
     last_z(1)
-    early.finish(steps - 1)
+    early.finish(3)
+    for step in range(4, steps):
+        early.start(step)
+        early.finish(step)
+    late.finish(1)
     late_out[2:, :] = sums[steps]
-    late.finish(1)
     for k in range(2 * lines):
         late_out[k // lines : k // lines + 1, k % lines * LANES : (k % lines + 1) * LANES] = compact[k : k + 1, :]
     for copy in over_x + over_y + [core_near, core_far]:
@@ -1140,16 +1152,23 @@
     over_core[0].start()
     over_y.wait_recv()
     over_core[1].start()
-    rows_sum.end()
-    spread.onward()
-
-    def norm(rows):
-        after = rows_ref[rows, :].astype(F32) + rows_sum.total(rows) + biases_ref[2:3, :]
-        after_out[rows, :] = after
-        xhat, _ = normalized(after)
-        second_out[rows, :] = (xhat * norm_ref[1, 0:1, :] + norm_ref[1, 1:2, :]).astype(BF16)
-
-    by_rows(after_out.shape[0], 64, norm)
+
+    def norm(part):
+        def one(rows):
+            rows = pl.ds(pl.multiple_of(part.start + rows.start, 64), 64)
+            after = rows_ref[rows, :].astype(F32) + rows_sum.total(rows) + biases_ref[2:3, :]
+            after_out[rows, :] = after
+            xhat, _ = normalized(after)
+            second_out[rows, :] = (xhat * norm_ref[1, 0:1, :] + norm_ref[1, 1:2, :]).astype(BF16)
+
+        by_rows(part.size, 64, one)
+
+    for k, part in enumerate(rows_sum.parts):
+        rows_sum.end(k)
+        if k == 1:
+            spread.onward()
+        norm(part)
+    rows_sum.drain()
     over_y.wait_send()
     spread.end()
     over_z.wait()
@@ -1174,7 +1193,7 @@
         ],
         scratch_shapes=row_sum_scratch(count, model)
         + [pltpu.VMEM((m, r, c), BF16), pltpu.VMEM((2, 2, r, c), BF16)]
-        + link_scratch(7 + spread_z_copies(2 * m), 8),
+        + link_scratch(8 + spread_z_copies(2 * m), 8),
         compiler_params=pltpu.CompilerParams(
             vmem_limit_bytes=VMEM_LIMIT, collective_id=8, has_side_effects=True
         ),

time: 465 us -> 461 us (level)
  no operation moved by 1% of the time
where the time goes in v17:
time: 461 us; the launch traced here: 455 us
  Pallas kernels  450 us (98%)
    pallas_call x1, Pallas kernels, self_backward(): pl.pallas_call(functools.partial(self_backward_kernel, bq=bq, heads=heads...  69.8 us
    pallas_call x1, Pallas kernels, tail(): pl.pallas_call(functools.partial(tail_kernel, n=n, step_rows=512), in_spe...  64.9 us
    pallas_call x1, Pallas kernels, cross_backward(): pl.pallas_call(functools.partial(cross_backward_kernel, heads=heads, bk=2...  60 us
    pallas_call x1, Pallas kernels, start_gather(): pl.pallas_call(functools.partial(start_kernel, n=n), in_specs=[pl.BlockSp...  58.3 us
    pallas_call x1, Pallas kernels, feed_forward(): pl.pallas_call(functools.partial(feed_forward_kernel, chunks=chunks), gri...  53.2 us
    pallas_call x1, Pallas kernels, self_forward(): pl.pallas_call(functools.partial(self_forward_kernel, heads=heads, safe=s...  48.6 us
    pallas_call x1, Pallas kernels, sum_after_self(): pl.pallas_call(functools.partial(after_self_kernel, n=2 * m), in_specs=[A...  46.2 us
    pallas_call x1, Pallas kernels, cross_forward(): pl.pallas_call(functools.partial(cross_forward_kernel, heads=heads, n=2 *...  41.6 us

profile of v17, /device:TPU:0, one launch (start us, length us, event | category | flops | bytes accessed | tf_op | source)
XLA Modules:
  0.0 454.8 jit_solution(7925478516333092156)
XLA Ops:
  1.3 1.8 copy.28.qkv_ref
  3.1 58.3 %start_gather.1 = (bf16[2560,1024]{1,0:T(8,128)(2,1)}, bf16[4,2,128,1024]{3,2,1,0:T(8,128)(2,1)}, bf16[4,128,1024]{2,1,0:T(8,128)(2,1)}, bf16[2,2,128,1024]{3,2,1,0:T(8,128)(2,1)}, bf16[1024,1024]{1,0:T(8,128)(2,1)}) custom-call(bf16[640,1024]{1,0:T(8,128)(2,1)} %rows_hbm.1, f32[3,2,1024]{2,1,0:T(2,128)} %norm_ref.11, bf16[128,3,256]{2,1,0:T(4,128)(2,1)} %copy.28.qkv_ref, ...), custom_call_target="tpu_custom_call" | custom-call | bytes 104857600 | tf_op jit(solution)/shard_map/start_gather/pallas_call | solution.py:947
  61.4 48.6 %self_forward.1 = (bf16[2560,256]{1,0:T(8,128)(2,1)}, bf16[2560,256]{1,0:T(8,128)(2,1)}, bf16[2560,256]{1,0:T(8,128)(2,1)}, bf16[256,2560]{1,0:T(8,128)(2,1)}, b...) custom-call(s32[1,2]{1,0:T(1,128)} %b_ref.3, ...), custom_call_target="tpu_custom_call" | custom-call | flops 20132659200 | bytes 5242880 | tf_op jit(solution)/shard_map/self_forward/pallas_call | solution.py:1071
  110.1 46.2 %sum_after_self.1 = (f32[640,1024]{1,0:T(8,128)}, bf16[640,1024]{1,0:T(8,128)(2,1)}, bf16[2,4,2,128,1024]{4,3,2,1,0:T(8,128)(2,1)}, bf16[2,4,2,128,1024]{4,3,2,1,0:T(8,128)(2,1)}, bf16[2,128,1024]{2,1,0:T(8,128)(2,1)}) custom-call(bf16[2560,1024]{1,0:T(8,128)(2,1)} %get-tuple-element.91.terms_ref, bf16[640,1024]{1,0:T(8,128)(2,1)} %rows_hbm.1, ...), custom_call_target="tpu_custom_call" | custom-call | bytes 104857600 | tf_op jit(solution)/shard_map/sum_after_self/pallas_call | solution.py:1183
  156.3 41.6 %cross_forward.1 = (bf16[4,640,256]{2,1,0:T(8,128)(2,1)}, bf16[4,1024,256]{2,1,0:T(8,128)(2,1)}, bf16[4,1024,256]{2,1,0:T(8,128)(2,1)}, bf16[4,256,640]{2,1,0:T(...) custom-call(s32[1]{0:T(128)S(6)} %copy.30.len_ref, ...), custom_call_target="tpu_custom_call" | custom-call | flops 16106127360 | bytes 8388608 | tf_op jit(solution)/shard_map/cross_forward/pallas_call | solution.py:1578
  197.9 53.2 %feed_forward.1 = (f32[640,1024]{1,0:T(8,128)}, f32[640,1024]{1,0:T(8,128)}, bf16[640,1024]{1,0:T(8,128)(2,1)}, f32[8,1024]{1,0:T(8,128)}, bf16[2,1024,1024]{2,1...) custom-call(bf16[640,1024]{1,0:T(8,128)(2,1)} %get-tuple-element.99., ...), custom_call_target="tpu_custom_call" | custom-call | flops 32212254720 | bytes 41943040 | tf_op jit(solution)/shard_map/feed_forward/pallas_call | solution.py:1777
  251.1 60.0 %cross_backward.1 = (f32[640,1024]{1,0:T(8,128)}, bf16[1024,1024]{1,0:T(8,128)(2,1)}, bf16[2,1024,1024]{2,1,0:T(8,128)(2,1)}, f32[4,1,256]{2,1,0:T(1,128)}, f32[...) custom-call(s32[1]{0:T(128)S(6)} %copy.30.len_ref, ...), custom_call_target="tpu_custom_call" | custom-call | flops 32212254720 | bytes 16777216 | tf_op jit(solution)/shard_map/cross_backward/pallas_call | solution.py:1943
  311.1 69.8 %self_backward.1 = (bf16[2560,256]{1,0:T(8,128)(2,1)}, bf16[2560,256]{1,0:T(8,128)(2,1)}, bf16[2560,256]{1,0:T(8,128)(2,1)}, bf16[2560,1024]{1,0:T(8,128)(2,1)},...) custom-call(s32[1,2]{1,0:T(1,128)} %b_ref.3, ...), custom_call_target="tpu_custom_call" | custom-call | flops 40265318400 | bytes 10485760 | tf_op jit(solution)/shard_map/self_backward/pallas_call | solution.py:1416
  380.9 64.9 %tail.1 = (f32[640,1024]{1,0:T(8,128)}, f32[128,1024]{1,0:T(8,128)}, f32[18,1024]{1,0:T(8,128)}, f32[128,1024]{1,0:T(8,128)}, f32[256,1024]{1,0:T(8,128)}) custom-call(bf16[2560,256]{1,0:T(8,128)(2,1)} %get-tuple-element.128.dq_ref, bf16[2560,256]{1,0:T(8,128)(2,1)} %get-tuple-element.129.dk_ref, bf16[2560,256]{1,0:T(8,128)(2,1)} %get-tuple-element.130.dv_ref, ...), custom_call_target="tpu_custom_call" | custom-call | bytes 104857600 | tf_op jit(solution)/shard_map/tail/pallas_call | solution.py:760
  445.8 6.9 %results.1 = (f32[640,1024]{1,0:T(8,128)}, f32[640,1024]{1,0:T(8,128)}, f32[256,1024]{1,0:T(8,128)}, f32[128,3,256]{2,1,0:T(4,128)}, f32[256,128]{1,0:T(8,128)},...) custom-call(f32[640,1024]{1,0:T(8,128)} %get-tuple-element.105.outpu, ...), custom_call_target="tpu_custom_call" | custom-call | bytes 20971520 | tf_op jit(solution)/shard_map/results/pallas_call | solution.py:836
  452.8 1.9 copy.29
